TPU v7x, 128 devices: a whole 4x4x4 slice. The times are simulated.
128 devices in a mesh: view: 2 (over z_lo), dp: 64 (over y, z_hi, x, core).
Axes of the slice: x: 4, y: 4, z: 4 (z_hi: 2, z_lo: 2; z = z_hi * 2 + z_lo), core: 2. Of those that a mesh axis runs over, the one named last changes fastest.
Arguments:
- hidden: bfloat16 [2, 896, 4096], P('view', 'dp')
- weight: bfloat16 [4096, 8192], P(None, 'dp')
Outputs:
- grad_hidden: float32 [2, 896, 4096], P('view', 'dp')
- grad_weight: float32 [4096, 8192], P(None, 'dp')
All inputs are finite; a program needn't handle non-finite values.
Results may differ from a plain program's by a relative error of at most 0.003.
Values may be sent and summed in bfloat16 or wider, within the bound.
No kernel may reach another device: no remote copies, remote signals or barrier semaphores. Data moves between devices by JAX's collectives and lax.ppermute only.
A program may use at most 128 MiB of HBM per device.

v0:
```python
import jax
import jax.numpy as jnp
from jax import lax
from jax.sharding import PartitionSpec as P


def from_partner(block, axis, apart):
    count = lax.axis_size(axis)
    route = []
    for low in range(count):
        high = low | 1 << apart
        if high != low and high < count:
            route += [(low, high), (high, low)]
    return lax.ppermute(block, axis, route)


def split_parts(values):
    upper = values.astype(jnp.bfloat16)
    lower = (values - upper.astype(jnp.float32)).astype(jnp.bfloat16)
    return (upper, lower)


def coupling_term(centered):
    segment = lax.all_gather(centered, "dp", axis=1, tiled=True)
    product_tile = lax.dot_general(
        centered, segment, (((0,), (0,)), ((), ())), preferred_element_type=jnp.float32
    )
    tile_upper, tile_lower = split_parts(product_tile)
    dims = (((1,), (1,)), ((), ()))
    running = lax.dot_general(segment, tile_upper, dims, preferred_element_type=jnp.float32)
    return running + lax.dot_general(segment, tile_lower, dims, preferred_element_type=jnp.float32)


def view_gradient(embedded, partner, weight):
    total_rows = embedded.shape[0]
    embed_wide = embedded.astype(jnp.float32)
    centered = (embed_wide - jnp.mean(embed_wide, axis=0, keepdims=True)).astype(jnp.bfloat16)
    centered_wide = centered.astype(jnp.float32)
    sum_squares = jnp.sum(centered_wide * centered_wide, axis=0, keepdims=True)
    spread_std = jnp.sqrt(sum_squares / (total_rows - 1) + 0.0001)
    coupled = coupling_term(centered)
    coef_var = total_rows / (2.0 * (total_rows - 1))
    coef_cov = 0.08 * total_rows / ((total_rows - 1) * (total_rows - 1))
    hinge_weight = jax.nn.sigmoid(10.0 * (1.0 - spread_std))
    combined = (
        embed_wide
        - partner.astype(jnp.float32)
        - coef_var * hinge_weight * centered_wide / spread_std
    )
    combined = combined + coef_cov * (coupled - centered_wide * sum_squares)
    grad_embed = combined.astype(jnp.bfloat16)
    grad_rows = lax.psum_scatter(
        lax.dot_general(
            grad_embed, weight, (((1,), (1,)), ((), ())), preferred_element_type=jnp.float32
        ),
        "dp",
        scatter_dimension=0,
        tiled=True,
    )
    return (grad_embed, grad_rows)


def on_device(hidden, weight):
    local_views = hidden.shape[0]
    gathered = lax.all_gather(hidden, "dp", axis=1, tiled=True)
    total_rows = gathered.shape[1]
    in_width = gathered.shape[2]
    flat = gathered.reshape(local_views * total_rows, in_width)
    embedded = jnp.dot(flat, weight, preferred_element_type=jnp.float32).astype(jnp.bfloat16)
    embedded = embedded.reshape(local_views, total_rows, weight.shape[1])
    partners = from_partner(embedded, "view", 0)
    grad_embed, grad_rows = view_gradient(embedded[0], partners[0], weight)
    grad_list = [grad_rows]
    weight_part = lax.dot_general(
        gathered[0], grad_embed, (((0,), (0,)), ((), ())), preferred_element_type=jnp.float32
    )
    grad_weight = lax.psum(weight_part, "view") / jnp.sqrt(2.0 * total_rows)
    return (jnp.stack(grad_list), grad_weight)


def solution(mesh):
    return jax.shard_map(
        on_device,
        mesh=mesh,
        in_specs=(P("view", "dp", None), P(None, "dp")),
        out_specs=(P("view", "dp", None), P(None, "dp")),
        check_vma=False,
    )
```

profile of v0, /device:TPU:1, one launch (start us, length us, event | category | flops | bytes accessed | tf_op | source)
XLA Modules:
  0.0 557.0 jit_solution(7315536405936615213)
XLA Ops:
  7.2 0.0 copy-start
  7.2 0.0 all-gather.3.cloned.1.call-start
  7.2 1.9 copy.9
  9.1 0.0 all-gather.3.cloned.1.call-update
  9.1 0.0 all-gather.5.cloned.1.call-start
  9.2 106.5 %all-gather.3.cloned.1.call-done = bf16[1,896,4096]{2,0,1:T(2,128)(2,1)} async-done(((bf16[1,14,4096]{2,0,1:T(2,128)(2,1)}), bf16[1,896,4096]{2,0,1:T(2,128)(2,1)}) %all-gather.3.cloned.1.call-update) | async-done | bytes 7340048 | tf_op jit(solution)/shard_map/all_gather | solution.py:65
  115.7 12.9 %convert_reduce_fusion = (f32[128]{0:T(128)S(1)}, bf16[896,128]{1,0:T(8,128)(2,1)S(1)}) fusion(bf16[4096,128]{1,0:T(8,128)(2,1)S(1)} %copy-done, bf16[1,896,4096]{2,0,1:T(2,128)(2,1)} %all-gather.3.cloned.1.call-done), kind=kOutput, calls=%fused_computation.21 | convolution fusion | flops 939868032 | bytes 8618496 | tf_op jit(solution)/shard_map/dot_general | solution.py:69
  128.6 0.8 fusion.24
  129.4 0.0 all-gather.5.cloned.1.call-update
  129.4 0.0 all-reduce.4.cloned.1.call-start
  129.5 0.6 collective-permute-start
  130.1 130.8 %all-gather.5.cloned.1.call-done = bf16[896,8192]{1,0:T(8,128)(2,1)} async-done(((bf16[896,128]{1,0:T(8,128)(2,1)}), bf16[896,8192]{1,0:T(8,128)(2,1)}) %all-gather.5.cloned.1.call-update) | async-done | bytes 14680080 | tf_op jit(solution)/shard_map/all_gather | solution.py:24
  260.9 8.0 %fusion.26 = f32[128,8192]{1,0:T(8,128)S(1)} fusion(bf16[896,8192]{1,0:T(8,128)(2,1)} %all-gather.5.cloned.1.call-done, bf16[896,128]{1,0:T(8,128)(2,1)S(1)} %get-tuple-element.13, f32[128]{0:T(128)S(1)} %broadcast_multiply_fusion.1), kind=kOutput, calls=%fused_computation.30 | convolution fusion | flops 1879392256 | bytes 19104256 | tf_op jit(solution)/shard_map/dot_general | solution.py:25
  268.9 1.4 copy-done.1
  270.3 3.9 fusion.18
  274.2 0.0 collective-permute-done
  274.2 4.2 fusion.22
  278.4 7.5 %fusion.28 = f32[896,4096]{1,0:T(8,128)} fusion(bf16[896,128]{1,0:T(8,128)(2,1)S(1)} %fusion.22, bf16[4096,128]{1,0:T(8,128)(2,1)S(1)} %copy-done), kind=kOutput, calls=%fused_computation.34 | convolution fusion | flops 939524096 | bytes 15958016 | tf_op jit(solution)/shard_map/dot_general | solution.py:53
  285.9 14.8 %fusion.5 = f32[4096,128]{0,1:T(8,128)} fusion(bf16[896,128]{1,0:T(8,128)(2,1)S(1)} %fusion.22, bf16[1,896,4096]{2,0,1:T(2,128)(2,1)} %all-gather.3.cloned.1.call-done), kind=kOutput, calls=%fused_computation.4 | convolution fusion | flops 939524096 | bytes 9666560 | tf_op jit(solution)/shard_map/dot_general | solution.py:74
  300.8 0.0 all-reduce.4.cloned.1.call-update
  300.8 0.0 copy-start.10
  300.8 189.0 %fusion = f32[16,4096]{1,0:T(8,128)S(1)} fusion(f32[896,4096]{1,0:T(8,128)} %fusion.28), kind=kCustom, calls=%all-reduce-scatter | all-reduce-scatter fusion | flops 4194305 | bytes 14942720
  489.8 1.9 collective-permute-start.1
  491.8 1.3 collective-permute-start.2
  493.1 1.3 collective-permute-start.8
  494.4 1.3 collective-permute-start.3
  495.7 1.3 collective-permute-start.4
  497.0 7.9 %collective-permute-done.8 = f32[14,4096]{1,0:T(8,128)S(1)} collective-permute-done((f32[14,4096]{1,0:T(8,128)S(1)}, f32[14,4096]{1,0:T(8,128)S(1)}, u32[]{:S(2)}, u32[]{:S(2)}) %collective-permute-start.8) | collective-permute-done | bytes 229408
  504.9 1.3 collective-permute-start.5
  506.2 0.0 collective-permute-done.1
  506.2 1.3 collective-permute-start.6
  507.5 0.0 collective-permute-done.2
  507.6 0.0 copy-done.3
  507.6 7.9 %collective-permute-start.7 = (f32[16,4096]{1,0:T(8,128)S(1)}, f32[16,4096]{1,0:T(8,128)}, u32[]{:S(2)}, u32[]{:S(2)}) collective-permute-start(f32[16,4096]{1,0:T(8,128)S(1)} %fusion), channel_id=1, source_target_pairs={{0,7},{1,8},{2,9},{3,10},{4,11},{5,12},{6,13},{7,14},{8,15},{9,16}... | collective-permute-start | bytes 786440
  515.5 0.6 dynamic-slice.4
  516.7 0.0 collective-permute-done.3
  516.8 0.0 collective-permute-done.4
  516.8 0.0 collective-permute-done.5
  516.8 0.0 collective-permute-done.6
  516.8 0.6 copy-done.6
  517.5 0.1 copy-done.7
  517.6 0.1 copy-done.8
  517.6 0.7 copy-done.9
  518.3 10.8 %collective-permute-done.7 = f32[16,4096]{1,0:T(8,128)} collective-permute-done((f32[16,4096]{1,0:T(8,128)S(1)}, f32[16,4096]{1,0:T(8,128)}, u32[]{:S(2)}, u32[]{:S(2)}) %collective-permute-start.7) | collective-permute-done | bytes 262176
  529.1 16.7 %concatenate = f32[142,4096]{1,0:T(8,128)S(1)} concatenate(f32[14,4096]{1,0:T(8,128)} %copy-done.5, f32[16,4096]{1,0:T(8,128)} %collective-permute-done.7, f32[16,4096]{1,0:T(8,128)} %copy-done.9, f32[16,4096]{1,0:T(8,128)} %copy-done.8, f32[16,4096]{1,0:T(8,128)} %copy-done.7, f32[16,4096]{1,0:T(8,128)} %copy-done.6, f32[16,4096]{1,0:T(8,128)} %copy-done.4, ...), dimensions={0} | concatenate | bytes 4653056
  545.9 0.9 copy.10
  546.8 1.8 broadcast_multiply_fusion
  548.6 1.8 copy.11
  (19 shorter events, 0.1 us)
Async XLA Ops:
  7.2 108.5 %copy-start = (bf16[4096,128]{1,0:T(8,128)(2,1)S(1)}, bf16[4096,128]{1,0:T(8,128)(2,1)}, u32[]{:S(2)}) copy-start(bf16[4096,128]{1,0:T(8,128)(2,1)} %param.3) | copy-start | bytes 3145732
  7.2 108.5 %all-gather.3.cloned.1.call-start = ((), (), s32[]{:S(2)}) async-start(), calls=%async_computation | async-start | bytes 14909440 | tf_op jit(solution)/shard_map/all_gather | solution.py:65
  9.1 251.8 %all-gather.5.cloned.1.call-start = ((), (), s32[]{:S(2)}) async-start(), calls=%async_computation.1 | async-start | bytes 14909440 | tf_op jit(solution)/shard_map/all_gather | solution.py:24
  129.4 417.4 %all-reduce.4.cloned.1.call-start = ((), (), s32[]{:S(2)}) async-start(), calls=%async_computation.2 | async-start | bytes 4194304 | tf_op jit(solution)/shard_map/psum | solution.py:77
  129.5 144.8 %collective-permute-start = (bf16[1,896,128]{2,1,0:T(8,128)(2,1)S(1)}, bf16[1,896,128]{2,1,0:T(8,128)(2,1)S(1)}, u32[]{:S(2)}, u32[]{:S(2)}) collective-permute-start(bf16[1,896,128]{2,1,0:T(8,128)(2,1)S(1)} %bitcast.29), channel_id=1, source_target_pairs={{0,64},{64,0},{1,65},{65,1},{2,66},{66,2},{3,67},{67,3},{4,68},{68... | collective-permute-start | bytes 688136 | tf_op jit(solution)/shard_map/ppermute | solution.py:14
  260.9 9.3 %copy-start.1 = (bf16[896,8192]{1,0:T(8,128)(2,1)S(1)}, bf16[896,8192]{1,0:T(8,128)(2,1)}, u32[]{:S(2)}) copy-start(bf16[896,8192]{1,0:T(8,128)(2,1)} %all-gather.5.cloned.1.call-done) | copy-start | bytes 44040196
  300.8 214.7 %copy-start.10 = (u32[128]{0:T(128)S(1)}, u32[128]{0:T(128)}, u32[]{:S(2)}) copy-start(u32[128]{0:T(128)} %constant.24) | copy-start | bytes 1540
  489.8 27.0 %copy-start.2 = (f32[16,4096]{1,0:T(8,128)}, f32[16,4096]{1,0:T(8,128)S(1)}, u32[]{:S(2)}) copy-start(f32[16,4096]{1,0:T(8,128)S(1)} %fusion) | copy-start | bytes 786436
  489.8 16.4 %collective-permute-start.1 = (f32[16,4096]{1,0:T(8,128)S(1)}, f32[16,4096]{1,0:T(8,128)S(1)}, u32[]{:S(2)}, u32[]{:S(2)}) collective-permute-start(f32[16,4096]{1,0:T(8,128)S(1)} %fusion), channel_id=1, source_target_pairs={{0,1},{1,2},{2,3},{3,4},{4,5},{5,6},{6,7},{7,8},{8,9},{9,10},{10,1... | collective-permute-start | bytes 786440
  491.8 15.8 %collective-permute-start.2 = (f32[16,4096]{1,0:T(8,128)S(1)}, f32[16,4096]{1,0:T(8,128)S(1)}, u32[]{:S(2)}, u32[]{:S(2)}) collective-permute-start(f32[16,4096]{1,0:T(8,128)S(1)} %fusion), channel_id=1, source_target_pairs={{0,2},{1,3},{2,4},{3,5},{4,6},{5,7},{6,8},{7,9},{8,10},{9,11},{10,... | collective-permute-start | bytes 786440
  493.1 11.8 %collective-permute-start.8 = (f32[14,4096]{1,0:T(8,128)S(1)}, f32[14,4096]{1,0:T(8,128)S(1)}, u32[]{:S(2)}, u32[]{:S(2)}) collective-permute-start(f32[14,4096]{1,0:T(8,128)S(1)} %slice), channel_id=1, source_target_pairs={{0,8},{1,9},{2,10},{3,11},{4,12},{5,13},{6,14},{7,15},{8,16},{9,17... | collective-permute-start | bytes 688136
  494.4 22.3 %collective-permute-start.3 = (f32[16,4096]{1,0:T(8,128)S(1)}, f32[16,4096]{1,0:T(8,128)S(1)}, u32[]{:S(2)}, u32[]{:S(2)}) collective-permute-start(f32[16,4096]{1,0:T(8,128)S(1)} %fusion), channel_id=1, source_target_pairs={{0,3},{1,4},{2,5},{3,6},{4,7},{5,8},{6,9},{7,10},{8,11},{9,12},{10... | collective-permute-start | bytes 786440
  495.7 21.0 %collective-permute-start.4 = (f32[16,4096]{1,0:T(8,128)S(1)}, f32[16,4096]{1,0:T(8,128)S(1)}, u32[]{:S(2)}, u32[]{:S(2)}) collective-permute-start(f32[16,4096]{1,0:T(8,128)S(1)} %fusion), channel_id=1, source_target_pairs={{0,4},{1,5},{2,6},{3,7},{4,8},{5,9},{6,10},{7,11},{8,12},{9,13},{1... | collective-permute-start | bytes 786440
  504.9 10.6 %copy-start.5 = (f32[14,4096]{1,0:T(8,128)}, f32[14,4096]{1,0:T(8,128)S(1)}, u32[]{:S(2)}) copy-start(f32[14,4096]{1,0:T(8,128)S(1)} %collective-permute-done.8) | copy-start | bytes 688132
  504.9 11.9 %collective-permute-start.5 = (f32[16,4096]{1,0:T(8,128)S(1)}, f32[16,4096]{1,0:T(8,128)S(1)}, u32[]{:S(2)}, u32[]{:S(2)}) collective-permute-start(f32[16,4096]{1,0:T(8,128)S(1)} %fusion), channel_id=1, source_target_pairs={{0,5},{1,6},{2,7},{3,8},{4,9},{5,10},{6,11},{7,12},{8,13},{9,14},{... | collective-permute-start | bytes 786440
  506.2 1.3 copy-start.3
  506.2 10.6 %collective-permute-start.6 = (f32[16,4096]{1,0:T(8,128)S(1)}, f32[16,4096]{1,0:T(8,128)S(1)}, u32[]{:S(2)}, u32[]{:S(2)}) collective-permute-start(f32[16,4096]{1,0:T(8,128)S(1)} %fusion), channel_id=1, source_target_pairs={{0,6},{1,7},{2,8},{3,9},{4,10},{5,11},{6,12},{7,13},{8,14},{9,15},... | collective-permute-start | bytes 786440
  507.6 7.9 %copy-start.4 = (f32[16,4096]{1,0:T(8,128)}, f32[16,4096]{1,0:T(8,128)S(1)}, u32[]{:S(2)}) copy-start(f32[16,4096]{1,0:T(8,128)S(1)} %collective-permute-done.2) | copy-start | bytes 786436
  507.6 21.6 %collective-permute-start.7 = (f32[16,4096]{1,0:T(8,128)S(1)}, f32[16,4096]{1,0:T(8,128)}, u32[]{:S(2)}, u32[]{:S(2)}) collective-permute-start(f32[16,4096]{1,0:T(8,128)S(1)} %fusion), channel_id=1, source_target_pairs={{0,7},{1,8},{2,9},{3,10},{4,11},{5,12},{6,13},{7,14},{8,15},{9,16}... | collective-permute-start | bytes 786440
  516.8 0.7 copy-start.6
  516.8 0.8 copy-start.7
  516.8 0.8 copy-start.8
  517.6 0.7 copy-start.9
Sparse Core Ops, SparseCore 0:
  11.7 103.9 all-gather.2
  129.6 131.3 all-gather.4
  300.9 131.0 all-reduce.3
where the time goes:
time: 560 us; the launch traced here: 557 us
  waiting for transfers between devices  256 us (46%)
  blocking collectives  189 us (34%)
  matrix products  51.4 us (9%)
  local copies, waits for them, and re-layouts  24.9 us (4%)
  starting transfers between devices  18.4 us (3%)
  between operations  14.7 us (3%)
    unnamed x1, blocking collectives  189 us
    all_gather x1, waiting for transfers between devices, coupling_term(): segment = lax.all_gather(centered, 'dp', axis=1, tiled=True)  131 us
    all_gather x1, waiting for transfers between devices, on_device(): gathered = lax.all_gather(hidden, 'dp', axis=1, tiled=True)  106 us
    unnamed x28, local copies, waits for them, and re-layouts  24.9 us
    unnamed x11, waiting for transfers between devices  18.7 us
    unnamed x8, starting transfers between devices  17.7 us
    dot_general x1, matrix products, on_device(): lax.dot_general(gathered[0], grad_embed, (((0,), (0,)), ((), ())), prefer...  14.8 us
    dot_general x1, matrix products, on_device(): jnp.dot(flat, weight, preferred_element_type=jnp.float32)  12.9 us
  transfers between devices with their start and end apart: 12, of which 4 were waited for; matrix products, arithmetic and copies ran while one was open for 39% of the time, Pallas kernels for 0%

commit v1 on v0

v1 whole, which is shorter than its diff:
```python
import jax
import jax.numpy as jnp
from jax import lax
from jax.sharding import PartitionSpec as P

YS, ZS, XS, CS = 4, 2, 4, 2
DP = YS * ZS * XS * CS
PAD = 16


def place(d):
    return (d // (ZS * XS * CS), d // (XS * CS) % ZS, d // CS % XS, d % CS)


def index(y, z, x, c):
    return ((y * ZS + z) * XS + x) * CS + c


def groups(axes):
    found = {}
    for d in range(DP):
        key = tuple(p for p, name in zip(place(d), "yzxc") if name not in axes)
        found.setdefault(key, []).append(d)
    return list(found.values())


def swap(block, view=0, z=0, c=0):
    route = []
    for v in range(2):
        for d in range(DP):
            y, zd, x, cd = place(d)
            route.append((v * DP + d, (v ^ view) * DP + index(y, zd ^ z, x, cd ^ c)))
    return lax.ppermute(block, ("view", "dp"), route)


def exchange(blocks, axes):
    return lax.all_to_all(blocks, "dp", 0, 0, tiled=True, axis_index_groups=groups(axes))


def matmul(a, b, a_dim, b_dim):
    return lax.dot_general(
        a, b, (((a_dim,), (b_dim,)), ((), ())), preferred_element_type=jnp.float32
    )


def rounded(values):
    return lax.optimization_barrier(values.astype(jnp.bfloat16))


def flip(block):
    n = block.shape[1] // 128
    runs = [block[:, 128 * (i ^ 1) : 128 * (i ^ 1) + 128] for i in range(n)]
    return jnp.concatenate(runs, axis=1)


def ordered(first, second, swapped):
    return jnp.where(
        swapped,
        jnp.concatenate([second, first], axis=0),
        jnp.concatenate([first, second], axis=0),
    )


def on_device(hidden, weight):
    rows = hidden.shape[1]
    samples = rows * DP
    half = hidden.shape[2] // 2
    units = weight.shape[1]
    d = lax.axis_index("dp")
    core = d % CS
    z = d // (XS * CS) % ZS

    w_own = lax.dynamic_slice(weight, (core * half, 0), (half, units))
    w_give = lax.dynamic_slice(weight, ((1 - core) * half, 0), (half, units))
    w_far = swap(w_own, view=1, z=1)
    w_far_sib = swap(w_give, view=1, z=1, c=1)
    w_sib = swap(w_give, c=1)

    padded = jnp.pad(hidden[0], ((0, PAD - rows), (0, 0)))
    halves = padded.reshape(PAD, 2, half).transpose(1, 0, 2)
    copies = jnp.broadcast_to(halves[None], (YS * XS, 2, PAD, half))
    plane = exchange(copies.reshape(YS * XS * 2 * PAD, half), "yxc")
    other_plane = swap(plane, z=1)
    span = plane.shape[0]

    w_all = jnp.concatenate([w_own, w_sib, w_far, w_far_sib], axis=1)
    part = matmul(plane, w_all, 1, 0)
    embedded = rounded(part + flip(swap(part, c=1)))
    chip = 2 * units
    from_other = swap(embedded[:, chip:], z=1)
    embedded = ordered(embedded[:, :chip], from_other, z == 1)

    wide = embedded.astype(jnp.float32)
    real = (lax.broadcasted_iota(jnp.int32, (2 * span, 1), 0) % PAD) < rows
    mean = jnp.sum(wide, axis=0, keepdims=True) / samples
    centered = rounded(jnp.where(real, wide - mean, 0.0))
    centered_wide = centered.astype(jnp.float32)
    sum_squares = jnp.sum(centered_wide * centered_wide, axis=0, keepdims=True)
    spread_std = jnp.sqrt(sum_squares / (samples - 1) + 0.0001)

    embedded_half = lax.dynamic_slice(embedded, (core * span, 0), (span, chip))
    partner = swap(embedded_half, view=1)
    centered_half = lax.dynamic_slice(centered, (core * span, 0), (span, chip))

    gram = matmul(centered_half, centered, 1, 1).astype(jnp.bfloat16)
    gram = exchange(gram, "yzx").reshape(YS * ZS * XS, PAD, 2 * span)
    gram = jnp.sum(gram.astype(jnp.float32), axis=0).astype(jnp.bfloat16)
    gram = jnp.broadcast_to(gram[None], (YS * ZS * XS, PAD, 2 * span))
    gram = exchange(gram.reshape(span, 2 * span), "yzx")
    coupled = matmul(gram, centered, 1, 0)

    coef_var = samples / (2.0 * (samples - 1))
    coef_cov = 0.08 * samples / ((samples - 1) * (samples - 1))
    hinge = jax.nn.sigmoid(10.0 * (1.0 - spread_std))
    wide_half = centered_half.astype(jnp.float32)
    combined = (
        embedded_half.astype(jnp.float32)
        - partner.astype(jnp.float32)
        - coef_var * hinge * wide_half / spread_std
        + coef_cov * (coupled - wide_half * sum_squares)
    )
    grad = rounded(combined)
    grad = ordered(grad, flip(swap(grad, c=1)), core == 1)
    grad_plane = lax.dynamic_slice(grad, (z * span, 0), (span, chip))
    grad_other = lax.dynamic_slice(grad, ((1 - z) * span, 0), (span, chip))
    grad_far = swap(grad_other, z=1)

    w_part = rounded(matmul(plane, grad_plane, 0, 0) + matmul(other_plane, grad_other, 0, 0))
    mine = w_part[:, :units]
    theirs = w_part[:, units:]
    mine_view = swap(mine, view=1)
    sib_view = swap(theirs, view=1, c=1)
    sib = swap(theirs, c=1)

    grad_all = jnp.concatenate([grad_plane, grad_far], axis=1)
    h_part = matmul(grad_all, w_all, 1, 1).astype(jnp.bfloat16)
    pieces = exchange(h_part, "yxc").reshape(YS * XS, 2, PAD, half)
    total = jnp.sum(pieces.astype(jnp.float32), axis=0)
    grad_rows = total.transpose(1, 0, 2).reshape(PAD, 2 * half)[:rows]

    wide_sum = lambda a, b: a.astype(jnp.float32) + b.astype(jnp.float32)
    grad_weight = ordered(wide_sum(mine, mine_view), wide_sum(sib, sib_view), core == 1)
    return (grad_rows[None], grad_weight / jnp.sqrt(2.0 * samples))


def solution(mesh):
    return jax.shard_map(
        on_device,
        mesh=mesh,
        in_specs=(P("view", "dp", None), P(None, "dp")),
        out_specs=(P("view", "dp", None), P(None, "dp")),
        check_vma=False,
    )
```

time: 560 us -> 209 us (0.37)
  blocking collectives: 189 us -> 22.2 us
  waiting for transfers between devices: 256 us -> 122 us
  matrix products: 51.4 us -> 11.6 us
  starting transfers between devices: 18.4 us -> 40.4 us
  local copies, waits for them, and re-layouts: 24.9 us -> 6 us
  between operations: 14.7 us -> 0.9 us
    all_gather x2 -> x0, waiting for transfers between devices: 237 us -> none  [the longest x1 131 us: coupling_term(): segment = lax.all_gather(centered, 'dp', axis=1, tiled=True)]
    unnamed x1 -> x0, blocking collectives: 189 us -> none
    ppermute x1 -> x12, waiting for transfers between devices: 0.01 us -> 120 us  [swap(): return lax.ppermute(block, ('view', 'dp'), route)]
    dot_general x6, matrix products: 51.4 us -> 11.6 us  [matmul(): lax.dot_general(a, b, (((a_dim,), (b_dim,)), ((), ())), preferred_element...]
    unnamed x28 -> x16, local copies, waits for them, and re-layouts: 24.9 us -> 0.74 us
    all_to_all x0 -> x1, blocking collectives: none -> 22.2 us  [exchange(): lax.all_to_all(blocks, 'dp', 0, 0, tiled=True, axis_index_groups=groups(a...]
    all_to_all x0 -> x3, starting transfers between devices: none -> 20.3 us  [exchange(): lax.all_to_all(blocks, 'dp', 0, 0, tiled=True, axis_index_groups=groups(a...]
    ppermute x1 -> x12, starting transfers between devices: 0.64 us -> 20.1 us  [swap(): return lax.ppermute(block, ('view', 'dp'), route)]
  transfers between devices with their start and end apart: 12 -> 15, of which waited for: 4 -> 11; matrix products, arithmetic and copies ran while one was open for 39% -> 4% of each run, Pallas kernels for 0% -> 0%
where the time goes in v1:
time: 209 us; the launch traced here: 207 us
  waiting for transfers between devices  122 us (58%)
  starting transfers between devices  40.4 us (19%)
  blocking collectives  22.2 us (11%)
  matrix products  11.6 us (6%)
  local copies, waits for them, and re-layouts  6 us (3%)
  other arithmetic  4.64 us (2%)
    ppermute x12, waiting for transfers between devices, swap(): return lax.ppermute(block, ('view', 'dp'), route)  120 us
    all_to_all x1, blocking collectives, exchange(): lax.all_to_all(blocks, 'dp', 0, 0, tiled=True, axis_index_groups=groups(a...  22.2 us
    all_to_all x3, starting transfers between devices, exchange(): lax.all_to_all(blocks, 'dp', 0, 0, tiled=True, axis_index_groups=groups(a...  20.3 us
    ppermute x12, starting transfers between devices, swap(): return lax.ppermute(block, ('view', 'dp'), route)  20.1 us
    dot_general x6, matrix products, matmul(): lax.dot_general(a, b, (((a_dim,), (b_dim,)), ((), ())), preferred_element...  11.6 us
  transfers between devices with their start and end apart: 15, of which 11 were waited for; matrix products, arithmetic and copies ran while one was open for 4% of the time, Pallas kernels for 0%

profile of v1, /device:TPU:1, one launch (start us, length us, event | category | flops | bytes accessed | tf_op | source)
XLA Modules:
  0.0 207.3 jit_solution(14922516982362333260)
XLA Ops:
  0.6 0.9 pad.4
  1.6 0.1 reshape.76
  1.7 1.6 broadcast_in_dim.18
  3.3 8.7 %all-to-all-start = ((bf16[32,16,2048]{2,1,0:T(8,128)(2,1)}), bf16[32,16,2048]{2,1,0:T(8,128)(2,1)S(1)}, u32[]{:S(2)}, u32[]{:S(2)}) async-start(bf16[32,16,2048]{2,1,0:T(8,128)(2,1)} %bitcast.22), calls=%async_computation | async-start | bytes 4194304 | tf_op jit(solution)/shard_map/all_to_all | solution.py:37
  12.1 4.0 %collective-permute-start.2 = (bf16[2048,128]{1,0:T(8,128)(2,1)S(1)}, bf16[2048,128]{1,0:T(8,128)(2,1)S(1)}, u32[]{:S(2)}, u32[]{:S(2)}) collective-permute-start(bf16[2048,128]{1,0:T(8,128)(2,1)S(1)} %get-tuple-element.13), channel_id=1, source_target_pairs={{0,73},{1,72},{2,75},{3,74},{4,77},{5,76},{6,79},{7,78},{8,65},{9,... | collective-permute-start | bytes 1572872 | tf_op jit(solution)/shard_map/ppermute | solution.py:33
  16.1 0.5 collective-permute-start
  16.6 12.2 %collective-permute-done.2 = bf16[2048,128]{1,0:T(8,128)(2,1)S(1)} collective-permute-done((bf16[2048,128]{1,0:T(8,128)(2,1)S(1)}, bf16[2048,128]{1,0:T(8,128)(2,1)S(1)}, u32[]{:S(2)}, u32[]{:S(2)}) %collective-permute-start.2) | collective-permute-done | bytes 524320 | tf_op jit(solution)/shard_map/ppermute | solution.py:33
  28.8 10.6 %collective-permute-done.1 = bf16[2048,128]{1,0:T(8,128)(2,1)S(1)} collective-permute-done((bf16[2048,128]{1,0:T(8,128)(2,1)S(1)}, bf16[2048,128]{1,0:T(8,128)(2,1)S(1)}, u32[]{:S(2)}, u32[]{:S(2)}) %collective-permute-start.1) | collective-permute-done | bytes 524320 | tf_op jit(solution)/shard_map/ppermute | solution.py:33
  39.3 0.5 all-to-all-done
  39.8 2.4 %fusion.13 = f32[512,512]{1,0:T(8,128)S(1)} fusion(bf16[512,2048]{1,0:T(8,128)(2,1)S(1)} %bitcast.19, bf16[2048,128]{1,0:T(8,128)(2,1)S(1)} %collective-permute-done.2, bf16[2048,128]{1,0:T(8,128)(2,1)S(1)} %collective-permute-done.1, bf16[2048,128]{1,0:T(8,128)(2,1)} %collective-permute-done, bf16[2048,128]{1,0:T(8,128)(2,1)} %copy-done.1), kind=kOutput, calls=%fused_computation.30 | convolution fusion | flops 1082130432 | bytes 5242880 | tf_op jit(solution)/shard_map/dot_general | solution.py:41
  42.3 2.5 %collective-permute-start.3 = (f32[512,512]{1,0:T(8,128)S(1)}, f32[512,512]{1,0:T(8,128)S(1)}, u32[]{:S(2)}, u32[]{:S(2)}) collective-permute-start(f32[512,512]{1,0:T(8,128)S(1)} %fusion.13), channel_id=1, source_target_pairs={{0,1},{1,0},{2,3},{3,2},{4,5},{5,4},{6,7},{7,6},{8,9},{9,8},{10,11... | collective-permute-start | bytes 3145736 | tf_op jit(solution)/shard_map/ppermute | solution.py:33
  44.8 2.3 %collective-permute-done.3 = f32[512,512]{1,0:T(8,128)S(1)} collective-permute-done((f32[512,512]{1,0:T(8,128)S(1)}, f32[512,512]{1,0:T(8,128)S(1)}, u32[]{:S(2)}, u32[]{:S(2)}) %collective-permute-start.3) | collective-permute-done | bytes 1048608 | tf_op jit(solution)/shard_map/ppermute | solution.py:33
  47.1 0.2 fusion.5
  47.4 3.7 %collective-permute-start.4 = (bf16[512,256]{1,0:T(8,128)(2,1)S(1)}, bf16[512,256]{1,0:T(8,128)(2,1)S(1)}, u32[]{:S(2)}, u32[]{:S(2)}) collective-permute-start(bf16[512,256]{1,0:T(8,128)(2,1)S(1)} %get-tuple-element.17), channel_id=1, source_target_pairs={{0,8},{1,9},{2,10},{3,11},{4,12},{5,13},{6,14},{7,15},{8,0},{9,1},... | collective-permute-start | bytes 786440 | tf_op jit(solution)/shard_map/ppermute | solution.py:33
  51.1 6.4 %collective-permute-done.4 = bf16[512,256]{1,0:T(8,128)(2,1)S(1)} collective-permute-done((bf16[512,256]{1,0:T(8,128)(2,1)S(1)}, bf16[512,256]{1,0:T(8,128)(2,1)S(1)}, u32[]{:S(2)}, u32[]{:S(2)}) %collective-permute-start.4) | collective-permute-done | bytes 262176 | tf_op jit(solution)/shard_map/ppermute | solution.py:33
  57.4 0.3 convert_reduce_fusion.1
  57.7 0.2 fusion.4
  57.9 0.5 convolution_convert_fusion.1
  58.4 22.2 %all_to_all.39 = bf16[32,16,1024]{2,1,0:T(8,128)(2,1)} all-to-all(bf16[32,16,1024]{2,1,0:T(8,128)(2,1)S(1)} %bitcast.24), channel_id=1, replica_groups={{0,2,4,6,8,10,12,14,16,18,20,22,24,26,28,30,32,34,36,38,40,42,44,46,48,..., dimensions={0} | all-to-all | bytes 2097152 | tf_op jit(solution)/shard_map/all_to_all | solution.py:37
  80.6 1.4 reduce_sum.41
  81.9 1.1 broadcast_in_dim.32
  83.0 4.7 %all-to-all-start.2 = ((bf16[32,16,1024]{2,1,0:T(8,128)(2,1)}), bf16[32,16,1024]{2,1,0:T(8,128)(2,1)}, u32[]{:S(2)}, u32[]{:S(2)}) async-start(bf16[32,16,1024]{2,1,0:T(8,128)(2,1)} %broadcast_in_dim.32), calls=%async_computation.2 | async-start | bytes 2097152 | tf_op jit(solution)/shard_map/all_to_all | solution.py:37
  87.8 2.7 %collective-permute-start.8 = (bf16[512,2048]{1,0:T(8,128)(2,1)S(1)}, bf16[512,2048]{1,0:T(8,128)(2,1)}, u32[]{:S(2)}, u32[]{:S(2)}) collective-permute-start(bf16[512,2048]{1,0:T(8,128)(2,1)S(1)} %bitcast.20), channel_id=1, source_target_pairs={{0,8},{1,9},{2,10},{3,11},{4,12},{5,13},{6,14},{7,15},{8,0},{9,1},... | collective-permute-start | bytes 6291464 | tf_op jit(solution)/shard_map/ppermute | solution.py:33
  90.6 1.6 collective-permute-start.5
  92.1 0.2 multiply_reduce_fusion
  92.3 60.7 %collective-permute-done.5 = bf16[512,256]{1,0:T(8,128)(2,1)S(1)} collective-permute-done((bf16[512,256]{1,0:T(8,128)(2,1)S(1)}, bf16[512,256]{1,0:T(8,128)(2,1)S(1)}, u32[]{:S(2)}, u32[]{:S(2)}) %collective-permute-start.5) | collective-permute-done | bytes 262176 | tf_op jit(solution)/shard_map/ppermute | solution.py:33
  153.0 0.7 copy-done.7
  153.7 1.7 fusion.12
  155.4 1.3 collective-permute-start.6
  156.7 1.2 collective-permute-done.6
  157.9 0.2 maximum_select_fusion.2
  158.2 1.9 collective-permute-start.7
  160.1 0.8 fusion.26
  160.9 2.5 %fusion = bf16[2048,256]{1,0:T(8,128)(2,1)S(1)} fusion(f32[2048,256]{1,0:T(8,128)S(1)} %fusion.26, bf16[512,2048]{1,0:T(8,128)(2,1)} %collective-permute-done.8, bf16[512,256]{1,0:T(8,128)(2,1)S(1)} %get-tuple-element.15), kind=kOutput, calls=%fused_computation.3 | convolution fusion | flops 537919488 | bytes 5505024 | tf_op jit(solution)/shard_map/dot_general | solution.py:41
  163.4 3.9 %collective-permute-done.7 = bf16[512,256]{1,0:T(8,128)(2,1)S(1)} collective-permute-done((bf16[512,256]{1,0:T(8,128)(2,1)S(1)}, bf16[512,256]{1,0:T(8,128)(2,1)S(1)}, u32[]{:S(2)}, u32[]{:S(2)}) %collective-permute-start.7) | collective-permute-done | bytes 262176 | tf_op jit(solution)/shard_map/ppermute | solution.py:33
  167.3 3.7 %convolution_convert_fusion = bf16[512,2048]{1,0:T(8,128)(2,1)} fusion(bf16[512,256]{1,0:T(8,128)(2,1)S(1)} %collective-permute-done.7, bf16[512,256]{1,0:T(8,128)(2,1)S(1)} %get-tuple-element.14, bf16[2048,128]{1,0:T(8,128)(2,1)S(1)} %copy-done.4, bf16[2048,128]{1,0:T(8,128)(2,1)S(1)} %copy-done.6, bf16[2048,128]{1,0:T(8,128)(2,1)} %collective-permute-done, ...), kind=kOutput, calls=%fused_computation.1 | convolution fusion | flops 1084227584 | bytes 4718592 | tf_op jit(solution)/shard_map/dot_general | solution.py:41
  171.0 6.9 %all-to-all-start.3 = ((bf16[32,16,2048]{2,1,0:T(8,128)(2,1)}), bf16[32,16,2048]{2,1,0:T(8,128)(2,1)S(1)}, u32[]{:S(2)}, u32[]{:S(2)}) async-start(bf16[32,16,2048]{2,1,0:T(8,128)(2,1)} %bitcast.25), calls=%async_computation.3 | async-start | bytes 4194304 | tf_op jit(solution)/shard_map/all_to_all | solution.py:37
  177.9 0.1 collective-permute-start.11
  178.0 1.9 collective-permute-start.10
  179.9 11.4 %collective-permute-done.11 = bf16[2048,128]{1,0:T(8,128)(2,1)S(1)} collective-permute-done((bf16[2048,128]{1,0:T(8,128)(2,1)S(1)}, bf16[2048,128]{1,0:T(8,128)(2,1)S(1)}, u32[]{:S(2)}, u32[]{:S(2)}) %collective-permute-start.11) | collective-permute-done | bytes 524320 | tf_op jit(solution)/shard_map/ppermute | solution.py:33
  191.3 0.1 convert_add_fusion
  191.4 11.7 %collective-permute-done.10 = bf16[2048,128]{1,0:T(8,128)(2,1)S(1)} collective-permute-done((bf16[2048,128]{1,0:T(8,128)(2,1)S(1)}, bf16[2048,128]{1,0:T(8,128)(2,1)S(1)}, u32[]{:S(2)}, u32[]{:S(2)}) %collective-permute-start.10) | collective-permute-done | bytes 524320 | tf_op jit(solution)/shard_map/ppermute | solution.py:33
  203.1 0.1 convert_add_fusion.1
  203.3 1.6 fusion.1
  204.8 0.9 all-to-all-done.3
  205.7 0.4 convert_reduce_fusion
  206.1 0.2 copy.7
  206.3 1.0 broadcast_in_dim.34
  (32 shorter events, 0.5 us)
Async XLA Ops:
  3.3 8.8 %copy-start = (bf16[4096,128]{1,0:T(8,128)(2,1)S(1)}, bf16[4096,128]{1,0:T(8,128)(2,1)}, u32[]{:S(2)}) copy-start(bf16[4096,128]{1,0:T(8,128)(2,1)} %param.3) | copy-start | bytes 3145732
  3.3 36.6 %all-to-all-start = ((bf16[32,16,2048]{2,1,0:T(8,128)(2,1)}), bf16[32,16,2048]{2,1,0:T(8,128)(2,1)S(1)}, u32[]{:S(2)}, u32[]{:S(2)}) async-start(bf16[32,16,2048]{2,1,0:T(8,128)(2,1)} %bitcast.22), calls=%async_computation | async-start | bytes 4194304 | tf_op jit(solution)/shard_map/all_to_all | solution.py:37
  12.1 27.2 %copy-start.1 = (bf16[2048,128]{1,0:T(8,128)(2,1)}, bf16[2048,128]{1,0:T(8,128)(2,1)S(1)}, u32[]{:S(2)}) copy-start(bf16[2048,128]{1,0:T(8,128)(2,1)S(1)} %get-tuple-element.12) | copy-start | bytes 1572868
  12.1 16.6 %collective-permute-start.2 = (bf16[2048,128]{1,0:T(8,128)(2,1)S(1)}, bf16[2048,128]{1,0:T(8,128)(2,1)S(1)}, u32[]{:S(2)}, u32[]{:S(2)}) collective-permute-start(bf16[2048,128]{1,0:T(8,128)(2,1)S(1)} %get-tuple-element.13), channel_id=1, source_target_pairs={{0,73},{1,72},{2,75},{3,74},{4,77},{5,76},{6,79},{7,78},{8,65},{9,... | collective-permute-start | bytes 1572872 | tf_op jit(solution)/shard_map/ppermute | solution.py:33
  16.1 23.2 %collective-permute-start.1 = (bf16[2048,128]{1,0:T(8,128)(2,1)S(1)}, bf16[2048,128]{1,0:T(8,128)(2,1)S(1)}, u32[]{:S(2)}, u32[]{:S(2)}) collective-permute-start(bf16[2048,128]{1,0:T(8,128)(2,1)S(1)} %get-tuple-element.12), channel_id=1, source_target_pairs={{0,72},{1,73},{2,74},{3,75},{4,76},{5,77},{6,78},{7,79},{8,64},{9,... | collective-permute-start | bytes 1572872 | tf_op jit(solution)/shard_map/ppermute | solution.py:33
  16.1 23.3 %collective-permute-start = (bf16[2048,128]{1,0:T(8,128)(2,1)S(1)}, bf16[2048,128]{1,0:T(8,128)(2,1)}, u32[]{:S(2)}, u32[]{:S(2)}) collective-permute-start(bf16[2048,128]{1,0:T(8,128)(2,1)S(1)} %get-tuple-element.13), channel_id=1, source_target_pairs={{0,1},{1,0},{2,3},{3,2},{4,5},{5,4},{6,7},{7,6},{8,9},{9,8},{10,11... | collective-permute-start | bytes 1572872 | tf_op jit(solution)/shard_map/ppermute | solution.py:33
  28.8 13.5 %copy-start.3 = (bf16[2048,128]{1,0:T(8,128)(2,1)}, bf16[2048,128]{1,0:T(8,128)(2,1)S(1)}, u32[]{:S(2)}) copy-start(bf16[2048,128]{1,0:T(8,128)(2,1)S(1)} %collective-permute-done.2) | copy-start | bytes 1572868
  39.3 3.0 %copy-start.5 = (bf16[2048,128]{1,0:T(8,128)(2,1)}, bf16[2048,128]{1,0:T(8,128)(2,1)S(1)}, u32[]{:S(2)}) copy-start(bf16[2048,128]{1,0:T(8,128)(2,1)S(1)} %collective-permute-done.1) | copy-start | bytes 1572868
  42.3 4.7 %collective-permute-start.3 = (f32[512,512]{1,0:T(8,128)S(1)}, f32[512,512]{1,0:T(8,128)S(1)}, u32[]{:S(2)}, u32[]{:S(2)}) collective-permute-start(f32[512,512]{1,0:T(8,128)S(1)} %fusion.13), channel_id=1, source_target_pairs={{0,1},{1,0},{2,3},{3,2},{4,5},{5,4},{6,7},{7,6},{8,9},{9,8},{10,11... | collective-permute-start | bytes 3145736 | tf_op jit(solution)/shard_map/ppermute | solution.py:33
  47.4 10.1 %collective-permute-start.4 = (bf16[512,256]{1,0:T(8,128)(2,1)S(1)}, bf16[512,256]{1,0:T(8,128)(2,1)S(1)}, u32[]{:S(2)}, u32[]{:S(2)}) collective-permute-start(bf16[512,256]{1,0:T(8,128)(2,1)S(1)} %get-tuple-element.17), channel_id=1, source_target_pairs={{0,8},{1,9},{2,10},{3,11},{4,12},{5,13},{6,14},{7,15},{8,0},{9,1},... | collective-permute-start | bytes 786440 | tf_op jit(solution)/shard_map/ppermute | solution.py:33
  83.0 69.9 %all-to-all-start.2 = ((bf16[32,16,1024]{2,1,0:T(8,128)(2,1)}), bf16[32,16,1024]{2,1,0:T(8,128)(2,1)}, u32[]{:S(2)}, u32[]{:S(2)}) async-start(bf16[32,16,1024]{2,1,0:T(8,128)(2,1)} %broadcast_in_dim.32), calls=%async_computation.2 | async-start | bytes 2097152 | tf_op jit(solution)/shard_map/all_to_all | solution.py:37
  87.8 73.1 %collective-permute-start.8 = (bf16[512,2048]{1,0:T(8,128)(2,1)S(1)}, bf16[512,2048]{1,0:T(8,128)(2,1)}, u32[]{:S(2)}, u32[]{:S(2)}) collective-permute-start(bf16[512,2048]{1,0:T(8,128)(2,1)S(1)} %bitcast.20), channel_id=1, source_target_pairs={{0,8},{1,9},{2,10},{3,11},{4,12},{5,13},{6,14},{7,15},{8,0},{9,1},... | collective-permute-start | bytes 6291464 | tf_op jit(solution)/shard_map/ppermute | solution.py:33
  90.6 62.4 %collective-permute-start.5 = (bf16[512,256]{1,0:T(8,128)(2,1)S(1)}, bf16[512,256]{1,0:T(8,128)(2,1)S(1)}, u32[]{:S(2)}, u32[]{:S(2)}) collective-permute-start(bf16[512,256]{1,0:T(8,128)(2,1)S(1)} %constant_dynamic-slice_fusion.2), channel_id=1, source_target_pairs={{0,64},{1,65},{2,66},{3,67},{4,68},{5,69},{6,70},{7,71},{8,72},{9,... | collective-permute-start | bytes 786440 | tf_op jit(solution)/shard_map/ppermute | solution.py:33
  153.0 0.7 copy-start.7
  155.4 2.4 %collective-permute-start.6 = (bf16[512,256]{1,0:T(8,128)(2,1)S(1)}, bf16[512,256]{1,0:T(8,128)(2,1)S(1)}, u32[]{:S(2)}, u32[]{:S(2)}) collective-permute-start(bf16[512,256]{1,0:T(8,128)(2,1)S(1)} %fusion.12), channel_id=1, source_target_pairs={{0,1},{1,0},{2,3},{3,2},{4,5},{5,4},{6,7},{7,6},{8,9},{9,8},{10,11... | collective-permute-start | bytes 786440 | tf_op jit(solution)/shard_map/ppermute | solution.py:33
  158.2 9.1 %collective-permute-start.7 = (bf16[512,256]{1,0:T(8,128)(2,1)S(1)}, bf16[512,256]{1,0:T(8,128)(2,1)S(1)}, u32[]{:S(2)}, u32[]{:S(2)}) collective-permute-start(bf16[512,256]{1,0:T(8,128)(2,1)S(1)} %get-tuple-element.15), channel_id=1, source_target_pairs={{0,8},{1,9},{2,10},{3,11},{4,12},{5,13},{6,14},{7,15},{8,0},{9,1},... | collective-permute-start | bytes 786440 | tf_op jit(solution)/shard_map/ppermute | solution.py:33
  160.9 6.4 %copy-start.2 = (bf16[2048,128]{1,0:T(8,128)(2,1)S(1)}, bf16[2048,128]{1,0:T(8,128)(2,1)}, u32[]{:S(2)}) copy-start(bf16[2048,128]{1,0:T(8,128)(2,1)} %copy-done.1) | copy-start | bytes 1572868
  160.9 6.4 %copy-start.4 = (bf16[2048,128]{1,0:T(8,128)(2,1)S(1)}, bf16[2048,128]{1,0:T(8,128)(2,1)}, u32[]{:S(2)}) copy-start(bf16[2048,128]{1,0:T(8,128)(2,1)} %copy-done.3) | copy-start | bytes 1572868
  160.9 6.4 %copy-start.6 = (bf16[2048,128]{1,0:T(8,128)(2,1)S(1)}, bf16[2048,128]{1,0:T(8,128)(2,1)}, u32[]{:S(2)}) copy-start(bf16[2048,128]{1,0:T(8,128)(2,1)} %copy-done.5) | copy-start | bytes 1572868
  171.0 34.7 %all-to-all-start.3 = ((bf16[32,16,2048]{2,1,0:T(8,128)(2,1)}), bf16[32,16,2048]{2,1,0:T(8,128)(2,1)S(1)}, u32[]{:S(2)}, u32[]{:S(2)}) async-start(bf16[32,16,2048]{2,1,0:T(8,128)(2,1)} %bitcast.25), calls=%async_computation.3 | async-start | bytes 4194304 | tf_op jit(solution)/shard_map/all_to_all | solution.py:37
  177.9 13.4 %collective-permute-start.11 = (bf16[2048,128]{1,0:T(8,128)(2,1)S(1)}, bf16[2048,128]{1,0:T(8,128)(2,1)S(1)}, u32[]{:S(2)}, u32[]{:S(2)}) collective-permute-start(bf16[2048,128]{1,0:T(8,128)(2,1)S(1)} %get-tuple-element.7), channel_id=1, source_target_pairs={{0,64},{1,65},{2,66},{3,67},{4,68},{5,69},{6,70},{7,71},{8,72},{9,... | collective-permute-start | bytes 1572872 | tf_op jit(solution)/shard_map/ppermute | solution.py:33
  178.0 25.1 %collective-permute-start.10 = (bf16[2048,128]{1,0:T(8,128)(2,1)S(1)}, bf16[2048,128]{1,0:T(8,128)(2,1)S(1)}, u32[]{:S(2)}, u32[]{:S(2)}) collective-permute-start(bf16[2048,128]{1,0:T(8,128)(2,1)S(1)} %get-tuple-element.6), channel_id=1, source_target_pairs={{0,65},{1,64},{2,67},{3,66},{4,69},{5,68},{6,71},{7,70},{8,73},{9,... | collective-permute-start | bytes 1572872 | tf_op jit(solution)/shard_map/ppermute | solution.py:33
  179.9 23.2 %collective-permute-start.9 = (bf16[2048,128]{1,0:T(8,128)(2,1)S(1)}, bf16[2048,128]{1,0:T(8,128)(2,1)S(1)}, u32[]{:S(2)}, u32[]{:S(2)}) collective-permute-start(bf16[2048,128]{1,0:T(8,128)(2,1)S(1)} %get-tuple-element.6), channel_id=1, source_target_pairs={{0,1},{1,0},{2,3},{3,2},{4,5},{5,4},{6,7},{7,6},{8,9},{9,8},{10,11... | collective-permute-start | bytes 1572872 | tf_op jit(solution)/shard_map/ppermute | solution.py:33

commit v2 on v1

v2 whole, which is shorter than its diff:
```python
import jax
import jax.numpy as jnp
from jax import lax
from jax.sharding import PartitionSpec as P

YS, ZS, XS, CS = 4, 2, 4, 2
DP = YS * ZS * XS * CS
PAD = 16


def place(d):
    return (d // (ZS * XS * CS), d // (XS * CS) % ZS, d // CS % XS, d % CS)


def index(y, z, x, c):
    return ((y * ZS + z) * XS + x) * CS + c


def groups(axes):
    found = {}
    for d in range(DP):
        key = tuple(p for p, name in zip(place(d), "yzxc") if name not in axes)
        found.setdefault(key, []).append(d)
    return list(found.values())


def swap(block, view=0, z=0, c=0):
    route = []
    for v in range(2):
        for d in range(DP):
            y, zd, x, cd = place(d)
            route.append((v * DP + d, (v ^ view) * DP + index(y, zd ^ z, x, cd ^ c)))
    return lax.ppermute(block, ("view", "dp"), route)


def exchange(blocks, axes):
    return lax.all_to_all(blocks, "dp", 0, 0, tiled=True, axis_index_groups=groups(axes))


def matmul(a, b, a_dim, b_dim):
    return lax.dot_general(
        a, b, (((a_dim,), (b_dim,)), ((), ())), preferred_element_type=jnp.float32
    )


def rounded(values):
    return lax.optimization_barrier(values.astype(jnp.bfloat16))


def flip(block):
    n = block.shape[1] // 2
    return jnp.concatenate([block[:, n:], block[:, :n]], axis=1)


def ordered(first, second, swapped):
    return jnp.where(
        swapped,
        jnp.concatenate([second, first], axis=0),
        jnp.concatenate([first, second], axis=0),
    )


def wide_sum(a, b):
    return a.astype(jnp.float32) + b.astype(jnp.float32)


def on_device(hidden, weight):
    rows = hidden.shape[1]
    samples = rows * DP
    half = hidden.shape[2] // 2
    units = weight.shape[1]
    d = lax.axis_index("dp")
    core = d % CS
    z = d // (XS * CS) % ZS

    w_own = lax.dynamic_slice(weight, (core * half, 0), (half, units))
    w_give = lax.dynamic_slice(weight, ((1 - core) * half, 0), (half, units))
    w_far = swap(w_own, view=1, z=1)
    w_far_sib = swap(w_give, view=1, z=1, c=1)
    w_sib = swap(w_give, c=1)

    padded = jnp.pad(hidden[0], ((0, PAD - rows), (0, 0)))
    halves = padded.reshape(PAD, 2, half).transpose(1, 0, 2)
    copies = jnp.broadcast_to(halves[None], (YS * XS, 2, PAD, half))
    plane = exchange(copies.reshape(YS * XS * 2 * PAD, half), "yxc")
    span = plane.shape[0]
    pair = 2 * units

    w_all = jnp.concatenate([w_own, w_far, w_sib, w_far_sib], axis=1)
    part = matmul(plane, w_all, 1, 0)
    embedded = rounded(part[:, :pair] + swap(part[:, pair:], c=1))
    from_other = swap(embedded, z=1)
    embedded = ordered(embedded, flip(from_other), z == 1)
    embedded = jnp.concatenate([embedded, swap(embedded, c=1)], axis=1)

    cuts = ((0, 896), (896, 1536), (1536, half))
    plane_late, _ = lax.optimization_barrier((plane, from_other))
    others = [swap(plane_late[:, low:high], z=1) for low, high in cuts]

    wide = embedded.astype(jnp.float32)
    real = (lax.broadcasted_iota(jnp.int32, (2 * span, 1), 0) % PAD) < rows
    mean = jnp.sum(wide, axis=0, keepdims=True) / samples
    centered = rounded(jnp.where(real, wide - mean, 0.0))
    centered_wide = centered.astype(jnp.float32)
    sum_squares = jnp.sum(centered_wide * centered_wide, axis=0, keepdims=True)
    spread_std = jnp.sqrt(sum_squares / (samples - 1) + 0.0001)

    quarter = span // 2
    at = (z * 2 + core) * quarter
    embedded_part = lax.dynamic_slice(embedded, (at, 0), (quarter, 2 * pair))
    partner = swap(embedded_part, view=1)
    centered_part = lax.dynamic_slice(centered, (at, 0), (quarter, 2 * pair))

    peers = YS * XS
    gram = matmul(centered_part, centered, 1, 1).astype(jnp.bfloat16)
    gram = exchange(gram, "yx").reshape(peers, PAD, 2 * span)
    gram = jnp.sum(gram.astype(jnp.float32), axis=0).astype(jnp.bfloat16)
    gram, others[0] = lax.optimization_barrier((gram, others[0]))
    gram = jnp.broadcast_to(gram[None], (peers, PAD, 2 * span))
    gram = exchange(gram.reshape(quarter, 2 * span), "yx")
    gram, others[1] = lax.optimization_barrier((gram, others[1]))
    coupled = matmul(gram, centered, 1, 0)

    coef_var = samples / (2.0 * (samples - 1))
    coef_cov = 0.08 * samples / ((samples - 1) * (samples - 1))
    hinge = jax.nn.sigmoid(10.0 * (1.0 - spread_std))
    wide_part = centered_part.astype(jnp.float32)
    combined = (
        embedded_part.astype(jnp.float32)
        - partner.astype(jnp.float32)
        - coef_var * hinge * wide_part / spread_std
        + coef_cov * (coupled - wide_part * sum_squares)
    )
    grad = rounded(combined)
    grad_plane = ordered(grad, flip(swap(grad, c=1)), core == 1)
    far = jnp.concatenate([grad_plane[:, units:pair], grad_plane[:, pair + units :]], axis=1)
    near = jnp.concatenate([grad_plane[:, :units], grad_plane[:, pair : pair + units]], axis=1)
    grad_other = swap(far, z=1)

    h_part = matmul(grad_plane, w_all, 1, 1).astype(jnp.bfloat16)
    pieces = exchange(h_part, "yxc").reshape(peers, 2, PAD, half)
    total = jnp.sum(pieces.astype(jnp.float32), axis=0)
    grad_rows = total.transpose(1, 0, 2).reshape(PAD, 2 * half)[:rows]

    own_runs, sib_runs = [], []
    for low, high, parts in ((0, 896, others[:1]), (896, half, others[1:])):
        w_part = [matmul(part, grad_other, 0, 0) for part in parts]
        w_part = jnp.concatenate(w_part, axis=0) + matmul(plane[:, low:high], near, 0, 0)
        w_part = rounded(w_part)
        mine = w_part[:, :units]
        theirs = w_part[:, units:]
        own_runs.append(wide_sum(mine, swap(mine, view=1)))
        sib_runs.append(wide_sum(swap(theirs, c=1), swap(theirs, view=1, c=1)))
    grad_weight = ordered(
        jnp.concatenate(own_runs, axis=0), jnp.concatenate(sib_runs, axis=0), core == 1
    )
    return (grad_rows[None], grad_weight / jnp.sqrt(2.0 * samples))


def solution(mesh):
    return jax.shard_map(
        on_device,
        mesh=mesh,
        in_specs=(P("view", "dp", None), P(None, "dp")),
        out_specs=(P("view", "dp", None), P(None, "dp")),
        check_vma=False,
    )
```

time: 209 us -> 160 us (0.77)
  waiting for transfers between devices: 122 us -> 78.8 us
  blocking collectives: 22.2 us -> 0 us
  starting transfers between devices: 40.4 us -> 46.1 us
  other arithmetic: 4.64 us -> 10.2 us
  matrix products: 11.6 us -> 15.1 us
  local copies, waits for them, and re-layouts: 6 us -> 8.22 us
    ppermute x12 -> x18, waiting for transfers between devices: 120 us -> 67.4 us  [swap(): return lax.ppermute(block, ('view', 'dp'), route)]
    all_to_all x1 -> x0, blocking collectives: 22.2 us -> none  [exchange(): lax.all_to_all(blocks, 'dp', 0, 0, tiled=True, axis_index_groups=groups(a...]
    all_to_all x3 -> x4, waiting for transfers between devices: 1.38 us -> 11.4 us  [exchange(): lax.all_to_all(blocks, 'dp', 0, 0, tiled=True, axis_index_groups=groups(a...]
    ppermute x12 -> x18, starting transfers between devices: 20.1 us -> 24 us  [swap(): return lax.ppermute(block, ('view', 'dp'), route)]
    dot_general x6 -> x9, matrix products: 11.6 us -> 15.1 us  [matmul(): lax.dot_general(a, b, (((a_dim,), (b_dim,)), ((), ())), preferred_element...]
    slice x3 -> x7, local copies, waits for them, and re-layouts: 0.12 us -> 2.76 us  [the longest x3 1.94 us: on_device(): others = [swap(plane_late[:, low:high], z=1) for low, high in cuts]]
    all_to_all x3 -> x4, starting transfers between devices: 20.3 us -> 22.1 us  [exchange(): lax.all_to_all(blocks, 'dp', 0, 0, tiled=True, axis_index_groups=groups(a...]
  transfers between devices with their start and end apart: 15 -> 22, of which waited for: 11 -> 14; matrix products, arithmetic and copies ran while one was open for 4% -> 14% of each run, Pallas kernels for 0% -> 0%
where the time goes in v2:
time: 160 us; the launch traced here: 159 us
  waiting for transfers between devices  78.8 us (49%)
  starting transfers between devices  46.1 us (29%)
  matrix products  15.1 us (9%)
  other arithmetic  10.2 us (6%)
  local copies, waits for them, and re-layouts  8.22 us (5%)
    ppermute x18, waiting for transfers between devices, swap(): return lax.ppermute(block, ('view', 'dp'), route)  67.4 us
    ppermute x18, starting transfers between devices, swap(): return lax.ppermute(block, ('view', 'dp'), route)  24 us
    all_to_all x4, starting transfers between devices, exchange(): lax.all_to_all(blocks, 'dp', 0, 0, tiled=True, axis_index_groups=groups(a...  22.1 us
    dot_general x9, matrix products, matmul(): lax.dot_general(a, b, (((a_dim,), (b_dim,)), ((), ())), preferred_element...  15.1 us
    all_to_all x4, waiting for transfers between devices, exchange(): lax.all_to_all(blocks, 'dp', 0, 0, tiled=True, axis_index_groups=groups(a...  11.4 us
  transfers between devices with their start and end apart: 22, of which 14 were waited for; matrix products, arithmetic and copies ran while one was open for 14% of the time, Pallas kernels for 0%

profile of v2, /device:TPU:1, one launch (start us, length us, event | category | flops | bytes accessed | tf_op | source)
XLA Modules:
  0.0 159.4 jit_solution(17307174411403201888)
XLA Ops:
  0.6 0.9 pad.4
  1.7 1.6 broadcast_in_dim.18
  3.3 8.7 %all-to-all-start = ((bf16[32,16,2048]{2,1,0:T(8,128)(2,1)}), bf16[32,16,2048]{2,1,0:T(8,128)(2,1)S(1)}, u32[]{:S(2)}, u32[]{:S(2)}) async-start(bf16[32,16,2048]{2,1,0:T(8,128)(2,1)} %bitcast.28), calls=%async_computation | async-start | bytes 4194304 | tf_op jit(solution)/shard_map/all_to_all | solution.py:37
  12.1 3.8 %collective-permute-start = (bf16[2048,128]{1,0:T(8,128)(2,1)S(1)}, bf16[2048,128]{1,0:T(8,128)(2,1)S(1)}, u32[]{:S(2)}, u32[]{:S(2)}) collective-permute-start(bf16[2048,128]{1,0:T(8,128)(2,1)S(1)} %get-tuple-element.14), channel_id=1, source_target_pairs={{0,72},{1,73},{2,74},{3,75},{4,76},{5,77},{6,78},{7,79},{8,64},{9,... | collective-permute-start | bytes 1572872 | tf_op jit(solution)/shard_map/ppermute | solution.py:33
  16.5 11.6 %collective-permute-done = bf16[2048,128]{1,0:T(8,128)(2,1)S(1)} collective-permute-done((bf16[2048,128]{1,0:T(8,128)(2,1)S(1)}, bf16[2048,128]{1,0:T(8,128)(2,1)S(1)}, u32[]{:S(2)}, u32[]{:S(2)}) %collective-permute-start) | collective-permute-done | bytes 524320 | tf_op jit(solution)/shard_map/ppermute | solution.py:33
  28.1 11.4 %collective-permute-done.2 = bf16[2048,128]{1,0:T(8,128)(2,1)} collective-permute-done((bf16[2048,128]{1,0:T(8,128)(2,1)S(1)}, bf16[2048,128]{1,0:T(8,128)(2,1)}, u32[]{:S(2)}, u32[]{:S(2)}) %collective-permute-start.2) | collective-permute-done | bytes 524320 | tf_op jit(solution)/shard_map/ppermute | solution.py:33
  39.8 2.4 %fusion.15 = f32[512,512]{1,0:T(8,128)S(1)} fusion(bf16[512,2048]{1,0:T(8,128)(2,1)S(1)} %bitcast.22, bf16[2048,128]{1,0:T(8,128)(2,1)} %collective-permute-done.2, bf16[2048,128]{1,0:T(8,128)(2,1)S(1)} %collective-permute-done.1, bf16[2048,128]{1,0:T(8,128)(2,1)S(1)} %collective-permute-done, bf16[2048,128]{1,0:T(8,128)(2,1)} %copy-done.3), kind=kOutput, calls=%fused_computation.38 | convolution fusion | flops 1082130432 | bytes 5242880 | tf_op jit(solution)/shard_map/dot_general | solution.py:41
  42.3 2.5 %collective-permute-start.3 = (f32[512,256]{1,0:T(8,128)S(1)}, f32[512,256]{1,0:T(8,128)S(1)}, u32[]{:S(2)}, u32[]{:S(2)}) collective-permute-start(f32[512,256]{1,0:T(8,128)S(1)} %slice.82), channel_id=1, source_target_pairs={{0,1},{1,0},{2,3},{3,2},{4,5},{5,4},{6,7},{7,6},{8,9},{9,8},{10,11... | collective-permute-start | bytes 1572872 | tf_op jit(solution)/shard_map/ppermute | solution.py:33
  44.8 1.5 collective-permute-done.3
  46.5 3.7 %collective-permute-start.4 = (bf16[512,256]{1,0:T(8,128)(2,1)S(1)}, bf16[512,256]{1,0:T(8,128)(2,1)S(1)}, u32[]{:S(2)}, u32[]{:S(2)}) collective-permute-start(bf16[512,256]{1,0:T(8,128)(2,1)S(1)} %fusion.14), channel_id=1, source_target_pairs={{0,8},{1,9},{2,10},{3,11},{4,12},{5,13},{6,14},{7,15},{8,0},{9,1},... | collective-permute-start | bytes 786440 | tf_op jit(solution)/shard_map/ppermute | solution.py:33
  50.1 6.4 %collective-permute-done.4 = bf16[512,256]{1,0:T(8,128)(2,1)S(1)} collective-permute-done((bf16[512,256]{1,0:T(8,128)(2,1)S(1)}, bf16[512,256]{1,0:T(8,128)(2,1)S(1)}, u32[]{:S(2)}, u32[]{:S(2)}) %collective-permute-start.4) | collective-permute-done | bytes 262176 | tf_op jit(solution)/shard_map/ppermute | solution.py:33
  56.8 1.0 collective-permute-start.5
  57.8 1.0 slice.65
  58.8 3.0 %collective-permute-start.7 = (bf16[512,896]{1,0:T(8,128)(2,1)}, bf16[512,896]{1,0:T(8,128)(2,1)}, u32[]{:S(2)}, u32[]{:S(2)}) collective-permute-start(bf16[512,896]{1,0:T(8,128)(2,1)} %slice.65), channel_id=1, source_target_pairs={{0,8},{1,9},{2,10},{3,11},{4,12},{5,13},{6,14},{7,15},{8,0},{9,1},... | collective-permute-start | bytes 2752520 | tf_op jit(solution)/shard_map/ppermute | solution.py:33
  62.5 1.5 fusion.1
  64.1 1.3 convolution_convert_fusion.1
  65.3 4.2 %all-to-all-start.1 = ((bf16[16,16,1024]{2,1,0:T(8,128)(2,1)}), bf16[16,16,1024]{2,1,0:T(8,128)(2,1)}, u32[]{:S(2)}, u32[]{:S(2)}) async-start(bf16[16,16,1024]{2,1,0:T(8,128)(2,1)} %bitcast.30), calls=%async_computation.1 | async-start | bytes 1048576 | tf_op jit(solution)/shard_map/all_to_all | solution.py:37
  69.6 0.9 slice.66
  71.0 9.6 %all-to-all-done.1 = bf16[16,16,1024]{2,1,0:T(8,128)(2,1)} async-done(((bf16[16,16,1024]{2,1,0:T(8,128)(2,1)}), bf16[16,16,1024]{2,1,0:T(8,128)(2,1)}, u32[]{:S(2)}, u32[]{:S(2)}) %all-to-all-start.1) | async-done | bytes 524320 | tf_op jit(solution)/shard_map/all_to_all | solution.py:37
  80.7 1.1 reduce_sum.41
  81.8 0.8 collective-permute-done.7
  82.5 0.9 broadcast_in_dim.32
  83.4 4.2 %all-to-all-start.2 = ((bf16[16,16,1024]{2,1,0:T(8,128)(2,1)}), bf16[16,16,1024]{2,1,0:T(8,128)(2,1)}, u32[]{:S(2)}, u32[]{:S(2)}) async-start(bf16[16,16,1024]{2,1,0:T(8,128)(2,1)} %broadcast_in_dim.32), calls=%async_computation.2 | async-start | bytes 1048576 | tf_op jit(solution)/shard_map/all_to_all | solution.py:37
  87.6 1.0 fusion.16
  88.6 1.1 collective-permute-start.6
  90.0 6.6 %collective-permute-done.8 = bf16[512,640]{1,0:T(8,128)(2,1)} collective-permute-done((bf16[512,640]{1,0:T(8,128)(2,1)}, bf16[512,640]{1,0:T(8,128)(2,1)}, u32[]{:S(2)}, u32[]{:S(2)}) %collective-permute-start.8) | collective-permute-done | bytes 655392 | tf_op jit(solution)/shard_map/ppermute | solution.py:33
  96.6 1.4 all-to-all-done.2
  98.0 4.9 %collective-permute-done.6 = bf16[256,512]{1,0:T(8,128)(2,1)} collective-permute-done((bf16[256,512]{1,0:T(8,128)(2,1)S(1)}, bf16[256,512]{1,0:T(8,128)(2,1)}, u32[]{:S(2)}, u32[]{:S(2)}) %collective-permute-start.6) | collective-permute-done | bytes 262176 | tf_op jit(solution)/shard_map/ppermute | solution.py:33
  102.9 2.3 %fusion.13 = bf16[256,512]{1,0:T(8,128)(2,1)} fusion(bf16[256,1024]{1,0:T(8,128)(2,1)} %bitcast.5, bf16[1024,512]{1,0:T(8,128)(2,1)S(1)} %fusion.1, bf16[256,512]{1,0:T(8,128)(2,1)} %collective-permute-done.6, bf16[256,512]{1,0:T(8,128)(2,1)S(1)} %fusion.16, f32[512]{0:T(512)S(1)} %multiply_reduce_fusion, f32[512]{0:T(512)S(1)} %get-tuple-element.29, ...), kind=kOutput, calls=%fused_computation.31 | convolution fusion | flops 270008320 | bytes 2627588 | tf_op jit(solution)/shard_map/dot_general | solution.py:41
  105.3 0.8 collective-permute-start.9
  106.1 1.0 collective-permute-start.13
  107.5 1.2 maximum_select_fusion.2
  108.6 0.7 fusion.30
  110.1 1.7 %collective-permute-start.10 = (bf16[512,256]{1,0:T(8,128)(2,1)}, bf16[512,256]{1,0:T(8,128)(2,1)S(1)}, u32[]{:S(2)}, u32[]{:S(2)}) collective-permute-start(bf16[512,256]{1,0:T(8,128)(2,1)} %pad_maximum_fusion.4), channel_id=1, source_target_pairs={{0,8},{1,9},{2,10},{3,11},{4,12},{5,13},{6,14},{7,15},{8,0},{9,1},... | collective-permute-start | bytes 786440 | tf_op jit(solution)/shard_map/ppermute | solution.py:33
  111.9 3.7 %convolution_convert_fusion = bf16[512,2048]{1,0:T(8,128)(2,1)} fusion(bf16[512,512]{1,0:T(8,128)(2,1)S(1)} %maximum_select_fusion.2, bf16[2048,128]{1,0:T(8,128)(2,1)} %collective-permute-done.2, bf16[2048,128]{1,0:T(8,128)(2,1)S(1)} %copy-done.9, bf16[2048,128]{1,0:T(8,128)(2,1)S(1)} %copy-done.7, bf16[2048,128]{1,0:T(8,128)(2,1)S(1)} %copy-done.4), kind=kOutput, calls=%fused_computation.1 | convolution fusion | flops 1083179008 | bytes 4718592 | tf_op jit(solution)/shard_map/dot_general | solution.py:41
  115.6 4.9 %all-to-all-start.3 = ((bf16[32,16,2048]{2,1,0:T(8,128)(2,1)}), bf16[32,16,2048]{2,1,0:T(8,128)(2,1)}, u32[]{:S(2)}, u32[]{:S(2)}) async-start(bf16[32,16,2048]{2,1,0:T(8,128)(2,1)} %bitcast.29), calls=%async_computation.3 | async-start | bytes 4194304 | tf_op jit(solution)/shard_map/all_to_all | solution.py:37
  120.5 1.3 fusion.8
  121.8 5.2 %collective-permute-done.10 = bf16[512,256]{1,0:T(8,128)(2,1)S(1)} collective-permute-done((bf16[512,256]{1,0:T(8,128)(2,1)}, bf16[512,256]{1,0:T(8,128)(2,1)S(1)}, u32[]{:S(2)}, u32[]{:S(2)}) %collective-permute-start.10) | collective-permute-done | bytes 262176 | tf_op jit(solution)/shard_map/ppermute | solution.py:33
  127.0 1.6 %fusion.3 = bf16[896,256]{1,0:T(8,128)(2,1)S(1)} fusion(f32[896,256]{1,0:T(8,128)S(1)} %fusion.8, bf16[512,896]{1,0:T(8,128)(2,1)} %collective-permute-done.7, bf16[512,256]{1,0:T(8,128)(2,1)S(1)} %collective-permute-done.10), kind=kOutput, calls=%fused_computation.12 | convolution fusion | flops 235339776 | bytes 2555904 | tf_op jit(solution)/shard_map/dot_general | solution.py:41
  128.7 0.8 collective-permute-start.11
  129.4 0.9 collective-permute-start.12
  130.3 1.5 fusion.34
  132.7 0.8 collective-permute-start.16
  134.9 7.0 %collective-permute-done.16 = bf16[896,128]{1,0:T(8,128)(2,1)S(1)} collective-permute-done((bf16[896,128]{1,0:T(8,128)(2,1)S(1)}, bf16[896,128]{1,0:T(8,128)(2,1)S(1)}, u32[]{:S(2)}, u32[]{:S(2)}) %collective-permute-start.16) | collective-permute-done | bytes 229408 | tf_op jit(solution)/shard_map/ppermute | solution.py:33
  142.8 11.7 %collective-permute-done.17 = bf16[1152,128]{1,0:T(8,128)(2,1)S(1)} collective-permute-done((bf16[1152,128]{1,0:T(8,128)(2,1)S(1)}, bf16[1152,128]{1,0:T(8,128)(2,1)S(1)}, u32[]{:S(2)}, u32[]{:S(2)}) %collective-permute-start.17) | collective-permute-done | bytes 294944 | tf_op jit(solution)/shard_map/ppermute | solution.py:33
  154.6 1.6 fusion.2
  156.2 2.0 %convert_reduce_fusion = f32[2,16,2048]{2,1,0:T(8,128)S(1)} fusion(bf16[16,2,16,2048]{3,2,1,0:T(8,128)(2,1)} %bitcast.9), kind=kLoop, calls=%fused_computation | loop fusion | flops 2031616 | bytes 2359296 | tf_op jit(solution)/shard_map/reduce_sum | solution.py:142
  158.4 1.0 broadcast_in_dim.34
  (60 shorter events, 7.7 us)
Async XLA Ops:
  3.3 8.8 %copy-start.2 = (bf16[4096,128]{1,0:T(8,128)(2,1)S(1)}, bf16[4096,128]{1,0:T(8,128)(2,1)}, u32[]{:S(2)}) copy-start(bf16[4096,128]{1,0:T(8,128)(2,1)} %param.3) | copy-start | bytes 3145732
  3.3 36.6 %all-to-all-start = ((bf16[32,16,2048]{2,1,0:T(8,128)(2,1)}), bf16[32,16,2048]{2,1,0:T(8,128)(2,1)S(1)}, u32[]{:S(2)}, u32[]{:S(2)}) async-start(bf16[32,16,2048]{2,1,0:T(8,128)(2,1)} %bitcast.28), calls=%async_computation | async-start | bytes 4194304 | tf_op jit(solution)/shard_map/all_to_all | solution.py:37
  12.1 16.0 %copy-start.3 = (bf16[2048,128]{1,0:T(8,128)(2,1)}, bf16[2048,128]{1,0:T(8,128)(2,1)S(1)}, u32[]{:S(2)}) copy-start(bf16[2048,128]{1,0:T(8,128)(2,1)S(1)} %get-tuple-element.14) | copy-start | bytes 1572868
  12.1 16.0 %collective-permute-start = (bf16[2048,128]{1,0:T(8,128)(2,1)S(1)}, bf16[2048,128]{1,0:T(8,128)(2,1)S(1)}, u32[]{:S(2)}, u32[]{:S(2)}) collective-permute-start(bf16[2048,128]{1,0:T(8,128)(2,1)S(1)} %get-tuple-element.14), channel_id=1, source_target_pairs={{0,72},{1,73},{2,74},{3,75},{4,76},{5,77},{6,78},{7,79},{8,64},{9,... | collective-permute-start | bytes 1572872 | tf_op jit(solution)/shard_map/ppermute | solution.py:33
  15.9 12.2 %collective-permute-start.1 = (bf16[2048,128]{1,0:T(8,128)(2,1)S(1)}, bf16[2048,128]{1,0:T(8,128)(2,1)S(1)}, u32[]{:S(2)}, u32[]{:S(2)}) collective-permute-start(bf16[2048,128]{1,0:T(8,128)(2,1)S(1)} %get-tuple-element.15), channel_id=1, source_target_pairs={{0,1},{1,0},{2,3},{3,2},{4,5},{5,4},{6,7},{7,6},{8,9},{9,8},{10,11... | collective-permute-start | bytes 1572872 | tf_op jit(solution)/shard_map/ppermute | solution.py:33
  16.5 23.0 %collective-permute-start.2 = (bf16[2048,128]{1,0:T(8,128)(2,1)S(1)}, bf16[2048,128]{1,0:T(8,128)(2,1)}, u32[]{:S(2)}, u32[]{:S(2)}) collective-permute-start(bf16[2048,128]{1,0:T(8,128)(2,1)S(1)} %get-tuple-element.15), channel_id=1, source_target_pairs={{0,73},{1,72},{2,75},{3,74},{4,77},{5,76},{6,79},{7,78},{8,65},{9,... | collective-permute-start | bytes 1572872 | tf_op jit(solution)/shard_map/ppermute | solution.py:33
  28.1 14.2 %copy-start.6 = (bf16[2048,128]{1,0:T(8,128)(2,1)}, bf16[2048,128]{1,0:T(8,128)(2,1)S(1)}, u32[]{:S(2)}) copy-start(bf16[2048,128]{1,0:T(8,128)(2,1)S(1)} %collective-permute-done) | copy-start | bytes 1572868
  28.1 14.2 %copy-start.8 = (bf16[2048,128]{1,0:T(8,128)(2,1)}, bf16[2048,128]{1,0:T(8,128)(2,1)S(1)}, u32[]{:S(2)}) copy-start(bf16[2048,128]{1,0:T(8,128)(2,1)S(1)} %collective-permute-done.1) | copy-start | bytes 1572868
  42.3 4.0 %collective-permute-start.3 = (f32[512,256]{1,0:T(8,128)S(1)}, f32[512,256]{1,0:T(8,128)S(1)}, u32[]{:S(2)}, u32[]{:S(2)}) collective-permute-start(f32[512,256]{1,0:T(8,128)S(1)} %slice.82), channel_id=1, source_target_pairs={{0,1},{1,0},{2,3},{3,2},{4,5},{5,4},{6,7},{7,6},{8,9},{9,8},{10,11... | collective-permute-start | bytes 1572872 | tf_op jit(solution)/shard_map/ppermute | solution.py:33
  46.5 10.1 %collective-permute-start.4 = (bf16[512,256]{1,0:T(8,128)(2,1)S(1)}, bf16[512,256]{1,0:T(8,128)(2,1)S(1)}, u32[]{:S(2)}, u32[]{:S(2)}) collective-permute-start(bf16[512,256]{1,0:T(8,128)(2,1)S(1)} %fusion.14), channel_id=1, source_target_pairs={{0,8},{1,9},{2,10},{3,11},{4,12},{5,13},{6,14},{7,15},{8,0},{9,1},... | collective-permute-start | bytes 786440 | tf_op jit(solution)/shard_map/ppermute | solution.py:33
  56.8 5.2 %copy-start = (bf16[1024,256]{1,0:T(8,128)(2,1)}, bf16[1024,256]{1,0:T(8,128)(2,1)S(1)}, u32[]{:S(2)}) copy-start(bf16[1024,256]{1,0:T(8,128)(2,1)S(1)} %maximum_select_fusion.1) | copy-start | bytes 1572868
  56.8 4.9 %collective-permute-start.5 = (bf16[1024,256]{1,0:T(8,128)(2,1)S(1)}, bf16[1024,256]{1,0:T(8,128)(2,1)S(1)}, u32[]{:S(2)}, u32[]{:S(2)}) collective-permute-start(bf16[1024,256]{1,0:T(8,128)(2,1)S(1)} %maximum_select_fusion.1), channel_id=1, source_target_pairs={{0,1},{1,0},{2,3},{3,2},{4,5},{5,4},{6,7},{7,6},{8,9},{9,8},{10,11... | collective-permute-start | bytes 1572872 | tf_op jit(solution)/shard_map/ppermute | solution.py:33
  58.8 23.8 %collective-permute-start.7 = (bf16[512,896]{1,0:T(8,128)(2,1)}, bf16[512,896]{1,0:T(8,128)(2,1)}, u32[]{:S(2)}, u32[]{:S(2)}) collective-permute-start(bf16[512,896]{1,0:T(8,128)(2,1)} %slice.65), channel_id=1, source_target_pairs={{0,8},{1,9},{2,10},{3,11},{4,12},{5,13},{6,14},{7,15},{8,0},{9,1},... | collective-permute-start | bytes 2752520 | tf_op jit(solution)/shard_map/ppermute | solution.py:33
  61.7 0.8 copy-start.1
  65.3 15.3 %all-to-all-start.1 = ((bf16[16,16,1024]{2,1,0:T(8,128)(2,1)}), bf16[16,16,1024]{2,1,0:T(8,128)(2,1)}, u32[]{:S(2)}, u32[]{:S(2)}) async-start(bf16[16,16,1024]{2,1,0:T(8,128)(2,1)} %bitcast.30), calls=%async_computation.1 | async-start | bytes 1048576 | tf_op jit(solution)/shard_map/all_to_all | solution.py:37
  70.5 26.1 %collective-permute-start.8 = (bf16[512,640]{1,0:T(8,128)(2,1)}, bf16[512,640]{1,0:T(8,128)(2,1)}, u32[]{:S(2)}, u32[]{:S(2)}) collective-permute-start(bf16[512,640]{1,0:T(8,128)(2,1)} %slice.66), channel_id=1, source_target_pairs={{0,8},{1,9},{2,10},{3,11},{4,12},{5,13},{6,14},{7,15},{8,0},{9,1},... | collective-permute-start | bytes 1966088 | tf_op jit(solution)/shard_map/ppermute | solution.py:33
  83.4 14.6 %all-to-all-start.2 = ((bf16[16,16,1024]{2,1,0:T(8,128)(2,1)}), bf16[16,16,1024]{2,1,0:T(8,128)(2,1)}, u32[]{:S(2)}, u32[]{:S(2)}) async-start(bf16[16,16,1024]{2,1,0:T(8,128)(2,1)} %broadcast_in_dim.32), calls=%async_computation.2 | async-start | bytes 1048576 | tf_op jit(solution)/shard_map/all_to_all | solution.py:37
  88.6 14.3 %collective-permute-start.6 = (bf16[256,512]{1,0:T(8,128)(2,1)S(1)}, bf16[256,512]{1,0:T(8,128)(2,1)}, u32[]{:S(2)}, u32[]{:S(2)}) collective-permute-start(bf16[256,512]{1,0:T(8,128)(2,1)S(1)} %fusion.16), channel_id=1, source_target_pairs={{0,64},{1,65},{2,66},{3,67},{4,68},{5,69},{6,70},{7,71},{8,72},{9,... | collective-permute-start | bytes 786440 | tf_op jit(solution)/shard_map/ppermute | solution.py:33
  105.3 2.2 %collective-permute-start.9 = (bf16[256,512]{1,0:T(8,128)(2,1)}, bf16[256,512]{1,0:T(8,128)(2,1)S(1)}, u32[]{:S(2)}, u32[]{:S(2)}) collective-permute-start(bf16[256,512]{1,0:T(8,128)(2,1)} %fusion.13), channel_id=1, source_target_pairs={{0,1},{1,0},{2,3},{3,2},{4,5},{5,4},{6,7},{7,6},{8,9},{9,8},{10,11... | collective-permute-start | bytes 786440 | tf_op jit(solution)/shard_map/ppermute | solution.py:33
  106.1 5.8 %copy-start.4 = (bf16[2048,128]{1,0:T(8,128)(2,1)S(1)}, bf16[2048,128]{1,0:T(8,128)(2,1)}, u32[]{:S(2)}) copy-start(bf16[2048,128]{1,0:T(8,128)(2,1)} %copy-done.3) | copy-start | bytes 1572868
  106.1 5.8 %copy-start.7 = (bf16[2048,128]{1,0:T(8,128)(2,1)S(1)}, bf16[2048,128]{1,0:T(8,128)(2,1)}, u32[]{:S(2)}) copy-start(bf16[2048,128]{1,0:T(8,128)(2,1)} %copy-done.6) | copy-start | bytes 1572868
  106.1 5.8 %copy-start.9 = (bf16[2048,128]{1,0:T(8,128)(2,1)S(1)}, bf16[2048,128]{1,0:T(8,128)(2,1)}, u32[]{:S(2)}) copy-start(bf16[2048,128]{1,0:T(8,128)(2,1)} %copy-done.8) | copy-start | bytes 1572868
  106.1 25.7 %collective-permute-start.13 = (bf16[512,512]{1,0:T(8,128)(2,1)S(1)}, bf16[512,512]{1,0:T(8,128)(2,1)S(1)}, u32[]{:S(2)}, u32[]{:S(2)}) collective-permute-start(bf16[512,512]{1,0:T(8,128)(2,1)S(1)} %slice.76), channel_id=1, source_target_pairs={{0,8},{1,9},{2,10},{3,11},{4,12},{5,13},{6,14},{7,15},{8,0},{9,1},... | collective-permute-start | bytes 1572872 | tf_op jit(solution)/shard_map/ppermute | solution.py:33
  110.1 16.9 %collective-permute-start.10 = (bf16[512,256]{1,0:T(8,128)(2,1)}, bf16[512,256]{1,0:T(8,128)(2,1)S(1)}, u32[]{:S(2)}, u32[]{:S(2)}) collective-permute-start(bf16[512,256]{1,0:T(8,128)(2,1)} %pad_maximum_fusion.4), channel_id=1, source_target_pairs={{0,8},{1,9},{2,10},{3,11},{4,12},{5,13},{6,14},{7,15},{8,0},{9,1},... | collective-permute-start | bytes 786440 | tf_op jit(solution)/shard_map/ppermute | solution.py:33
  115.6 40.6 %all-to-all-start.3 = ((bf16[32,16,2048]{2,1,0:T(8,128)(2,1)}), bf16[32,16,2048]{2,1,0:T(8,128)(2,1)}, u32[]{:S(2)}, u32[]{:S(2)}) async-start(bf16[32,16,2048]{2,1,0:T(8,128)(2,1)} %bitcast.29), calls=%async_computation.3 | async-start | bytes 4194304 | tf_op jit(solution)/shard_map/all_to_all | solution.py:37
  128.6 3.5 %copy-start.5 = (bf16[512,128]{1,0:T(8,128)(2,1)S(1)}, bf16[512,128]{1,0:T(8,128)(2,1)}, u32[]{:S(2)}) copy-start(bf16[512,128]{1,0:T(8,128)(2,1)} %get-tuple-element.19) | copy-start | bytes 393220
  128.7 14.0 %collective-permute-start.11 = (bf16[896,128]{1,0:T(8,128)(2,1)S(1)}, bf16[896,128]{1,0:T(8,128)(2,1)S(1)}, u32[]{:S(2)}, u32[]{:S(2)}) collective-permute-start(bf16[896,128]{1,0:T(8,128)(2,1)S(1)} %get-tuple-element.22), channel_id=1, source_target_pairs={{0,1},{1,0},{2,3},{3,2},{4,5},{5,4},{6,7},{7,6},{8,9},{9,8},{10,11... | collective-permute-start | bytes 688136 | tf_op jit(solution)/shard_map/ppermute | solution.py:33
  129.4 13.3 %collective-permute-start.12 = (bf16[896,128]{1,0:T(8,128)(2,1)S(1)}, bf16[896,128]{1,0:T(8,128)(2,1)S(1)}, u32[]{:S(2)}, u32[]{:S(2)}) collective-permute-start(bf16[896,128]{1,0:T(8,128)(2,1)S(1)} %get-tuple-element.22), channel_id=1, source_target_pairs={{0,65},{1,64},{2,67},{3,66},{4,69},{5,68},{6,71},{7,70},{8,73},{9,... | collective-permute-start | bytes 688136 | tf_op jit(solution)/shard_map/ppermute | solution.py:33
  132.7 9.2 %collective-permute-start.16 = (bf16[896,128]{1,0:T(8,128)(2,1)S(1)}, bf16[896,128]{1,0:T(8,128)(2,1)S(1)}, u32[]{:S(2)}, u32[]{:S(2)}) collective-permute-start(bf16[896,128]{1,0:T(8,128)(2,1)S(1)} %get-tuple-element.23), channel_id=1, source_target_pairs={{0,64},{1,65},{2,66},{3,67},{4,68},{5,69},{6,70},{7,71},{8,72},{9,... | collective-permute-start | bytes 688136 | tf_op jit(solution)/shard_map/ppermute | solution.py:33
  133.6 21.0 %collective-permute-start.14 = (bf16[1152,128]{1,0:T(8,128)(2,1)S(1)}, bf16[1152,128]{1,0:T(8,128)(2,1)S(1)}, u32[]{:S(2)}, u32[]{:S(2)}) collective-permute-start(bf16[1152,128]{1,0:T(8,128)(2,1)S(1)} %get-tuple-element.16), channel_id=1, source_target_pairs={{0,1},{1,0},{2,3},{3,2},{4,5},{5,4},{6,7},{7,6},{8,9},{9,8},{10,11... | collective-permute-start | bytes 884744 | tf_op jit(solution)/shard_map/ppermute | solution.py:33
  134.2 20.4 %collective-permute-start.15 = (bf16[1152,128]{1,0:T(8,128)(2,1)S(1)}, bf16[1152,128]{1,0:T(8,128)(2,1)S(1)}, u32[]{:S(2)}, u32[]{:S(2)}) collective-permute-start(bf16[1152,128]{1,0:T(8,128)(2,1)S(1)} %get-tuple-element.16), channel_id=1, source_target_pairs={{0,65},{1,64},{2,67},{3,66},{4,69},{5,68},{6,71},{7,70},{8,73},{9,... | collective-permute-start | bytes 884744 | tf_op jit(solution)/shard_map/ppermute | solution.py:33
  141.9 12.5 %collective-permute-start.17 = (bf16[1152,128]{1,0:T(8,128)(2,1)S(1)}, bf16[1152,128]{1,0:T(8,128)(2,1)S(1)}, u32[]{:S(2)}, u32[]{:S(2)}) collective-permute-start(bf16[1152,128]{1,0:T(8,128)(2,1)S(1)} %get-tuple-element.17), channel_id=1, source_target_pairs={{0,64},{1,65},{2,66},{3,67},{4,68},{5,69},{6,70},{7,71},{8,72},{9,... | collective-permute-start | bytes 884744 | tf_op jit(solution)/shard_map/ppermute | solution.py:33

commit v3 on v1

v3 whole, which is shorter than its diff:
```python
import jax
import jax.numpy as jnp
from jax import lax
from jax.sharding import PartitionSpec as P

YS, ZS, XS, CS = 4, 2, 4, 2
DP = YS * ZS * XS * CS
PAD = 16


def place(d):
    return (d // (ZS * XS * CS), d // (XS * CS) % ZS, d // CS % XS, d % CS)


def index(y, z, x, c):
    return ((y * ZS + z) * XS + x) * CS + c


def groups(axes):
    found = {}
    for d in range(DP):
        key = tuple(p for p, name in zip(place(d), "yzxc") if name not in axes)
        found.setdefault(key, []).append(d)
    return list(found.values())


def swap(block, view=0, z=0, c=0):
    route = []
    for v in range(2):
        for d in range(DP):
            y, zd, x, cd = place(d)
            route.append((v * DP + d, (v ^ view) * DP + index(y, zd ^ z, x, cd ^ c)))
    return lax.ppermute(block, ("view", "dp"), route)


def exchange(blocks, axes):
    return lax.all_to_all(blocks, "dp", 0, 0, tiled=True, axis_index_groups=groups(axes))


def matmul(a, b, a_dim, b_dim):
    return lax.dot_general(
        a, b, (((a_dim,), (b_dim,)), ((), ())), preferred_element_type=jnp.float32
    )


def rounded(values):
    return lax.optimization_barrier(values.astype(jnp.bfloat16))


def reordered(block, order):
    return jnp.concatenate([block[:, 128 * i : 128 * i + 128] for i in order], axis=1)


def wide_sum(a, b):
    return a.astype(jnp.float32) + b.astype(jnp.float32)


def on_device(hidden, weight):
    rows = hidden.shape[1]
    width = hidden.shape[2]
    samples = rows * DP
    units = weight.shape[1]
    peers = YS * XS

    w_far = swap(weight, view=1, z=1)
    w_sib = swap(weight, c=1)
    w_far_sib = swap(w_far, c=1)

    padded = jnp.pad(hidden[0], ((0, PAD - rows), (0, 0)))
    copies = jnp.broadcast_to(padded[None], (peers, PAD, width))
    plane = exchange(copies.reshape(peers * PAD, width), "yx")
    quarter = plane.shape[0]

    part = [matmul(plane, w, 1, 0) for w in (weight, w_sib, w_far, w_far_sib)]
    mine = rounded(jnp.concatenate(part, axis=1))
    from_sib = swap(mine, c=1)
    from_far = swap(mine, z=1)
    from_far_sib = swap(from_far, c=1)
    partner = swap(mine, view=1)
    embedded = jnp.concatenate(
        [
            mine,
            reordered(from_sib, (1, 0, 3, 2)),
            reordered(from_far, (2, 3, 0, 1)),
            reordered(from_far_sib, (3, 2, 1, 0)),
        ],
        axis=0,
    )

    cuts = ((0, 1792), (1792, 3072), (3072, width))
    plane_late, _ = lax.optimization_barrier((plane, from_far))
    h_sib = swap(plane, c=1)
    h_far = [swap(plane_late[:, low:high], z=1) for low, high in cuts]

    wide = embedded.astype(jnp.float32)
    real = (lax.broadcasted_iota(jnp.int32, (4 * quarter, 1), 0) % PAD) < rows
    mean = jnp.sum(wide, axis=0, keepdims=True) / samples
    centered = rounded(jnp.where(real, wide - mean, 0.0))
    centered_wide = centered.astype(jnp.float32)
    sum_squares = jnp.sum(centered_wide * centered_wide, axis=0, keepdims=True)
    spread_std = jnp.sqrt(sum_squares / (samples - 1) + 0.0001)

    gram = matmul(centered[:quarter], centered, 1, 1).astype(jnp.bfloat16)
    gram = exchange(gram, "yx").reshape(peers, PAD, 4 * quarter)
    gram = jnp.sum(gram.astype(jnp.float32), axis=0).astype(jnp.bfloat16)
    gram, h_far[0] = lax.optimization_barrier((gram, h_far[0]))
    gram = jnp.broadcast_to(gram[None], (peers, PAD, 4 * quarter))
    gram = exchange(gram.reshape(quarter, 4 * quarter), "yx")
    gram, h_far[1] = lax.optimization_barrier((gram, h_far[1]))
    coupled = matmul(gram, centered, 1, 0)

    coef_var = samples / (2.0 * (samples - 1))
    coef_cov = 0.08 * samples / ((samples - 1) * (samples - 1))
    hinge = jax.nn.sigmoid(10.0 * (1.0 - spread_std))
    centered_part = centered_wide[:quarter]
    combined = (
        mine.astype(jnp.float32)
        - partner.astype(jnp.float32)
        - coef_var * hinge * centered_part / spread_std
        + coef_cov * (coupled - centered_part * sum_squares)
    )
    grad = combined.astype(jnp.bfloat16)
    grad, h_far[2] = lax.optimization_barrier((grad, h_far[2]))
    run = lambda i: grad[:, units * i : units * i + units]
    g_far = swap(run(2), z=1)
    g_far_sib = swap(run(3), z=1, c=1)
    g_sib = swap(run(1), c=1)

    w_all = jnp.concatenate([weight, w_sib, w_far, w_far_sib], axis=1)
    h_part = matmul(grad, w_all, 1, 1).astype(jnp.bfloat16)
    pieces = exchange(h_part, "yx").reshape(peers, PAD, width)
    grad_rows = jnp.sum(pieces.astype(jnp.float32), axis=0)[:rows]

    runs = []
    for (low, high), far in zip(cuts, h_far):
        far_sib = swap(far, c=1)
        total = matmul(plane[:, low:high], run(0), 0, 0)
        total = total + matmul(h_sib[:, low:high], g_sib, 0, 0)
        total = total + matmul(far, g_far, 0, 0)
        total = rounded(total + matmul(far_sib, g_far_sib, 0, 0))
        runs.append(wide_sum(total, swap(total, view=1)))
    grad_weight = jnp.concatenate(runs, axis=0) / jnp.sqrt(2.0 * samples)
    return (grad_rows[None], grad_weight)


def solution(mesh):
    return jax.shard_map(
        on_device,
        mesh=mesh,
        in_specs=(P("view", "dp", None), P(None, "dp")),
        out_specs=(P("view", "dp", None), P(None, "dp")),
        check_vma=False,
    )
```

time: 209 us -> 171 us (0.82)
  waiting for transfers between devices: 122 us -> 62.6 us
  blocking collectives: 22.2 us -> 0 us
  matrix products: 11.6 us -> 27.1 us
  starting transfers between devices: 40.4 us -> 55.4 us
  other arithmetic: 4.64 us -> 16.8 us
    ppermute x12 -> x20, waiting for transfers between devices: 120 us -> 48.2 us  [swap(): return lax.ppermute(block, ('view', 'dp'), route)]
    all_to_all x1 -> x0, blocking collectives: 22.2 us -> none  [exchange(): lax.all_to_all(blocks, 'dp', 0, 0, tiled=True, axis_index_groups=groups(a...]
    dot_general x6 -> x19, matrix products: 11.6 us -> 27.1 us  [matmul(): lax.dot_general(a, b, (((a_dim,), (b_dim,)), ((), ())), preferred_element...]
    all_to_all x3 -> x4, waiting for transfers between devices: 1.38 us -> 14.4 us  [exchange(): lax.all_to_all(blocks, 'dp', 0, 0, tiled=True, axis_index_groups=groups(a...]
    ppermute x12 -> x20, starting transfers between devices: 20.1 us -> 32.6 us  [swap(): return lax.ppermute(block, ('view', 'dp'), route)]
    reduce_sum x1, other arithmetic: 0.27 us -> 8.54 us  [on_device(): mean = jnp.sum(wide, axis=0, keepdims=True) / samples]
    convert_element_type x0 -> x2, other arithmetic: none -> 2.9 us  [the longest x1 1.56 us: on_device(): centered_wide = centered.astype(jnp.float32)]
    slice x5 -> x7, local copies, waits for them, and re-layouts: 0.37 us -> 2.91 us  [the longest x3 2.84 us: on_device(): h_far = [swap(plane_late[:, low:high], z=1) for low, high in cuts]]
  transfers between devices with their start and end apart: 15 -> 24, of which waited for: 11 -> 9; matrix products, arithmetic and copies ran while one was open for 4% -> 26% of each run, Pallas kernels for 0% -> 0%
where the time goes in v3:
time: 171 us; the launch traced here: 170 us
  waiting for transfers between devices  62.6 us (37%)
  starting transfers between devices  55.4 us (32%)
  matrix products  27.1 us (16%)
  other arithmetic  16.8 us (10%)
  local copies, waits for them, and re-layouts  7.17 us (4%)
    ppermute x20, waiting for transfers between devices, swap(): return lax.ppermute(block, ('view', 'dp'), route)  48.2 us
    ppermute x20, starting transfers between devices, swap(): return lax.ppermute(block, ('view', 'dp'), route)  32.6 us
    dot_general x19, matrix products, matmul(): lax.dot_general(a, b, (((a_dim,), (b_dim,)), ((), ())), preferred_element...  27.1 us
    all_to_all x4, starting transfers between devices, exchange(): lax.all_to_all(blocks, 'dp', 0, 0, tiled=True, axis_index_groups=groups(a...  22.8 us
    all_to_all x4, waiting for transfers between devices, exchange(): lax.all_to_all(blocks, 'dp', 0, 0, tiled=True, axis_index_groups=groups(a...  14.4 us
    reduce_sum x1, other arithmetic, on_device(): mean = jnp.sum(wide, axis=0, keepdims=True) / samples  8.54 us
  transfers between devices with their start and end apart: 24, of which 9 were waited for; matrix products, arithmetic and copies ran while one was open for 26% of the time, Pallas kernels for 0%

profile of v3, /device:TPU:1, one launch (start us, length us, event | category | flops | bytes accessed | tf_op | source)
XLA Modules:
  0.0 170.1 jit_solution(8299162060672437582)
XLA Ops:
  0.6 0.9 pad.4
  1.6 1.6 broadcast_in_dim.18
  3.1 7.7 %all-to-all-start = ((bf16[16,16,4096]{2,1,0:T(8,128)(2,1)}), bf16[16,16,4096]{2,1,0:T(8,128)(2,1)S(1)}, u32[]{:S(2)}, u32[]{:S(2)}) async-start(bf16[16,16,4096]{2,1,0:T(8,128)(2,1)} %broadcast_in_dim.18), calls=%async_computation | async-start | bytes 4194304 | tf_op jit(solution)/shard_map/all_to_all | solution.py:37
  10.8 3.8 %collective-permute-start.1 = (bf16[4096,128]{1,0:T(8,128)(2,1)S(1)}, bf16[4096,128]{1,0:T(8,128)(2,1)}, u32[]{:S(2)}, u32[]{:S(2)}) collective-permute-start(bf16[4096,128]{1,0:T(8,128)(2,1)S(1)} %copy-done), channel_id=1, source_target_pairs={{0,72},{1,73},{2,74},{3,75},{4,76},{5,77},{6,78},{7,79},{8,64},{9,... | collective-permute-start | bytes 3145736 | tf_op jit(solution)/shard_map/ppermute | solution.py:33
  14.7 1.2 collective-permute-start
  15.9 21.4 %collective-permute-done.1 = bf16[4096,128]{1,0:T(8,128)(2,1)} collective-permute-done((bf16[4096,128]{1,0:T(8,128)(2,1)S(1)}, bf16[4096,128]{1,0:T(8,128)(2,1)}, u32[]{:S(2)}, u32[]{:S(2)}) %collective-permute-start.1) | collective-permute-done | bytes 1048608 | tf_op jit(solution)/shard_map/ppermute | solution.py:33
  37.4 1.5 collective-permute-start.2
  38.9 2.4 %all-to-all-done = bf16[16,16,4096]{2,1,0:T(8,128)(2,1)S(1)} async-done(((bf16[16,16,4096]{2,1,0:T(8,128)(2,1)}), bf16[16,16,4096]{2,1,0:T(8,128)(2,1)S(1)}, u32[]{:S(2)}, u32[]{:S(2)}) %all-to-all-start) | async-done | bytes 2097184 | tf_op jit(solution)/shard_map/all_to_all | solution.py:37
  42.2 2.1 %convolution_convert_fusion.3 = bf16[256,128]{0,1:T(8,128)(2,1)S(1)} fusion(bf16[256,4096]{1,0:T(8,128)(2,1)S(1)} %bitcast.34, bf16[4096,128]{1,0:T(8,128)(2,1)} %collective-permute-done.1), kind=kOutput, calls=%fused_computation.31 | convolution fusion | flops 268468224 | bytes 3211264 | tf_op jit(solution)/shard_map/dot_general | solution.py:41
  44.2 2.1 %convolution_convert_fusion.4 = bf16[256,128]{0,1:T(8,128)(2,1)S(1)} fusion(bf16[256,4096]{1,0:T(8,128)(2,1)S(1)} %bitcast.35, bf16[4096,128]{1,0:T(8,128)(2,1)} %collective-permute-done), kind=kOutput, calls=%fused_computation.32 | convolution fusion | flops 268468224 | bytes 3211264 | tf_op jit(solution)/shard_map/dot_general | solution.py:41
  46.3 2.1 %convolution_convert_fusion.2 = bf16[256,128]{0,1:T(8,128)(2,1)S(1)} fusion(bf16[256,4096]{1,0:T(8,128)(2,1)S(1)} %bitcast.36, bf16[4096,128]{1,0:T(8,128)(2,1)} %collective-permute-done.2), kind=kOutput, calls=%fused_computation.30 | convolution fusion | flops 268468224 | bytes 3211264 | tf_op jit(solution)/shard_map/dot_general | solution.py:41
  48.4 3.7 %collective-permute-start.5 = (bf16[256,512]{0,1:T(8,128)(2,1)S(1)}, bf16[256,512]{0,1:T(8,128)(2,1)S(1)}, u32[]{:S(2)}, u32[]{:S(2)}) collective-permute-start(bf16[256,512]{0,1:T(8,128)(2,1)S(1)} %pad_maximum_fusion), channel_id=1, source_target_pairs={{0,8},{1,9},{2,10},{3,11},{4,12},{5,13},{6,14},{7,15},{8,0},{9,1},... | collective-permute-start | bytes 786440 | tf_op jit(solution)/shard_map/ppermute | solution.py:33
  52.1 2.4 %collective-permute-start.4 = (bf16[256,512]{0,1:T(8,128)(2,1)S(1)}, bf16[256,512]{0,1:T(8,128)(2,1)S(1)}, u32[]{:S(2)}, u32[]{:S(2)}) collective-permute-start(bf16[256,512]{0,1:T(8,128)(2,1)S(1)} %pad_maximum_fusion), channel_id=1, source_target_pairs={{0,1},{1,0},{2,3},{3,2},{4,5},{5,4},{6,7},{7,6},{8,9},{9,8},{10,11... | collective-permute-start | bytes 786440 | tf_op jit(solution)/shard_map/ppermute | solution.py:33
  54.5 2.1 %collective-permute-done.5 = bf16[256,512]{0,1:T(8,128)(2,1)S(1)} collective-permute-done((bf16[256,512]{0,1:T(8,128)(2,1)S(1)}, bf16[256,512]{0,1:T(8,128)(2,1)S(1)}, u32[]{:S(2)}, u32[]{:S(2)}) %collective-permute-start.5) | collective-permute-done | bytes 262176 | tf_op jit(solution)/shard_map/ppermute | solution.py:33
  56.6 1.0 slice.96
  57.6 2.7 %collective-permute-start.7 = (bf16[256,1792]{1,0:T(8,128)(2,1)}, bf16[256,1792]{1,0:T(8,128)(2,1)}, u32[]{:S(2)}, u32[]{:S(2)}) collective-permute-start(bf16[256,1792]{1,0:T(8,128)(2,1)} %slice.96), channel_id=1, source_target_pairs={{0,8},{1,9},{2,10},{3,11},{4,12},{5,13},{6,14},{7,15},{8,0},{9,1},... | collective-permute-start | bytes 2752520 | tf_op jit(solution)/shard_map/ppermute | solution.py:33
  60.2 3.3 %collective-permute-start.6 = (bf16[256,512]{0,1:T(8,128)(2,1)S(1)}, bf16[256,512]{0,1:T(8,128)(2,1)S(1)}, u32[]{:S(2)}, u32[]{:S(2)}) collective-permute-start(bf16[256,512]{0,1:T(8,128)(2,1)S(1)} %collective-permute-done.5), channel_id=1, source_target_pairs={{0,1},{1,0},{2,3},{3,2},{4,5},{5,4},{6,7},{7,6},{8,9},{9,8},{10,11... | collective-permute-start | bytes 786440 | tf_op jit(solution)/shard_map/ppermute | solution.py:33
  63.6 1.1 collective-permute-done.6
  64.8 8.5 %convert_reduce_fusion.1 = (f32[512]{0:T(512)S(1)}, bf16[1024,512]{0,1:T(8,128)(2,1)S(1)}) fusion(bf16[256,128]{0,1:T(8,128)(2,1)S(1)} %get-tuple-element.28, bf16[256,128]{0,1:T(8,128)(2,1)S(1)} %get-tuple-element.29, bf16[256,128]{0,1:T(8,128)(2,1)S(1)} %get-tuple-element.30, bf16[256,128]{0,1:T(8,128)(2,1)S(1)} %get-tuple-element.27, ...), kind=kLoop, calls=%fused_computation.10 | loop fusion | flops 12582400 | bytes 2099200 | tf_op jit(solution)/shard_map/reduce_sum | solution.py:97
  73.6 1.3 convolution_convert_fusion.1
  74.9 4.3 %all-to-all-start.1 = ((bf16[16,16,1024]{2,1,0:T(8,128)(2,1)}), bf16[16,16,1024]{2,1,0:T(8,128)(2,1)}, u32[]{:S(2)}, u32[]{:S(2)}) async-start(bf16[16,16,1024]{2,1,0:T(8,128)(2,1)} %bitcast.44), calls=%async_computation.1 | async-start | bytes 1048576 | tf_op jit(solution)/shard_map/all_to_all | solution.py:37
  79.2 1.0 slice.97
  80.2 0.9 collective-permute-start.10
  81.1 8.8 %all-to-all-done.1 = bf16[16,16,1024]{2,1,0:T(8,128)(2,1)} async-done(((bf16[16,16,1024]{2,1,0:T(8,128)(2,1)}), bf16[16,16,1024]{2,1,0:T(8,128)(2,1)}, u32[]{:S(2)}, u32[]{:S(2)}) %all-to-all-start.1) | async-done | bytes 524320 | tf_op jit(solution)/shard_map/all_to_all | solution.py:37
  90.0 1.1 reduce_sum.41
  92.0 4.2 %all-to-all-start.2 = ((bf16[16,16,1024]{2,1,0:T(8,128)(2,1)}), bf16[16,16,1024]{2,1,0:T(8,128)(2,1)}, u32[]{:S(2)}, u32[]{:S(2)}) async-start(bf16[16,16,1024]{2,1,0:T(8,128)(2,1)} %broadcast_in_dim.32), calls=%async_computation.2 | async-start | bytes 1048576 | tf_op jit(solution)/shard_map/all_to_all | solution.py:37
  98.8 1.6 convert_element_type.63
  100.7 2.4 %collective-permute-start.13 = (bf16[256,1792]{1,0:T(8,128)(2,1)}, bf16[256,1792]{1,0:T(8,128)(2,1)}, u32[]{:S(2)}, u32[]{:S(2)}) collective-permute-start(bf16[256,1792]{1,0:T(8,128)(2,1)} %collective-permute-done.7), channel_id=1, source_target_pairs={{0,1},{1,0},{2,3},{3,2},{4,5},{5,4},{6,7},{7,6},{8,9},{9,8},{10,11... | collective-permute-start | bytes 2752520 | tf_op jit(solution)/shard_map/ppermute | solution.py:33
  103.1 3.1 %all-to-all-done.2 = bf16[16,16,1024]{2,1,0:T(8,128)(2,1)} async-done(((bf16[16,16,1024]{2,1,0:T(8,128)(2,1)}), bf16[16,16,1024]{2,1,0:T(8,128)(2,1)}, u32[]{:S(2)}, u32[]{:S(2)}) %all-to-all-start.2) | async-done | bytes 524320 | tf_op jit(solution)/shard_map/all_to_all | solution.py:37
  106.2 1.8 %fusion.13 = f32[256,512]{0,1:T(8,128)S(1)} fusion(bf16[256,1024]{1,0:T(8,128)(2,1)} %bitcast.3, bf16[1024,512]{0,1:T(8,128)(2,1)S(1)} %fusion.12, f32[1024,512]{0,1:T(8,128)} %convert_element_type.63, f32[512]{0:T(512)S(1)} %multiply_reduce_fusion), kind=kOutput, calls=%fused_computation.25 | convolution fusion | flops 268828672 | bytes 2623488 | tf_op jit(solution)/shard_map/dot_general | solution.py:41
  108.0 1.3 add_convert_fusion
  109.4 4.5 %collective-permute-done.9 = bf16[256,1024]{1,0:T(8,128)(2,1)} collective-permute-done((bf16[256,1024]{1,0:T(8,128)(2,1)}, bf16[256,1024]{1,0:T(8,128)(2,1)}, u32[]{:S(2)}, u32[]{:S(2)}) %collective-permute-start.9) | collective-permute-done | bytes 524320 | tf_op jit(solution)/shard_map/ppermute | solution.py:33
  113.9 2.8 %collective-permute-start.11 = (bf16[256,128]{0,1:T(8,128)(2,1)S(1)}, bf16[256,128]{0,1:T(8,128)(2,1)S(1)}, u32[]{:S(2)}, u32[]{:S(2)}) collective-permute-start(bf16[256,128]{0,1:T(8,128)(2,1)S(1)} %get-tuple-element.20), channel_id=1, source_target_pairs={{0,1},{1,0},{2,3},{3,2},{4,5},{5,4},{6,7},{7,6},{8,9},{9,8},{10,11... | collective-permute-start | bytes 196616 | tf_op jit(solution)/shard_map/ppermute | solution.py:33
  116.6 4.6 %convolution_convert_fusion = bf16[256,4096]{1,0:T(8,128)(2,1)} fusion(bf16[256,512]{0,1:T(8,128)(2,1)S(1)} %add_convert_fusion, bf16[4096,128]{1,0:T(8,128)(2,1)} %collective-permute-done.2, bf16[4096,128]{1,0:T(8,128)(2,1)} %collective-permute-done.1, bf16[4096,128]{1,0:T(8,128)(2,1)} %collective-permute-done, bf16[4096,128]{1,0:T(8,128)(2,1)S(1)} %copy-done.1), kind=kOutput, calls=%fused_computation | convolution fusion | flops 1091567616 | bytes 6553600 | tf_op jit(solution)/shard_map/dot_general | solution.py:41
  121.2 6.5 %all-to-all-start.3 = ((bf16[16,16,4096]{2,1,0:T(8,128)(2,1)}), bf16[16,16,4096]{2,1,0:T(8,128)(2,1)}, u32[]{:S(2)}, u32[]{:S(2)}) async-start(bf16[16,16,4096]{2,1,0:T(8,128)(2,1)} %bitcast.45), calls=%async_computation.3 | async-start | bytes 4194304 | tf_op jit(solution)/shard_map/all_to_all | solution.py:37
  128.1 2.2 %collective-permute-start.14 = (bf16[256,128]{0,1:T(8,128)(2,1)S(1)}, bf16[256,128]{0,1:T(8,128)(2,1)S(1)}, u32[]{:S(2)}, u32[]{:S(2)}) collective-permute-start(bf16[256,128]{0,1:T(8,128)(2,1)S(1)} %get-tuple-element.19), channel_id=1, source_target_pairs={{0,9},{1,8},{2,11},{3,10},{4,13},{5,12},{6,15},{7,14},{8,1},{9,0},... | collective-permute-start | bytes 196616 | tf_op jit(solution)/shard_map/ppermute | solution.py:33
  131.8 1.5 fusion.19
  133.2 1.6 fusion.16
  134.9 1.4 fusion.22
  137.5 1.6 fusion.38
  139.1 1.6 fusion.9
  141.6 1.4 fusion.15
  143.0 1.2 collective-permute-start.19
  144.5 1.5 fusion.10
  146.5 12.2 %collective-permute-done.19 = bf16[1024,128]{1,0:T(8,128)(2,1)S(1)} collective-permute-done((bf16[1024,128]{1,0:T(8,128)(2,1)S(1)}, bf16[1024,128]{1,0:T(8,128)(2,1)S(1)}, u32[]{:S(2)}, u32[]{:S(2)}) %collective-permute-start.19) | collective-permute-done | bytes 262176 | tf_op jit(solution)/shard_map/ppermute | solution.py:33
  158.8 6.9 %collective-permute-done.17 = bf16[1280,128]{1,0:T(8,128)(2,1)S(1)} collective-permute-done((bf16[1280,128]{1,0:T(8,128)(2,1)S(1)}, bf16[1280,128]{1,0:T(8,128)(2,1)S(1)}, u32[]{:S(2)}, u32[]{:S(2)}) %collective-permute-start.17) | collective-permute-done | bytes 327712 | tf_op jit(solution)/shard_map/ppermute | solution.py:33
  165.7 1.5 maximum_multiply_fusion
  167.2 1.9 %convert_reduce_fusion = f32[16,4096]{1,0:T(8,128)S(1)} fusion(bf16[16,16,4096]{2,1,0:T(8,128)(2,1)} %all-to-all-done.3), kind=kLoop, calls=%fused_computation.8 | loop fusion | flops 2031616 | bytes 2359296 | tf_op jit(solution)/shard_map/reduce_sum | solution.py:132
  (49 shorter events, 10.8 us)
Async XLA Ops:
  3.1 7.7 %copy-start = (bf16[4096,128]{1,0:T(8,128)(2,1)S(1)}, bf16[4096,128]{1,0:T(8,128)(2,1)}, u32[]{:S(2)}) copy-start(bf16[4096,128]{1,0:T(8,128)(2,1)} %param.3) | copy-start | bytes 3145732
  3.1 38.2 %all-to-all-start = ((bf16[16,16,4096]{2,1,0:T(8,128)(2,1)}), bf16[16,16,4096]{2,1,0:T(8,128)(2,1)S(1)}, u32[]{:S(2)}, u32[]{:S(2)}) async-start(bf16[16,16,4096]{2,1,0:T(8,128)(2,1)} %broadcast_in_dim.18), calls=%async_computation | async-start | bytes 4194304 | tf_op jit(solution)/shard_map/all_to_all | solution.py:37
  10.8 26.5 %collective-permute-start.1 = (bf16[4096,128]{1,0:T(8,128)(2,1)S(1)}, bf16[4096,128]{1,0:T(8,128)(2,1)}, u32[]{:S(2)}, u32[]{:S(2)}) collective-permute-start(bf16[4096,128]{1,0:T(8,128)(2,1)S(1)} %copy-done), channel_id=1, source_target_pairs={{0,72},{1,73},{2,74},{3,75},{4,76},{5,77},{6,78},{7,79},{8,64},{9,... | collective-permute-start | bytes 3145736 | tf_op jit(solution)/shard_map/ppermute | solution.py:33
  14.7 29.5 %collective-permute-start = (bf16[4096,128]{1,0:T(8,128)(2,1)S(1)}, bf16[4096,128]{1,0:T(8,128)(2,1)}, u32[]{:S(2)}, u32[]{:S(2)}) collective-permute-start(bf16[4096,128]{1,0:T(8,128)(2,1)S(1)} %copy-done), channel_id=1, source_target_pairs={{0,1},{1,0},{2,3},{3,2},{4,5},{5,4},{6,7},{7,6},{8,9},{9,8},{10,11... | collective-permute-start | bytes 3145736 | tf_op jit(solution)/shard_map/ppermute | solution.py:33
  37.4 8.9 %collective-permute-start.2 = (bf16[4096,128]{1,0:T(8,128)(2,1)}, bf16[4096,128]{1,0:T(8,128)(2,1)}, u32[]{:S(2)}, u32[]{:S(2)}) collective-permute-start(bf16[4096,128]{1,0:T(8,128)(2,1)} %collective-permute-done.1), channel_id=1, source_target_pairs={{0,1},{1,0},{2,3},{3,2},{4,5},{5,4},{6,7},{7,6},{8,9},{9,8},{10,11... | collective-permute-start | bytes 3145736 | tf_op jit(solution)/shard_map/ppermute | solution.py:33
  48.4 8.2 %collective-permute-start.5 = (bf16[256,512]{0,1:T(8,128)(2,1)S(1)}, bf16[256,512]{0,1:T(8,128)(2,1)S(1)}, u32[]{:S(2)}, u32[]{:S(2)}) collective-permute-start(bf16[256,512]{0,1:T(8,128)(2,1)S(1)} %pad_maximum_fusion), channel_id=1, source_target_pairs={{0,8},{1,9},{2,10},{3,11},{4,12},{5,13},{6,14},{7,15},{8,0},{9,1},... | collective-permute-start | bytes 786440 | tf_op jit(solution)/shard_map/ppermute | solution.py:33
  52.1 11.5 %collective-permute-start.4 = (bf16[256,512]{0,1:T(8,128)(2,1)S(1)}, bf16[256,512]{0,1:T(8,128)(2,1)S(1)}, u32[]{:S(2)}, u32[]{:S(2)}) collective-permute-start(bf16[256,512]{0,1:T(8,128)(2,1)S(1)} %pad_maximum_fusion), channel_id=1, source_target_pairs={{0,1},{1,0},{2,3},{3,2},{4,5},{5,4},{6,7},{7,6},{8,9},{9,8},{10,11... | collective-permute-start | bytes 786440 | tf_op jit(solution)/shard_map/ppermute | solution.py:33
  57.6 33.6 %collective-permute-start.7 = (bf16[256,1792]{1,0:T(8,128)(2,1)}, bf16[256,1792]{1,0:T(8,128)(2,1)}, u32[]{:S(2)}, u32[]{:S(2)}) collective-permute-start(bf16[256,1792]{1,0:T(8,128)(2,1)} %slice.96), channel_id=1, source_target_pairs={{0,8},{1,9},{2,10},{3,11},{4,12},{5,13},{6,14},{7,15},{8,0},{9,1},... | collective-permute-start | bytes 2752520 | tf_op jit(solution)/shard_map/ppermute | solution.py:33
  60.2 4.5 %collective-permute-start.6 = (bf16[256,512]{0,1:T(8,128)(2,1)S(1)}, bf16[256,512]{0,1:T(8,128)(2,1)S(1)}, u32[]{:S(2)}, u32[]{:S(2)}) collective-permute-start(bf16[256,512]{0,1:T(8,128)(2,1)S(1)} %collective-permute-done.5), channel_id=1, source_target_pairs={{0,1},{1,0},{2,3},{3,2},{4,5},{5,4},{6,7},{7,6},{8,9},{9,8},{10,11... | collective-permute-start | bytes 786440 | tf_op jit(solution)/shard_map/ppermute | solution.py:33
  74.9 15.1 %all-to-all-start.1 = ((bf16[16,16,1024]{2,1,0:T(8,128)(2,1)}), bf16[16,16,1024]{2,1,0:T(8,128)(2,1)}, u32[]{:S(2)}, u32[]{:S(2)}) async-start(bf16[16,16,1024]{2,1,0:T(8,128)(2,1)} %bitcast.44), calls=%async_computation.1 | async-start | bytes 1048576 | tf_op jit(solution)/shard_map/all_to_all | solution.py:37
  80.2 22.9 %collective-permute-start.8 = (bf16[256,1280]{1,0:T(8,128)(2,1)}, bf16[256,1280]{1,0:T(8,128)(2,1)}, u32[]{:S(2)}, u32[]{:S(2)}) collective-permute-start(bf16[256,1280]{1,0:T(8,128)(2,1)} %slice.97), channel_id=1, source_target_pairs={{0,8},{1,9},{2,10},{3,11},{4,12},{5,13},{6,14},{7,15},{8,0},{9,1},... | collective-permute-start | bytes 1966088 | tf_op jit(solution)/shard_map/ppermute | solution.py:33
  80.2 51.0 %collective-permute-start.10 = (bf16[256,4096]{1,0:T(8,128)(2,1)S(1)}, bf16[256,4096]{1,0:T(8,128)(2,1)}, u32[]{:S(2)}, u32[]{:S(2)}) collective-permute-start(bf16[256,4096]{1,0:T(8,128)(2,1)S(1)} %bitcast.39), channel_id=1, source_target_pairs={{0,1},{1,0},{2,3},{3,2},{4,5},{5,4},{6,7},{7,6},{8,9},{9,8},{10,11... | collective-permute-start | bytes 6291464 | tf_op jit(solution)/shard_map/ppermute | solution.py:33
  92.0 14.3 %all-to-all-start.2 = ((bf16[16,16,1024]{2,1,0:T(8,128)(2,1)}), bf16[16,16,1024]{2,1,0:T(8,128)(2,1)}, u32[]{:S(2)}, u32[]{:S(2)}) async-start(bf16[16,16,1024]{2,1,0:T(8,128)(2,1)} %broadcast_in_dim.32), calls=%async_computation.2 | async-start | bytes 1048576 | tf_op jit(solution)/shard_map/all_to_all | solution.py:37
  96.2 11.8 %collective-permute-start.3 = (bf16[256,512]{0,1:T(8,128)(2,1)S(1)}, bf16[256,512]{0,1:T(8,128)(2,1)}, u32[]{:S(2)}, u32[]{:S(2)}) collective-permute-start(bf16[256,512]{0,1:T(8,128)(2,1)S(1)} %pad_maximum_fusion), channel_id=1, source_target_pairs={{0,64},{1,65},{2,66},{3,67},{4,68},{5,69},{6,70},{7,71},{8,72},{9,... | collective-permute-start | bytes 786440 | tf_op jit(solution)/shard_map/ppermute | solution.py:33
  97.9 15.9 %collective-permute-start.9 = (bf16[256,1024]{1,0:T(8,128)(2,1)}, bf16[256,1024]{1,0:T(8,128)(2,1)}, u32[]{:S(2)}, u32[]{:S(2)}) collective-permute-start(bf16[256,1024]{1,0:T(8,128)(2,1)} %slice.98), channel_id=1, source_target_pairs={{0,8},{1,9},{2,10},{3,11},{4,12},{5,13},{6,14},{7,15},{8,0},{9,1},... | collective-permute-start | bytes 1572872 | tf_op jit(solution)/shard_map/ppermute | solution.py:33
  100.7 36.8 %collective-permute-start.13 = (bf16[256,1792]{1,0:T(8,128)(2,1)}, bf16[256,1792]{1,0:T(8,128)(2,1)}, u32[]{:S(2)}, u32[]{:S(2)}) collective-permute-start(bf16[256,1792]{1,0:T(8,128)(2,1)} %collective-permute-done.7), channel_id=1, source_target_pairs={{0,1},{1,0},{2,3},{3,2},{4,5},{5,4},{6,7},{7,6},{8,9},{9,8},{10,11... | collective-permute-start | bytes 2752520 | tf_op jit(solution)/shard_map/ppermute | solution.py:33
  106.2 10.4 %copy-start.1 = (bf16[4096,128]{1,0:T(8,128)(2,1)S(1)}, bf16[4096,128]{1,0:T(8,128)(2,1)}, u32[]{:S(2)}) copy-start(bf16[4096,128]{1,0:T(8,128)(2,1)} %param.3) | copy-start | bytes 3145732
  113.9 16.4 %collective-permute-start.11 = (bf16[256,128]{0,1:T(8,128)(2,1)S(1)}, bf16[256,128]{0,1:T(8,128)(2,1)S(1)}, u32[]{:S(2)}, u32[]{:S(2)}) collective-permute-start(bf16[256,128]{0,1:T(8,128)(2,1)S(1)} %get-tuple-element.20), channel_id=1, source_target_pairs={{0,1},{1,0},{2,3},{3,2},{4,5},{5,4},{6,7},{7,6},{8,9},{9,8},{10,11... | collective-permute-start | bytes 196616 | tf_op jit(solution)/shard_map/ppermute | solution.py:33
  121.2 46.0 %all-to-all-start.3 = ((bf16[16,16,4096]{2,1,0:T(8,128)(2,1)}), bf16[16,16,4096]{2,1,0:T(8,128)(2,1)}, u32[]{:S(2)}, u32[]{:S(2)}) async-start(bf16[16,16,4096]{2,1,0:T(8,128)(2,1)} %bitcast.45), calls=%async_computation.3 | async-start | bytes 4194304 | tf_op jit(solution)/shard_map/all_to_all | solution.py:37
  127.7 13.5 %collective-permute-start.18 = (bf16[256,1024]{1,0:T(8,128)(2,1)}, bf16[256,1024]{1,0:T(8,128)(2,1)S(1)}, u32[]{:S(2)}, u32[]{:S(2)}) collective-permute-start(bf16[256,1024]{1,0:T(8,128)(2,1)} %collective-permute-done.9), channel_id=1, source_target_pairs={{0,1},{1,0},{2,3},{3,2},{4,5},{5,4},{6,7},{7,6},{8,9},{9,8},{10,11... | collective-permute-start | bytes 1572872 | tf_op jit(solution)/shard_map/ppermute | solution.py:33
  128.1 9.4 %collective-permute-start.14 = (bf16[256,128]{0,1:T(8,128)(2,1)S(1)}, bf16[256,128]{0,1:T(8,128)(2,1)S(1)}, u32[]{:S(2)}, u32[]{:S(2)}) collective-permute-start(bf16[256,128]{0,1:T(8,128)(2,1)S(1)} %get-tuple-element.19), channel_id=1, source_target_pairs={{0,9},{1,8},{2,11},{3,10},{4,13},{5,12},{6,15},{7,14},{8,1},{9,0},... | collective-permute-start | bytes 196616 | tf_op jit(solution)/shard_map/ppermute | solution.py:33
  130.3 8.8 %collective-permute-start.12 = (bf16[256,128]{0,1:T(8,128)(2,1)S(1)}, bf16[256,128]{0,1:T(8,128)(2,1)S(1)}, u32[]{:S(2)}, u32[]{:S(2)}) collective-permute-start(bf16[256,128]{0,1:T(8,128)(2,1)S(1)} %get-tuple-element.18), channel_id=1, source_target_pairs={{0,8},{1,9},{2,10},{3,11},{4,12},{5,13},{6,14},{7,15},{8,0},{9,1},... | collective-permute-start | bytes 196616 | tf_op jit(solution)/shard_map/ppermute | solution.py:33
  131.2 13.0 %collective-permute-start.16 = (bf16[256,1280]{1,0:T(8,128)(2,1)}, bf16[256,1280]{1,0:T(8,128)(2,1)S(1)}, u32[]{:S(2)}, u32[]{:S(2)}) collective-permute-start(bf16[256,1280]{1,0:T(8,128)(2,1)} %collective-permute-done.8), channel_id=1, source_target_pairs={{0,1},{1,0},{2,3},{3,2},{4,5},{5,4},{6,7},{7,6},{8,9},{9,8},{10,11... | collective-permute-start | bytes 1966088 | tf_op jit(solution)/shard_map/ppermute | solution.py:33
  140.8 17.9 %collective-permute-start.15 = (bf16[1792,128]{1,0:T(8,128)(2,1)S(1)}, bf16[1792,128]{1,0:T(8,128)(2,1)S(1)}, u32[]{:S(2)}, u32[]{:S(2)}) collective-permute-start(bf16[1792,128]{1,0:T(8,128)(2,1)S(1)} %fusion.9), channel_id=1, source_target_pairs={{0,64},{1,65},{2,66},{3,67},{4,68},{5,69},{6,70},{7,71},{8,72},{9,... | collective-permute-start | bytes 1376264 | tf_op jit(solution)/shard_map/ppermute | solution.py:33
  143.0 15.7 %collective-permute-start.19 = (bf16[1024,128]{1,0:T(8,128)(2,1)S(1)}, bf16[1024,128]{1,0:T(8,128)(2,1)S(1)}, u32[]{:S(2)}, u32[]{:S(2)}) collective-permute-start(bf16[1024,128]{1,0:T(8,128)(2,1)S(1)} %fusion.15), channel_id=1, source_target_pairs={{0,64},{1,65},{2,66},{3,67},{4,68},{5,69},{6,70},{7,71},{8,72},{9,... | collective-permute-start | bytes 786440 | tf_op jit(solution)/shard_map/ppermute | solution.py:33
  146.0 19.6 %collective-permute-start.17 = (bf16[1280,128]{1,0:T(8,128)(2,1)S(1)}, bf16[1280,128]{1,0:T(8,128)(2,1)S(1)}, u32[]{:S(2)}, u32[]{:S(2)}) collective-permute-start(bf16[1280,128]{1,0:T(8,128)(2,1)S(1)} %fusion.10), channel_id=1, source_target_pairs={{0,64},{1,65},{2,66},{3,67},{4,68},{5,69},{6,70},{7,71},{8,72},{9,... | collective-permute-start | bytes 983048 | tf_op jit(solution)/shard_map/ppermute | solution.py:33

commit v4 on v3

v4 whole, which is shorter than its diff:
```python
import functools

import jax
import jax.numpy as jnp
from jax import lax
from jax.experimental import pallas as pl
from jax.experimental.pallas import tpu as pltpu
from jax.sharding import PartitionSpec as P

YS, ZS, XS, CS = 4, 2, 4, 2
DP = YS * ZS * XS * CS
PAD = 16
TILE = 512
VMEM = 40 * 1024 * 1024


def place(d):
    return (d // (ZS * XS * CS), d // (XS * CS) % ZS, d // CS % XS, d % CS)


def index(y, z, x, c):
    return ((y * ZS + z) * XS + x) * CS + c


def groups(axes):
    found = {}
    for d in range(DP):
        key = tuple(p for p, name in zip(place(d), "yzxc") if name not in axes)
        found.setdefault(key, []).append(d)
    return list(found.values())


def swap(block, view=0, z=0, c=0):
    route = []
    for v in range(2):
        for d in range(DP):
            y, zd, x, cd = place(d)
            route.append((v * DP + d, (v ^ view) * DP + index(y, zd ^ z, x, cd ^ c)))
    return lax.ppermute(block, ("view", "dp"), route)


def exchange(blocks, axes):
    return lax.all_to_all(blocks, "dp", 0, 0, tiled=True, axis_index_groups=groups(axes))


def matmul(a, b, a_dim, b_dim):
    return lax.dot_general(
        a, b, (((a_dim,), (b_dim,)), ((), ())), preferred_element_type=jnp.float32
    )


def reordered(block, order):
    return jnp.concatenate([block[:, 128 * i : 128 * i + 128] for i in order], axis=1)


def shape(dims, dtype=jnp.bfloat16):
    return jax.ShapeDtypeStruct(dims, dtype)


def params(steps=0):
    semantics = ("arbitrary",) * steps if steps else None
    return pltpu.CompilerParams(vmem_limit_bytes=VMEM, dimension_semantics=semantics)


def cost(flops, size):
    return pl.CostEstimate(flops=flops, bytes_accessed=size, transcendentals=0)


def without_padding(x, rows):
    n = x.shape[0] // PAD * rows
    out = lax.broadcasted_iota(jnp.int32, (n, x.shape[0]), 0)
    source = lax.broadcasted_iota(jnp.int32, (n, x.shape[0]), 1)
    pick = out + out // rows * (PAD - rows) == source
    return matmul(jnp.where(pick, 1.0, 0.0).astype(x.dtype), x, 1, 0).astype(x.dtype)


def compact_kernel(rows, x_ref, *o_refs):
    at = 0
    for ref in o_refs:
        n = ref.shape[1]
        ref[...] = without_padding(x_ref[:, at : at + n], rows)
        at += n


def compact(block, rows, widths):
    n = block.shape[0] // PAD * rows
    return pl.pallas_call(
        functools.partial(compact_kernel, rows),
        out_shape=tuple(shape((n, width)) for width in widths),
        compiler_params=params(),
        cost_estimate=cost(2 * n * block.size, 4 * block.size),
    )(block)


def copies_kernel(x_ref, o_ref):
    x = x_ref[0]
    zeros = jnp.zeros((PAD - x.shape[0], x.shape[1]), x.dtype)
    x = jnp.concatenate([x, zeros], axis=0)
    for i in range(o_ref.shape[0] // PAD):
        o_ref[PAD * i : PAD * i + PAD, :] = x


def embed_kernel(h_ref, a_ref, b_ref, c_ref, d_ref, o_ref, acc_ref):
    step = pl.program_id(0)

    @pl.when(step == 0)
    def _():
        acc_ref[...] = jnp.zeros_like(acc_ref)

    w = jnp.concatenate([a_ref[...], b_ref[...], c_ref[...], d_ref[...]], axis=1)
    acc_ref[...] += matmul(h_ref[...], w, 1, 0)

    @pl.when(step == pl.num_programs(0) - 1)
    def _():
        o_ref[...] = acc_ref[...].astype(o_ref.dtype)


def center_kernel(rows, samples, own_ref, sib_ref, far_ref, far_sib_ref, c_ref, f_ref, g_ref):
    quarter = own_ref.shape[0]
    blocks = [
        own_ref[...],
        reordered(sib_ref[...], (1, 0, 3, 2)),
        reordered(far_ref[...], (2, 3, 0, 1)),
        reordered(far_sib_ref[...], (3, 2, 1, 0)),
    ]
    wide = [block.astype(jnp.float32) for block in blocks]
    total = wide[0] + wide[1] + wide[2] + wide[3]
    mean = jnp.sum(total, axis=0, keepdims=True) * (1.0 / samples)
    real = lax.broadcasted_iota(jnp.int32, wide[0].shape, 0) % PAD < rows
    squares = jnp.zeros_like(total)
    for i, block in enumerate(wide):
        centered = jnp.where(real, block - mean, 0.0).astype(jnp.bfloat16)
        c_ref[quarter * i : quarter * i + quarter, :] = centered
        centered = centered.astype(jnp.float32)
        squares += centered * centered
    sum_squares = jnp.sum(squares, axis=0, keepdims=True)
    spread_std = jnp.sqrt(sum_squares * (1.0 / (samples - 1)) + 0.0001)
    coef_var = samples / (2.0 * (samples - 1))
    hinge = jax.nn.sigmoid(10.0 * (1.0 - spread_std))
    coef_cov = 0.08 * samples / ((samples - 1) * (samples - 1))
    factor = coef_var * hinge / spread_std + coef_cov * sum_squares
    f_ref[...] = jnp.broadcast_to(factor, f_ref.shape)
    g_ref[...] = matmul(c_ref[:quarter, :], c_ref[...], 1, 1).astype(g_ref.dtype)


def total_kernel(x_ref, o_ref):
    x = x_ref[...].reshape(x_ref.shape[0] // PAD, PAD, x_ref.shape[1])
    total = jnp.sum(x.astype(jnp.float32), axis=0).astype(o_ref.dtype)
    for i in range(o_ref.shape[0] // PAD):
        o_ref[PAD * i : PAD * i + PAD, :] = total


def grad_kernel(rows, samples, m_ref, c_ref, f_ref, e_ref, p_ref, o_ref, *run_refs):
    coef_cov = 0.08 * samples / ((samples - 1) * (samples - 1))
    coupled = matmul(m_ref[...], c_ref[...], 1, 0)
    centered = c_ref[: e_ref.shape[0], :].astype(jnp.float32)
    apart = e_ref[...].astype(jnp.float32) - p_ref[...].astype(jnp.float32)
    grad = apart - f_ref[:1, :] * centered + coef_cov * coupled
    grad = grad.astype(jnp.bfloat16)
    o_ref[...] = grad
    for i, ref in enumerate(run_refs[:2]):
        ref[...] = grad[:, 128 * i : 128 * i + 128]
    packed = without_padding(grad[:, 256:], rows)
    for i, ref in enumerate(run_refs[2:]):
        ref[...] = packed[:, 128 * i : 128 * i + 128]


def hidden_kernel(g_ref, a_ref, b_ref, c_ref, d_ref, o_ref):
    w = jnp.concatenate([a_ref[...], b_ref[...], c_ref[...], d_ref[...]], axis=1)
    o_ref[...] = matmul(g_ref[...], w, 1, 1).astype(o_ref.dtype)


def weight_kernel(h0_ref, h1_ref, h2_ref, h3_ref, g0_ref, g1_ref, g2_ref, g3_ref, o_ref):
    h = jnp.concatenate([h0_ref[...], h1_ref[...], h2_ref[...], h3_ref[...]], axis=0)
    g = jnp.concatenate([g0_ref[...], g1_ref[...], g2_ref[...], g3_ref[...]], axis=0)
    o_ref[...] = matmul(h, g, 0, 0).astype(o_ref.dtype)


def copies_of(block, count):
    n = block.shape[-1]
    return pl.pallas_call(
        copies_kernel,
        out_shape=shape((count * PAD, n)),
        compiler_params=params(),
        cost_estimate=cost(0, 2 * count * PAD * n),
    )(block)


def embed(plane, weights, tile=TILE):
    rows, width = plane.shape
    units = weights[0].shape[1]
    return pl.pallas_call(
        embed_kernel,
        grid=(width // tile,),
        in_specs=[pl.BlockSpec((rows, tile), lambda k: (0, k))]
        + [pl.BlockSpec((tile, units), lambda k: (k, 0))] * 4,
        out_specs=pl.BlockSpec((rows, 4 * units), lambda k: (0, 0)),
        out_shape=shape((rows, 4 * units)),
        scratch_shapes=[pltpu.VMEM((rows, 4 * units), jnp.float32)],
        compiler_params=params(1),
        cost_estimate=cost(8 * rows * width * units, 2 * width * (rows + 4 * units)),
    )(plane, *weights)


def hidden_terms(grad, weights, tile=TILE):
    rows, units = grad.shape[0], weights[0].shape[1]
    width = weights[0].shape[0]
    return pl.pallas_call(
        hidden_kernel,
        grid=(width // tile,),
        in_specs=[pl.BlockSpec(grad.shape, lambda n: (0, 0))]
        + [pl.BlockSpec((tile, units), lambda n: (n, 0))] * 4,
        out_specs=pl.BlockSpec((rows, tile), lambda n: (0, n)),
        out_shape=shape((rows, width)),
        compiler_params=params(1),
        cost_estimate=cost(8 * rows * width * units, 2 * width * (rows + 4 * units)),
    )(grad, *weights)


def weight_terms(parts, grads, tile=TILE):
    rows, units = grads[-1].shape
    width = min(array.shape[1] for array, _ in parts)
    specs = [
        pl.BlockSpec((array.shape[0], tile), lambda n, first=first: (0, n + first))
        for array, first in parts
    ]
    return pl.pallas_call(
        weight_kernel,
        grid=(width // tile,),
        in_specs=specs + [pl.BlockSpec(g.shape, lambda n: (0, 0)) for g in grads],
        out_specs=pl.BlockSpec((tile, units), lambda n: (n, 0)),
        out_shape=shape((width, units)),
        compiler_params=params(1),
        cost_estimate=cost(8 * rows * width * units, 8 * width * rows + 2 * width * units),
    )(*[array for array, _ in parts], *grads)


def wide_sum(a, b):
    return a.astype(jnp.float32) + b.astype(jnp.float32)


def on_device(hidden, weight):
    rows = hidden.shape[1]
    width = hidden.shape[2]
    samples = rows * DP
    units = weight.shape[1]
    peers = YS * XS
    quarter = peers * PAD

    w_far = swap(weight, view=1, z=1)
    w_sib = swap(weight, c=1)
    w_far_sib = swap(w_far, c=1)
    weights = (weight, w_sib, w_far, w_far_sib)

    plane = exchange(copies_of(hidden, peers), "yx")
    plane, w_far_sib = lax.optimization_barrier((plane, w_far_sib))

    mine = embed(plane, weights)
    from_sib = swap(mine, c=1)
    from_far = swap(mine, z=1)
    from_far_sib = swap(from_far, c=1)
    partner = swap(mine, view=1)

    cuts = (0, width // 2, 3 * width // 4, width)
    late, _ = lax.optimization_barrier((plane, from_far))
    h_far = compact(late, rows, [high - low for low, high in zip(cuts, cuts[1:])])
    h_far = [swap(block, z=1) for block in h_far]
    h_sib = swap(plane, c=1)

    centered, factor, gram = pl.pallas_call(
        functools.partial(center_kernel, rows, samples),
        out_shape=(
            shape((4 * quarter, 4 * units)),
            shape((8, 4 * units), jnp.float32),
            shape((quarter, 4 * quarter)),
        ),
        compiler_params=params(),
        cost_estimate=cost(8 * 4 * quarter * quarter * units, 16 * quarter * units * 2),
    )(mine, from_sib, from_far, from_far_sib)

    gram = exchange(gram, "yx")
    gram = pl.pallas_call(
        total_kernel,
        out_shape=shape(gram.shape),
        compiler_params=params(),
        cost_estimate=cost(gram.size, 4 * gram.size),
    )(gram)
    gram, h_far[0] = lax.optimization_barrier((gram, h_far[0]))
    gram = exchange(gram, "yx")
    gram, h_far[0], h_far[1] = lax.optimization_barrier((gram, h_far[0], h_far[1]))

    grad, *runs = pl.pallas_call(
        functools.partial(grad_kernel, rows, samples),
        out_shape=(shape((quarter, 4 * units)),)
        + (shape((quarter, units)),) * 2
        + (shape((peers * rows, units)),) * 2,
        compiler_params=params(),
        cost_estimate=cost(8 * 4 * quarter * quarter * units, 16 * quarter * units * 2),
    )(gram, centered, factor, mine, partner)
    grads = (
        swap(runs[2], z=1),
        swap(runs[3], z=1, c=1),
        runs[0],
        swap(runs[1], c=1),
    )

    h_part = hidden_terms(grad, weights)
    h_part, h_far[2] = lax.optimization_barrier((h_part, h_far[2]))
    pieces = exchange(h_part, "yx").reshape(peers, PAD, width)
    grad_rows = jnp.sum(pieces.astype(jnp.float32), axis=0)[:rows]

    runs = []
    for at, far in zip(cuts, h_far):
        first = at // TILE
        total = weight_terms(
            ((far, 0), (swap(far, c=1), 0), (plane, first), (h_sib, first)), grads
        )
        runs.append(wide_sum(total, swap(total, view=1)))
    grad_weight = jnp.concatenate(runs, axis=0) / jnp.sqrt(2.0 * samples)
    return (grad_rows[None], grad_weight)


def solution(mesh):
    return jax.shard_map(
        on_device,
        mesh=mesh,
        in_specs=(P("view", "dp", None), P(None, "dp")),
        out_specs=(P("view", "dp", None), P(None, "dp")),
        check_vma=False,
    )
```

time: 171 us -> 181 us (1.058)
  matrix products: 27.1 us -> 0 us
  Pallas kernels: 0 us -> 24.3 us
  waiting for transfers between devices: 62.6 us -> 78.7 us
  blocking collectives: 0 us -> 15.1 us
  other arithmetic: 16.8 us -> 3.62 us
  starting transfers between devices: 55.4 us -> 46.3 us
  local copies, waits for them, and re-layouts: 7.17 us -> 11.4 us
    dot_general x19 -> x0, matrix products: 27.1 us -> none  [matmul(): lax.dot_general(a, b, (((a_dim,), (b_dim,)), ((), ())), preferred_element...]
    pallas_call x0 -> x10, Pallas kernels: none -> 24.3 us  [the longest x3 8.22 us: weight_terms(): pl.pallas_call(weight_kernel, grid=(width // tile,), in_specs=specs + [pl...]
    ppermute x20, waiting for transfers between devices: 48.2 us -> 64.1 us  [swap(): return lax.ppermute(block, ('view', 'dp'), route)]
    all_to_all x0 -> x1, blocking collectives: none -> 15.1 us  [exchange(): lax.all_to_all(blocks, 'dp', 0, 0, tiled=True, axis_index_groups=groups(a...]
    unnamed x4 -> x26, local copies, waits for them, and re-layouts: 0.01 us -> 10.5 us
    reduce_sum x3 -> x0, other arithmetic: 9.95 us -> none  [the longest x1 8.54 us: on_device(): mean = jnp.sum(wide, axis=0, keepdims=True) / samples]
    all_to_all x4 -> x3, starting transfers between devices: 22.8 us -> 17.8 us  [exchange(): lax.all_to_all(blocks, 'dp', 0, 0, tiled=True, axis_index_groups=groups(a...]
    ppermute x20, starting transfers between devices: 32.6 us -> 28.6 us  [swap(): return lax.ppermute(block, ('view', 'dp'), route)]
  transfers between devices with their start and end apart: 24 -> 23, of which waited for: 9 -> 10; matrix products, arithmetic and copies ran while one was open for 26% -> 1% of each run, Pallas kernels for 0% -> 10%
where the time goes in v4:
time: 181 us; the launch traced here: 180 us
  waiting for transfers between devices  78.7 us (43%)
  starting transfers between devices  46.3 us (26%)
  Pallas kernels  24.3 us (13%)
  blocking collectives  15.1 us (8%)
  local copies, waits for them, and re-layouts  11.4 us (6%)
  other arithmetic  3.62 us (2%)
    ppermute x20, waiting for transfers between devices, swap(): return lax.ppermute(block, ('view', 'dp'), route)  64.1 us
    ppermute x20, starting transfers between devices, swap(): return lax.ppermute(block, ('view', 'dp'), route)  28.6 us
    all_to_all x3, starting transfers between devices, exchange(): lax.all_to_all(blocks, 'dp', 0, 0, tiled=True, axis_index_groups=groups(a...  17.8 us
    all_to_all x1, blocking collectives, exchange(): lax.all_to_all(blocks, 'dp', 0, 0, tiled=True, axis_index_groups=groups(a...  15.1 us
    all_to_all x3, waiting for transfers between devices, exchange(): lax.all_to_all(blocks, 'dp', 0, 0, tiled=True, axis_index_groups=groups(a...  14.6 us
    unnamed x26, local copies, waits for them, and re-layouts  10.5 us
    pallas_call x3, Pallas kernels, weight_terms(): pl.pallas_call(weight_kernel, grid=(width // tile,), in_specs=specs + [pl...  8.22 us
    pallas_call x1, Pallas kernels, hidden_terms(): pl.pallas_call(hidden_kernel, grid=(width // tile,), in_specs=[pl.BlockSp...  5.96 us
  transfers between devices with their start and end apart: 23, of which 10 were waited for; matrix products, arithmetic and copies ran while one was open for 1% of the time, Pallas kernels for 10%

profile of v4, /device:TPU:1, one launch (start us, length us, event | category | flops | bytes accessed | tf_op | source)
XLA Modules:
  0.0 180.3 jit_solution(18091313531972722168)
XLA Ops:
  0.6 4.7 %collective-permute-start = (bf16[4096,128]{1,0:T(8,128)(2,1)}, bf16[4096,128]{1,0:T(8,128)(2,1)}, u32[]{:S(2)}, u32[]{:S(2)}) collective-permute-start(bf16[4096,128]{1,0:T(8,128)(2,1)} %a_ref.3), channel_id=1, source_target_pairs={{0,72},{1,73},{2,74},{3,75},{4,76},{5,77},{6,78},{7,79},{8,64},{9,... | collective-permute-start | bytes 3145736 | tf_op jit(solution)/shard_map/ppermute | solution.py:39
  5.3 0.9 copy-done.8
  6.4 1.3 copy-done.1
  7.7 6.9 %all-to-all-start = ((bf16[16,16,4096]{2,1,0:T(8,128)(2,1)}), bf16[16,16,4096]{2,1,0:T(8,128)(2,1)S(1)}, u32[]{:S(2)}, u32[]{:S(2)}) async-start(bf16[16,16,4096]{2,1,0:T(8,128)(2,1)} %bitcast.15), calls=%async_computation | async-start | bytes 4194304 | tf_op jit(solution)/shard_map/all_to_all | solution.py:43
  14.6 13.9 %collective-permute-done.c_ref = bf16[4096,128]{1,0:T(8,128)(2,1)} collective-permute-done((bf16[4096,128]{1,0:T(8,128)(2,1)}, bf16[4096,128]{1,0:T(8,128)(2,1)}, u32[]{:S(2)}, u32[]{:S(2)}) %collective-permute-start) | collective-permute-done | bytes 1048608 | tf_op jit(solution)/shard_map/ppermute | solution.py:39
  28.5 1.2 collective-permute-start.1
  29.7 14.6 %all-to-all-done = bf16[16,16,4096]{2,1,0:T(8,128)(2,1)S(1)} async-done(((bf16[16,16,4096]{2,1,0:T(8,128)(2,1)}), bf16[16,16,4096]{2,1,0:T(8,128)(2,1)S(1)}, u32[]{:S(2)}, u32[]{:S(2)}) %all-to-all-start) | async-done | bytes 2097184 | tf_op jit(solution)/shard_map/all_to_all | solution.py:43
  44.3 5.9 %shard_map.42.own_ref.e_ref = bf16[256,512]{1,0:T(8,128)(2,1)S(1)} custom-call(bf16[256,4096]{1,0:T(8,128)(2,1)S(1)} %bitcast.8, bf16[4096,128]{1,0:T(8,128)(2,1)S(1)} %copy-done.2, bf16[4096,128]{1,0:T(8,128)(2,1)} %collective-permute-done.2.b_ref, bf16[4096,128]{1,0:T(8,128)(2,1)} %collective-permute-done.c_ref, bf16[4096,128]{1,0:T(8,128)(2,1)} %collective-permute-done.1.d_ref), custom_call_target="tpu_custom_call" | custom-call | flops 1073741824 | bytes 6291456 | tf_op jit(solution)/shard_map/pallas_call | solution.py:192
  50.7 6.4 %collective-permute-done.4.far_ref = bf16[256,512]{1,0:T(8,128)(2,1)S(1)} collective-permute-done((bf16[256,512]{1,0:T(8,128)(2,1)S(1)}, bf16[256,512]{1,0:T(8,128)(2,1)S(1)}, u32[]{:S(2)}, u32[]{:S(2)}) %collective-permute-start.4) | collective-permute-done | bytes 262176 | tf_op jit(solution)/shard_map/ppermute | solution.py:39
  57.1 0.6 shard_map.45
  57.7 0.8 copy-done.9
  58.5 0.8 copy-done.10
  59.3 0.7 collective-permute-start.6
  60.0 3.4 %collective-permute-start.11 = (bf16[256,4096]{1,0:T(8,128)(2,1)S(1)}, bf16[256,4096]{1,0:T(8,128)(2,1)}, u32[]{:S(2)}, u32[]{:S(2)}) collective-permute-start(bf16[256,4096]{1,0:T(8,128)(2,1)S(1)} %bitcast.10), channel_id=1, source_target_pairs={{0,1},{1,0},{2,3},{3,2},{4,5},{5,4},{6,7},{7,6},{8,9},{9,8},{10,11... | collective-permute-start | bytes 6291464 | tf_op jit(solution)/shard_map/ppermute | solution.py:39
  63.5 0.5 collective-permute-start.5
  64.0 3.5 %collective-permute-done.3.sib_ref = bf16[256,512]{1,0:T(8,128)(2,1)S(1)} collective-permute-done((bf16[256,512]{1,0:T(8,128)(2,1)S(1)}, bf16[256,512]{1,0:T(8,128)(2,1)S(1)}, u32[]{:S(2)}, u32[]{:S(2)}) %collective-permute-start.3) | collective-permute-done | bytes 262176 | tf_op jit(solution)/shard_map/ppermute | solution.py:39
  67.9 0.9 shard_map.43
  68.8 1.0 copy-done.4
  69.8 15.1 %all_to_all.44 = bf16[16,16,1024]{2,1,0:T(8,128)(2,1)S(1)} all-to-all(bf16[16,16,1024]{2,1,0:T(8,128)(2,1)S(1)} %bitcast.18), channel_id=1, replica_groups={{0,2,4,6,16,18,20,22,32,34,36,38,48,50,52,54},{1,3,5,7,17,19,21,23,33,3..., dimensions={0} | all-to-all | bytes 1048576 | tf_op jit(solution)/shard_map/all_to_all | solution.py:43
  84.9 0.8 copy-done.3
  85.7 4.2 %all-to-all-start.2 = ((bf16[16,16,1024]{2,1,0:T(8,128)(2,1)}), bf16[16,16,1024]{2,1,0:T(8,128)(2,1)}, u32[]{:S(2)}, u32[]{:S(2)}) async-start(bf16[16,16,1024]{2,1,0:T(8,128)(2,1)} %bitcast.16), calls=%async_computation.2 | async-start | bytes 1048576 | tf_op jit(solution)/shard_map/all_to_all | solution.py:43
  90.0 3.0 %collective-permute-start.7 = (bf16[224,1024]{1,0:T(8,128)(2,1)}, bf16[224,1024]{1,0:T(8,128)(2,1)}, u32[]{:S(2)}, u32[]{:S(2)}) collective-permute-start(bf16[224,1024]{1,0:T(8,128)(2,1)} %copy-done.10), channel_id=1, source_target_pairs={{0,8},{1,9},{2,10},{3,11},{4,12},{5,13},{6,14},{7,15},{8,0},{9,1},... | collective-permute-start | bytes 1376264 | tf_op jit(solution)/shard_map/ppermute | solution.py:39
  93.1 0.8 collective-permute-start.8
  94.0 8.4 %collective-permute-done.7.h0_ref = bf16[224,1024]{1,0:T(8,128)(2,1)} collective-permute-done((bf16[224,1024]{1,0:T(8,128)(2,1)}, bf16[224,1024]{1,0:T(8,128)(2,1)}, u32[]{:S(2)}, u32[]{:S(2)}) %collective-permute-start.7) | collective-permute-done | bytes 458784 | tf_op jit(solution)/shard_map/ppermute | solution.py:39
  102.3 4.6 %collective-permute-start.10 = (bf16[224,2048]{1,0:T(8,128)(2,1)}, bf16[224,2048]{1,0:T(8,128)(2,1)}, u32[]{:S(2)}, u32[]{:S(2)}) collective-permute-start(bf16[224,2048]{1,0:T(8,128)(2,1)} %collective-permute-done.6.h0_ref), channel_id=1, source_target_pairs={{0,1},{1,0},{2,3},{3,2},{4,5},{5,4},{6,7},{7,6},{8,9},{9,8},{10,11... | collective-permute-start | bytes 2752520 | tf_op jit(solution)/shard_map/ppermute | solution.py:39
  106.9 10.4 %collective-permute-done.8.p_ref = bf16[256,512]{1,0:T(8,128)(2,1)} collective-permute-done((bf16[256,512]{1,0:T(8,128)(2,1)S(1)}, bf16[256,512]{1,0:T(8,128)(2,1)}, u32[]{:S(2)}, u32[]{:S(2)}) %collective-permute-start.8) | collective-permute-done | bytes 262176 | tf_op jit(solution)/shard_map/ppermute | solution.py:39
  117.3 1.2 copy-done.5
  118.5 2.4 %shard_map.46 = (bf16[256,512]{1,0:T(8,128)(2,1)S(1)}, bf16[256,128]{1,0:T(8,128)(2,1)S(1)}, bf16[256,128]{1,0:T(8,128)(2,1)S(1)}, bf16[224,128]{1,0:T(8,128)(2,1)}, bf16[224,128]{1,0:T(8,128)(2,1)S(1)}) custom-call(bf16[256,1024]{1,0:T(8,128)(2,1)} %bitcast.5.m_ref, bf16[1024,512]{1,0:T(8,128)(2,1)S(1)} %copy-done.5, f32[8,512]{1,0:T(8,128)S(1)} %get-tuple-element.31.f_ref, ...), custom_call_target="tpu_custom_call" | custom-call | flops 268435456 | bytes 1048576 | tf_op jit(solution)/shard_map/pallas_call | solution.py:292
  120.9 0.6 copy-done.11
  121.5 6.0 %shard_map.47 = bf16[256,4096]{1,0:T(8,128)(2,1)S(1)} custom-call(bf16[256,512]{1,0:T(8,128)(2,1)S(1)} %get-tuple-element.32.g_ref, bf16[4096,128]{1,0:T(8,128)(2,1)S(1)} %copy-done.2, bf16[4096,128]{1,0:T(8,128)(2,1)} %collective-permute-done.2.b_ref, bf16[4096,128]{1,0:T(8,128)(2,1)} %collective-permute-done.c_ref, ...), custom_call_target="tpu_custom_call" | custom-call | flops 1073741824 | bytes 6291456 | tf_op jit(solution)/shard_map/pallas_call | solution.py:208
  127.5 1.3 copy-done
  128.8 2.5 %collective-permute-start.18 = (bf16[224,1024]{1,0:T(8,128)(2,1)}, bf16[224,1024]{1,0:T(8,128)(2,1)S(1)}, u32[]{:S(2)}, u32[]{:S(2)}) collective-permute-start(bf16[224,1024]{1,0:T(8,128)(2,1)} %collective-permute-done.9.h0_ref), channel_id=1, source_target_pairs={{0,1},{1,0},{2,3},{3,2},{4,5},{5,4},{6,7},{7,6},{8,9},{9,8},{10,11... | collective-permute-start | bytes 1376264 | tf_op jit(solution)/shard_map/ppermute | solution.py:39
  131.3 2.0 %collective-permute-start.12 = (bf16[224,128]{1,0:T(8,128)(2,1)}, bf16[224,128]{1,0:T(8,128)(2,1)S(1)}, u32[]{:S(2)}, u32[]{:S(2)}) collective-permute-start(bf16[224,128]{1,0:T(8,128)(2,1)} %get-tuple-element.36), channel_id=1, source_target_pairs={{0,8},{1,9},{2,10},{3,11},{4,12},{5,13},{6,14},{7,15},{8,0},{9,1},... | collective-permute-start | bytes 172040 | tf_op jit(solution)/shard_map/ppermute | solution.py:39
  133.3 6.6 %all-to-all-start.3 = ((bf16[16,16,4096]{2,1,0:T(8,128)(2,1)}), bf16[16,16,4096]{2,1,0:T(8,128)(2,1)}, u32[]{:S(2)}, u32[]{:S(2)}) async-start(bf16[16,16,4096]{2,1,0:T(8,128)(2,1)} %bitcast.14), calls=%async_computation.3 | async-start | bytes 4194304 | tf_op jit(solution)/shard_map/all_to_all | solution.py:43
  140.0 2.0 %collective-permute-start.13 = (bf16[224,128]{1,0:T(8,128)(2,1)S(1)}, bf16[224,128]{1,0:T(8,128)(2,1)S(1)}, u32[]{:S(2)}, u32[]{:S(2)}) collective-permute-start(bf16[224,128]{1,0:T(8,128)(2,1)S(1)} %copy-done.12), channel_id=1, source_target_pairs={{0,9},{1,8},{2,11},{3,10},{4,13},{5,12},{6,15},{7,14},{8,1},{9,0},... | collective-permute-start | bytes 172040 | tf_op jit(solution)/shard_map/ppermute | solution.py:39
  142.0 3.8 %collective-permute-done.13.g1_ref = bf16[224,128]{1,0:T(8,128)(2,1)S(1)} collective-permute-done((bf16[224,128]{1,0:T(8,128)(2,1)S(1)}, bf16[224,128]{1,0:T(8,128)(2,1)S(1)}, u32[]{:S(2)}, u32[]{:S(2)}) %collective-permute-start.13) | collective-permute-done | bytes 57376 | tf_op jit(solution)/shard_map/ppermute | solution.py:39
  145.8 0.7 collective-permute-start.14
  146.5 0.9 collective-permute-done.14.g3_ref
  147.4 0.8 copy-done.6
  148.2 1.0 copy-done.7
  149.2 2.1 %shard_map.50 = bf16[1024,128]{1,0:T(8,128)(2,1)S(1)} custom-call(bf16[224,1024]{1,0:T(8,128)(2,1)} %collective-permute-done.9.h0_ref, bf16[224,1024]{1,0:T(8,128)(2,1)S(1)} %copy-done.7, bf16[256,4096]{1,0:T(8,128)(2,1)S(1)} %bitcast.11, bf16[256,4096]{1,0:T(8,128)(2,1)} %collective-permute-done.11.h3_ref, ...), custom_call_target="tpu_custom_call" | custom-call | flops 268435456 | bytes 2359296 | tf_op jit(solution)/shard_map/pallas_call | solution.py:227
  151.5 3.9 %shard_map.48 = bf16[2048,128]{1,0:T(8,128)(2,1)S(1)} custom-call(bf16[224,2048]{1,0:T(8,128)(2,1)} %collective-permute-done.6.h0_ref, bf16[224,2048]{1,0:T(8,128)(2,1)} %collective-permute-done.10.h1_ref, bf16[256,4096]{1,0:T(8,128)(2,1)S(1)} %bitcast.12, bf16[256,4096]{1,0:T(8,128)(2,1)} %collective-permute-done.11.h3_ref, ...), custom_call_target="tpu_custom_call" | custom-call | flops 536870912 | bytes 4718592 | tf_op jit(solution)/shard_map/pallas_call | solution.py:227
  155.4 1.5 collective-permute-start.15
  156.8 2.2 %shard_map.49 = bf16[1024,128]{1,0:T(8,128)(2,1)S(1)} custom-call(bf16[224,1024]{1,0:T(8,128)(2,1)} %collective-permute-done.7.h0_ref, bf16[224,1024]{1,0:T(8,128)(2,1)} %collective-permute-done.16.h1_ref, bf16[256,4096]{1,0:T(8,128)(2,1)S(1)} %bitcast.13, bf16[256,4096]{1,0:T(8,128)(2,1)} %collective-permute-done.11.h3_ref, ...), custom_call_target="tpu_custom_call" | custom-call | flops 268435456 | bytes 2359296 | tf_op jit(solution)/shard_map/pallas_call | solution.py:227
  159.3 16.5 %collective-permute-done.17 = bf16[1024,128]{1,0:T(8,128)(2,1)S(1)} collective-permute-done((bf16[1024,128]{1,0:T(8,128)(2,1)S(1)}, bf16[1024,128]{1,0:T(8,128)(2,1)S(1)}, u32[]{:S(2)}, u32[]{:S(2)}) %collective-permute-start.17) | collective-permute-done | bytes 262176 | tf_op jit(solution)/shard_map/ppermute | solution.py:39
  176.0 1.5 maximum_multiply_fusion
  177.5 1.9 %convert_reduce_fusion = f32[16,4096]{1,0:T(8,128)S(1)} fusion(bf16[16,16,4096]{2,1,0:T(8,128)(2,1)} %all-to-all-done.3), kind=kLoop, calls=%fused_computation | loop fusion | flops 2031616 | bytes 2359296 | tf_op jit(solution)/shard_map/reduce_sum | solution.py:310
  179.4 0.9 broadcast_in_dim.3
  (41 shorter events, 1.8 us)
Async XLA Ops:
  0.6 27.9 %collective-permute-start = (bf16[4096,128]{1,0:T(8,128)(2,1)}, bf16[4096,128]{1,0:T(8,128)(2,1)}, u32[]{:S(2)}, u32[]{:S(2)}) collective-permute-start(bf16[4096,128]{1,0:T(8,128)(2,1)} %a_ref.3), channel_id=1, source_target_pairs={{0,72},{1,73},{2,74},{3,75},{4,76},{5,77},{6,78},{7,79},{8,64},{9,... | collective-permute-start | bytes 3145736 | tf_op jit(solution)/shard_map/ppermute | solution.py:39
  5.3 0.9 copy-start.8
  6.4 1.3 copy-start.1
  7.7 22.0 %copy-start.2 = (bf16[4096,128]{1,0:T(8,128)(2,1)S(1)}, bf16[4096,128]{1,0:T(8,128)(2,1)}, u32[]{:S(2)}) copy-start(bf16[4096,128]{1,0:T(8,128)(2,1)} %a_ref.3) | copy-start | bytes 3145732
  7.7 36.6 %all-to-all-start = ((bf16[16,16,4096]{2,1,0:T(8,128)(2,1)}), bf16[16,16,4096]{2,1,0:T(8,128)(2,1)S(1)}, u32[]{:S(2)}, u32[]{:S(2)}) async-start(bf16[16,16,4096]{2,1,0:T(8,128)(2,1)} %bitcast.15), calls=%async_computation | async-start | bytes 4194304 | tf_op jit(solution)/shard_map/all_to_all | solution.py:43
  28.5 15.8 %collective-permute-start.1 = (bf16[4096,128]{1,0:T(8,128)(2,1)}, bf16[4096,128]{1,0:T(8,128)(2,1)}, u32[]{:S(2)}, u32[]{:S(2)}) collective-permute-start(bf16[4096,128]{1,0:T(8,128)(2,1)} %collective-permute-done.c_ref), channel_id=1, source_target_pairs={{0,1},{1,0},{2,3},{3,2},{4,5},{5,4},{6,7},{7,6},{8,9},{9,8},{10,11... | collective-permute-start | bytes 3145736 | tf_op jit(solution)/shard_map/ppermute | solution.py:39
  29.7 14.6 %collective-permute-start.2 = (bf16[4096,128]{1,0:T(8,128)(2,1)S(1)}, bf16[4096,128]{1,0:T(8,128)(2,1)}, u32[]{:S(2)}, u32[]{:S(2)}) collective-permute-start(bf16[4096,128]{1,0:T(8,128)(2,1)S(1)} %copy-done.2), channel_id=1, source_target_pairs={{0,1},{1,0},{2,3},{3,2},{4,5},{5,4},{6,7},{7,6},{8,9},{9,8},{10,11... | collective-permute-start | bytes 3145736 | tf_op jit(solution)/shard_map/ppermute | solution.py:39
  50.3 6.8 %collective-permute-start.4 = (bf16[256,512]{1,0:T(8,128)(2,1)S(1)}, bf16[256,512]{1,0:T(8,128)(2,1)S(1)}, u32[]{:S(2)}, u32[]{:S(2)}) collective-permute-start(bf16[256,512]{1,0:T(8,128)(2,1)S(1)} %shard_map.42.own_ref.e_ref), channel_id=1, source_target_pairs={{0,8},{1,9},{2,10},{3,11},{4,12},{5,13},{6,14},{7,15},{8,0},{9,1},... | collective-permute-start | bytes 786440 | tf_op jit(solution)/shard_map/ppermute | solution.py:39
  57.7 0.8 copy-start.9
  58.5 0.8 copy-start.10
  59.3 26.4 %collective-permute-start.6 = (bf16[224,2048]{1,0:T(8,128)(2,1)S(1)}, bf16[224,2048]{1,0:T(8,128)(2,1)}, u32[]{:S(2)}, u32[]{:S(2)}) collective-permute-start(bf16[224,2048]{1,0:T(8,128)(2,1)S(1)} %get-tuple-element.25), channel_id=1, source_target_pairs={{0,8},{1,9},{2,10},{3,11},{4,12},{5,13},{6,14},{7,15},{8,0},{9,1},... | collective-permute-start | bytes 2752520 | tf_op jit(solution)/shard_map/ppermute | solution.py:39
  60.0 87.4 %collective-permute-start.11 = (bf16[256,4096]{1,0:T(8,128)(2,1)S(1)}, bf16[256,4096]{1,0:T(8,128)(2,1)}, u32[]{:S(2)}, u32[]{:S(2)}) collective-permute-start(bf16[256,4096]{1,0:T(8,128)(2,1)S(1)} %bitcast.10), channel_id=1, source_target_pairs={{0,1},{1,0},{2,3},{3,2},{4,5},{5,4},{6,7},{7,6},{8,9},{9,8},{10,11... | collective-permute-start | bytes 6291464 | tf_op jit(solution)/shard_map/ppermute | solution.py:39
  63.5 4.0 %collective-permute-start.3 = (bf16[256,512]{1,0:T(8,128)(2,1)S(1)}, bf16[256,512]{1,0:T(8,128)(2,1)S(1)}, u32[]{:S(2)}, u32[]{:S(2)}) collective-permute-start(bf16[256,512]{1,0:T(8,128)(2,1)S(1)} %shard_map.42.own_ref.e_ref), channel_id=1, source_target_pairs={{0,1},{1,0},{2,3},{3,2},{4,5},{5,4},{6,7},{7,6},{8,9},{9,8},{10,11... | collective-permute-start | bytes 786440 | tf_op jit(solution)/shard_map/ppermute | solution.py:39
  63.5 4.4 %collective-permute-start.5 = (bf16[256,512]{1,0:T(8,128)(2,1)S(1)}, bf16[256,512]{1,0:T(8,128)(2,1)S(1)}, u32[]{:S(2)}, u32[]{:S(2)}) collective-permute-start(bf16[256,512]{1,0:T(8,128)(2,1)S(1)} %collective-permute-done.4.far_ref), channel_id=1, source_target_pairs={{0,1},{1,0},{2,3},{3,2},{4,5},{5,4},{6,7},{7,6},{8,9},{9,8},{10,11... | collective-permute-start | bytes 786440 | tf_op jit(solution)/shard_map/ppermute | solution.py:39
  68.8 1.0 copy-start.4
  84.9 0.8 copy-start.3
  85.7 16.6 %all-to-all-start.2 = ((bf16[16,16,1024]{2,1,0:T(8,128)(2,1)}), bf16[16,16,1024]{2,1,0:T(8,128)(2,1)}, u32[]{:S(2)}, u32[]{:S(2)}) async-start(bf16[16,16,1024]{2,1,0:T(8,128)(2,1)} %bitcast.16), calls=%async_computation.2 | async-start | bytes 1048576 | tf_op jit(solution)/shard_map/all_to_all | solution.py:43
  90.0 12.3 %collective-permute-start.7 = (bf16[224,1024]{1,0:T(8,128)(2,1)}, bf16[224,1024]{1,0:T(8,128)(2,1)}, u32[]{:S(2)}, u32[]{:S(2)}) collective-permute-start(bf16[224,1024]{1,0:T(8,128)(2,1)} %copy-done.10), channel_id=1, source_target_pairs={{0,8},{1,9},{2,10},{3,11},{4,12},{5,13},{6,14},{7,15},{8,0},{9,1},... | collective-permute-start | bytes 1376264 | tf_op jit(solution)/shard_map/ppermute | solution.py:39
  93.0 35.8 %collective-permute-start.9 = (bf16[224,1024]{1,0:T(8,128)(2,1)}, bf16[224,1024]{1,0:T(8,128)(2,1)}, u32[]{:S(2)}, u32[]{:S(2)}) collective-permute-start(bf16[224,1024]{1,0:T(8,128)(2,1)} %copy-done.9), channel_id=1, source_target_pairs={{0,8},{1,9},{2,10},{3,11},{4,12},{5,13},{6,14},{7,15},{8,0},{9,1},... | collective-permute-start | bytes 1376264 | tf_op jit(solution)/shard_map/ppermute | solution.py:39
  93.1 24.1 %collective-permute-start.8 = (bf16[256,512]{1,0:T(8,128)(2,1)S(1)}, bf16[256,512]{1,0:T(8,128)(2,1)}, u32[]{:S(2)}, u32[]{:S(2)}) collective-permute-start(bf16[256,512]{1,0:T(8,128)(2,1)S(1)} %shard_map.42.own_ref.e_ref), channel_id=1, source_target_pairs={{0,64},{1,65},{2,66},{3,67},{4,68},{5,69},{6,70},{7,71},{8,72},{9,... | collective-permute-start | bytes 786440 | tf_op jit(solution)/shard_map/ppermute | solution.py:39
  102.3 49.1 %collective-permute-start.10 = (bf16[224,2048]{1,0:T(8,128)(2,1)}, bf16[224,2048]{1,0:T(8,128)(2,1)}, u32[]{:S(2)}, u32[]{:S(2)}) collective-permute-start(bf16[224,2048]{1,0:T(8,128)(2,1)} %collective-permute-done.6.h0_ref), channel_id=1, source_target_pairs={{0,1},{1,0},{2,3},{3,2},{4,5},{5,4},{6,7},{7,6},{8,9},{9,8},{10,11... | collective-permute-start | bytes 2752520 | tf_op jit(solution)/shard_map/ppermute | solution.py:39
  117.3 1.2 copy-start.5
  120.9 0.6 copy-start.11
  127.5 1.3 copy-start
  128.8 18.6 %collective-permute-start.18 = (bf16[224,1024]{1,0:T(8,128)(2,1)}, bf16[224,1024]{1,0:T(8,128)(2,1)S(1)}, u32[]{:S(2)}, u32[]{:S(2)}) collective-permute-start(bf16[224,1024]{1,0:T(8,128)(2,1)} %collective-permute-done.9.h0_ref), channel_id=1, source_target_pairs={{0,1},{1,0},{2,3},{3,2},{4,5},{5,4},{6,7},{7,6},{8,9},{9,8},{10,11... | collective-permute-start | bytes 1376264 | tf_op jit(solution)/shard_map/ppermute | solution.py:39
  131.3 25.5 %collective-permute-start.16 = (bf16[224,1024]{1,0:T(8,128)(2,1)}, bf16[224,1024]{1,0:T(8,128)(2,1)}, u32[]{:S(2)}, u32[]{:S(2)}) collective-permute-start(bf16[224,1024]{1,0:T(8,128)(2,1)} %collective-permute-done.7.h0_ref), channel_id=1, source_target_pairs={{0,1},{1,0},{2,3},{3,2},{4,5},{5,4},{6,7},{7,6},{8,9},{9,8},{10,11... | collective-permute-start | bytes 1376264 | tf_op jit(solution)/shard_map/ppermute | solution.py:39
  131.3 8.7 %collective-permute-start.12 = (bf16[224,128]{1,0:T(8,128)(2,1)}, bf16[224,128]{1,0:T(8,128)(2,1)S(1)}, u32[]{:S(2)}, u32[]{:S(2)}) collective-permute-start(bf16[224,128]{1,0:T(8,128)(2,1)} %get-tuple-element.36), channel_id=1, source_target_pairs={{0,8},{1,9},{2,10},{3,11},{4,12},{5,13},{6,14},{7,15},{8,0},{9,1},... | collective-permute-start | bytes 172040 | tf_op jit(solution)/shard_map/ppermute | solution.py:39
  133.3 6.7 %copy-start.12 = (bf16[224,128]{1,0:T(8,128)(2,1)S(1)}, bf16[224,128]{1,0:T(8,128)(2,1)}, u32[]{:S(2)}) copy-start(bf16[224,128]{1,0:T(8,128)(2,1)} %copy-done.11) | copy-start | bytes 172036
  133.3 44.1 %all-to-all-start.3 = ((bf16[16,16,4096]{2,1,0:T(8,128)(2,1)}), bf16[16,16,4096]{2,1,0:T(8,128)(2,1)}, u32[]{:S(2)}, u32[]{:S(2)}) async-start(bf16[16,16,4096]{2,1,0:T(8,128)(2,1)} %bitcast.14), calls=%async_computation.3 | async-start | bytes 4194304 | tf_op jit(solution)/shard_map/all_to_all | solution.py:43
  140.0 5.8 %collective-permute-start.13 = (bf16[224,128]{1,0:T(8,128)(2,1)S(1)}, bf16[224,128]{1,0:T(8,128)(2,1)S(1)}, u32[]{:S(2)}, u32[]{:S(2)}) collective-permute-start(bf16[224,128]{1,0:T(8,128)(2,1)S(1)} %copy-done.12), channel_id=1, source_target_pairs={{0,9},{1,8},{2,11},{3,10},{4,13},{5,12},{6,15},{7,14},{8,1},{9,0},... | collective-permute-start | bytes 172040 | tf_op jit(solution)/shard_map/ppermute | solution.py:39
  145.8 1.6 collective-permute-start.14
  147.4 0.8 copy-start.6
  148.2 1.0 copy-start.7
  151.3 7.9 %collective-permute-start.19 = (bf16[1024,128]{1,0:T(8,128)(2,1)S(1)}, bf16[1024,128]{1,0:T(8,128)(2,1)S(1)}, u32[]{:S(2)}, u32[]{:S(2)}) collective-permute-start(bf16[1024,128]{1,0:T(8,128)(2,1)S(1)} %shard_map.50), channel_id=1, source_target_pairs={{0,64},{1,65},{2,66},{3,67},{4,68},{5,69},{6,70},{7,71},{8,72},{9,... | collective-permute-start | bytes 786440 | tf_op jit(solution)/shard_map/ppermute | solution.py:39
  155.4 20.5 %collective-permute-start.15 = (bf16[2048,128]{1,0:T(8,128)(2,1)S(1)}, bf16[2048,128]{1,0:T(8,128)(2,1)S(1)}, u32[]{:S(2)}, u32[]{:S(2)}) collective-permute-start(bf16[2048,128]{1,0:T(8,128)(2,1)S(1)} %shard_map.48), channel_id=1, source_target_pairs={{0,64},{1,65},{2,66},{3,67},{4,68},{5,69},{6,70},{7,71},{8,72},{9,... | collective-permute-start | bytes 1572872 | tf_op jit(solution)/shard_map/ppermute | solution.py:39
  159.1 16.7 %collective-permute-start.17 = (bf16[1024,128]{1,0:T(8,128)(2,1)S(1)}, bf16[1024,128]{1,0:T(8,128)(2,1)S(1)}, u32[]{:S(2)}, u32[]{:S(2)}) collective-permute-start(bf16[1024,128]{1,0:T(8,128)(2,1)S(1)} %shard_map.49), channel_id=1, source_target_pairs={{0,64},{1,65},{2,66},{3,67},{4,68},{5,69},{6,70},{7,71},{8,72},{9,... | collective-permute-start | bytes 786440 | tf_op jit(solution)/shard_map/ppermute | solution.py:39

commit v5 on v4

--- a/solution.py
+++ b/solution.py
@@ -10,7 +10,7 @@
 YS, ZS, XS, CS = 4, 2, 4, 2
 DP = YS * ZS * XS * CS
 PAD = 16
-TILE = 512
+TILE = 2048
 VMEM = 40 * 1024 * 1024
 
 
@@ -47,6 +47,10 @@
     return lax.dot_general(
         a, b, (((a_dim,), (b_dim,)), ((), ())), preferred_element_type=jnp.float32
     )
+
+
+def rounded(values):
+    return lax.optimization_barrier(values.astype(jnp.bfloat16))
 
 
 def reordered(block, order):
@@ -158,11 +162,10 @@
     grad = apart - f_ref[:1, :] * centered + coef_cov * coupled
     grad = grad.astype(jnp.bfloat16)
     o_ref[...] = grad
-    for i, ref in enumerate(run_refs[:2]):
-        ref[...] = grad[:, 128 * i : 128 * i + 128]
-    packed = without_padding(grad[:, 256:], rows)
-    for i, ref in enumerate(run_refs[2:]):
-        ref[...] = packed[:, 128 * i : 128 * i + 128]
+    own_ref, far_ref = run_refs
+    n = own_ref.shape[1]
+    own_ref[...] = grad[:, :n]
+    far_ref[...] = without_padding(grad[:, n:], rows)
 
 
 def hidden_kernel(g_ref, a_ref, b_ref, c_ref, d_ref, o_ref):
@@ -170,10 +173,16 @@
     o_ref[...] = matmul(g_ref[...], w, 1, 1).astype(o_ref.dtype)
 
 
-def weight_kernel(h0_ref, h1_ref, h2_ref, h3_ref, g0_ref, g1_ref, g2_ref, g3_ref, o_ref):
-    h = jnp.concatenate([h0_ref[...], h1_ref[...], h2_ref[...], h3_ref[...]], axis=0)
-    g = jnp.concatenate([g0_ref[...], g1_ref[...], g2_ref[...], g3_ref[...]], axis=0)
-    o_ref[...] = matmul(h, g, 0, 0).astype(o_ref.dtype)
+def weight_kernel(low, n_far, *refs):
+    fars, (own_ref, gf_ref, go_ref, mine_ref, sib_ref) = refs[:n_far], refs[n_far:]
+    n = mine_ref.shape[0]
+    far = jnp.concatenate([ref[...] for ref in fars], axis=1)
+    h = jnp.concatenate([own_ref[:, low : low + n], far], axis=0)
+    g = jnp.concatenate([go_ref[...], gf_ref[...]], axis=0)
+    out = matmul(h, g, 0, 0)
+    units = mine_ref.shape[1]
+    mine_ref[...] = out[:, :units]
+    sib_ref[...] = out[:, units:].astype(sib_ref.dtype)
 
 
 def copies_of(block, count):
@@ -217,22 +226,16 @@
     )(grad, *weights)
 
 
-def weight_terms(parts, grads, tile=TILE):
-    rows, units = grads[-1].shape
-    width = min(array.shape[1] for array, _ in parts)
-    specs = [
-        pl.BlockSpec((array.shape[0], tile), lambda n, first=first: (0, n + first))
-        for array, first in parts
-    ]
-    return pl.pallas_call(
-        weight_kernel,
-        grid=(width // tile,),
-        in_specs=specs + [pl.BlockSpec(g.shape, lambda n: (0, 0)) for g in grads],
-        out_specs=pl.BlockSpec((tile, units), lambda n: (n, 0)),
-        out_shape=shape((width, units)),
-        compiler_params=params(1),
-        cost_estimate=cost(8 * rows * width * units, 8 * width * rows + 2 * width * units),
-    )(*[array for array, _ in parts], *grads)
+def weight_terms(plane, low, fars, g_far, g_own):
+    rows = plane.shape[0]
+    width = sum(far.shape[1] for far in fars)
+    units = g_own.shape[1] // 2
+    return pl.pallas_call(
+        functools.partial(weight_kernel, low, len(fars)),
+        out_shape=(shape((width, units), jnp.float32), shape((width, units))),
+        compiler_params=params(),
+        cost_estimate=cost(8 * rows * width * units, 4 * width * (rows + 2 * units)),
+    )(*fars, plane, g_far, g_own)
 
 
 def wide_sum(a, b):
@@ -261,11 +264,10 @@
     from_far_sib = swap(from_far, c=1)
     partner = swap(mine, view=1)
 
-    cuts = (0, width // 2, 3 * width // 4, width)
+    cuts = (0, width // 2, 7 * width // 8, width)
     late, _ = lax.optimization_barrier((plane, from_far))
     h_far = compact(late, rows, [high - low for low, high in zip(cuts, cuts[1:])])
     h_far = [swap(block, z=1) for block in h_far]
-    h_sib = swap(plane, c=1)
 
     centered, factor, gram = pl.pallas_call(
         functools.partial(center_kernel, rows, samples),
@@ -279,6 +281,7 @@
     )(mine, from_sib, from_far, from_far_sib)
 
     gram = exchange(gram, "yx")
+    gram, partner = lax.optimization_barrier((gram, partner))
     gram = pl.pallas_call(
         total_kernel,
         out_shape=shape(gram.shape),
@@ -289,20 +292,14 @@
     gram = exchange(gram, "yx")
     gram, h_far[0], h_far[1] = lax.optimization_barrier((gram, h_far[0], h_far[1]))
 
-    grad, *runs = pl.pallas_call(
+    grad, g_own, g_far = pl.pallas_call(
         functools.partial(grad_kernel, rows, samples),
         out_shape=(shape((quarter, 4 * units)),)
-        + (shape((quarter, units)),) * 2
-        + (shape((peers * rows, units)),) * 2,
+        + (shape((quarter, 2 * units)), shape((peers * rows, 2 * units))),
         compiler_params=params(),
         cost_estimate=cost(8 * 4 * quarter * quarter * units, 16 * quarter * units * 2),
     )(gram, centered, factor, mine, partner)
-    grads = (
-        swap(runs[2], z=1),
-        swap(runs[3], z=1, c=1),
-        runs[0],
-        swap(runs[1], c=1),
-    )
+    g_far = swap(g_far, z=1)
 
     h_part = hidden_terms(grad, weights)
     h_part, h_far[2] = lax.optimization_barrier((h_part, h_far[2]))
@@ -310,11 +307,9 @@
     grad_rows = jnp.sum(pieces.astype(jnp.float32), axis=0)[:rows]
 
     runs = []
-    for at, far in zip(cuts, h_far):
-        first = at // TILE
-        total = weight_terms(
-            ((far, 0), (swap(far, c=1), 0), (plane, first), (h_sib, first)), grads
-        )
+    for low, fars in ((0, h_far[:1]), (cuts[1], h_far[1:])):
+        mine, theirs = weight_terms(plane, low, fars, g_far, g_own)
+        total = rounded(mine + swap(theirs, c=1).astype(jnp.float32))
         runs.append(wide_sum(total, swap(total, view=1)))
     grad_weight = jnp.concatenate(runs, axis=0) / jnp.sqrt(2.0 * samples)
     return (grad_rows[None], grad_weight)

time: 181 us -> 165 us (0.912)
  blocking collectives: 15.1 us -> 0 us
  Pallas kernels: 24.3 us -> 16.7 us
  starting transfers between devices: 46.3 us -> 49.3 us
  other arithmetic: 3.62 us -> 5.92 us
    all_to_all x1 -> x0, blocking collectives: 15.1 us -> none  [exchange(): lax.all_to_all(blocks, 'dp', 0, 0, tiled=True, axis_index_groups=groups(a...]
    all_to_all x3 -> x4, waiting for transfers between devices: 14.6 us -> 24.8 us  [exchange(): lax.all_to_all(blocks, 'dp', 0, 0, tiled=True, axis_index_groups=groups(a...]
    ppermute x20 -> x15, waiting for transfers between devices: 64.1 us -> 54.9 us  [swap(): return lax.ppermute(block, ('view', 'dp'), route)]
    all_to_all x3 -> x4, starting transfers between devices: 17.8 us -> 23.6 us  [exchange(): lax.all_to_all(blocks, 'dp', 0, 0, tiled=True, axis_index_groups=groups(a...]
    pallas_call x1, Pallas kernels: 5.94 us -> 2.95 us  [embed(): pl.pallas_call(embed_kernel, grid=(width // tile,), in_specs=[pl.BlockSpe...]
    pallas_call x1, Pallas kernels: 5.96 us -> 3 us  [hidden_terms(): pl.pallas_call(hidden_kernel, grid=(width // tile,), in_specs=[pl.BlockSp...]
    ppermute x20 -> x15, starting transfers between devices: 28.6 us -> 25.7 us  [swap(): return lax.ppermute(block, ('view', 'dp'), route)]
    pallas_call x3 -> x2, Pallas kernels: 8.22 us -> 5.46 us  [weight_terms(): pl.pallas_call(functools.partial(weight_kernel, low, len(fars)), out_shap...]
  transfers between devices with their start and end apart: 23 -> 19, of which waited for: 10 -> 11; matrix products, arithmetic and copies ran while one was open for 1% -> 2% of each run, Pallas kernels for 10% -> 6%
where the time goes in v5:
time: 165 us
  waiting for transfers between devices  79.7 us (48%)
  starting transfers between devices  49.3 us (30%)
  Pallas kernels  16.7 us (10%)
  local copies, waits for them, and re-layouts  12.3 us (7%)
  other arithmetic  5.92 us (4%)
    ppermute x15, waiting for transfers between devices, swap(): return lax.ppermute(block, ('view', 'dp'), route)  54.9 us
    ppermute x15, starting transfers between devices, swap(): return lax.ppermute(block, ('view', 'dp'), route)  25.7 us
    all_to_all x4, waiting for transfers between devices, exchange(): lax.all_to_all(blocks, 'dp', 0, 0, tiled=True, axis_index_groups=groups(a...  24.8 us
    all_to_all x4, starting transfers between devices, exchange(): lax.all_to_all(blocks, 'dp', 0, 0, tiled=True, axis_index_groups=groups(a...  23.6 us
    unnamed x30, local copies, waits for them, and re-layouts  11.4 us
    pallas_call x2, Pallas kernels, weight_terms(): pl.pallas_call(functools.partial(weight_kernel, low, len(fars)), out_shap...  5.46 us
  transfers between devices with their start and end apart: 19, of which 11 were waited for; matrix products, arithmetic and copies ran while one was open for 2% of the time, Pallas kernels for 6%

profile of v5, /device:TPU:1, one launch (start us, length us, event | category | flops | bytes accessed | tf_op | source)
XLA Modules:
  0.0 164.6 jit_solution(1806798790430429253)
XLA Ops:
  0.6 4.7 %collective-permute-start = (bf16[4096,128]{1,0:T(8,128)(2,1)}, bf16[4096,128]{1,0:T(8,128)(2,1)}, u32[]{:S(2)}, u32[]{:S(2)}) collective-permute-start(bf16[4096,128]{1,0:T(8,128)(2,1)} %a_ref.3), channel_id=1, source_target_pairs={{0,72},{1,73},{2,74},{3,75},{4,76},{5,77},{6,78},{7,79},{8,64},{9,... | collective-permute-start | bytes 3145736 | tf_op jit(solution)/shard_map/ppermute | solution.py:39
  5.3 0.9 copy-done.11
  6.4 1.3 copy-done.1
  7.7 6.9 %all-to-all-start = ((bf16[16,16,4096]{2,1,0:T(8,128)(2,1)}), bf16[16,16,4096]{2,1,0:T(8,128)(2,1)S(1)}, u32[]{:S(2)}, u32[]{:S(2)}) async-start(bf16[16,16,4096]{2,1,0:T(8,128)(2,1)} %bitcast.13), calls=%async_computation | async-start | bytes 4194304 | tf_op jit(solution)/shard_map/all_to_all | solution.py:43
  14.6 13.9 %collective-permute-done.c_ref = bf16[4096,128]{1,0:T(8,128)(2,1)} collective-permute-done((bf16[4096,128]{1,0:T(8,128)(2,1)}, bf16[4096,128]{1,0:T(8,128)(2,1)}, u32[]{:S(2)}, u32[]{:S(2)}) %collective-permute-start) | collective-permute-done | bytes 1048608 | tf_op jit(solution)/shard_map/ppermute | solution.py:39
  28.5 1.2 collective-permute-start.1
  29.7 14.6 %all-to-all-done = bf16[16,16,4096]{2,1,0:T(8,128)(2,1)S(1)} async-done(((bf16[16,16,4096]{2,1,0:T(8,128)(2,1)}), bf16[16,16,4096]{2,1,0:T(8,128)(2,1)S(1)}, u32[]{:S(2)}, u32[]{:S(2)}) %all-to-all-start) | async-done | bytes 2097184 | tf_op jit(solution)/shard_map/all_to_all | solution.py:43
  44.3 2.9 %shard_map.42.own_ref.e_ref = bf16[256,512]{1,0:T(8,128)(2,1)S(1)} custom-call(bf16[256,4096]{1,0:T(8,128)(2,1)S(1)} %bitcast.8, bf16[4096,128]{1,0:T(8,128)(2,1)S(1)} %copy-done.2, bf16[4096,128]{1,0:T(8,128)(2,1)} %collective-permute-done.2.b_ref, bf16[4096,128]{1,0:T(8,128)(2,1)} %collective-permute-done.c_ref, bf16[4096,128]{1,0:T(8,128)(2,1)} %collective-permute-done.1.d_ref), custom_call_target="tpu_custom_call" | custom-call | flops 1073741824 | bytes 6291456 | tf_op jit(solution)/shard_map/pallas_call | solution.py:201
  47.7 6.4 %collective-permute-done.4.far_ref = bf16[256,512]{1,0:T(8,128)(2,1)S(1)} collective-permute-done((bf16[256,512]{1,0:T(8,128)(2,1)S(1)}, bf16[256,512]{1,0:T(8,128)(2,1)S(1)}, u32[]{:S(2)}, u32[]{:S(2)}) %collective-permute-start.4) | collective-permute-done | bytes 262176 | tf_op jit(solution)/shard_map/ppermute | solution.py:39
  54.1 1.4 shard_map.45
  55.5 0.9 copy-done.12
  57.0 0.7 collective-permute-start.7
  57.7 3.4 %collective-permute-start.3 = (bf16[256,512]{1,0:T(8,128)(2,1)S(1)}, bf16[256,512]{1,0:T(8,128)(2,1)S(1)}, u32[]{:S(2)}, u32[]{:S(2)}) collective-permute-start(bf16[256,512]{1,0:T(8,128)(2,1)S(1)} %shard_map.42.own_ref.e_ref), channel_id=1, source_target_pairs={{0,1},{1,0},{2,3},{3,2},{4,5},{5,4},{6,7},{7,6},{8,9},{9,8},{10,11... | collective-permute-start | bytes 786440 | tf_op jit(solution)/shard_map/ppermute | solution.py:39
  61.2 1.2 collective-permute-done.3.sib_ref
  62.7 0.9 shard_map.43
  63.6 1.0 copy-done.4
  64.6 0.8 copy-done.8
  65.4 4.4 %all-to-all-start.1 = ((bf16[16,16,1024]{2,1,0:T(8,128)(2,1)}), bf16[16,16,1024]{2,1,0:T(8,128)(2,1)}, u32[]{:S(2)}, u32[]{:S(2)}) async-start(bf16[16,16,1024]{2,1,0:T(8,128)(2,1)} %bitcast.15), calls=%async_computation.1 | async-start | bytes 1048576 | tf_op jit(solution)/shard_map/all_to_all | solution.py:43
  69.8 1.0 collective-permute-start.6
  70.8 2.2 %collective-permute-start.8 = (bf16[224,1536]{1,0:T(8,128)(2,1)}, bf16[224,1536]{1,0:T(8,128)(2,1)}, u32[]{:S(2)}, u32[]{:S(2)}) collective-permute-start(bf16[224,1536]{1,0:T(8,128)(2,1)} %copy-done.12), channel_id=1, source_target_pairs={{0,8},{1,9},{2,10},{3,11},{4,12},{5,13},{6,14},{7,15},{8,0},{9,1},... | collective-permute-start | bytes 2064392 | tf_op jit(solution)/shard_map/ppermute | solution.py:39
  73.0 9.1 %collective-permute-done.6.p_ref = bf16[256,512]{1,0:T(8,128)(2,1)S(1)} collective-permute-done((bf16[256,512]{1,0:T(8,128)(2,1)S(1)}, bf16[256,512]{1,0:T(8,128)(2,1)S(1)}, u32[]{:S(2)}, u32[]{:S(2)}) %collective-permute-start.6) | collective-permute-done | bytes 262176 | tf_op jit(solution)/shard_map/ppermute | solution.py:39
  82.8 1.1 shard_map.44
  84.0 0.8 copy-done.3
  84.8 7.7 %all-to-all-start.2 = ((bf16[16,16,1024]{2,1,0:T(8,128)(2,1)}), bf16[16,16,1024]{2,1,0:T(8,128)(2,1)}, u32[]{:S(2)}, u32[]{:S(2)}) async-start(bf16[16,16,1024]{2,1,0:T(8,128)(2,1)} %bitcast.14), calls=%async_computation.2 | async-start | bytes 1048576 | tf_op jit(solution)/shard_map/all_to_all | solution.py:43
  92.5 2.1 %collective-permute-start.9 = (bf16[224,512]{1,0:T(8,128)(2,1)}, bf16[224,512]{1,0:T(8,128)(2,1)}, u32[]{:S(2)}, u32[]{:S(2)}) collective-permute-start(bf16[224,512]{1,0:T(8,128)(2,1)} %copy-done.13), channel_id=1, source_target_pairs={{0,8},{1,9},{2,10},{3,11},{4,12},{5,13},{6,14},{7,15},{8,0},{9,1},... | collective-permute-start | bytes 688136 | tf_op jit(solution)/shard_map/ppermute | solution.py:39
  94.6 2.8 %collective-permute-done.8.refs_0_ = bf16[224,1536]{1,0:T(8,128)(2,1)} collective-permute-done((bf16[224,1536]{1,0:T(8,128)(2,1)}, bf16[224,1536]{1,0:T(8,128)(2,1)}, u32[]{:S(2)}, u32[]{:S(2)}) %collective-permute-start.8) | collective-permute-done | bytes 688160 | tf_op jit(solution)/shard_map/ppermute | solution.py:39
  97.5 4.2 %all-to-all-done.2 = bf16[16,16,1024]{2,1,0:T(8,128)(2,1)} async-done(((bf16[16,16,1024]{2,1,0:T(8,128)(2,1)}), bf16[16,16,1024]{2,1,0:T(8,128)(2,1)}, u32[]{:S(2)}, u32[]{:S(2)}) %all-to-all-start.2) | async-done | bytes 524320 | tf_op jit(solution)/shard_map/all_to_all | solution.py:43
  101.7 1.2 copy-done.5
  102.9 0.9 copy-done.10
  103.8 1.7 %shard_map.46 = (bf16[256,512]{1,0:T(8,128)(2,1)S(1)}, bf16[256,256]{1,0:T(8,128)(2,1)S(1)}, bf16[224,256]{1,0:T(8,128)(2,1)S(1)}) custom-call(bf16[256,1024]{1,0:T(8,128)(2,1)} %bitcast.5.m_ref, bf16[1024,512]{1,0:T(8,128)(2,1)S(1)} %copy-done.5, f32[8,512]{1,0:T(8,128)S(1)} %get-tuple-element.36.f_ref, bf16[256,512]{1,0:T(8,128)(2,1)S(1)} %shard_map.42.own_ref.e_ref, ...), custom_call_target="tpu_custom_call" | custom-call | flops 268435456 | bytes 1048576 | tf_op jit(solution)/shard_map/pallas_call | solution.py:295
  105.5 2.1 %collective-permute-start.10 = (bf16[224,256]{1,0:T(8,128)(2,1)S(1)}, bf16[224,256]{1,0:T(8,128)(2,1)S(1)}, u32[]{:S(2)}, u32[]{:S(2)}) collective-permute-start(bf16[224,256]{1,0:T(8,128)(2,1)S(1)} %get-tuple-element.42), channel_id=1, source_target_pairs={{0,8},{1,9},{2,10},{3,11},{4,12},{5,13},{6,14},{7,15},{8,0},{9,1},... | collective-permute-start | bytes 344072 | tf_op jit(solution)/shard_map/ppermute | solution.py:39
  107.7 3.0 %shard_map.47 = bf16[256,4096]{1,0:T(8,128)(2,1)S(1)} custom-call(bf16[256,512]{1,0:T(8,128)(2,1)S(1)} %get-tuple-element.38.g_ref, bf16[4096,128]{1,0:T(8,128)(2,1)S(1)} %copy-done.2, bf16[4096,128]{1,0:T(8,128)(2,1)} %collective-permute-done.2.b_ref, bf16[4096,128]{1,0:T(8,128)(2,1)} %collective-permute-done.c_ref, ...), custom_call_target="tpu_custom_call" | custom-call | flops 1073741824 | bytes 6291456 | tf_op jit(solution)/shard_map/pallas_call | solution.py:217
  110.7 1.3 copy-done
  112.0 2.7 %shard_map.49 = (f32[2048,128]{1,0:T(8,128)S(1)}, bf16[2048,128]{1,0:T(8,128)(2,1)}) custom-call(bf16[224,1536]{1,0:T(8,128)(2,1)} %collective-permute-done.8.refs_0_, bf16[224,512]{1,0:T(8,128)(2,1)} %collective-permute-done.9.refs_1_, bf16[256,4096]{1,0:T(8,128)(2,1)S(1)} %bitcast.10, bf16[224,256]{1,0:T(8,128)(2,1)S(1)} %collective-permute-done.10.refs_2_.refs_3_, ...), custom_call_target="tpu_custom_call" | custom-call | flops 536870912 | bytes 4194304 | tf_op jit(solution)/shard_map/pallas_call | solution.py:233
  114.7 5.7 %collective-permute-start.13 = (bf16[2048,128]{1,0:T(8,128)(2,1)}, bf16[2048,128]{1,0:T(8,128)(2,1)}, u32[]{:S(2)}, u32[]{:S(2)}) collective-permute-start(bf16[2048,128]{1,0:T(8,128)(2,1)} %get-tuple-element.49), channel_id=1, source_target_pairs={{0,1},{1,0},{2,3},{3,2},{4,5},{5,4},{6,7},{7,6},{8,9},{9,8},{10,11... | collective-permute-start | bytes 1572872 | tf_op jit(solution)/shard_map/ppermute | solution.py:39
  120.5 2.7 %shard_map.48 = (f32[2048,128]{1,0:T(8,128)S(1)}, bf16[2048,128]{1,0:T(8,128)(2,1)}) custom-call(bf16[224,2048]{1,0:T(8,128)(2,1)} %collective-permute-done.7.refs_0_, bf16[256,4096]{1,0:T(8,128)(2,1)S(1)} %bitcast.11, bf16[224,256]{1,0:T(8,128)(2,1)S(1)} %collective-permute-done.10.refs_2_.refs_3_, bf16[256,256]{1,0:T(8,128)(2,1)S(1)} %get-tuple-element.43.refs_3_.refs_4_), custom_call_target="tpu_custom_call" | custom-call | flops 536870912 | bytes 4194304 | tf_op jit(solution)/shard_map/pallas_call | solution.py:233
  123.6 4.6 %all-to-all-start.3 = ((bf16[16,16,4096]{2,1,0:T(8,128)(2,1)}), bf16[16,16,4096]{2,1,0:T(8,128)(2,1)}, u32[]{:S(2)}, u32[]{:S(2)}) async-start(bf16[16,16,4096]{2,1,0:T(8,128)(2,1)} %bitcast.12), calls=%async_computation.3 | async-start | bytes 4194304 | tf_op jit(solution)/shard_map/all_to_all | solution.py:43
  128.2 1.1 add_convert_fusion
  129.3 0.8 collective-permute-start.14
  130.2 0.8 copy-done.14
  131.0 1.1 add_convert_fusion.1
  132.1 0.8 collective-permute-start.12
  132.9 10.0 %collective-permute-done.14 = bf16[2048,128]{1,0:T(8,128)(2,1)S(1)} collective-permute-done((bf16[2048,128]{1,0:T(8,128)(2,1)S(1)}, bf16[2048,128]{1,0:T(8,128)(2,1)S(1)}, u32[]{:S(2)}, u32[]{:S(2)}) %collective-permute-start.14) | collective-permute-done | bytes 524320 | tf_op jit(solution)/shard_map/ppermute | solution.py:39
  143.0 11.1 %collective-permute-done.12 = bf16[2048,128]{1,0:T(8,128)(2,1)S(1)} collective-permute-done((bf16[2048,128]{1,0:T(8,128)(2,1)S(1)}, bf16[2048,128]{1,0:T(8,128)(2,1)S(1)}, u32[]{:S(2)}, u32[]{:S(2)}) %collective-permute-start.12) | collective-permute-done | bytes 524320 | tf_op jit(solution)/shard_map/ppermute | solution.py:39
  154.3 1.5 maximum_multiply_fusion
  155.8 6.0 %all-to-all-done.3 = bf16[16,16,4096]{2,1,0:T(8,128)(2,1)} async-done(((bf16[16,16,4096]{2,1,0:T(8,128)(2,1)}), bf16[16,16,4096]{2,1,0:T(8,128)(2,1)}, u32[]{:S(2)}, u32[]{:S(2)}) %all-to-all-start.3) | async-done | bytes 2097184 | tf_op jit(solution)/shard_map/all_to_all | solution.py:43
  161.8 1.9 %convert_reduce_fusion = f32[16,4096]{1,0:T(8,128)S(1)} fusion(bf16[16,16,4096]{2,1,0:T(8,128)(2,1)} %all-to-all-done.3), kind=kLoop, calls=%fused_computation | loop fusion | flops 2031616 | bytes 2359296 | tf_op jit(solution)/shard_map/reduce_sum | solution.py:307
  163.7 0.9 broadcast_in_dim.3
  (36 shorter events, 3.1 us)
Async XLA Ops:
  0.6 27.9 %collective-permute-start = (bf16[4096,128]{1,0:T(8,128)(2,1)}, bf16[4096,128]{1,0:T(8,128)(2,1)}, u32[]{:S(2)}, u32[]{:S(2)}) collective-permute-start(bf16[4096,128]{1,0:T(8,128)(2,1)} %a_ref.3), channel_id=1, source_target_pairs={{0,72},{1,73},{2,74},{3,75},{4,76},{5,77},{6,78},{7,79},{8,64},{9,... | collective-permute-start | bytes 3145736 | tf_op jit(solution)/shard_map/ppermute | solution.py:39
  5.3 0.9 copy-start.11
  6.4 1.3 copy-start.1
  7.7 22.0 %copy-start.2 = (bf16[4096,128]{1,0:T(8,128)(2,1)S(1)}, bf16[4096,128]{1,0:T(8,128)(2,1)}, u32[]{:S(2)}) copy-start(bf16[4096,128]{1,0:T(8,128)(2,1)} %a_ref.3) | copy-start | bytes 3145732
  7.7 36.6 %all-to-all-start = ((bf16[16,16,4096]{2,1,0:T(8,128)(2,1)}), bf16[16,16,4096]{2,1,0:T(8,128)(2,1)S(1)}, u32[]{:S(2)}, u32[]{:S(2)}) async-start(bf16[16,16,4096]{2,1,0:T(8,128)(2,1)} %bitcast.13), calls=%async_computation | async-start | bytes 4194304 | tf_op jit(solution)/shard_map/all_to_all | solution.py:43
  28.5 15.8 %collective-permute-start.1 = (bf16[4096,128]{1,0:T(8,128)(2,1)}, bf16[4096,128]{1,0:T(8,128)(2,1)}, u32[]{:S(2)}, u32[]{:S(2)}) collective-permute-start(bf16[4096,128]{1,0:T(8,128)(2,1)} %collective-permute-done.c_ref), channel_id=1, source_target_pairs={{0,1},{1,0},{2,3},{3,2},{4,5},{5,4},{6,7},{7,6},{8,9},{9,8},{10,11... | collective-permute-start | bytes 3145736 | tf_op jit(solution)/shard_map/ppermute | solution.py:39
  29.7 14.6 %collective-permute-start.2 = (bf16[4096,128]{1,0:T(8,128)(2,1)S(1)}, bf16[4096,128]{1,0:T(8,128)(2,1)}, u32[]{:S(2)}, u32[]{:S(2)}) collective-permute-start(bf16[4096,128]{1,0:T(8,128)(2,1)S(1)} %copy-done.2), channel_id=1, source_target_pairs={{0,1},{1,0},{2,3},{3,2},{4,5},{5,4},{6,7},{7,6},{8,9},{9,8},{10,11... | collective-permute-start | bytes 3145736 | tf_op jit(solution)/shard_map/ppermute | solution.py:39
  47.3 6.8 %collective-permute-start.4 = (bf16[256,512]{1,0:T(8,128)(2,1)S(1)}, bf16[256,512]{1,0:T(8,128)(2,1)S(1)}, u32[]{:S(2)}, u32[]{:S(2)}) collective-permute-start(bf16[256,512]{1,0:T(8,128)(2,1)S(1)} %shard_map.42.own_ref.e_ref), channel_id=1, source_target_pairs={{0,8},{1,9},{2,10},{3,11},{4,12},{5,13},{6,14},{7,15},{8,0},{9,1},... | collective-permute-start | bytes 786440 | tf_op jit(solution)/shard_map/ppermute | solution.py:39
  55.5 0.9 copy-start.12
  56.3 0.7 copy-start.13
  57.0 27.8 %collective-permute-start.7 = (bf16[224,2048]{1,0:T(8,128)(2,1)}, bf16[224,2048]{1,0:T(8,128)(2,1)}, u32[]{:S(2)}, u32[]{:S(2)}) collective-permute-start(bf16[224,2048]{1,0:T(8,128)(2,1)} %get-tuple-element.30), channel_id=1, source_target_pairs={{0,8},{1,9},{2,10},{3,11},{4,12},{5,13},{6,14},{7,15},{8,0},{9,1},... | collective-permute-start | bytes 2752520 | tf_op jit(solution)/shard_map/ppermute | solution.py:39
  57.7 4.6 %collective-permute-start.3 = (bf16[256,512]{1,0:T(8,128)(2,1)S(1)}, bf16[256,512]{1,0:T(8,128)(2,1)S(1)}, u32[]{:S(2)}, u32[]{:S(2)}) collective-permute-start(bf16[256,512]{1,0:T(8,128)(2,1)S(1)} %shard_map.42.own_ref.e_ref), channel_id=1, source_target_pairs={{0,1},{1,0},{2,3},{3,2},{4,5},{5,4},{6,7},{7,6},{8,9},{9,8},{10,11... | collective-permute-start | bytes 786440 | tf_op jit(solution)/shard_map/ppermute | solution.py:39
  61.2 1.5 collective-permute-start.5
  63.6 1.0 copy-start.4
  64.6 0.8 copy-start.8
  65.4 17.4 %all-to-all-start.1 = ((bf16[16,16,1024]{2,1,0:T(8,128)(2,1)}), bf16[16,16,1024]{2,1,0:T(8,128)(2,1)}, u32[]{:S(2)}, u32[]{:S(2)}) async-start(bf16[16,16,1024]{2,1,0:T(8,128)(2,1)} %bitcast.15), calls=%async_computation.1 | async-start | bytes 1048576 | tf_op jit(solution)/shard_map/all_to_all | solution.py:43
  69.8 12.3 %collective-permute-start.6 = (bf16[256,512]{1,0:T(8,128)(2,1)S(1)}, bf16[256,512]{1,0:T(8,128)(2,1)S(1)}, u32[]{:S(2)}, u32[]{:S(2)}) collective-permute-start(bf16[256,512]{1,0:T(8,128)(2,1)S(1)} %shard_map.42.own_ref.e_ref), channel_id=1, source_target_pairs={{0,64},{1,65},{2,66},{3,67},{4,68},{5,69},{6,70},{7,71},{8,72},{9,... | collective-permute-start | bytes 786440 | tf_op jit(solution)/shard_map/ppermute | solution.py:39
  70.8 26.7 %collective-permute-start.8 = (bf16[224,1536]{1,0:T(8,128)(2,1)}, bf16[224,1536]{1,0:T(8,128)(2,1)}, u32[]{:S(2)}, u32[]{:S(2)}) collective-permute-start(bf16[224,1536]{1,0:T(8,128)(2,1)} %copy-done.12), channel_id=1, source_target_pairs={{0,8},{1,9},{2,10},{3,11},{4,12},{5,13},{6,14},{7,15},{8,0},{9,1},... | collective-permute-start | bytes 2064392 | tf_op jit(solution)/shard_map/ppermute | solution.py:39
  82.1 0.7 copy-start.9
  84.0 0.8 copy-start.3
  84.8 16.9 %all-to-all-start.2 = ((bf16[16,16,1024]{2,1,0:T(8,128)(2,1)}), bf16[16,16,1024]{2,1,0:T(8,128)(2,1)}, u32[]{:S(2)}, u32[]{:S(2)}) async-start(bf16[16,16,1024]{2,1,0:T(8,128)(2,1)} %bitcast.14), calls=%async_computation.2 | async-start | bytes 1048576 | tf_op jit(solution)/shard_map/all_to_all | solution.py:43
  92.5 19.5 %collective-permute-start.9 = (bf16[224,512]{1,0:T(8,128)(2,1)}, bf16[224,512]{1,0:T(8,128)(2,1)}, u32[]{:S(2)}, u32[]{:S(2)}) collective-permute-start(bf16[224,512]{1,0:T(8,128)(2,1)} %copy-done.13), channel_id=1, source_target_pairs={{0,8},{1,9},{2,10},{3,11},{4,12},{5,13},{6,14},{7,15},{8,0},{9,1},... | collective-permute-start | bytes 688136 | tf_op jit(solution)/shard_map/ppermute | solution.py:39
  101.7 1.2 copy-start.5
  102.9 0.9 copy-start.10
  105.5 6.5 %collective-permute-start.10 = (bf16[224,256]{1,0:T(8,128)(2,1)S(1)}, bf16[224,256]{1,0:T(8,128)(2,1)S(1)}, u32[]{:S(2)}, u32[]{:S(2)}) collective-permute-start(bf16[224,256]{1,0:T(8,128)(2,1)S(1)} %get-tuple-element.42), channel_id=1, source_target_pairs={{0,8},{1,9},{2,10},{3,11},{4,12},{5,13},{6,14},{7,15},{8,0},{9,1},... | collective-permute-start | bytes 344072 | tf_op jit(solution)/shard_map/ppermute | solution.py:39
  110.7 1.4 copy-start
  114.7 8.5 %copy-start.6 = (f32[2048,128]{1,0:T(8,128)}, f32[2048,128]{1,0:T(8,128)S(1)}, u32[]{:S(2)}) copy-start(f32[2048,128]{1,0:T(8,128)S(1)} %get-tuple-element.48) | copy-start | bytes 3145732
  114.7 13.4 %collective-permute-start.13 = (bf16[2048,128]{1,0:T(8,128)(2,1)}, bf16[2048,128]{1,0:T(8,128)(2,1)}, u32[]{:S(2)}, u32[]{:S(2)}) collective-permute-start(bf16[2048,128]{1,0:T(8,128)(2,1)} %get-tuple-element.49), channel_id=1, source_target_pairs={{0,1},{1,0},{2,3},{3,2},{4,5},{5,4},{6,7},{7,6},{8,9},{9,8},{10,11... | collective-permute-start | bytes 1572872 | tf_op jit(solution)/shard_map/ppermute | solution.py:39
  123.2 7.0 %collective-permute-start.11 = (bf16[2048,128]{1,0:T(8,128)(2,1)}, bf16[2048,128]{1,0:T(8,128)(2,1)S(1)}, u32[]{:S(2)}, u32[]{:S(2)}) collective-permute-start(bf16[2048,128]{1,0:T(8,128)(2,1)} %get-tuple-element.45), channel_id=1, source_target_pairs={{0,1},{1,0},{2,3},{3,2},{4,5},{5,4},{6,7},{7,6},{8,9},{9,8},{10,11... | collective-permute-start | bytes 1572872 | tf_op jit(solution)/shard_map/ppermute | solution.py:39
  123.6 4.6 %copy-start.7 = (f32[2048,128]{1,0:T(8,128)S(1)}, f32[2048,128]{1,0:T(8,128)}, u32[]{:S(2)}) copy-start(f32[2048,128]{1,0:T(8,128)} %copy-done.6) | copy-start | bytes 3145732
  123.6 38.2 %all-to-all-start.3 = ((bf16[16,16,4096]{2,1,0:T(8,128)(2,1)}), bf16[16,16,4096]{2,1,0:T(8,128)(2,1)}, u32[]{:S(2)}, u32[]{:S(2)}) async-start(bf16[16,16,4096]{2,1,0:T(8,128)(2,1)} %bitcast.12), calls=%async_computation.3 | async-start | bytes 4194304 | tf_op jit(solution)/shard_map/all_to_all | solution.py:43
  129.3 13.6 %collective-permute-start.14 = (bf16[2048,128]{1,0:T(8,128)(2,1)S(1)}, bf16[2048,128]{1,0:T(8,128)(2,1)S(1)}, u32[]{:S(2)}, u32[]{:S(2)}) collective-permute-start(bf16[2048,128]{1,0:T(8,128)(2,1)S(1)} %add_convert_fusion), channel_id=1, source_target_pairs={{0,64},{1,65},{2,66},{3,67},{4,68},{5,69},{6,70},{7,71},{8,72},{9,... | collective-permute-start | bytes 1572872 | tf_op jit(solution)/shard_map/ppermute | solution.py:39
  130.2 0.8 copy-start.14
  132.1 22.0 %collective-permute-start.12 = (bf16[2048,128]{1,0:T(8,128)(2,1)S(1)}, bf16[2048,128]{1,0:T(8,128)(2,1)S(1)}, u32[]{:S(2)}, u32[]{:S(2)}) collective-permute-start(bf16[2048,128]{1,0:T(8,128)(2,1)S(1)} %add_convert_fusion.1), channel_id=1, source_target_pairs={{0,64},{1,65},{2,66},{3,67},{4,68},{5,69},{6,70},{7,71},{8,72},{9,... | collective-permute-start | bytes 1572872 | tf_op jit(solution)/shard_map/ppermute | solution.py:39

commit v6 on v5

--- a/solution.py
+++ b/solution.py
@@ -11,7 +11,7 @@
 DP = YS * ZS * XS * CS
 PAD = 16
 TILE = 2048
-VMEM = 40 * 1024 * 1024
+VMEM = 24 * 1024 * 1024
 
 
 def place(d):
@@ -67,7 +67,7 @@
 
 
 def cost(flops, size):
-    return pl.CostEstimate(flops=flops, bytes_accessed=size, transcendentals=0)
+    return pl.CostEstimate(flops=flops // 1000, bytes_accessed=size // 1000, transcendentals=0)
 
 
 def without_padding(x, rows):
@@ -79,7 +79,7 @@
 
 
 def compact_kernel(rows, x_ref, *o_refs):
-    at = 0
+    at = x_ref.shape[1] - sum(ref.shape[1] for ref in o_refs)
     for ref in o_refs:
         n = ref.shape[1]
         ref[...] = without_padding(x_ref[:, at : at + n], rows)
@@ -92,8 +92,37 @@
         functools.partial(compact_kernel, rows),
         out_shape=tuple(shape((n, width)) for width in widths),
         compiler_params=params(),
-        cost_estimate=cost(2 * n * block.size, 4 * block.size),
+        cost_estimate=cost(2 * n * block.shape[0] * sum(widths), 4 * block.size),
     )(block)
+
+
+def pad_rows(blocks):
+    zeros = jnp.zeros((PAD - blocks[0].shape[0], blocks[0].shape[1]), blocks[0].dtype)
+    return jnp.concatenate([part for block in blocks for part in (block, zeros)], axis=0)
+
+
+def settle_kernel(rows, at_ref, *refs):
+    blocks, (o_ref, all_ref) = refs[:YS], refs[YS:]
+    for i, ref in enumerate(blocks):
+        y = lax.rem(at_ref[0] + (YS - i), YS)
+        for j in range(XS):
+            x = lax.rem(at_ref[1] + (XS - j), XS)
+            home = pl.multiple_of((y * XS + x) * PAD, PAD)
+            all_ref[pl.ds(home, PAD), :] = ref[PAD * j : PAD * j + PAD, :]
+    o_ref[...] = without_padding(all_ref[...], rows)
+
+
+def settle(at, blocks, rows):
+    n, width = YS * XS * PAD, blocks[0].shape[1]
+    return pl.pallas_call(
+        functools.partial(settle_kernel, rows),
+        in_specs=[pl.BlockSpec(memory_space=pltpu.SMEM)]
+        + [pl.BlockSpec(memory_space=pltpu.VMEM)] * YS,
+        out_shape=shape((YS * XS * rows, width)),
+        scratch_shapes=[pltpu.VMEM((n, width), jnp.bfloat16)],
+        compiler_params=params(),
+        cost_estimate=cost(2 * n * n * width, 4 * n * width),
+    )(at, *blocks)
 
 
 def copies_kernel(x_ref, o_ref):
@@ -162,10 +191,11 @@
     grad = apart - f_ref[:1, :] * centered + coef_cov * coupled
     grad = grad.astype(jnp.bfloat16)
     o_ref[...] = grad
-    own_ref, far_ref = run_refs
-    n = own_ref.shape[1]
-    own_ref[...] = grad[:, :n]
-    far_ref[...] = without_padding(grad[:, n:], rows)
+    packed = without_padding(grad[:, 256:], rows)
+    for i, ref in enumerate(run_refs[:2]):
+        ref[...] = grad[:, 128 * i : 128 * i + 128]
+    for i, ref in enumerate(run_refs[2:]):
+        ref[...] = packed[:, 128 * i : 128 * i + 128]
 
 
 def hidden_kernel(g_ref, a_ref, b_ref, c_ref, d_ref, o_ref):
@@ -174,15 +204,25 @@
 
 
 def weight_kernel(low, n_far, *refs):
-    fars, (own_ref, gf_ref, go_ref, mine_ref, sib_ref) = refs[:n_far], refs[n_far:]
-    n = mine_ref.shape[0]
-    far = jnp.concatenate([ref[...] for ref in fars], axis=1)
-    h = jnp.concatenate([own_ref[:, low : low + n], far], axis=0)
-    g = jnp.concatenate([go_ref[...], gf_ref[...]], axis=0)
-    out = matmul(h, g, 0, 0)
-    units = mine_ref.shape[1]
-    mine_ref[...] = out[:, :units]
-    sib_ref[...] = out[:, units:].astype(sib_ref.dtype)
+    fars, sibs, (own_ref, sib_ref), gs, (o_ref,) = (
+        refs[:n_far],
+        refs[n_far : 2 * n_far],
+        refs[2 * n_far : 2 * n_far + 2],
+        refs[2 * n_far + 2 : -1],
+        refs[-1:],
+    )
+    n = o_ref.shape[0]
+    h = jnp.concatenate(
+        [
+            own_ref[:, low : low + n],
+            sib_ref[:, low : low + n],
+            jnp.concatenate([ref[...] for ref in fars], axis=1),
+            jnp.concatenate([ref[...] for ref in sibs], axis=1),
+        ],
+        axis=0,
+    )
+    g = jnp.concatenate([ref[...] for ref in gs], axis=0)
+    o_ref[...] = matmul(h, g, 0, 0).astype(o_ref.dtype)
 
 
 def copies_of(block, count):
@@ -226,20 +266,28 @@
     )(grad, *weights)
 
 
-def weight_terms(plane, low, fars, g_far, g_own):
-    rows = plane.shape[0]
+def weight_terms(low, fars, sibs, plane, h_sib, grads):
     width = sum(far.shape[1] for far in fars)
-    units = g_own.shape[1] // 2
+    units = grads[0].shape[1]
+    rows = 4 * plane.shape[0]
     return pl.pallas_call(
         functools.partial(weight_kernel, low, len(fars)),
-        out_shape=(shape((width, units), jnp.float32), shape((width, units))),
-        compiler_params=params(),
-        cost_estimate=cost(8 * rows * width * units, 4 * width * (rows + 2 * units)),
-    )(*fars, plane, g_far, g_own)
+        out_shape=shape((width, units)),
+        compiler_params=params(),
+        cost_estimate=cost(2 * rows * width * units, 2 * width * (rows + units)),
+    )(*fars, *sibs, plane, h_sib, *grads)
 
 
 def wide_sum(a, b):
     return a.astype(jnp.float32) + b.astype(jnp.float32)
+
+
+def shift(block, y=0, x=0):
+    route = []
+    for d in range(DP):
+        yd, z, xd, c = place(d)
+        route.append((d, index((yd + y) % YS, z, (xd + x) % XS, c)))
+    return lax.ppermute(block, "dp", route)
 
 
 def on_device(hidden, weight):
@@ -255,8 +303,13 @@
     w_far_sib = swap(w_far, c=1)
     weights = (weight, w_sib, w_far, w_far_sib)
 
+    d = lax.axis_index("dp")
+    at = jnp.stack([d // (ZS * XS * CS), d // CS % XS]).astype(jnp.int32)
+    far = swap(hidden[0, :, : width // 2], z=1)
+    far = pad_rows([far] + [shift(far, x=k) for k in (1, 2, 3)])
+
     plane = exchange(copies_of(hidden, peers), "yx")
-    plane, w_far_sib = lax.optimization_barrier((plane, w_far_sib))
+    plane, w_far_sib, far = lax.optimization_barrier((plane, w_far_sib, far))
 
     mine = embed(plane, weights)
     from_sib = swap(mine, c=1)
@@ -264,10 +317,13 @@
     from_far_sib = swap(from_far, c=1)
     partner = swap(mine, view=1)
 
-    cuts = (0, width // 2, 7 * width // 8, width)
-    late, _ = lax.optimization_barrier((plane, from_far))
-    h_far = compact(late, rows, [high - low for low, high in zip(cuts, cuts[1:])])
-    h_far = [swap(block, z=1) for block in h_far]
+    far, _ = lax.optimization_barrier((far, mine))
+    far = [far] + [shift(far, y=k) for k in (1, 2, 3)]
+    h_right = compact(plane, rows, (width // 4, width // 4))
+    *h_right, from_far_sib, _, _ = lax.optimization_barrier(
+        (*h_right, from_far_sib, from_far, from_sib)
+    )
+    h_right = [swap(block, z=1) for block in h_right]
 
     centered, factor, gram = pl.pallas_call(
         functools.partial(center_kernel, rows, samples),
@@ -280,36 +336,44 @@
         cost_estimate=cost(8 * 4 * quarter * quarter * units, 16 * quarter * units * 2),
     )(mine, from_sib, from_far, from_far_sib)
 
+    gram, *far = lax.optimization_barrier((gram, *far))
     gram = exchange(gram, "yx")
-    gram, partner = lax.optimization_barrier((gram, partner))
+    h_left = settle(at, far, rows)
+    gram, partner, plane_late, h_left, h_right[0] = lax.optimization_barrier(
+        (gram, partner, plane, h_left, h_right[0])
+    )
+    h_left_sib = [swap(h_left, c=1)]
+    h_sib = swap(plane_late, c=1)
     gram = pl.pallas_call(
         total_kernel,
         out_shape=shape(gram.shape),
         compiler_params=params(),
         cost_estimate=cost(gram.size, 4 * gram.size),
     )(gram)
-    gram, h_far[0] = lax.optimization_barrier((gram, h_far[0]))
     gram = exchange(gram, "yx")
-    gram, h_far[0], h_far[1] = lax.optimization_barrier((gram, h_far[0], h_far[1]))
-
-    grad, g_own, g_far = pl.pallas_call(
+    gram, *h_right, h_left_sib[0], h_sib = lax.optimization_barrier(
+        (gram, *h_right, h_left_sib[0], h_sib)
+    )
+    h_right_sib = [swap(block, c=1) for block in h_right]
+
+    grad, *runs = pl.pallas_call(
         functools.partial(grad_kernel, rows, samples),
         out_shape=(shape((quarter, 4 * units)),)
-        + (shape((quarter, 2 * units)), shape((peers * rows, 2 * units))),
+        + (shape((quarter, units)),) * 2
+        + (shape((peers * rows, units)),) * 2,
         compiler_params=params(),
         cost_estimate=cost(8 * 4 * quarter * quarter * units, 16 * quarter * units * 2),
     )(gram, centered, factor, mine, partner)
-    g_far = swap(g_far, z=1)
+    grads = (runs[0], swap(runs[1], c=1), swap(runs[2], z=1), swap(runs[3], z=1, c=1))
 
     h_part = hidden_terms(grad, weights)
-    h_part, h_far[2] = lax.optimization_barrier((h_part, h_far[2]))
+    h_part, *grads = lax.optimization_barrier((h_part, *grads))
     pieces = exchange(h_part, "yx").reshape(peers, PAD, width)
     grad_rows = jnp.sum(pieces.astype(jnp.float32), axis=0)[:rows]
 
     runs = []
-    for low, fars in ((0, h_far[:1]), (cuts[1], h_far[1:])):
-        mine, theirs = weight_terms(plane, low, fars, g_far, g_own)
-        total = rounded(mine + swap(theirs, c=1).astype(jnp.float32))
+    for low, fars, sibs in ((0, [h_left], h_left_sib), (width // 2, h_right, h_right_sib)):
+        total = weight_terms(low, fars, sibs, plane, h_sib, grads)
         runs.append(wide_sum(total, swap(total, view=1)))
     grad_weight = jnp.concatenate(runs, axis=0) / jnp.sqrt(2.0 * samples)
     return (grad_rows[None], grad_weight)

time: 165 us -> 190 us (1.15)
  local copies, waits for them, and re-layouts: 12.3 us -> 28.4 us
  starting transfers between devices: 49.3 us -> 59.4 us
  waiting for transfers between devices: 79.7 us -> 76.6 us
  Pallas kernels: 16.7 us -> 18.7 us
    all_to_all x4, waiting for transfers between devices: 24.8 us -> 10.3 us  [exchange(): lax.all_to_all(blocks, 'dp', 0, 0, tiled=True, axis_index_groups=groups(a...]
    ppermute x0 -> x6, waiting for transfers between devices: none -> 13.9 us  [shift(): return lax.ppermute(block, 'dp', route)]
    concatenate x0 -> x1, local copies, waits for them, and re-layouts: none -> 8.12 us  [pad_rows(): jnp.concatenate([part for block in blocks for part in (block, zeros)], ax...]
    unnamed x30 -> x50, local copies, waits for them, and re-layouts: 11.4 us -> 19.4 us
    ppermute x0 -> x6, starting transfers between devices: none -> 6.87 us  [shift(): return lax.ppermute(block, 'dp', route)]
    ppermute x15 -> x19, waiting for transfers between devices: 54.9 us -> 52.3 us  [swap(): return lax.ppermute(block, ('view', 'dp'), route)]
    convert_element_type x2 -> x0, other arithmetic: 2.29 us -> none  [rounded(): return lax.optimization_barrier(values.astype(jnp.bfloat16))]
    ppermute x15 -> x19, starting transfers between devices: 25.7 us -> 27.7 us  [swap(): return lax.ppermute(block, ('view', 'dp'), route)]
  transfers between devices with their start and end apart: 19 -> 29, of which waited for: 11 -> 11; matrix products, arithmetic and copies ran while one was open for 2% -> 6% of each run, Pallas kernels for 6% -> 5%
where the time goes in v6:
time: 190 us; the launch traced here: 189 us
  waiting for transfers between devices  76.6 us (40%)
  starting transfers between devices  59.4 us (31%)
  local copies, waits for them, and re-layouts  28.4 us (15%)
  Pallas kernels  18.7 us (10%)
  other arithmetic  4.89 us (3%)
    ppermute x19, waiting for transfers between devices, swap(): return lax.ppermute(block, ('view', 'dp'), route)  52.3 us
    ppermute x19, starting transfers between devices, swap(): return lax.ppermute(block, ('view', 'dp'), route)  27.7 us
    all_to_all x4, starting transfers between devices, exchange(): lax.all_to_all(blocks, 'dp', 0, 0, tiled=True, axis_index_groups=groups(a...  24.8 us
    unnamed x50, local copies, waits for them, and re-layouts  19.4 us
    ppermute x6, waiting for transfers between devices, shift(): return lax.ppermute(block, 'dp', route)  13.9 us
    all_to_all x4, waiting for transfers between devices, exchange(): lax.all_to_all(blocks, 'dp', 0, 0, tiled=True, axis_index_groups=groups(a...  10.3 us
    concatenate x1, local copies, waits for them, and re-layouts, pad_rows(): jnp.concatenate([part for block in blocks for part in (block, zeros)], ax...  8.12 us
    pallas_call x2, Pallas kernels, weight_terms(): pl.pallas_call(functools.partial(weight_kernel, low, len(fars)), out_shap...  7.28 us
  transfers between devices with their start and end apart: 29, of which 11 were waited for; matrix products, arithmetic and copies ran while one was open for 6% of the time, Pallas kernels for 5%

profile of v6, /device:TPU:1, one launch (start us, length us, event | category | flops | bytes accessed | tf_op | source)
XLA Modules:
  0.0 189.0 jit_solution(11189491994256192741)
XLA Ops:
  0.6 4.7 %collective-permute-start = (bf16[4096,128]{1,0:T(8,128)(2,1)}, bf16[4096,128]{1,0:T(8,128)(2,1)}, u32[]{:S(2)}, u32[]{:S(2)}) collective-permute-start(bf16[4096,128]{1,0:T(8,128)(2,1)} %a_ref.3), channel_id=1, source_target_pairs={{0,72},{1,73},{2,74},{3,75},{4,76},{5,77},{6,78},{7,79},{8,64},{9,... | collective-permute-start | bytes 3145736 | tf_op jit(solution)/shard_map/ppermute | solution.py:39
  6.4 1.3 copy-done.1
  7.7 6.9 %all-to-all-start = ((bf16[16,16,4096]{2,1,0:T(8,128)(2,1)}), bf16[16,16,4096]{2,1,0:T(8,128)(2,1)S(1)}, u32[]{:S(2)}, u32[]{:S(2)}) async-start(bf16[16,16,4096]{2,1,0:T(8,128)(2,1)} %bitcast.18), calls=%async_computation | async-start | bytes 4194304 | tf_op jit(solution)/shard_map/all_to_all | solution.py:43
  14.6 13.9 %collective-permute-done.c_ref = bf16[4096,128]{1,0:T(8,128)(2,1)} collective-permute-done((bf16[4096,128]{1,0:T(8,128)(2,1)}, bf16[4096,128]{1,0:T(8,128)(2,1)}, u32[]{:S(2)}, u32[]{:S(2)}) %collective-permute-start) | collective-permute-done | bytes 1048608 | tf_op jit(solution)/shard_map/ppermute | solution.py:39
  28.5 1.2 collective-permute-start.1
  29.8 1.4 collective-permute-start.2
  31.1 3.6 %collective-permute-done.2 = bf16[14,2048]{1,0:T(8,128)(2,1)S(1)} collective-permute-done((bf16[14,2048]{1,0:T(8,128)(2,1)S(1)}, bf16[14,2048]{1,0:T(8,128)(2,1)S(1)}, u32[]{:S(2)}, u32[]{:S(2)}) %collective-permute-start.2) | collective-permute-done | bytes 57376 | tf_op jit(solution)/shard_map/ppermute | solution.py:39
  34.8 2.5 %collective-permute-start.5 = (bf16[14,2048]{1,0:T(8,128)(2,1)S(1)}, bf16[14,2048]{1,0:T(8,128)(2,1)S(1)}, u32[]{:S(2)}, u32[]{:S(2)}) collective-permute-start(bf16[14,2048]{1,0:T(8,128)(2,1)S(1)} %collective-permute-done.2), channel_id=1, source_target_pairs={{0,6},{1,7},{2,0},{3,1},{4,2},{5,3},{6,4},{7,5},{8,14},{9,15},{10,... | collective-permute-start | bytes 172040 | tf_op jit(solution)/shard_map/ppermute | solution.py:290
  38.4 3.9 %collective-permute-done.5 = bf16[14,2048]{1,0:T(8,128)(2,1)S(1)} collective-permute-done((bf16[14,2048]{1,0:T(8,128)(2,1)S(1)}, bf16[14,2048]{1,0:T(8,128)(2,1)S(1)}, u32[]{:S(2)}, u32[]{:S(2)}) %collective-permute-start.5) | collective-permute-done | bytes 57376 | tf_op jit(solution)/shard_map/ppermute | solution.py:290
  42.3 2.3 %collective-permute-done.4 = bf16[14,2048]{1,0:T(8,128)(2,1)S(1)} collective-permute-done((bf16[14,2048]{1,0:T(8,128)(2,1)S(1)}, bf16[14,2048]{1,0:T(8,128)(2,1)S(1)}, u32[]{:S(2)}, u32[]{:S(2)}) %collective-permute-start.4) | collective-permute-done | bytes 57376 | tf_op jit(solution)/shard_map/ppermute | solution.py:290
  44.5 8.1 %concatenate.6.refs_0_ = bf16[64,2048]{1,0:T(8,128)(2,1)} concatenate(bf16[14,2048]{1,0:T(8,128)(2,1)S(1)} %collective-permute-done.2, bf16[2,2048]{1,0:T(2,128)(2,1)S(1)} %broadcast_in_dim.6, bf16[14,2048]{1,0:T(8,128)(2,1)S(1)} %collective-permute-done.3, bf16[2,2048]{1,0:T(2,128)(2,1)S(1)} %broadcast_in_dim.6, bf16[14,2048]{1,0:T(8,128)(2,1)S(1)} %collective-permute-done.4, ...), dimensions={0} | concatenate | bytes 524288 | tf_op jit(solution)/shard_map/concatenate | solution.py:101
  52.7 3.0 %shard_map.42.own_ref.e_ref = bf16[256,512]{1,0:T(8,128)(2,1)S(1)} custom-call(bf16[256,4096]{1,0:T(8,128)(2,1)S(1)} %bitcast.12, bf16[4096,128]{1,0:T(8,128)(2,1)S(1)} %copy-done.2, bf16[4096,128]{1,0:T(8,128)(2,1)} %collective-permute-done.6.b_ref, bf16[4096,128]{1,0:T(8,128)(2,1)} %collective-permute-done.c_ref, ...), custom_call_target="tpu_custom_call" | custom-call | flops 1073741 | bytes 6291 | tf_op jit(solution)/shard_map/pallas_call | solution.py:241
  55.6 1.2 collective-permute-start.8
  56.9 2.9 %collective-permute-start.7 = (bf16[256,512]{1,0:T(8,128)(2,1)S(1)}, bf16[256,512]{1,0:T(8,128)(2,1)S(1)}, u32[]{:S(2)}, u32[]{:S(2)}) collective-permute-start(bf16[256,512]{1,0:T(8,128)(2,1)S(1)} %shard_map.42.own_ref.e_ref), channel_id=1, source_target_pairs={{0,1},{1,0},{2,3},{3,2},{4,5},{5,4},{6,7},{7,6},{8,9},{9,8},{10,11... | collective-permute-start | bytes 786440 | tf_op jit(solution)/shard_map/ppermute | solution.py:39
  59.8 2.7 %collective-permute-done.8.far_ref = bf16[256,512]{1,0:T(8,128)(2,1)S(1)} collective-permute-done((bf16[256,512]{1,0:T(8,128)(2,1)S(1)}, bf16[256,512]{1,0:T(8,128)(2,1)S(1)}, u32[]{:S(2)}, u32[]{:S(2)}) %collective-permute-start.8) | collective-permute-done | bytes 262176 | tf_op jit(solution)/shard_map/ppermute | solution.py:39
  62.5 4.2 %collective-permute-start.9 = (bf16[256,512]{1,0:T(8,128)(2,1)S(1)}, bf16[256,512]{1,0:T(8,128)(2,1)S(1)}, u32[]{:S(2)}, u32[]{:S(2)}) collective-permute-start(bf16[256,512]{1,0:T(8,128)(2,1)S(1)} %collective-permute-done.8.far_ref), channel_id=1, source_target_pairs={{0,1},{1,0},{2,3},{3,2},{4,5},{5,4},{6,7},{7,6},{8,9},{9,8},{10,11... | collective-permute-start | bytes 786440 | tf_op jit(solution)/shard_map/ppermute | solution.py:39
  66.6 1.8 collective-permute-start.12
  72.8 1.0 copy-done.8
  75.3 2.3 %collective-permute-done.11.refs_2_ = bf16[64,2048]{1,0:T(8,128)(2,1)S(1)} collective-permute-done((bf16[64,2048]{1,0:T(8,128)(2,1)S(1)}, bf16[64,2048]{1,0:T(8,128)(2,1)S(1)}, u32[]{:S(2)}, u32[]{:S(2)}) %collective-permute-start.11) | collective-permute-done | bytes 262176 | tf_op jit(solution)/shard_map/ppermute | solution.py:290
  78.3 5.5 %collective-permute-done.10.refs_1_ = bf16[64,2048]{1,0:T(8,128)(2,1)S(1)} collective-permute-done((bf16[64,2048]{1,0:T(8,128)(2,1)S(1)}, bf16[64,2048]{1,0:T(8,128)(2,1)S(1)}, u32[]{:S(2)}, u32[]{:S(2)}) %collective-permute-start.10) | collective-permute-done | bytes 262176 | tf_op jit(solution)/shard_map/ppermute | solution.py:290
  84.5 4.8 %all-to-all-start.1 = ((bf16[16,16,1024]{2,1,0:T(8,128)(2,1)}), bf16[16,16,1024]{2,1,0:T(8,128)(2,1)}, u32[]{:S(2)}, u32[]{:S(2)}) async-start(bf16[16,16,1024]{2,1,0:T(8,128)(2,1)} %bitcast.20), calls=%async_computation.1 | async-start | bytes 1048576 | tf_op jit(solution)/shard_map/all_to_all | solution.py:43
  91.0 0.9 copy-done.7
  92.0 0.9 copy-done.18
  92.9 0.9 copy-done.20
  94.8 1.0 shard_map.45.refs_0_
  96.8 10.2 %collective-permute-done.13.p_ref = bf16[256,512]{1,0:T(8,128)(2,1)} collective-permute-done((bf16[256,512]{1,0:T(8,128)(2,1)S(1)}, bf16[256,512]{1,0:T(8,128)(2,1)}, u32[]{:S(2)}, u32[]{:S(2)}) %collective-permute-start.13) | collective-permute-done | bytes 262176 | tf_op jit(solution)/shard_map/ppermute | solution.py:39
  107.1 1.3 collective-permute-start.17
  108.5 1.1 shard_map.46
  110.4 6.5 %all-to-all-start.2 = ((bf16[16,16,1024]{2,1,0:T(8,128)(2,1)}), bf16[16,16,1024]{2,1,0:T(8,128)(2,1)}, u32[]{:S(2)}, u32[]{:S(2)}) async-start(bf16[16,16,1024]{2,1,0:T(8,128)(2,1)} %bitcast.19), calls=%async_computation.2 | async-start | bytes 1048576 | tf_op jit(solution)/shard_map/all_to_all | solution.py:43
  117.0 2.2 %collective-permute-start.15 = (bf16[224,1024]{1,0:T(8,128)(2,1)}, bf16[224,1024]{1,0:T(8,128)(2,1)}, u32[]{:S(2)}, u32[]{:S(2)}) collective-permute-start(bf16[224,1024]{1,0:T(8,128)(2,1)} %copy-done.23), channel_id=1, source_target_pairs={{0,8},{1,9},{2,10},{3,11},{4,12},{5,13},{6,14},{7,15},{8,0},{9,1},... | collective-permute-start | bytes 1376264 | tf_op jit(solution)/shard_map/ppermute | solution.py:39
  119.1 11.1 %collective-permute-done.15.refs_1_ = bf16[224,1024]{1,0:T(8,128)(2,1)} collective-permute-done((bf16[224,1024]{1,0:T(8,128)(2,1)}, bf16[224,1024]{1,0:T(8,128)(2,1)}, u32[]{:S(2)}, u32[]{:S(2)}) %collective-permute-start.15) | collective-permute-done | bytes 458784 | tf_op jit(solution)/shard_map/ppermute | solution.py:39
  130.2 1.2 copy-done.9
  131.4 1.7 shard_map.47
  133.2 1.7 collective-permute-start.18
  134.9 2.1 %collective-permute-start.19 = (bf16[224,128]{1,0:T(8,128)(2,1)S(1)}, bf16[224,128]{1,0:T(8,128)(2,1)S(1)}, u32[]{:S(2)}, u32[]{:S(2)}) collective-permute-start(bf16[224,128]{1,0:T(8,128)(2,1)S(1)} %get-tuple-element.63), channel_id=1, source_target_pairs={{0,8},{1,9},{2,10},{3,11},{4,12},{5,13},{6,14},{7,15},{8,0},{9,1},... | collective-permute-start | bytes 172040 | tf_op jit(solution)/shard_map/ppermute | solution.py:39
  137.0 1.1 collective-permute-start.20
  138.1 3.1 %shard_map.48 = bf16[256,4096]{1,0:T(8,128)(2,1)S(1)} custom-call(bf16[256,512]{1,0:T(8,128)(2,1)S(1)} %get-tuple-element.60.g_ref, bf16[4096,128]{1,0:T(8,128)(2,1)S(1)} %copy-done.2, bf16[4096,128]{1,0:T(8,128)(2,1)} %collective-permute-done.6.b_ref, bf16[4096,128]{1,0:T(8,128)(2,1)} %collective-permute-done.c_ref, ...), custom_call_target="tpu_custom_call" | custom-call | flops 1073741 | bytes 6291 | tf_op jit(solution)/shard_map/pallas_call | solution.py:257
  141.2 1.4 copy-done
  142.6 4.0 %shard_map.49 = bf16[2048,128]{1,0:T(8,128)(2,1)} custom-call(bf16[224,2048]{1,0:T(8,128)(2,1)S(1)} %copy-done.4, bf16[224,2048]{1,0:T(8,128)(2,1)} %collective-permute-done.16.refs_1_, bf16[256,4096]{1,0:T(8,128)(2,1)S(1)} %bitcast.15, bf16[256,4096]{1,0:T(8,128)(2,1)} %collective-permute-done.17.refs_3_.refs_5_, ...), custom_call_target="tpu_custom_call" | custom-call | flops 536870 | bytes 4718 | tf_op jit(solution)/shard_map/pallas_call | solution.py:273
  147.9 6.6 %all-to-all-start.3 = ((bf16[16,16,4096]{2,1,0:T(8,128)(2,1)}), bf16[16,16,4096]{2,1,0:T(8,128)(2,1)}, u32[]{:S(2)}, u32[]{:S(2)}) async-start(bf16[16,16,4096]{2,1,0:T(8,128)(2,1)} %bitcast.17), calls=%async_computation.3 | async-start | bytes 4194304 | tf_op jit(solution)/shard_map/all_to_all | solution.py:43
  156.0 1.0 copy-done.12
  157.0 1.0 copy-done.14
  158.0 3.2 %shard_map.50 = bf16[2048,128]{1,0:T(8,128)(2,1)S(1)} custom-call(bf16[224,1024]{1,0:T(8,128)(2,1)} %collective-permute-done.14.refs_0_, bf16[224,1024]{1,0:T(8,128)(2,1)} %collective-permute-done.15.refs_1_, bf16[224,1024]{1,0:T(8,128)(2,1)S(1)} %copy-done.12, bf16[224,1024]{1,0:T(8,128)(2,1)S(1)} %copy-done.14, bf16[256,4096]{1,0:T(8,128)(2,1)S(1)} %bitcast.16, ...), custom_call_target="tpu_custom_call" | custom-call | flops 536870 | bytes 4718 | tf_op jit(solution)/shard_map/pallas_call | solution.py:273
  162.1 1.3 convert_add_fusion.1
  163.4 10.8 %collective-permute-done.24 = bf16[2048,128]{1,0:T(8,128)(2,1)S(1)} collective-permute-done((bf16[2048,128]{1,0:T(8,128)(2,1)S(1)}, bf16[2048,128]{1,0:T(8,128)(2,1)S(1)}, u32[]{:S(2)}, u32[]{:S(2)}) %collective-permute-start.24) | collective-permute-done | bytes 524320 | tf_op jit(solution)/shard_map/ppermute | solution.py:39
  174.3 1.5 maximum_multiply_fusion
  175.8 10.3 %all-to-all-done.3 = bf16[16,16,4096]{2,1,0:T(8,128)(2,1)} async-done(((bf16[16,16,4096]{2,1,0:T(8,128)(2,1)}), bf16[16,16,4096]{2,1,0:T(8,128)(2,1)}, u32[]{:S(2)}, u32[]{:S(2)}) %all-to-all-start.3) | async-done | bytes 2097184 | tf_op jit(solution)/shard_map/all_to_all | solution.py:43
  186.2 1.9 %convert_reduce_fusion = f32[16,4096]{1,0:T(8,128)S(1)} fusion(bf16[16,16,4096]{2,1,0:T(8,128)(2,1)} %all-to-all-done.3), kind=kLoop, calls=%fused_computation | loop fusion | flops 2031616 | bytes 2359296 | tf_op jit(solution)/shard_map/reduce_sum | solution.py:372
  (79 shorter events, 18.7 us)
Async XLA Ops:
  0.6 27.9 %collective-permute-start = (bf16[4096,128]{1,0:T(8,128)(2,1)}, bf16[4096,128]{1,0:T(8,128)(2,1)}, u32[]{:S(2)}, u32[]{:S(2)}) collective-permute-start(bf16[4096,128]{1,0:T(8,128)(2,1)} %a_ref.3), channel_id=1, source_target_pairs={{0,72},{1,73},{2,74},{3,75},{4,76},{5,77},{6,78},{7,79},{8,64},{9,... | collective-permute-start | bytes 3145736 | tf_op jit(solution)/shard_map/ppermute | solution.py:39
  5.3 0.9 copy-start.15
  6.4 1.3 copy-start.1
  7.7 22.0 %copy-start.2 = (bf16[4096,128]{1,0:T(8,128)(2,1)S(1)}, bf16[4096,128]{1,0:T(8,128)(2,1)}, u32[]{:S(2)}) copy-start(bf16[4096,128]{1,0:T(8,128)(2,1)} %a_ref.3) | copy-start | bytes 3145732
  7.7 22.0 %copy-start.16 = (bf16[1,14,4096]{2,1,0:T(8,128)(2,1)S(1)}, bf16[1,14,4096]{2,1,0:T(8,128)(2,1)}, u32[]{:S(2)}) copy-start(bf16[1,14,4096]{2,1,0:T(8,128)(2,1)} %x_ref.1) | copy-start | bytes 344068
  7.7 44.9 %all-to-all-start = ((bf16[16,16,4096]{2,1,0:T(8,128)(2,1)}), bf16[16,16,4096]{2,1,0:T(8,128)(2,1)S(1)}, u32[]{:S(2)}, u32[]{:S(2)}) async-start(bf16[16,16,4096]{2,1,0:T(8,128)(2,1)} %bitcast.18), calls=%async_computation | async-start | bytes 4194304 | tf_op jit(solution)/shard_map/all_to_all | solution.py:43
  28.5 24.2 %collective-permute-start.1 = (bf16[4096,128]{1,0:T(8,128)(2,1)}, bf16[4096,128]{1,0:T(8,128)(2,1)}, u32[]{:S(2)}, u32[]{:S(2)}) collective-permute-start(bf16[4096,128]{1,0:T(8,128)(2,1)} %collective-permute-done.c_ref), channel_id=1, source_target_pairs={{0,1},{1,0},{2,3},{3,2},{4,5},{5,4},{6,7},{7,6},{8,9},{9,8},{10,11... | collective-permute-start | bytes 3145736 | tf_op jit(solution)/shard_map/ppermute | solution.py:39
  29.7 22.9 %collective-permute-start.6 = (bf16[4096,128]{1,0:T(8,128)(2,1)S(1)}, bf16[4096,128]{1,0:T(8,128)(2,1)}, u32[]{:S(2)}, u32[]{:S(2)}) collective-permute-start(bf16[4096,128]{1,0:T(8,128)(2,1)S(1)} %copy-done.2), channel_id=1, source_target_pairs={{0,1},{1,0},{2,3},{3,2},{4,5},{5,4},{6,7},{7,6},{8,9},{9,8},{10,11... | collective-permute-start | bytes 3145736 | tf_op jit(solution)/shard_map/ppermute | solution.py:39
  29.8 5.0 %collective-permute-start.2 = (bf16[14,2048]{1,0:T(8,128)(2,1)S(1)}, bf16[14,2048]{1,0:T(8,128)(2,1)S(1)}, u32[]{:S(2)}, u32[]{:S(2)}) collective-permute-start(bf16[14,2048]{1,0:T(8,128)(2,1)S(1)} %slice_bitcast_fusion), channel_id=1, source_target_pairs={{0,8},{1,9},{2,10},{3,11},{4,12},{5,13},{6,14},{7,15},{8,0},{9,1},... | collective-permute-start | bytes 172040 | tf_op jit(solution)/shard_map/ppermute | solution.py:39
  34.8 7.5 %collective-permute-start.5 = (bf16[14,2048]{1,0:T(8,128)(2,1)S(1)}, bf16[14,2048]{1,0:T(8,128)(2,1)S(1)}, u32[]{:S(2)}, u32[]{:S(2)}) collective-permute-start(bf16[14,2048]{1,0:T(8,128)(2,1)S(1)} %collective-permute-done.2), channel_id=1, source_target_pairs={{0,6},{1,7},{2,0},{3,1},{4,2},{5,3},{6,4},{7,5},{8,14},{9,15},{10,... | collective-permute-start | bytes 172040 | tf_op jit(solution)/shard_map/ppermute | solution.py:290
  37.2 7.3 %collective-permute-start.4 = (bf16[14,2048]{1,0:T(8,128)(2,1)S(1)}, bf16[14,2048]{1,0:T(8,128)(2,1)S(1)}, u32[]{:S(2)}, u32[]{:S(2)}) collective-permute-start(bf16[14,2048]{1,0:T(8,128)(2,1)S(1)} %collective-permute-done.2), channel_id=1, source_target_pairs={{0,4},{1,5},{2,6},{3,7},{4,0},{5,1},{6,2},{7,3},{8,12},{9,13},{10,... | collective-permute-start | bytes 172040 | tf_op jit(solution)/shard_map/ppermute | solution.py:290
  37.7 6.8 %collective-permute-start.3 = (bf16[14,2048]{1,0:T(8,128)(2,1)S(1)}, bf16[14,2048]{1,0:T(8,128)(2,1)S(1)}, u32[]{:S(2)}, u32[]{:S(2)}) collective-permute-start(bf16[14,2048]{1,0:T(8,128)(2,1)S(1)} %collective-permute-done.2), channel_id=1, source_target_pairs={{0,2},{1,3},{2,4},{3,5},{4,6},{5,7},{6,0},{7,1},{8,10},{9,11},{10,... | collective-permute-start | bytes 172040 | tf_op jit(solution)/shard_map/ppermute | solution.py:290
  52.7 14.0 %copy-start.6 = (bf16[64,2048]{1,0:T(8,128)(2,1)S(1)}, bf16[64,2048]{1,0:T(8,128)(2,1)}, u32[]{:S(2)}) copy-start(bf16[64,2048]{1,0:T(8,128)(2,1)} %concatenate.6.refs_0_) | copy-start | bytes 786436
  55.6 6.8 %collective-permute-start.8 = (bf16[256,512]{1,0:T(8,128)(2,1)S(1)}, bf16[256,512]{1,0:T(8,128)(2,1)S(1)}, u32[]{:S(2)}, u32[]{:S(2)}) collective-permute-start(bf16[256,512]{1,0:T(8,128)(2,1)S(1)} %shard_map.42.own_ref.e_ref), channel_id=1, source_target_pairs={{0,8},{1,9},{2,10},{3,11},{4,12},{5,13},{6,14},{7,15},{8,0},{9,1},... | collective-permute-start | bytes 786440 | tf_op jit(solution)/shard_map/ppermute | solution.py:39
  56.9 15.0 %collective-permute-start.7 = (bf16[256,512]{1,0:T(8,128)(2,1)S(1)}, bf16[256,512]{1,0:T(8,128)(2,1)S(1)}, u32[]{:S(2)}, u32[]{:S(2)}) collective-permute-start(bf16[256,512]{1,0:T(8,128)(2,1)S(1)} %shard_map.42.own_ref.e_ref), channel_id=1, source_target_pairs={{0,1},{1,0},{2,3},{3,2},{4,5},{5,4},{6,7},{7,6},{8,9},{9,8},{10,11... | collective-permute-start | bytes 786440 | tf_op jit(solution)/shard_map/ppermute | solution.py:39
  62.5 9.4 %collective-permute-start.9 = (bf16[256,512]{1,0:T(8,128)(2,1)S(1)}, bf16[256,512]{1,0:T(8,128)(2,1)S(1)}, u32[]{:S(2)}, u32[]{:S(2)}) collective-permute-start(bf16[256,512]{1,0:T(8,128)(2,1)S(1)} %collective-permute-done.8.far_ref), channel_id=1, source_target_pairs={{0,1},{1,0},{2,3},{3,2},{4,5},{5,4},{6,7},{7,6},{8,9},{9,8},{10,11... | collective-permute-start | bytes 786440 | tf_op jit(solution)/shard_map/ppermute | solution.py:39
  66.6 8.0 %collective-permute-start.12 = (bf16[64,2048]{1,0:T(8,128)(2,1)S(1)}, bf16[64,2048]{1,0:T(8,128)(2,1)S(1)}, u32[]{:S(2)}, u32[]{:S(2)}) collective-permute-start(bf16[64,2048]{1,0:T(8,128)(2,1)S(1)} %copy-done.6), channel_id=1, source_target_pairs={{0,48},{1,49},{2,50},{3,51},{4,52},{5,53},{6,54},{7,55},{8,56},{9,... | collective-permute-start | bytes 786440 | tf_op jit(solution)/shard_map/ppermute | solution.py:290
  68.4 9.2 %collective-permute-start.11 = (bf16[64,2048]{1,0:T(8,128)(2,1)S(1)}, bf16[64,2048]{1,0:T(8,128)(2,1)S(1)}, u32[]{:S(2)}, u32[]{:S(2)}) collective-permute-start(bf16[64,2048]{1,0:T(8,128)(2,1)S(1)} %copy-done.6), channel_id=1, source_target_pairs={{0,32},{1,33},{2,34},{3,35},{4,36},{5,37},{6,38},{7,39},{8,40},{9,... | collective-permute-start | bytes 786440 | tf_op jit(solution)/shard_map/ppermute | solution.py:290
  69.1 14.7 %collective-permute-start.10 = (bf16[64,2048]{1,0:T(8,128)(2,1)S(1)}, bf16[64,2048]{1,0:T(8,128)(2,1)S(1)}, u32[]{:S(2)}, u32[]{:S(2)}) collective-permute-start(bf16[64,2048]{1,0:T(8,128)(2,1)S(1)} %copy-done.6), channel_id=1, source_target_pairs={{0,16},{1,17},{2,18},{3,19},{4,20},{5,21},{6,22},{7,23},{8,24},{9,... | collective-permute-start | bytes 786440 | tf_op jit(solution)/shard_map/ppermute | solution.py:290
  71.1 0.8 copy-start.24
  72.8 1.0 copy-start.8
  73.8 0.8 copy-start.10
  84.5 22.5 %all-to-all-start.1 = ((bf16[16,16,1024]{2,1,0:T(8,128)(2,1)}), bf16[16,16,1024]{2,1,0:T(8,128)(2,1)}, u32[]{:S(2)}, u32[]{:S(2)}) async-start(bf16[16,16,1024]{2,1,0:T(8,128)(2,1)} %bitcast.20), calls=%async_computation.1 | async-start | bytes 1048576 | tf_op jit(solution)/shard_map/all_to_all | solution.py:43
  89.3 17.7 %collective-permute-start.14 = (bf16[224,1024]{1,0:T(8,128)(2,1)}, bf16[224,1024]{1,0:T(8,128)(2,1)}, u32[]{:S(2)}, u32[]{:S(2)}) collective-permute-start(bf16[224,1024]{1,0:T(8,128)(2,1)} %copy-done.24), channel_id=1, source_target_pairs={{0,8},{1,9},{2,10},{3,11},{4,12},{5,13},{6,14},{7,15},{8,0},{9,1},... | collective-permute-start | bytes 1376264 | tf_op jit(solution)/shard_map/ppermute | solution.py:39
  90.3 16.8 %collective-permute-start.13 = (bf16[256,512]{1,0:T(8,128)(2,1)S(1)}, bf16[256,512]{1,0:T(8,128)(2,1)}, u32[]{:S(2)}, u32[]{:S(2)}) collective-permute-start(bf16[256,512]{1,0:T(8,128)(2,1)S(1)} %shard_map.42.own_ref.e_ref), channel_id=1, source_target_pairs={{0,64},{1,65},{2,66},{3,67},{4,68},{5,69},{6,70},{7,71},{8,72},{9,... | collective-permute-start | bytes 786440 | tf_op jit(solution)/shard_map/ppermute | solution.py:39
  91.0 0.9 copy-start.7
  92.0 0.9 copy-start.18
  92.9 0.9 copy-start.20
  93.9 0.9 copy-start.22
  95.9 0.9 copy-start.3
  107.1 23.2 %collective-permute-start.17 = (bf16[256,4096]{1,0:T(8,128)(2,1)S(1)}, bf16[256,4096]{1,0:T(8,128)(2,1)}, u32[]{:S(2)}, u32[]{:S(2)}) collective-permute-start(bf16[256,4096]{1,0:T(8,128)(2,1)S(1)} %bitcast.14), channel_id=1, source_target_pairs={{0,1},{1,0},{2,3},{3,2},{4,5},{5,4},{6,7},{7,6},{8,9},{9,8},{10,11... | collective-permute-start | bytes 6291464 | tf_op jit(solution)/shard_map/ppermute | solution.py:39
  108.4 21.8 %collective-permute-start.16 = (bf16[224,2048]{1,0:T(8,128)(2,1)}, bf16[224,2048]{1,0:T(8,128)(2,1)}, u32[]{:S(2)}, u32[]{:S(2)}) collective-permute-start(bf16[224,2048]{1,0:T(8,128)(2,1)} %copy-done.3), channel_id=1, source_target_pairs={{0,1},{1,0},{2,3},{3,2},{4,5},{5,4},{6,7},{7,6},{8,9},{9,8},{10,11... | collective-permute-start | bytes 2752520 | tf_op jit(solution)/shard_map/ppermute | solution.py:39
  109.6 0.8 copy-start.5
  110.4 19.8 %all-to-all-start.2 = ((bf16[16,16,1024]{2,1,0:T(8,128)(2,1)}), bf16[16,16,1024]{2,1,0:T(8,128)(2,1)}, u32[]{:S(2)}, u32[]{:S(2)}) async-start(bf16[16,16,1024]{2,1,0:T(8,128)(2,1)} %bitcast.19), calls=%async_computation.2 | async-start | bytes 1048576 | tf_op jit(solution)/shard_map/all_to_all | solution.py:43
  117.0 13.3 %collective-permute-start.15 = (bf16[224,1024]{1,0:T(8,128)(2,1)}, bf16[224,1024]{1,0:T(8,128)(2,1)}, u32[]{:S(2)}, u32[]{:S(2)}) collective-permute-start(bf16[224,1024]{1,0:T(8,128)(2,1)} %copy-done.23), channel_id=1, source_target_pairs={{0,8},{1,9},{2,10},{3,11},{4,12},{5,13},{6,14},{7,15},{8,0},{9,1},... | collective-permute-start | bytes 1376264 | tf_op jit(solution)/shard_map/ppermute | solution.py:39
  130.2 1.2 copy-start.9
  133.2 9.4 %collective-permute-start.18 = (bf16[256,128]{1,0:T(8,128)(2,1)S(1)}, bf16[256,128]{1,0:T(8,128)(2,1)S(1)}, u32[]{:S(2)}, u32[]{:S(2)}) collective-permute-start(bf16[256,128]{1,0:T(8,128)(2,1)S(1)} %get-tuple-element.62), channel_id=1, source_target_pairs={{0,1},{1,0},{2,3},{3,2},{4,5},{5,4},{6,7},{7,6},{8,9},{9,8},{10,11... | collective-permute-start | bytes 196616 | tf_op jit(solution)/shard_map/ppermute | solution.py:39
  134.9 7.7 %collective-permute-start.19 = (bf16[224,128]{1,0:T(8,128)(2,1)S(1)}, bf16[224,128]{1,0:T(8,128)(2,1)S(1)}, u32[]{:S(2)}, u32[]{:S(2)}) collective-permute-start(bf16[224,128]{1,0:T(8,128)(2,1)S(1)} %get-tuple-element.63), channel_id=1, source_target_pairs={{0,8},{1,9},{2,10},{3,11},{4,12},{5,13},{6,14},{7,15},{8,0},{9,1},... | collective-permute-start | bytes 172040 | tf_op jit(solution)/shard_map/ppermute | solution.py:39
  137.0 5.6 %collective-permute-start.20 = (bf16[224,128]{1,0:T(8,128)(2,1)S(1)}, bf16[224,128]{1,0:T(8,128)(2,1)S(1)}, u32[]{:S(2)}, u32[]{:S(2)}) collective-permute-start(bf16[224,128]{1,0:T(8,128)(2,1)S(1)} %get-tuple-element.64), channel_id=1, source_target_pairs={{0,9},{1,8},{2,11},{3,10},{4,13},{5,12},{6,15},{7,14},{8,1},{9,0},... | collective-permute-start | bytes 172040 | tf_op jit(solution)/shard_map/ppermute | solution.py:39
  138.1 4.5 %copy-start.4 = (bf16[224,2048]{1,0:T(8,128)(2,1)S(1)}, bf16[224,2048]{1,0:T(8,128)(2,1)}, u32[]{:S(2)}) copy-start(bf16[224,2048]{1,0:T(8,128)(2,1)} %copy-done.3) | copy-start | bytes 2752516
  141.2 1.4 copy-start
  146.6 15.5 %collective-permute-start.21 = (bf16[2048,128]{1,0:T(8,128)(2,1)}, bf16[2048,128]{1,0:T(8,128)(2,1)}, u32[]{:S(2)}, u32[]{:S(2)}) collective-permute-start(bf16[2048,128]{1,0:T(8,128)(2,1)} %shard_map.49), channel_id=1, source_target_pairs={{0,64},{1,65},{2,66},{3,67},{4,68},{5,69},{6,70},{7,71},{8,72},{9,... | collective-permute-start | bytes 1572872 | tf_op jit(solution)/shard_map/ppermute | solution.py:39
  147.4 7.1 %collective-permute-start.22 = (bf16[224,1024]{1,0:T(8,128)(2,1)}, bf16[224,1024]{1,0:T(8,128)(2,1)S(1)}, u32[]{:S(2)}, u32[]{:S(2)}) collective-permute-start(bf16[224,1024]{1,0:T(8,128)(2,1)} %collective-permute-done.14.refs_0_), channel_id=1, source_target_pairs={{0,1},{1,0},{2,3},{3,2},{4,5},{5,4},{6,7},{7,6},{8,9},{9,8},{10,11... | collective-permute-start | bytes 1376264 | tf_op jit(solution)/shard_map/ppermute | solution.py:39
  147.8 7.4 %collective-permute-start.23 = (bf16[224,1024]{1,0:T(8,128)(2,1)}, bf16[224,1024]{1,0:T(8,128)(2,1)S(1)}, u32[]{:S(2)}, u32[]{:S(2)}) collective-permute-start(bf16[224,1024]{1,0:T(8,128)(2,1)} %collective-permute-done.15.refs_1_), channel_id=1, source_target_pairs={{0,1},{1,0},{2,3},{3,2},{4,5},{5,4},{6,7},{7,6},{8,9},{9,8},{10,11... | collective-permute-start | bytes 1376264 | tf_op jit(solution)/shard_map/ppermute | solution.py:39
  147.9 38.3 %all-to-all-start.3 = ((bf16[16,16,4096]{2,1,0:T(8,128)(2,1)}), bf16[16,16,4096]{2,1,0:T(8,128)(2,1)}, u32[]{:S(2)}, u32[]{:S(2)}) async-start(bf16[16,16,4096]{2,1,0:T(8,128)(2,1)} %bitcast.17), calls=%async_computation.3 | async-start | bytes 4194304 | tf_op jit(solution)/shard_map/all_to_all | solution.py:43
  156.0 1.0 copy-start.12
  157.0 1.0 copy-start.14
  161.3 12.9 %collective-permute-start.24 = (bf16[2048,128]{1,0:T(8,128)(2,1)S(1)}, bf16[2048,128]{1,0:T(8,128)(2,1)S(1)}, u32[]{:S(2)}, u32[]{:S(2)}) collective-permute-start(bf16[2048,128]{1,0:T(8,128)(2,1)S(1)} %shard_map.50), channel_id=1, source_target_pairs={{0,64},{1,65},{2,66},{3,67},{4,68},{5,69},{6,70},{7,71},{8,72},{9,... | collective-permute-start | bytes 1572872 | tf_op jit(solution)/shard_map/ppermute | solution.py:39
  (6 other events, 4.4 us)

commit v7 on v5

--- a/solution.py
+++ b/solution.py
@@ -10,8 +10,8 @@
 YS, ZS, XS, CS = 4, 2, 4, 2
 DP = YS * ZS * XS * CS
 PAD = 16
-TILE = 2048
-VMEM = 40 * 1024 * 1024
+TILE = 1024
+VMEM = 24 * 1024 * 1024
 
 
 def place(d):
@@ -61,9 +61,10 @@
     return jax.ShapeDtypeStruct(dims, dtype)
 
 
-def params(steps=0):
-    semantics = ("arbitrary",) * steps if steps else None
-    return pltpu.CompilerParams(vmem_limit_bytes=VMEM, dimension_semantics=semantics)
+def params(steps):
+    return pltpu.CompilerParams(
+        vmem_limit_bytes=VMEM, dimension_semantics=("arbitrary",) * steps
+    )
 
 
 def cost(flops, size):
@@ -78,30 +79,58 @@
     return matmul(jnp.where(pick, 1.0, 0.0).astype(x.dtype), x, 1, 0).astype(x.dtype)
 
 
-def compact_kernel(rows, x_ref, *o_refs):
-    at = 0
-    for ref in o_refs:
-        n = ref.shape[1]
-        ref[...] = without_padding(x_ref[:, at : at + n], rows)
-        at += n
-
-
-def compact(block, rows, widths):
-    n = block.shape[0] // PAD * rows
+def whole(*dims):
+    return pl.BlockSpec(dims, lambda *_: (0,) * len(dims))
+
+
+def columns(array_or_shape):
+    peers, _, rows, tile = array_or_shape.shape
+    return pl.BlockSpec((peers, 1, rows, tile), lambda k: (0, k, 0, 0))
+
+
+def joined(ref):
+    return ref[...].reshape(ref.shape[0] * ref.shape[2], ref.shape[3])
+
+
+def compact_kernel(rows, x_ref, left_ref, right_ref):
+    k = pl.program_id(0)
+    packed = without_padding(joined(x_ref), rows)
+
+    @pl.when(k < pl.num_programs(0) // 2)
+    def _():
+        left_ref[...] = packed
+
+    @pl.when(k >= pl.num_programs(0) // 2)
+    def _():
+        right_ref[...] = packed
+
+
+def compact(plane, rows):
+    peers, blocks, _, tile = plane.shape
+    half = blocks // 2
+    out = shape((peers * rows, half * tile))
     return pl.pallas_call(
         functools.partial(compact_kernel, rows),
-        out_shape=tuple(shape((n, width)) for width in widths),
-        compiler_params=params(),
-        cost_estimate=cost(2 * n * block.size, 4 * block.size),
-    )(block)
+        grid=(blocks,),
+        in_specs=[columns(plane)],
+        out_specs=(
+            pl.BlockSpec((peers * rows, tile), lambda k: (0, jnp.minimum(k, half - 1))),
+            pl.BlockSpec((peers * rows, tile), lambda k: (0, jnp.maximum(k, half) - half)),
+        ),
+        out_shape=(out, out),
+        compiler_params=params(1),
+        cost_estimate=cost(4 * plane.size, 4 * plane.size),
+    )(plane)
 
 
 def copies_kernel(x_ref, o_ref):
     x = x_ref[0]
     zeros = jnp.zeros((PAD - x.shape[0], x.shape[1]), x.dtype)
     x = jnp.concatenate([x, zeros], axis=0)
-    for i in range(o_ref.shape[0] // PAD):
-        o_ref[PAD * i : PAD * i + PAD, :] = x
+    for k in range(o_ref.shape[1]):
+        block = x[:, TILE * k : TILE * k + TILE]
+        for i in range(o_ref.shape[0]):
+            o_ref[i, k] = block
 
 
 def embed_kernel(h_ref, a_ref, b_ref, c_ref, d_ref, o_ref, acc_ref):
@@ -112,7 +141,7 @@
         acc_ref[...] = jnp.zeros_like(acc_ref)
 
     w = jnp.concatenate([a_ref[...], b_ref[...], c_ref[...], d_ref[...]], axis=1)
-    acc_ref[...] += matmul(h_ref[...], w, 1, 0)
+    acc_ref[...] += matmul(joined(h_ref), w, 1, 0)
 
     @pl.when(step == pl.num_programs(0) - 1)
     def _():
@@ -170,14 +199,11 @@
 
 def hidden_kernel(g_ref, a_ref, b_ref, c_ref, d_ref, o_ref):
     w = jnp.concatenate([a_ref[...], b_ref[...], c_ref[...], d_ref[...]], axis=1)
-    o_ref[...] = matmul(g_ref[...], w, 1, 1).astype(o_ref.dtype)
-
-
-def weight_kernel(low, n_far, *refs):
-    fars, (own_ref, gf_ref, go_ref, mine_ref, sib_ref) = refs[:n_far], refs[n_far:]
-    n = mine_ref.shape[0]
-    far = jnp.concatenate([ref[...] for ref in fars], axis=1)
-    h = jnp.concatenate([own_ref[:, low : low + n], far], axis=0)
+    o_ref[...] = matmul(g_ref[...], w, 1, 1).astype(o_ref.dtype).reshape(o_ref.shape)
+
+
+def weight_kernel(own_ref, far_ref, go_ref, gf_ref, mine_ref, sib_ref):
+    h = jnp.concatenate([joined(own_ref), far_ref[...]], axis=0)
     g = jnp.concatenate([go_ref[...], gf_ref[...]], axis=0)
     out = matmul(h, g, 0, 0)
     units = mine_ref.shape[1]
@@ -185,25 +211,32 @@
     sib_ref[...] = out[:, units:].astype(sib_ref.dtype)
 
 
+def rows_kernel(x_ref, o_ref):
+    total = jnp.sum(x_ref[:, 0].astype(jnp.float32), axis=0)
+    o_ref[0] = total[: o_ref.shape[1]]
+
+
 def copies_of(block, count):
-    n = block.shape[-1]
+    out = shape((count, block.shape[2] // TILE, PAD, TILE))
     return pl.pallas_call(
         copies_kernel,
-        out_shape=shape((count * PAD, n)),
-        compiler_params=params(),
-        cost_estimate=cost(0, 2 * count * PAD * n),
+        grid=(1,),
+        in_specs=[whole(*block.shape)],
+        out_specs=whole(*out.shape),
+        out_shape=out,
+        compiler_params=params(1),
+        cost_estimate=cost(0, 2 * count * block.size),
     )(block)
 
 
-def embed(plane, weights, tile=TILE):
-    rows, width = plane.shape
-    units = weights[0].shape[1]
+def embed(plane, weights):
+    width, units = weights[0].shape
+    rows = plane.size // width
     return pl.pallas_call(
         embed_kernel,
-        grid=(width // tile,),
-        in_specs=[pl.BlockSpec((rows, tile), lambda k: (0, k))]
-        + [pl.BlockSpec((tile, units), lambda k: (k, 0))] * 4,
-        out_specs=pl.BlockSpec((rows, 4 * units), lambda k: (0, 0)),
+        grid=(width // TILE,),
+        in_specs=[columns(plane)] + [pl.BlockSpec((TILE, units), lambda k: (k, 0))] * 4,
+        out_specs=whole(rows, 4 * units),
         out_shape=shape((rows, 4 * units)),
         scratch_shapes=[pltpu.VMEM((rows, 4 * units), jnp.float32)],
         compiler_params=params(1),
@@ -211,31 +244,52 @@
     )(plane, *weights)
 
 
-def hidden_terms(grad, weights, tile=TILE):
-    rows, units = grad.shape[0], weights[0].shape[1]
-    width = weights[0].shape[0]
+def hidden_terms(grad, weights):
+    rows = grad.shape[0]
+    width, units = weights[0].shape
+    out = shape((rows // PAD, width // TILE, PAD, TILE))
     return pl.pallas_call(
         hidden_kernel,
-        grid=(width // tile,),
-        in_specs=[pl.BlockSpec(grad.shape, lambda n: (0, 0))]
-        + [pl.BlockSpec((tile, units), lambda n: (n, 0))] * 4,
-        out_specs=pl.BlockSpec((rows, tile), lambda n: (0, n)),
-        out_shape=shape((rows, width)),
+        grid=(width // TILE,),
+        in_specs=[whole(*grad.shape)] + [pl.BlockSpec((TILE, units), lambda k: (k, 0))] * 4,
+        out_specs=columns(out),
+        out_shape=out,
         compiler_params=params(1),
         cost_estimate=cost(8 * rows * width * units, 2 * width * (rows + 4 * units)),
     )(grad, *weights)
 
 
-def weight_terms(plane, low, fars, g_far, g_own):
-    rows = plane.shape[0]
-    width = sum(far.shape[1] for far in fars)
+def hidden_rows(pieces, rows):
+    peers, blocks, _, tile = pieces.shape
+    return pl.pallas_call(
+        rows_kernel,
+        grid=(blocks,),
+        in_specs=[columns(pieces)],
+        out_specs=pl.BlockSpec((1, rows, tile), lambda k: (0, 0, k)),
+        out_shape=shape((1, rows, blocks * tile), jnp.float32),
+        compiler_params=params(1),
+        cost_estimate=cost(pieces.size, 3 * pieces.size),
+    )(pieces)
+
+
+def weight_terms(plane, first, far, g_own, g_far):
+    peers, _, rows, tile = plane.shape
+    width = far.shape[1]
     units = g_own.shape[1] // 2
     return pl.pallas_call(
-        functools.partial(weight_kernel, low, len(fars)),
+        weight_kernel,
+        grid=(width // tile,),
+        in_specs=[
+            pl.BlockSpec((peers, 1, rows, tile), lambda k: (0, k + first, 0, 0)),
+            pl.BlockSpec((far.shape[0], tile), lambda k: (0, k)),
+            whole(*g_own.shape),
+            whole(*g_far.shape),
+        ],
+        out_specs=(pl.BlockSpec((tile, units), lambda k: (k, 0)),) * 2,
         out_shape=(shape((width, units), jnp.float32), shape((width, units))),
-        compiler_params=params(),
-        cost_estimate=cost(8 * rows * width * units, 4 * width * (rows + 2 * units)),
-    )(*fars, plane, g_far, g_own)
+        compiler_params=params(1),
+        cost_estimate=cost(8 * far.size * units, 4 * far.size),
+    )(plane, far, g_own, g_far)
 
 
 def wide_sum(a, b):
@@ -264,55 +318,74 @@
     from_far_sib = swap(from_far, c=1)
     partner = swap(mine, view=1)
 
-    cuts = (0, width // 2, 7 * width // 8, width)
-    late, _ = lax.optimization_barrier((plane, from_far))
-    h_far = compact(late, rows, [high - low for low, high in zip(cuts, cuts[1:])])
-    h_far = [swap(block, z=1) for block in h_far]
+    h_left, h_right = compact(plane, rows)
+    h_left, h_right, from_far_sib, _, _ = lax.optimization_barrier(
+        (h_left, h_right, from_far_sib, from_far, from_sib)
+    )
+    h_left = swap(h_left, z=1)
+    h_right = swap(h_right, z=1)
 
     centered, factor, gram = pl.pallas_call(
         functools.partial(center_kernel, rows, samples),
+        grid=(1,),
+        in_specs=[whole(quarter, 4 * units)] * 4,
+        out_specs=(whole(4 * quarter, 4 * units), whole(8, 4 * units), whole(quarter, 4 * quarter)),
         out_shape=(
             shape((4 * quarter, 4 * units)),
             shape((8, 4 * units), jnp.float32),
             shape((quarter, 4 * quarter)),
         ),
-        compiler_params=params(),
+        compiler_params=params(1),
         cost_estimate=cost(8 * 4 * quarter * quarter * units, 16 * quarter * units * 2),
     )(mine, from_sib, from_far, from_far_sib)
 
     gram = exchange(gram, "yx")
-    gram, partner = lax.optimization_barrier((gram, partner))
     gram = pl.pallas_call(
         total_kernel,
+        grid=(1,),
+        in_specs=[whole(*gram.shape)],
+        out_specs=whole(*gram.shape),
         out_shape=shape(gram.shape),
-        compiler_params=params(),
+        compiler_params=params(1),
         cost_estimate=cost(gram.size, 4 * gram.size),
     )(gram)
-    gram, h_far[0] = lax.optimization_barrier((gram, h_far[0]))
+    gram, h_left, partner = lax.optimization_barrier((gram, h_left, partner))
     gram = exchange(gram, "yx")
-    gram, h_far[0], h_far[1] = lax.optimization_barrier((gram, h_far[0], h_far[1]))
 
     grad, g_own, g_far = pl.pallas_call(
         functools.partial(grad_kernel, rows, samples),
+        grid=(1,),
+        in_specs=[
+            whole(quarter, 4 * quarter),
+            whole(4 * quarter, 4 * units),
+            whole(8, 4 * units),
+            whole(quarter, 4 * units),
+            whole(quarter, 4 * units),
+        ],
+        out_specs=(
+            whole(quarter, 4 * units),
+            whole(quarter, 2 * units),
+            whole(peers * rows, 2 * units),
+        ),
         out_shape=(shape((quarter, 4 * units)),)
         + (shape((quarter, 2 * units)), shape((peers * rows, 2 * units))),
-        compiler_params=params(),
+        compiler_params=params(1),
         cost_estimate=cost(8 * 4 * quarter * quarter * units, 16 * quarter * units * 2),
     )(gram, centered, factor, mine, partner)
     g_far = swap(g_far, z=1)
 
     h_part = hidden_terms(grad, weights)
-    h_part, h_far[2] = lax.optimization_barrier((h_part, h_far[2]))
-    pieces = exchange(h_part, "yx").reshape(peers, PAD, width)
-    grad_rows = jnp.sum(pieces.astype(jnp.float32), axis=0)[:rows]
-
-    runs = []
-    for low, fars in ((0, h_far[:1]), (cuts[1], h_far[1:])):
-        mine, theirs = weight_terms(plane, low, fars, g_far, g_own)
-        total = rounded(mine + swap(theirs, c=1).astype(jnp.float32))
-        runs.append(wide_sum(total, swap(total, view=1)))
+    h_part, g_far = lax.optimization_barrier((h_part, g_far))
+    grad_rows = hidden_rows(exchange(h_part, "yx"), rows)
+
+    first, theirs = weight_terms(plane, 0, h_left, g_own, g_far)
+    theirs, h_right = lax.optimization_barrier((swap(theirs, c=1), h_right))
+    first = rounded(first + theirs.astype(jnp.float32))
+    second, theirs = weight_terms(plane, width // TILE // 2, h_right, g_own, g_far)
+    second = rounded(second + swap(theirs, c=1).astype(jnp.float32))
+    runs = [wide_sum(part, swap(part, view=1)) for part in (first, second)]
     grad_weight = jnp.concatenate(runs, axis=0) / jnp.sqrt(2.0 * samples)
-    return (grad_rows[None], grad_weight)
+    return (grad_rows, grad_weight)
 
 
 def solution(mesh):

time: 165 us -> 172 us (1.042)
  waiting for transfers between devices: 79.7 us -> 90.8 us
  starting transfers between devices: 49.3 us -> 44.2 us
  Pallas kernels: 16.7 us -> 19.7 us
  other arithmetic: 5.92 us -> 4.09 us
    all_to_all x4, waiting for transfers between devices: 24.8 us -> 38.3 us  [exchange(): lax.all_to_all(blocks, 'dp', 0, 0, tiled=True, axis_index_groups=groups(a...]
    ppermute x15 -> x14, starting transfers between devices: 25.7 us -> 22.1 us  [swap(): return lax.ppermute(block, ('view', 'dp'), route)]
    pallas_call x9 -> x10, Pallas kernels: 16.7 us -> 19.7 us  [the longest x2 4.86 us: weight_terms(): pl.pallas_call(weight_kernel, grid=(width // tile,), in_specs=[pl.BlockSp...]
    ppermute x15 -> x14, waiting for transfers between devices: 54.9 us -> 52.5 us  [swap(): return lax.ppermute(block, ('view', 'dp'), route)]
    reduce_sum x1 -> x0, other arithmetic: 1.92 us -> none  [on_device(): grad_rows = jnp.sum(pieces.astype(jnp.float32), axis=0)[:rows]]
    unnamed x30 -> x27, local copies, waits for them, and re-layouts: 11.4 us -> 11.2 us
  transfers between devices with their start and end apart: 19 -> 18, of which waited for: 11 -> 11; matrix products, arithmetic and copies ran while one was open for 2% -> 2% of each run, Pallas kernels for 6% -> 7%
where the time goes in v7:
time: 172 us; the launch traced here: 171 us
  waiting for transfers between devices  90.8 us (53%)
  starting transfers between devices  44.2 us (26%)
  Pallas kernels  19.7 us (11%)
  local copies, waits for them, and re-layouts  11.2 us (7%)
  other arithmetic  4.09 us (2%)
    ppermute x14, waiting for transfers between devices, swap(): return lax.ppermute(block, ('view', 'dp'), route)  52.5 us
    all_to_all x4, waiting for transfers between devices, exchange(): lax.all_to_all(blocks, 'dp', 0, 0, tiled=True, axis_index_groups=groups(a...  38.3 us
    all_to_all x4, starting transfers between devices, exchange(): lax.all_to_all(blocks, 'dp', 0, 0, tiled=True, axis_index_groups=groups(a...  22.2 us
    ppermute x14, starting transfers between devices, swap(): return lax.ppermute(block, ('view', 'dp'), route)  22.1 us
    unnamed x27, local copies, waits for them, and re-layouts  11.2 us
    pallas_call x2, Pallas kernels, weight_terms(): pl.pallas_call(weight_kernel, grid=(width // tile,), in_specs=[pl.BlockSp...  4.86 us
    pallas_call x1, Pallas kernels, embed(): pl.pallas_call(embed_kernel, grid=(width // TILE,), in_specs=[columns(pla...  3.82 us
    pallas_call x1, Pallas kernels, hidden_terms(): pl.pallas_call(hidden_kernel, grid=(width // TILE,), in_specs=[whole(*gra...  3.8 us
  transfers between devices with their start and end apart: 18, of which 11 were waited for; matrix products, arithmetic and copies ran while one was open for 2% of the time, Pallas kernels for 7%

profile of v7, /device:TPU:1, one launch (start us, length us, event | category | flops | bytes accessed | tf_op | source)
XLA Modules:
  0.0 170.8 jit_solution(15905917132314614676)
XLA Ops:
  0.6 4.7 %collective-permute-start = (bf16[4096,128]{1,0:T(8,128)(2,1)}, bf16[4096,128]{1,0:T(8,128)(2,1)}, u32[]{:S(2)}, u32[]{:S(2)}) collective-permute-start(bf16[4096,128]{1,0:T(8,128)(2,1)} %a_ref.3), channel_id=1, source_target_pairs={{0,72},{1,73},{2,74},{3,75},{4,76},{5,77},{6,78},{7,79},{8,64},{9,... | collective-permute-start | bytes 3145736 | tf_op jit(solution)/shard_map/ppermute | solution.py:39
  5.3 0.9 copy-done.11
  6.4 1.3 copy-done.1
  7.7 6.9 %all-to-all-start = ((bf16[16,4,16,1024]{3,2,1,0:T(8,128)(2,1)}), bf16[16,4,16,1024]{3,2,1,0:T(8,128)(2,1)S(1)}, u32[]{:S(2)}, u32[]{:S(2)}) async-start(bf16[16,4,16,1024]{3,2,1,0:T(8,128)(2,1)} %copy-done.1), calls=%async_computation | async-start | bytes 4194304 | tf_op jit(solution)/shard_map/all_to_all | solution.py:43
  14.6 13.9 %collective-permute-done.c_ref = bf16[4096,128]{1,0:T(8,128)(2,1)} collective-permute-done((bf16[4096,128]{1,0:T(8,128)(2,1)}, bf16[4096,128]{1,0:T(8,128)(2,1)}, u32[]{:S(2)}, u32[]{:S(2)}) %collective-permute-start) | collective-permute-done | bytes 1048608 | tf_op jit(solution)/shard_map/ppermute | solution.py:39
  28.5 1.2 collective-permute-start.1
  29.7 14.6 %all-to-all-done.h_ref.x_ref.own_ref = bf16[16,4,16,1024]{3,2,1,0:T(8,128)(2,1)S(1)} async-done(((bf16[16,4,16,1024]{3,2,1,0:T(8,128)(2,1)}), bf16[16,4,16,1024]{3,2,1,0:T(8,128)(2,1)S(1)}, u32[]{:S(2)}, u32[]{:S(2)}) %all-to-all-start) | async-done | bytes 2097184 | tf_op jit(solution)/shard_map/all_to_all | solution.py:43
  44.3 3.8 %shard_map.42.own_ref.e_ref = bf16[256,512]{1,0:T(8,128)(2,1)S(1)} custom-call(bf16[16,4,16,1024]{3,2,1,0:T(8,128)(2,1)S(1)} %all-to-all-done.h_ref.x_ref.own_ref, bf16[4096,128]{1,0:T(8,128)(2,1)S(1)} %copy-done.2, bf16[4096,128]{1,0:T(8,128)(2,1)} %collective-permute-done.2.b_ref, bf16[4096,128]{1,0:T(8,128)(2,1)} %collective-permute-done.c_ref, ...), custom_call_target="tpu_custom_call" | custom-call | flops 1073741824 | bytes 6291456 | tf_op jit(solution)/shard_map/pallas_call | solution.py:235
  48.6 2.5 %collective-permute-start.3 = (bf16[256,512]{1,0:T(8,128)(2,1)S(1)}, bf16[256,512]{1,0:T(8,128)(2,1)S(1)}, u32[]{:S(2)}, u32[]{:S(2)}) collective-permute-start(bf16[256,512]{1,0:T(8,128)(2,1)S(1)} %shard_map.42.own_ref.e_ref), channel_id=1, source_target_pairs={{0,1},{1,0},{2,3},{3,2},{4,5},{5,4},{6,7},{7,6},{8,9},{9,8},{10,11... | collective-permute-start | bytes 786440 | tf_op jit(solution)/shard_map/ppermute | solution.py:39
  51.1 3.9 %collective-permute-done.4.far_ref = bf16[256,512]{1,0:T(8,128)(2,1)S(1)} collective-permute-done((bf16[256,512]{1,0:T(8,128)(2,1)S(1)}, bf16[256,512]{1,0:T(8,128)(2,1)S(1)}, u32[]{:S(2)}, u32[]{:S(2)}) %collective-permute-start.4) | collective-permute-done | bytes 262176 | tf_op jit(solution)/shard_map/ppermute | solution.py:39
  55.0 3.6 %collective-permute-start.5 = (bf16[256,512]{1,0:T(8,128)(2,1)S(1)}, bf16[256,512]{1,0:T(8,128)(2,1)S(1)}, u32[]{:S(2)}, u32[]{:S(2)}) collective-permute-start(bf16[256,512]{1,0:T(8,128)(2,1)S(1)} %collective-permute-done.4.far_ref), channel_id=1, source_target_pairs={{0,1},{1,0},{2,3},{3,2},{4,5},{5,4},{6,7},{7,6},{8,9},{9,8},{10,11... | collective-permute-start | bytes 786440 | tf_op jit(solution)/shard_map/ppermute | solution.py:39
  58.5 2.7 %shard_map.43 = (bf16[224,2048]{1,0:T(8,128)(2,1)}, bf16[224,2048]{1,0:T(8,128)(2,1)S(1)}) custom-call(bf16[16,4,16,1024]{3,2,1,0:T(8,128)(2,1)S(1)} %all-to-all-done.h_ref.x_ref.own_ref), custom_call_target="tpu_custom_call" | custom-call | flops 4194304 | bytes 4194304 | tf_op jit(solution)/shard_map/pallas_call | solution.py:112
  61.3 0.9 copy-done.12
  62.5 0.9 shard_map.44
  63.4 1.0 copy-done.4
  64.4 0.8 copy-done.10
  65.2 4.4 %all-to-all-start.1 = ((bf16[16,16,1024]{2,1,0:T(8,128)(2,1)}), bf16[16,16,1024]{2,1,0:T(8,128)(2,1)}, u32[]{:S(2)}, u32[]{:S(2)}) async-start(bf16[16,16,1024]{2,1,0:T(8,128)(2,1)} %bitcast.5), calls=%async_computation.1 | async-start | bytes 1048576 | tf_op jit(solution)/shard_map/all_to_all | solution.py:43
  69.6 1.0 collective-permute-start.7
  70.6 9.9 %all-to-all-done.1 = bf16[16,16,1024]{2,1,0:T(8,128)(2,1)} async-done(((bf16[16,16,1024]{2,1,0:T(8,128)(2,1)}), bf16[16,16,1024]{2,1,0:T(8,128)(2,1)}, u32[]{:S(2)}, u32[]{:S(2)}) %all-to-all-start.1) | async-done | bytes 524320 | tf_op jit(solution)/shard_map/all_to_all | solution.py:43
  80.5 1.1 shard_map.45
  81.6 0.8 copy-done.3
  82.4 7.5 %collective-permute-done.7.p_ref = bf16[256,512]{1,0:T(8,128)(2,1)} collective-permute-done((bf16[256,512]{1,0:T(8,128)(2,1)S(1)}, bf16[256,512]{1,0:T(8,128)(2,1)}, u32[]{:S(2)}, u32[]{:S(2)}) %collective-permute-start.7) | collective-permute-done | bytes 262176 | tf_op jit(solution)/shard_map/ppermute | solution.py:39
  90.0 4.3 %all-to-all-start.2 = ((bf16[16,16,1024]{2,1,0:T(8,128)(2,1)}), bf16[16,16,1024]{2,1,0:T(8,128)(2,1)}, u32[]{:S(2)}, u32[]{:S(2)}) async-start(bf16[16,16,1024]{2,1,0:T(8,128)(2,1)} %bitcast.4), calls=%async_computation.2 | async-start | bytes 1048576 | tf_op jit(solution)/shard_map/all_to_all | solution.py:43
  94.3 2.2 %collective-permute-start.10 = (bf16[224,2048]{1,0:T(8,128)(2,1)}, bf16[224,2048]{1,0:T(8,128)(2,1)}, u32[]{:S(2)}, u32[]{:S(2)}) collective-permute-start(bf16[224,2048]{1,0:T(8,128)(2,1)} %copy-done.12), channel_id=1, source_target_pairs={{0,8},{1,9},{2,10},{3,11},{4,12},{5,13},{6,14},{7,15},{8,0},{9,1},... | collective-permute-start | bytes 2752520 | tf_op jit(solution)/shard_map/ppermute | solution.py:39
  96.5 8.4 %all-to-all-done.2 = bf16[16,16,1024]{2,1,0:T(8,128)(2,1)} async-done(((bf16[16,16,1024]{2,1,0:T(8,128)(2,1)}), bf16[16,16,1024]{2,1,0:T(8,128)(2,1)}, u32[]{:S(2)}, u32[]{:S(2)}) %all-to-all-start.2) | async-done | bytes 524320 | tf_op jit(solution)/shard_map/all_to_all | solution.py:43
  104.9 1.2 copy-done.5
  106.1 1.7 %shard_map.46 = (bf16[256,512]{1,0:T(8,128)(2,1)S(1)}, bf16[256,256]{1,0:T(8,128)(2,1)S(1)}, bf16[224,256]{1,0:T(8,128)(2,1)S(1)}) custom-call(bf16[256,1024]{1,0:T(8,128)(2,1)} %bitcast.3.m_ref, bf16[1024,512]{1,0:T(8,128)(2,1)S(1)} %copy-done.5, f32[8,512]{1,0:T(8,128)S(1)} %get-tuple-element.33.f_ref, bf16[256,512]{1,0:T(8,128)(2,1)S(1)} %shard_map.42.own_ref.e_ref, ...), custom_call_target="tpu_custom_call" | custom-call | flops 268435456 | bytes 1048576 | tf_op jit(solution)/shard_map/pallas_call | solution.py:355
  107.9 2.2 %collective-permute-start.8 = (bf16[224,256]{1,0:T(8,128)(2,1)S(1)}, bf16[224,256]{1,0:T(8,128)(2,1)S(1)}, u32[]{:S(2)}, u32[]{:S(2)}) collective-permute-start(bf16[224,256]{1,0:T(8,128)(2,1)S(1)} %get-tuple-element.36), channel_id=1, source_target_pairs={{0,8},{1,9},{2,10},{3,11},{4,12},{5,13},{6,14},{7,15},{8,0},{9,1},... | collective-permute-start | bytes 344072 | tf_op jit(solution)/shard_map/ppermute | solution.py:39
  110.1 3.8 %shard_map.47 = bf16[16,4,16,1024]{3,2,1,0:T(8,128)(2,1)S(1)} custom-call(bf16[256,512]{1,0:T(8,128)(2,1)S(1)} %get-tuple-element.35.g_ref, bf16[4096,128]{1,0:T(8,128)(2,1)S(1)} %copy-done.2, bf16[4096,128]{1,0:T(8,128)(2,1)} %collective-permute-done.2.b_ref, bf16[4096,128]{1,0:T(8,128)(2,1)} %collective-permute-done.c_ref, ...), custom_call_target="tpu_custom_call" | custom-call | flops 1073741824 | bytes 6291456 | tf_op jit(solution)/shard_map/pallas_call | solution.py:251
  113.9 1.4 copy-done
  115.3 4.2 %collective-permute-done.8.gf_ref = bf16[224,256]{1,0:T(8,128)(2,1)S(1)} collective-permute-done((bf16[224,256]{1,0:T(8,128)(2,1)S(1)}, bf16[224,256]{1,0:T(8,128)(2,1)S(1)}, u32[]{:S(2)}, u32[]{:S(2)}) %collective-permute-start.8) | collective-permute-done | bytes 114720 | tf_op jit(solution)/shard_map/ppermute | solution.py:39
  119.5 2.1 %shard_map.49 = (f32[2048,128]{1,0:T(8,128)S(1)}, bf16[2048,128]{1,0:T(8,128)(2,1)S(1)}) custom-call(bf16[16,4,16,1024]{3,2,1,0:T(8,128)(2,1)S(1)} %all-to-all-done.h_ref.x_ref.own_ref, bf16[224,2048]{1,0:T(8,128)(2,1)} %collective-permute-done.6.far_ref, bf16[256,256]{1,0:T(8,128)(2,1)S(1)} %get-tuple-element.39.go_ref, ...), custom_call_target="tpu_custom_call" | custom-call | flops 469762048 | bytes 1835008 | tf_op jit(solution)/shard_map/pallas_call | solution.py:279
  121.6 1.0 copy-done.6
  122.5 1.9 %collective-permute-start.9 = (bf16[2048,128]{1,0:T(8,128)(2,1)S(1)}, bf16[2048,128]{1,0:T(8,128)(2,1)}, u32[]{:S(2)}, u32[]{:S(2)}) collective-permute-start(bf16[2048,128]{1,0:T(8,128)(2,1)S(1)} %get-tuple-element.42), channel_id=1, source_target_pairs={{0,1},{1,0},{2,3},{3,2},{4,5},{5,4},{6,7},{7,6},{8,9},{9,8},{10,11... | collective-permute-start | bytes 1572872 | tf_op jit(solution)/shard_map/ppermute | solution.py:39
  124.4 1.7 collective-permute-done.9
  126.1 2.8 %shard_map.50 = (f32[2048,128]{1,0:T(8,128)S(1)}, bf16[2048,128]{1,0:T(8,128)(2,1)}) custom-call(bf16[16,4,16,1024]{3,2,1,0:T(8,128)(2,1)S(1)} %all-to-all-done.h_ref.x_ref.own_ref, bf16[224,2048]{1,0:T(8,128)(2,1)} %collective-permute-done.10.far_ref, bf16[256,256]{1,0:T(8,128)(2,1)S(1)} %get-tuple-element.39.go_ref, ...), custom_call_target="tpu_custom_call" | custom-call | flops 469762048 | bytes 1835008 | tf_op jit(solution)/shard_map/pallas_call | solution.py:279
  128.9 1.0 copy-done.8
  130.2 6.5 %all-to-all-start.3 = ((bf16[16,4,16,1024]{3,2,1,0:T(8,128)(2,1)}), bf16[16,4,16,1024]{3,2,1,0:T(8,128)(2,1)S(1)}, u32[]{:S(2)}, u32[]{:S(2)}) async-start(bf16[16,4,16,1024]{3,2,1,0:T(8,128)(2,1)} %copy-done), calls=%async_computation.3 | async-start | bytes 4194304 | tf_op jit(solution)/shard_map/all_to_all | solution.py:43
  136.8 1.2 add_convert_fusion.1
  138.0 0.6 collective-permute-start.11
  138.6 1.1 add_convert_fusion
  139.8 1.0 collective-permute-start.13
  140.8 10.2 %collective-permute-done.11 = bf16[2048,128]{1,0:T(8,128)(2,1)S(1)} collective-permute-done((bf16[2048,128]{1,0:T(8,128)(2,1)S(1)}, bf16[2048,128]{1,0:T(8,128)(2,1)S(1)}, u32[]{:S(2)}, u32[]{:S(2)}) %collective-permute-start.11) | collective-permute-done | bytes 524320 | tf_op jit(solution)/shard_map/ppermute | solution.py:39
  151.1 11.1 %collective-permute-done.13 = bf16[2048,128]{1,0:T(8,128)(2,1)S(1)} collective-permute-done((bf16[2048,128]{1,0:T(8,128)(2,1)S(1)}, bf16[2048,128]{1,0:T(8,128)(2,1)S(1)}, u32[]{:S(2)}, u32[]{:S(2)}) %collective-permute-start.13) | collective-permute-done | bytes 524320 | tf_op jit(solution)/shard_map/ppermute | solution.py:39
  162.3 1.5 maximum_multiply_fusion
  163.9 5.5 %all-to-all-done.3.x_ref = bf16[16,4,16,1024]{3,2,1,0:T(8,128)(2,1)S(1)} async-done(((bf16[16,4,16,1024]{3,2,1,0:T(8,128)(2,1)}), bf16[16,4,16,1024]{3,2,1,0:T(8,128)(2,1)S(1)}, u32[]{:S(2)}, u32[]{:S(2)}) %all-to-all-start.3) | async-done | bytes 2097184 | tf_op jit(solution)/shard_map/all_to_all | solution.py:43
  169.4 0.5 shard_map.48
  169.9 0.9 copy.4
  (30 shorter events, 1.6 us)
Async XLA Ops:
  0.6 27.9 %collective-permute-start = (bf16[4096,128]{1,0:T(8,128)(2,1)}, bf16[4096,128]{1,0:T(8,128)(2,1)}, u32[]{:S(2)}, u32[]{:S(2)}) collective-permute-start(bf16[4096,128]{1,0:T(8,128)(2,1)} %a_ref.3), channel_id=1, source_target_pairs={{0,72},{1,73},{2,74},{3,75},{4,76},{5,77},{6,78},{7,79},{8,64},{9,... | collective-permute-start | bytes 3145736 | tf_op jit(solution)/shard_map/ppermute | solution.py:39
  5.3 0.9 copy-start.11
  6.4 1.3 copy-start.1
  7.7 22.0 %copy-start.2 = (bf16[4096,128]{1,0:T(8,128)(2,1)S(1)}, bf16[4096,128]{1,0:T(8,128)(2,1)}, u32[]{:S(2)}) copy-start(bf16[4096,128]{1,0:T(8,128)(2,1)} %a_ref.3) | copy-start | bytes 3145732
  7.7 36.6 %all-to-all-start = ((bf16[16,4,16,1024]{3,2,1,0:T(8,128)(2,1)}), bf16[16,4,16,1024]{3,2,1,0:T(8,128)(2,1)S(1)}, u32[]{:S(2)}, u32[]{:S(2)}) async-start(bf16[16,4,16,1024]{3,2,1,0:T(8,128)(2,1)} %copy-done.1), calls=%async_computation | async-start | bytes 4194304 | tf_op jit(solution)/shard_map/all_to_all | solution.py:43
  28.5 15.8 %collective-permute-start.1 = (bf16[4096,128]{1,0:T(8,128)(2,1)}, bf16[4096,128]{1,0:T(8,128)(2,1)}, u32[]{:S(2)}, u32[]{:S(2)}) collective-permute-start(bf16[4096,128]{1,0:T(8,128)(2,1)} %collective-permute-done.c_ref), channel_id=1, source_target_pairs={{0,1},{1,0},{2,3},{3,2},{4,5},{5,4},{6,7},{7,6},{8,9},{9,8},{10,11... | collective-permute-start | bytes 3145736 | tf_op jit(solution)/shard_map/ppermute | solution.py:39
  29.7 14.6 %collective-permute-start.2 = (bf16[4096,128]{1,0:T(8,128)(2,1)S(1)}, bf16[4096,128]{1,0:T(8,128)(2,1)}, u32[]{:S(2)}, u32[]{:S(2)}) collective-permute-start(bf16[4096,128]{1,0:T(8,128)(2,1)S(1)} %copy-done.2), channel_id=1, source_target_pairs={{0,1},{1,0},{2,3},{3,2},{4,5},{5,4},{6,7},{7,6},{8,9},{9,8},{10,11... | collective-permute-start | bytes 3145736 | tf_op jit(solution)/shard_map/ppermute | solution.py:39
  48.2 6.8 %collective-permute-start.4 = (bf16[256,512]{1,0:T(8,128)(2,1)S(1)}, bf16[256,512]{1,0:T(8,128)(2,1)S(1)}, u32[]{:S(2)}, u32[]{:S(2)}) collective-permute-start(bf16[256,512]{1,0:T(8,128)(2,1)S(1)} %shard_map.42.own_ref.e_ref), channel_id=1, source_target_pairs={{0,8},{1,9},{2,10},{3,11},{4,12},{5,13},{6,14},{7,15},{8,0},{9,1},... | collective-permute-start | bytes 786440 | tf_op jit(solution)/shard_map/ppermute | solution.py:39
  48.6 13.6 %collective-permute-start.3 = (bf16[256,512]{1,0:T(8,128)(2,1)S(1)}, bf16[256,512]{1,0:T(8,128)(2,1)S(1)}, u32[]{:S(2)}, u32[]{:S(2)}) collective-permute-start(bf16[256,512]{1,0:T(8,128)(2,1)S(1)} %shard_map.42.own_ref.e_ref), channel_id=1, source_target_pairs={{0,1},{1,0},{2,3},{3,2},{4,5},{5,4},{6,7},{7,6},{8,9},{9,8},{10,11... | collective-permute-start | bytes 786440 | tf_op jit(solution)/shard_map/ppermute | solution.py:39
  55.0 7.2 %collective-permute-start.5 = (bf16[256,512]{1,0:T(8,128)(2,1)S(1)}, bf16[256,512]{1,0:T(8,128)(2,1)S(1)}, u32[]{:S(2)}, u32[]{:S(2)}) collective-permute-start(bf16[256,512]{1,0:T(8,128)(2,1)S(1)} %collective-permute-done.4.far_ref), channel_id=1, source_target_pairs={{0,1},{1,0},{2,3},{3,2},{4,5},{5,4},{6,7},{7,6},{8,9},{9,8},{10,11... | collective-permute-start | bytes 786440 | tf_op jit(solution)/shard_map/ppermute | solution.py:39
  61.3 0.9 copy-start.12
  62.2 27.8 %collective-permute-start.6 = (bf16[224,2048]{1,0:T(8,128)(2,1)}, bf16[224,2048]{1,0:T(8,128)(2,1)}, u32[]{:S(2)}, u32[]{:S(2)}) collective-permute-start(bf16[224,2048]{1,0:T(8,128)(2,1)} %get-tuple-element.30), channel_id=1, source_target_pairs={{0,8},{1,9},{2,10},{3,11},{4,12},{5,13},{6,14},{7,15},{8,0},{9,1},... | collective-permute-start | bytes 2752520 | tf_op jit(solution)/shard_map/ppermute | solution.py:39
  63.4 1.0 copy-start.4
  64.4 0.8 copy-start.10
  65.2 15.3 %all-to-all-start.1 = ((bf16[16,16,1024]{2,1,0:T(8,128)(2,1)}), bf16[16,16,1024]{2,1,0:T(8,128)(2,1)}, u32[]{:S(2)}, u32[]{:S(2)}) async-start(bf16[16,16,1024]{2,1,0:T(8,128)(2,1)} %bitcast.5), calls=%async_computation.1 | async-start | bytes 1048576 | tf_op jit(solution)/shard_map/all_to_all | solution.py:43
  69.6 20.3 %collective-permute-start.7 = (bf16[256,512]{1,0:T(8,128)(2,1)S(1)}, bf16[256,512]{1,0:T(8,128)(2,1)}, u32[]{:S(2)}, u32[]{:S(2)}) collective-permute-start(bf16[256,512]{1,0:T(8,128)(2,1)S(1)} %shard_map.42.own_ref.e_ref), channel_id=1, source_target_pairs={{0,64},{1,65},{2,66},{3,67},{4,68},{5,69},{6,70},{7,71},{8,72},{9,... | collective-permute-start | bytes 786440 | tf_op jit(solution)/shard_map/ppermute | solution.py:39
  81.6 0.8 copy-start.3
  90.0 14.9 %all-to-all-start.2 = ((bf16[16,16,1024]{2,1,0:T(8,128)(2,1)}), bf16[16,16,1024]{2,1,0:T(8,128)(2,1)}, u32[]{:S(2)}, u32[]{:S(2)}) async-start(bf16[16,16,1024]{2,1,0:T(8,128)(2,1)} %bitcast.4), calls=%async_computation.2 | async-start | bytes 1048576 | tf_op jit(solution)/shard_map/all_to_all | solution.py:43
  94.3 30.1 %collective-permute-start.10 = (bf16[224,2048]{1,0:T(8,128)(2,1)}, bf16[224,2048]{1,0:T(8,128)(2,1)}, u32[]{:S(2)}, u32[]{:S(2)}) collective-permute-start(bf16[224,2048]{1,0:T(8,128)(2,1)} %copy-done.12), channel_id=1, source_target_pairs={{0,8},{1,9},{2,10},{3,11},{4,12},{5,13},{6,14},{7,15},{8,0},{9,1},... | collective-permute-start | bytes 2752520 | tf_op jit(solution)/shard_map/ppermute | solution.py:39
  104.9 1.2 copy-start.5
  107.9 11.6 %collective-permute-start.8 = (bf16[224,256]{1,0:T(8,128)(2,1)S(1)}, bf16[224,256]{1,0:T(8,128)(2,1)S(1)}, u32[]{:S(2)}, u32[]{:S(2)}) collective-permute-start(bf16[224,256]{1,0:T(8,128)(2,1)S(1)} %get-tuple-element.36), channel_id=1, source_target_pairs={{0,8},{1,9},{2,10},{3,11},{4,12},{5,13},{6,14},{7,15},{8,0},{9,1},... | collective-permute-start | bytes 344072 | tf_op jit(solution)/shard_map/ppermute | solution.py:39
  113.9 1.4 copy-start
  121.6 1.0 copy-start.6
  122.5 3.5 %collective-permute-start.9 = (bf16[2048,128]{1,0:T(8,128)(2,1)S(1)}, bf16[2048,128]{1,0:T(8,128)(2,1)}, u32[]{:S(2)}, u32[]{:S(2)}) collective-permute-start(bf16[2048,128]{1,0:T(8,128)(2,1)S(1)} %get-tuple-element.42), channel_id=1, source_target_pairs={{0,1},{1,0},{2,3},{3,2},{4,5},{5,4},{6,7},{7,6},{8,9},{9,8},{10,11... | collective-permute-start | bytes 1572872 | tf_op jit(solution)/shard_map/ppermute | solution.py:39
  128.9 1.0 copy-start.8
  129.8 6.9 %copy-start.7 = (f32[2048,128]{1,0:T(8,128)S(1)}, f32[2048,128]{1,0:T(8,128)}, u32[]{:S(2)}) copy-start(f32[2048,128]{1,0:T(8,128)} %copy-done.6) | copy-start | bytes 3145732
  129.8 8.8 %collective-permute-start.12 = (bf16[2048,128]{1,0:T(8,128)(2,1)}, bf16[2048,128]{1,0:T(8,128)(2,1)}, u32[]{:S(2)}, u32[]{:S(2)}) collective-permute-start(bf16[2048,128]{1,0:T(8,128)(2,1)} %get-tuple-element.47), channel_id=1, source_target_pairs={{0,1},{1,0},{2,3},{3,2},{4,5},{5,4},{6,7},{7,6},{8,9},{9,8},{10,11... | collective-permute-start | bytes 1572872 | tf_op jit(solution)/shard_map/ppermute | solution.py:39
  130.2 39.2 %all-to-all-start.3 = ((bf16[16,4,16,1024]{3,2,1,0:T(8,128)(2,1)}), bf16[16,4,16,1024]{3,2,1,0:T(8,128)(2,1)S(1)}, u32[]{:S(2)}, u32[]{:S(2)}) async-start(bf16[16,4,16,1024]{3,2,1,0:T(8,128)(2,1)} %copy-done), calls=%async_computation.3 | async-start | bytes 4194304 | tf_op jit(solution)/shard_map/all_to_all | solution.py:43
  136.7 1.9 %copy-start.9 = (f32[2048,128]{1,0:T(8,128)S(1)}, f32[2048,128]{1,0:T(8,128)}, u32[]{:S(2)}) copy-start(f32[2048,128]{1,0:T(8,128)} %copy-done.8) | copy-start | bytes 3145732
  138.0 13.0 %collective-permute-start.11 = (bf16[2048,128]{1,0:T(8,128)(2,1)S(1)}, bf16[2048,128]{1,0:T(8,128)(2,1)S(1)}, u32[]{:S(2)}, u32[]{:S(2)}) collective-permute-start(bf16[2048,128]{1,0:T(8,128)(2,1)S(1)} %add_convert_fusion.1), channel_id=1, source_target_pairs={{0,64},{1,65},{2,66},{3,67},{4,68},{5,69},{6,70},{7,71},{8,72},{9,... | collective-permute-start | bytes 1572872 | tf_op jit(solution)/shard_map/ppermute | solution.py:39
  139.8 22.5 %collective-permute-start.13 = (bf16[2048,128]{1,0:T(8,128)(2,1)S(1)}, bf16[2048,128]{1,0:T(8,128)(2,1)S(1)}, u32[]{:S(2)}, u32[]{:S(2)}) collective-permute-start(bf16[2048,128]{1,0:T(8,128)(2,1)S(1)} %add_convert_fusion), channel_id=1, source_target_pairs={{0,64},{1,65},{2,66},{3,67},{4,68},{5,69},{6,70},{7,71},{8,72},{9,... | collective-permute-start | bytes 1572872 | tf_op jit(solution)/shard_map/ppermute | solution.py:39

commit v8 on v7

--- a/solution.py
+++ b/solution.py
@@ -10,7 +10,7 @@
 YS, ZS, XS, CS = 4, 2, 4, 2
 DP = YS * ZS * XS * CS
 PAD = 16
-TILE = 1024
+TILE = 512
 VMEM = 24 * 1024 * 1024
 
 
@@ -83,41 +83,35 @@
     return pl.BlockSpec(dims, lambda *_: (0,) * len(dims))
 
 
-def columns(array_or_shape):
+def columns(array_or_shape, count=1):
     peers, _, rows, tile = array_or_shape.shape
-    return pl.BlockSpec((peers, 1, rows, tile), lambda k: (0, k, 0, 0))
+    return pl.BlockSpec((peers, count, rows, tile), lambda k: (0, k, 0, 0))
 
 
 def joined(ref):
-    return ref[...].reshape(ref.shape[0] * ref.shape[2], ref.shape[3])
-
-
-def compact_kernel(rows, x_ref, left_ref, right_ref):
-    k = pl.program_id(0)
-    packed = without_padding(joined(x_ref), rows)
-
-    @pl.when(k < pl.num_programs(0) // 2)
-    def _():
-        left_ref[...] = packed
-
-    @pl.when(k >= pl.num_programs(0) // 2)
-    def _():
-        right_ref[...] = packed
-
-
-def compact(plane, rows):
-    peers, blocks, _, tile = plane.shape
-    half = blocks // 2
-    out = shape((peers * rows, half * tile))
+    n = ref.shape[0] * ref.shape[2]
+    blocks = [ref[:, k].reshape(n, ref.shape[3]) for k in range(ref.shape[1])]
+    return blocks[0] if len(blocks) == 1 else jnp.concatenate(blocks, axis=1)
+
+
+def compact_kernel(rows, x_ref, *o_refs):
+    k = 0
+    for ref in o_refs:
+        for at in range(0, ref.shape[1], TILE):
+            block = x_ref[:, k].reshape(x_ref.shape[0] * x_ref.shape[2], TILE)
+            ref[:, at : at + TILE] = without_padding(block, rows)
+            k += 1
+
+
+def compact(plane, rows, counts):
+    peers = plane.shape[0]
+    out = tuple(shape((peers * rows, count * TILE)) for count in counts)
     return pl.pallas_call(
         functools.partial(compact_kernel, rows),
-        grid=(blocks,),
-        in_specs=[columns(plane)],
-        out_specs=(
-            pl.BlockSpec((peers * rows, tile), lambda k: (0, jnp.minimum(k, half - 1))),
-            pl.BlockSpec((peers * rows, tile), lambda k: (0, jnp.maximum(k, half) - half)),
-        ),
-        out_shape=(out, out),
+        grid=(1,),
+        in_specs=[whole(*plane.shape)],
+        out_specs=tuple(whole(*each.shape) for each in out),
+        out_shape=out,
         compiler_params=params(1),
         cost_estimate=cost(4 * plane.size, 4 * plane.size),
     )(plane)
@@ -191,24 +185,33 @@
     grad = apart - f_ref[:1, :] * centered + coef_cov * coupled
     grad = grad.astype(jnp.bfloat16)
     o_ref[...] = grad
-    own_ref, far_ref = run_refs
-    n = own_ref.shape[1]
-    own_ref[...] = grad[:, :n]
-    far_ref[...] = without_padding(grad[:, n:], rows)
+    packed = without_padding(grad[:, 256:], rows)
+    for i, ref in enumerate(run_refs[:2]):
+        ref[...] = grad[:, 128 * i : 128 * i + 128]
+    for i, ref in enumerate(run_refs[2:]):
+        ref[...] = packed[:, 128 * i : 128 * i + 128]
 
 
 def hidden_kernel(g_ref, a_ref, b_ref, c_ref, d_ref, o_ref):
     w = jnp.concatenate([a_ref[...], b_ref[...], c_ref[...], d_ref[...]], axis=1)
-    o_ref[...] = matmul(g_ref[...], w, 1, 1).astype(o_ref.dtype).reshape(o_ref.shape)
-
-
-def weight_kernel(own_ref, far_ref, go_ref, gf_ref, mine_ref, sib_ref):
-    h = jnp.concatenate([joined(own_ref), far_ref[...]], axis=0)
-    g = jnp.concatenate([go_ref[...], gf_ref[...]], axis=0)
-    out = matmul(h, g, 0, 0)
-    units = mine_ref.shape[1]
-    mine_ref[...] = out[:, :units]
-    sib_ref[...] = out[:, units:].astype(sib_ref.dtype)
+    out = matmul(g_ref[...], w, 1, 1).astype(o_ref.dtype)
+    peers, count, rows, tile = o_ref.shape
+    for k in range(count):
+        o_ref[:, k] = out[:, tile * k : tile * k + tile].reshape(peers, rows, tile)
+
+
+def weight_kernel(starts, *refs):
+    own_ref, sib_ref, *refs = refs
+    count = len(starts)
+    grads, o_ref = refs[2 * count : -1], refs[-1]
+    parts = [joined(own_ref), joined(sib_ref)]
+    for chunks in (refs[:count], refs[count : 2 * count]):
+        far = chunks[0][...]
+        for start, ref in zip(starts[1:], chunks[1:]):
+            far = jnp.where(pl.program_id(0) >= start, ref[...], far)
+        parts.append(far)
+    g = jnp.concatenate([ref[...] for ref in grads], axis=0)
+    o_ref[...] = matmul(jnp.concatenate(parts, axis=0), g, 0, 0).astype(o_ref.dtype)
 
 
 def rows_kernel(x_ref, o_ref):
@@ -234,8 +237,9 @@
     rows = plane.size // width
     return pl.pallas_call(
         embed_kernel,
-        grid=(width // TILE,),
-        in_specs=[columns(plane)] + [pl.BlockSpec((TILE, units), lambda k: (k, 0))] * 4,
+        grid=(width // TILE // 4,),
+        in_specs=[columns(plane, 4)]
+        + [pl.BlockSpec((4 * TILE, units), lambda k: (k, 0))] * 4,
         out_specs=whole(rows, 4 * units),
         out_shape=shape((rows, 4 * units)),
         scratch_shapes=[pltpu.VMEM((rows, 4 * units), jnp.float32)],
@@ -250,9 +254,10 @@
     out = shape((rows // PAD, width // TILE, PAD, TILE))
     return pl.pallas_call(
         hidden_kernel,
-        grid=(width // TILE,),
-        in_specs=[whole(*grad.shape)] + [pl.BlockSpec((TILE, units), lambda k: (k, 0))] * 4,
-        out_specs=columns(out),
+        grid=(width // TILE // 4,),
+        in_specs=[whole(*grad.shape)]
+        + [pl.BlockSpec((4 * TILE, units), lambda k: (k, 0))] * 4,
+        out_specs=columns(out, 4),
         out_shape=out,
         compiler_params=params(1),
         cost_estimate=cost(8 * rows * width * units, 2 * width * (rows + 4 * units)),
@@ -272,24 +277,31 @@
     )(pieces)
 
 
-def weight_terms(plane, first, far, g_own, g_far):
+def weight_terms(plane, plane_sib, first, fars, far_sibs, grads):
     peers, _, rows, tile = plane.shape
-    width = far.shape[1]
-    units = g_own.shape[1] // 2
-    return pl.pallas_call(
-        weight_kernel,
-        grid=(width // tile,),
-        in_specs=[
-            pl.BlockSpec((peers, 1, rows, tile), lambda k: (0, k + first, 0, 0)),
-            pl.BlockSpec((far.shape[0], tile), lambda k: (0, k)),
-            whole(*g_own.shape),
-            whole(*g_far.shape),
-        ],
-        out_specs=(pl.BlockSpec((tile, units), lambda k: (k, 0)),) * 2,
-        out_shape=(shape((width, units), jnp.float32), shape((width, units))),
-        compiler_params=params(1),
-        cost_estimate=cost(8 * far.size * units, 4 * far.size),
-    )(plane, far, g_own, g_far)
+    units = grads[0].shape[1]
+    starts, specs, blocks = [], [], 0
+    for far in fars:
+        count = far.shape[1] // tile
+        starts.append(blocks)
+        specs.append(
+            pl.BlockSpec(
+                (far.shape[0], tile),
+                lambda k, start=blocks, last=count - 1: (0, jnp.clip(k - start, 0, last)),
+            )
+        )
+        blocks += count
+    width = blocks * tile
+    own = pl.BlockSpec((peers, 1, rows, tile), lambda k: (0, k + first, 0, 0))
+    return pl.pallas_call(
+        functools.partial(weight_kernel, starts),
+        grid=(blocks,),
+        in_specs=[own, own] + specs + specs + [whole(*g.shape) for g in grads],
+        out_specs=pl.BlockSpec((tile, units), lambda k: (k, 0)),
+        out_shape=shape((width, units)),
+        compiler_params=params(1),
+        cost_estimate=cost(8 * peers * rows * width * units, 8 * peers * rows * width),
+    )(plane, plane_sib, *fars, *far_sibs, *grads)
 
 
 def wide_sum(a, b):
@@ -315,15 +327,12 @@
     mine = embed(plane, weights)
     from_sib = swap(mine, c=1)
     from_far = swap(mine, z=1)
+    from_far, *h_far = lax.optimization_barrier((from_far, *compact(plane, rows, (4, 3, 1))))
     from_far_sib = swap(from_far, c=1)
     partner = swap(mine, view=1)
 
-    h_left, h_right = compact(plane, rows)
-    h_left, h_right, from_far_sib, _, _ = lax.optimization_barrier(
-        (h_left, h_right, from_far_sib, from_far, from_sib)
-    )
-    h_left = swap(h_left, z=1)
-    h_right = swap(h_right, z=1)
+    h_far[0] = swap(h_far[0], z=1)
+    h_far[1] = swap(h_far[1], z=1)
 
     centered, factor, gram = pl.pallas_call(
         functools.partial(center_kernel, rows, samples),
@@ -349,10 +358,14 @@
         compiler_params=params(1),
         cost_estimate=cost(gram.size, 4 * gram.size),
     )(gram)
-    gram, h_left, partner = lax.optimization_barrier((gram, h_left, partner))
+    gram, h_far[0], partner, plane_late = lax.optimization_barrier(
+        (gram, h_far[0], partner, plane)
+    )
+    plane_sib = swap(plane_late, c=1)
     gram = exchange(gram, "yx")
-
-    grad, g_own, g_far = pl.pallas_call(
+    gram, h_far[1] = lax.optimization_barrier((gram, h_far[1]))
+
+    grad, *runs = pl.pallas_call(
         functools.partial(grad_kernel, rows, samples),
         grid=(1,),
         in_specs=[
@@ -362,28 +375,30 @@
             whole(quarter, 4 * units),
             whole(quarter, 4 * units),
         ],
-        out_specs=(
-            whole(quarter, 4 * units),
-            whole(quarter, 2 * units),
-            whole(peers * rows, 2 * units),
-        ),
+        out_specs=(whole(quarter, 4 * units),)
+        + (whole(quarter, units),) * 2
+        + (whole(peers * rows, units),) * 2,
         out_shape=(shape((quarter, 4 * units)),)
-        + (shape((quarter, 2 * units)), shape((peers * rows, 2 * units))),
+        + (shape((quarter, units)),) * 2
+        + (shape((peers * rows, units)),) * 2,
         compiler_params=params(1),
         cost_estimate=cost(8 * 4 * quarter * quarter * units, 16 * quarter * units * 2),
     )(gram, centered, factor, mine, partner)
-    g_far = swap(g_far, z=1)
-
+    g_far = swap(runs[2], z=1)
+    g_far_sib = swap(runs[3], z=1, c=1)
+    g_sib = swap(runs[1], c=1)
     h_part = hidden_terms(grad, weights)
-    h_part, g_far = lax.optimization_barrier((h_part, g_far))
+    h_part, *grads = lax.optimization_barrier((h_part, runs[0], g_sib, g_far, g_far_sib))
+    h_far[2], *grads = lax.optimization_barrier((h_far[2], *grads))
+    h_far[2] = swap(h_far[2], z=1)
+
     grad_rows = hidden_rows(exchange(h_part, "yx"), rows)
 
-    first, theirs = weight_terms(plane, 0, h_left, g_own, g_far)
-    theirs, h_right = lax.optimization_barrier((swap(theirs, c=1), h_right))
-    first = rounded(first + theirs.astype(jnp.float32))
-    second, theirs = weight_terms(plane, width // TILE // 2, h_right, g_own, g_far)
-    second = rounded(second + swap(theirs, c=1).astype(jnp.float32))
-    runs = [wide_sum(part, swap(part, view=1)) for part in (first, second)]
+    far_sibs = [swap(block, c=1) for block in h_far]
+    runs = []
+    for first, which in ((0, slice(0, 2)), (7, slice(2, 3))):
+        part = weight_terms(plane, plane_sib, first, h_far[which], far_sibs[which], grads)
+        runs.append(wide_sum(part, swap(part, view=1)))
     grad_weight = jnp.concatenate(runs, axis=0) / jnp.sqrt(2.0 * samples)
     return (grad_rows, grad_weight)
 

time: 172 us -> 176 us (1.023)
  starting transfers between devices: 44.2 us -> 50 us
  Pallas kernels: 19.7 us -> 23.2 us
  waiting for transfers between devices: 90.8 us -> 88.1 us
    all_to_all x4, waiting for transfers between devices: 38.3 us -> 24.5 us  [exchange(): lax.all_to_all(blocks, 'dp', 0, 0, tiled=True, axis_index_groups=groups(a...]
    ppermute x14 -> x19, waiting for transfers between devices: 52.5 us -> 63.6 us  [swap(): return lax.ppermute(block, ('view', 'dp'), route)]
    ppermute x14 -> x19, starting transfers between devices: 22.1 us -> 26.7 us  [swap(): return lax.ppermute(block, ('view', 'dp'), route)]
    pallas_call x1, Pallas kernels: 0.53 us -> 4.18 us  [hidden_rows(): pl.pallas_call(rows_kernel, grid=(blocks,), in_specs=[columns(pieces)], o...]
    convert_element_type x2 -> x0, other arithmetic: 2.38 us -> none  [rounded(): return lax.optimization_barrier(values.astype(jnp.bfloat16))]
    unnamed x27 -> x23, local copies, waits for them, and re-layouts: 11.2 us -> 9.82 us
  transfers between devices with their start and end apart: 18 -> 23, of which waited for: 11 -> 13; matrix products, arithmetic and copies ran while one was open for 2% -> 1% of each run, Pallas kernels for 7% -> 12%
where the time goes in v8:
time: 176 us; the launch traced here: 175 us
  waiting for transfers between devices  88.1 us (50%)
  starting transfers between devices  50 us (28%)
  Pallas kernels  23.2 us (13%)
  local copies, waits for them, and re-layouts  9.82 us (6%)
  other arithmetic  2.89 us (2%)
    ppermute x19, waiting for transfers between devices, swap(): return lax.ppermute(block, ('view', 'dp'), route)  63.6 us
    ppermute x19, starting transfers between devices, swap(): return lax.ppermute(block, ('view', 'dp'), route)  26.7 us
    all_to_all x4, waiting for transfers between devices, exchange(): lax.all_to_all(blocks, 'dp', 0, 0, tiled=True, axis_index_groups=groups(a...  24.5 us
    all_to_all x4, starting transfers between devices, exchange(): lax.all_to_all(blocks, 'dp', 0, 0, tiled=True, axis_index_groups=groups(a...  23.2 us
    unnamed x23, local copies, waits for them, and re-layouts  9.82 us
    pallas_call x2, Pallas kernels, weight_terms(): pl.pallas_call(functools.partial(weight_kernel, starts), grid=(blocks,),...  7.78 us
    pallas_call x1, Pallas kernels, hidden_rows(): pl.pallas_call(rows_kernel, grid=(blocks,), in_specs=[columns(pieces)], o...  4.18 us
  transfers between devices with their start and end apart: 23, of which 13 were waited for; matrix products, arithmetic and copies ran while one was open for 1% of the time, Pallas kernels for 12%

profile of v8, /device:TPU:1, one launch (start us, length us, event | category | flops | bytes accessed | tf_op | source)
XLA Modules:
  0.0 174.9 jit_solution(5516517875669609969)
XLA Ops:
  0.6 4.7 %collective-permute-start = (bf16[4096,128]{1,0:T(8,128)(2,1)}, bf16[4096,128]{1,0:T(8,128)(2,1)}, u32[]{:S(2)}, u32[]{:S(2)}) collective-permute-start(bf16[4096,128]{1,0:T(8,128)(2,1)} %a_ref.3), channel_id=1, source_target_pairs={{0,72},{1,73},{2,74},{3,75},{4,76},{5,77},{6,78},{7,79},{8,64},{9,... | collective-permute-start | bytes 3145736 | tf_op jit(solution)/shard_map/ppermute | solution.py:39
  5.3 0.9 copy-done.7
  6.4 1.3 copy-done.1
  7.7 6.9 %all-to-all-start = ((bf16[16,8,16,512]{3,2,1,0:T(8,128)(2,1)}), bf16[16,8,16,512]{3,2,1,0:T(8,128)(2,1)S(1)}, u32[]{:S(2)}, u32[]{:S(2)}) async-start(bf16[16,8,16,512]{3,2,1,0:T(8,128)(2,1)} %copy-done.1), calls=%async_computation | async-start | bytes 4194304 | tf_op jit(solution)/shard_map/all_to_all | solution.py:43
  14.6 13.9 %collective-permute-done.c_ref = bf16[4096,128]{1,0:T(8,128)(2,1)} collective-permute-done((bf16[4096,128]{1,0:T(8,128)(2,1)}, bf16[4096,128]{1,0:T(8,128)(2,1)}, u32[]{:S(2)}, u32[]{:S(2)}) %collective-permute-start) | collective-permute-done | bytes 1048608 | tf_op jit(solution)/shard_map/ppermute | solution.py:39
  28.5 1.2 collective-permute-start.1
  29.7 14.6 %all-to-all-done.h_ref.x_ref.refs_0_ = bf16[16,8,16,512]{3,2,1,0:T(8,128)(2,1)S(1)} async-done(((bf16[16,8,16,512]{3,2,1,0:T(8,128)(2,1)}), bf16[16,8,16,512]{3,2,1,0:T(8,128)(2,1)S(1)}, u32[]{:S(2)}, u32[]{:S(2)}) %all-to-all-start) | async-done | bytes 2097184 | tf_op jit(solution)/shard_map/all_to_all | solution.py:43
  44.3 2.9 %shard_map.42.own_ref.e_ref = bf16[256,512]{1,0:T(8,128)(2,1)S(1)} custom-call(bf16[16,8,16,512]{3,2,1,0:T(8,128)(2,1)S(1)} %all-to-all-done.h_ref.x_ref.refs_0_, bf16[4096,128]{1,0:T(8,128)(2,1)S(1)} %copy-done.2, bf16[4096,128]{1,0:T(8,128)(2,1)} %collective-permute-done.2.b_ref, bf16[4096,128]{1,0:T(8,128)(2,1)} %collective-permute-done.c_ref, ...), custom_call_target="tpu_custom_call" | custom-call | flops 1073741824 | bytes 6291456 | tf_op jit(solution)/shard_map/pallas_call | solution.py:238
  47.7 1.3 shard_map.43
  49.1 0.8 copy-done.8
  50.6 3.5 %collective-permute-done.4.far_ref = bf16[256,512]{1,0:T(8,128)(2,1)S(1)} collective-permute-done((bf16[256,512]{1,0:T(8,128)(2,1)S(1)}, bf16[256,512]{1,0:T(8,128)(2,1)S(1)}, u32[]{:S(2)}, u32[]{:S(2)}) %collective-permute-start.4) | collective-permute-done | bytes 262176 | tf_op jit(solution)/shard_map/ppermute | solution.py:39
  54.1 0.7 collective-permute-start.6
  54.8 3.4 %collective-permute-start.3 = (bf16[256,512]{1,0:T(8,128)(2,1)S(1)}, bf16[256,512]{1,0:T(8,128)(2,1)S(1)}, u32[]{:S(2)}, u32[]{:S(2)}) collective-permute-start(bf16[256,512]{1,0:T(8,128)(2,1)S(1)} %shard_map.42.own_ref.e_ref), channel_id=1, source_target_pairs={{0,1},{1,0},{2,3},{3,2},{4,5},{5,4},{6,7},{7,6},{8,9},{9,8},{10,11... | collective-permute-start | bytes 786440 | tf_op jit(solution)/shard_map/ppermute | solution.py:39
  58.3 1.2 collective-permute-done.3.sib_ref
  59.8 0.9 shard_map.44
  60.7 1.0 copy-done.4
  61.7 0.8 copy-done.6
  62.5 4.4 %all-to-all-start.1 = ((bf16[16,16,1024]{2,1,0:T(8,128)(2,1)}), bf16[16,16,1024]{2,1,0:T(8,128)(2,1)}, u32[]{:S(2)}, u32[]{:S(2)}) async-start(bf16[16,16,1024]{2,1,0:T(8,128)(2,1)} %bitcast.5), calls=%async_computation.1 | async-start | bytes 1048576 | tf_op jit(solution)/shard_map/all_to_all | solution.py:43
  66.9 1.0 collective-permute-start.7
  67.9 9.8 %all-to-all-done.1 = bf16[16,16,1024]{2,1,0:T(8,128)(2,1)} async-done(((bf16[16,16,1024]{2,1,0:T(8,128)(2,1)}), bf16[16,16,1024]{2,1,0:T(8,128)(2,1)}, u32[]{:S(2)}, u32[]{:S(2)}) %all-to-all-start.1) | async-done | bytes 524320 | tf_op jit(solution)/shard_map/all_to_all | solution.py:43
  77.7 1.1 shard_map.45
  78.8 0.8 copy-done.3
  79.6 3.5 %collective-permute-start.12 = (bf16[16,8,16,512]{3,2,1,0:T(8,128)(2,1)S(1)}, bf16[16,8,16,512]{3,2,1,0:T(8,128)(2,1)}, u32[]{:S(2)}, u32[]{:S(2)}) collective-permute-start(bf16[16,8,16,512]{3,2,1,0:T(8,128)(2,1)S(1)} %all-to-all-done.h_ref.x_ref.refs_0_), channel_id=1, source_target_pairs={{0,1},{1,0},{2,3},{3,2},{4,5},{5,4},{6,7},{7,6},{8,9},{9,8},{10,11... | collective-permute-start | bytes 6291464 | tf_op jit(solution)/shard_map/ppermute | solution.py:39
  83.2 1.3 collective-permute-start.8
  84.4 6.9 %all-to-all-start.2 = ((bf16[16,16,1024]{2,1,0:T(8,128)(2,1)}), bf16[16,16,1024]{2,1,0:T(8,128)(2,1)}, u32[]{:S(2)}, u32[]{:S(2)}) async-start(bf16[16,16,1024]{2,1,0:T(8,128)(2,1)} %bitcast.4), calls=%async_computation.2 | async-start | bytes 1048576 | tf_op jit(solution)/shard_map/all_to_all | solution.py:43
  91.4 10.7 %collective-permute-done.8.refs_3_ = bf16[224,1536]{1,0:T(8,128)(2,1)} collective-permute-done((bf16[224,1536]{1,0:T(8,128)(2,1)}, bf16[224,1536]{1,0:T(8,128)(2,1)}, u32[]{:S(2)}, u32[]{:S(2)}) %collective-permute-start.8) | collective-permute-done | bytes 688160 | tf_op jit(solution)/shard_map/ppermute | solution.py:39
  102.2 1.2 copy-done.5
  103.5 1.7 shard_map.46
  105.2 1.7 %collective-permute-start.9 = (bf16[256,128]{1,0:T(8,128)(2,1)S(1)}, bf16[256,128]{1,0:T(8,128)(2,1)S(1)}, u32[]{:S(2)}, u32[]{:S(2)}) collective-permute-start(bf16[256,128]{1,0:T(8,128)(2,1)S(1)} %get-tuple-element.49), channel_id=1, source_target_pairs={{0,1},{1,0},{2,3},{3,2},{4,5},{5,4},{6,7},{7,6},{8,9},{9,8},{10,11... | collective-permute-start | bytes 196616 | tf_op jit(solution)/shard_map/ppermute | solution.py:39
  107.0 0.8 collective-permute-start.10
  107.8 2.4 %collective-permute-start.11 = (bf16[224,128]{1,0:T(8,128)(2,1)S(1)}, bf16[224,128]{1,0:T(8,128)(2,1)S(1)}, u32[]{:S(2)}, u32[]{:S(2)}) collective-permute-start(bf16[224,128]{1,0:T(8,128)(2,1)S(1)} %get-tuple-element.51), channel_id=1, source_target_pairs={{0,9},{1,8},{2,11},{3,10},{4,13},{5,12},{6,15},{7,14},{8,1},{9,0},... | collective-permute-start | bytes 172040 | tf_op jit(solution)/shard_map/ppermute | solution.py:39
  110.2 3.0 %shard_map.47 = bf16[16,8,16,512]{3,2,1,0:T(8,128)(2,1)S(1)} custom-call(bf16[256,512]{1,0:T(8,128)(2,1)S(1)} %get-tuple-element.47.g_ref, bf16[4096,128]{1,0:T(8,128)(2,1)S(1)} %copy-done.2, bf16[4096,128]{1,0:T(8,128)(2,1)} %collective-permute-done.2.b_ref, bf16[4096,128]{1,0:T(8,128)(2,1)} %collective-permute-done.c_ref, ...), custom_call_target="tpu_custom_call" | custom-call | flops 1073741824 | bytes 6291456 | tf_op jit(solution)/shard_map/pallas_call | solution.py:255
  113.2 1.3 copy-done
  114.5 5.0 %all-to-all-start.3 = ((bf16[16,8,16,512]{3,2,1,0:T(8,128)(2,1)}), bf16[16,8,16,512]{3,2,1,0:T(8,128)(2,1)}, u32[]{:S(2)}, u32[]{:S(2)}) async-start(bf16[16,8,16,512]{3,2,1,0:T(8,128)(2,1)} %copy-done), calls=%async_computation.3 | async-start | bytes 4194304 | tf_op jit(solution)/shard_map/all_to_all | solution.py:43
  120.3 2.2 %collective-permute-done.13.refs_4_ = bf16[224,2048]{1,0:T(8,128)(2,1)S(1)} collective-permute-done((bf16[224,2048]{1,0:T(8,128)(2,1)}, bf16[224,2048]{1,0:T(8,128)(2,1)S(1)}, u32[]{:S(2)}, u32[]{:S(2)}) %collective-permute-start.13) | collective-permute-done | bytes 917536 | tf_op jit(solution)/shard_map/ppermute | solution.py:39
  122.5 1.0 collective-permute-done.14.refs_5_
  123.5 6.3 %shard_map.49 = bf16[3584,128]{1,0:T(8,128)(2,1)S(1)} custom-call(bf16[16,8,16,512]{3,2,1,0:T(8,128)(2,1)S(1)} %all-to-all-done.h_ref.x_ref.refs_0_, bf16[16,8,16,512]{3,2,1,0:T(8,128)(2,1)} %collective-permute-done.12.refs_1_, bf16[224,2048]{1,0:T(8,128)(2,1)} %collective-permute-done.6.refs_2_, bf16[224,1536]{1,0:T(8,128)(2,1)} %collective-permute-done.8.refs_3_, ...), custom_call_target="tpu_custom_call" | custom-call | flops 939524096 | bytes 7340032 | tf_op jit(solution)/shard_map/pallas_call | solution.py:296
  129.9 0.8 collective-permute-start.15
  130.7 2.6 %collective-permute-start.16 = (bf16[224,512]{1,0:T(8,128)(2,1)S(1)}, bf16[224,512]{1,0:T(8,128)(2,1)S(1)}, u32[]{:S(2)}, u32[]{:S(2)}) collective-permute-start(bf16[224,512]{1,0:T(8,128)(2,1)S(1)} %copy-done.10), channel_id=1, source_target_pairs={{0,8},{1,9},{2,10},{3,11},{4,12},{5,13},{6,14},{7,15},{8,0},{9,1},... | collective-permute-start | bytes 688136 | tf_op jit(solution)/shard_map/ppermute | solution.py:39
  133.3 25.0 %collective-permute-done.16.refs_2_ = bf16[224,512]{1,0:T(8,128)(2,1)S(1)} collective-permute-done((bf16[224,512]{1,0:T(8,128)(2,1)S(1)}, bf16[224,512]{1,0:T(8,128)(2,1)S(1)}, u32[]{:S(2)}, u32[]{:S(2)}) %collective-permute-start.16) | collective-permute-done | bytes 229408 | tf_op jit(solution)/shard_map/ppermute | solution.py:39
  158.3 1.2 collective-permute-start.17
  159.5 1.1 collective-permute-done.17.refs_3_
  160.6 1.4 shard_map.50
  162.1 4.7 %collective-permute-done.18 = bf16[512,128]{1,0:T(8,128)(2,1)S(1)} collective-permute-done((bf16[512,128]{1,0:T(8,128)(2,1)S(1)}, bf16[512,128]{1,0:T(8,128)(2,1)S(1)}, u32[]{:S(2)}, u32[]{:S(2)}) %collective-permute-start.18) | collective-permute-done | bytes 131104 | tf_op jit(solution)/shard_map/ppermute | solution.py:39
  166.9 4.2 %shard_map.48 = f32[1,14,4096]{2,1,0:T(8,128)S(1)} custom-call(bf16[16,8,16,512]{3,2,1,0:T(8,128)(2,1)} %all-to-all-done.3.x_ref), custom_call_target="tpu_custom_call" | custom-call | flops 1048576 | bytes 3145728 | tf_op jit(solution)/shard_map/pallas_call | solution.py:269
  171.1 0.9 copy.4
  172.0 1.4 convert_add_fusion
  173.4 1.5 maximum_multiply_fusion
  (34 shorter events, 2.9 us)
Async XLA Ops:
  0.6 27.9 %collective-permute-start = (bf16[4096,128]{1,0:T(8,128)(2,1)}, bf16[4096,128]{1,0:T(8,128)(2,1)}, u32[]{:S(2)}, u32[]{:S(2)}) collective-permute-start(bf16[4096,128]{1,0:T(8,128)(2,1)} %a_ref.3), channel_id=1, source_target_pairs={{0,72},{1,73},{2,74},{3,75},{4,76},{5,77},{6,78},{7,79},{8,64},{9,... | collective-permute-start | bytes 3145736 | tf_op jit(solution)/shard_map/ppermute | solution.py:39
  5.3 0.9 copy-start.7
  6.4 1.3 copy-start.1
  7.7 22.0 %copy-start.2 = (bf16[4096,128]{1,0:T(8,128)(2,1)S(1)}, bf16[4096,128]{1,0:T(8,128)(2,1)}, u32[]{:S(2)}) copy-start(bf16[4096,128]{1,0:T(8,128)(2,1)} %a_ref.3) | copy-start | bytes 3145732
  7.7 36.6 %all-to-all-start = ((bf16[16,8,16,512]{3,2,1,0:T(8,128)(2,1)}), bf16[16,8,16,512]{3,2,1,0:T(8,128)(2,1)S(1)}, u32[]{:S(2)}, u32[]{:S(2)}) async-start(bf16[16,8,16,512]{3,2,1,0:T(8,128)(2,1)} %copy-done.1), calls=%async_computation | async-start | bytes 4194304 | tf_op jit(solution)/shard_map/all_to_all | solution.py:43
  28.5 15.8 %collective-permute-start.1 = (bf16[4096,128]{1,0:T(8,128)(2,1)}, bf16[4096,128]{1,0:T(8,128)(2,1)}, u32[]{:S(2)}, u32[]{:S(2)}) collective-permute-start(bf16[4096,128]{1,0:T(8,128)(2,1)} %collective-permute-done.c_ref), channel_id=1, source_target_pairs={{0,1},{1,0},{2,3},{3,2},{4,5},{5,4},{6,7},{7,6},{8,9},{9,8},{10,11... | collective-permute-start | bytes 3145736 | tf_op jit(solution)/shard_map/ppermute | solution.py:39
  29.7 14.6 %collective-permute-start.2 = (bf16[4096,128]{1,0:T(8,128)(2,1)S(1)}, bf16[4096,128]{1,0:T(8,128)(2,1)}, u32[]{:S(2)}, u32[]{:S(2)}) collective-permute-start(bf16[4096,128]{1,0:T(8,128)(2,1)S(1)} %copy-done.2), channel_id=1, source_target_pairs={{0,1},{1,0},{2,3},{3,2},{4,5},{5,4},{6,7},{7,6},{8,9},{9,8},{10,11... | collective-permute-start | bytes 3145736 | tf_op jit(solution)/shard_map/ppermute | solution.py:39
  47.3 6.8 %collective-permute-start.4 = (bf16[256,512]{1,0:T(8,128)(2,1)S(1)}, bf16[256,512]{1,0:T(8,128)(2,1)S(1)}, u32[]{:S(2)}, u32[]{:S(2)}) collective-permute-start(bf16[256,512]{1,0:T(8,128)(2,1)S(1)} %shard_map.42.own_ref.e_ref), channel_id=1, source_target_pairs={{0,8},{1,9},{2,10},{3,11},{4,12},{5,13},{6,14},{7,15},{8,0},{9,1},... | collective-permute-start | bytes 786440 | tf_op jit(solution)/shard_map/ppermute | solution.py:39
  49.1 0.9 copy-start.8
  49.9 0.7 copy-start.9
  54.1 25.6 %collective-permute-start.6 = (bf16[224,2048]{1,0:T(8,128)(2,1)}, bf16[224,2048]{1,0:T(8,128)(2,1)}, u32[]{:S(2)}, u32[]{:S(2)}) collective-permute-start(bf16[224,2048]{1,0:T(8,128)(2,1)} %get-tuple-element.40), channel_id=1, source_target_pairs={{0,8},{1,9},{2,10},{3,11},{4,12},{5,13},{6,14},{7,15},{8,0},{9,1},... | collective-permute-start | bytes 2752520 | tf_op jit(solution)/shard_map/ppermute | solution.py:39
  54.8 4.6 %collective-permute-start.3 = (bf16[256,512]{1,0:T(8,128)(2,1)S(1)}, bf16[256,512]{1,0:T(8,128)(2,1)S(1)}, u32[]{:S(2)}, u32[]{:S(2)}) collective-permute-start(bf16[256,512]{1,0:T(8,128)(2,1)S(1)} %shard_map.42.own_ref.e_ref), channel_id=1, source_target_pairs={{0,1},{1,0},{2,3},{3,2},{4,5},{5,4},{6,7},{7,6},{8,9},{9,8},{10,11... | collective-permute-start | bytes 786440 | tf_op jit(solution)/shard_map/ppermute | solution.py:39
  58.2 1.5 collective-permute-start.5
  60.7 1.0 copy-start.4
  61.7 0.8 copy-start.6
  62.5 15.2 %all-to-all-start.1 = ((bf16[16,16,1024]{2,1,0:T(8,128)(2,1)}), bf16[16,16,1024]{2,1,0:T(8,128)(2,1)}, u32[]{:S(2)}, u32[]{:S(2)}) async-start(bf16[16,16,1024]{2,1,0:T(8,128)(2,1)} %bitcast.5), calls=%async_computation.1 | async-start | bytes 1048576 | tf_op jit(solution)/shard_map/all_to_all | solution.py:43
  66.9 12.7 %collective-permute-start.7 = (bf16[256,512]{1,0:T(8,128)(2,1)S(1)}, bf16[256,512]{1,0:T(8,128)(2,1)}, u32[]{:S(2)}, u32[]{:S(2)}) collective-permute-start(bf16[256,512]{1,0:T(8,128)(2,1)S(1)} %shard_map.42.own_ref.e_ref), channel_id=1, source_target_pairs={{0,64},{1,65},{2,66},{3,67},{4,68},{5,69},{6,70},{7,71},{8,72},{9,... | collective-permute-start | bytes 786440 | tf_op jit(solution)/shard_map/ppermute | solution.py:39
  78.8 0.8 copy-start.3
  79.6 43.9 %collective-permute-start.12 = (bf16[16,8,16,512]{3,2,1,0:T(8,128)(2,1)S(1)}, bf16[16,8,16,512]{3,2,1,0:T(8,128)(2,1)}, u32[]{:S(2)}, u32[]{:S(2)}) collective-permute-start(bf16[16,8,16,512]{3,2,1,0:T(8,128)(2,1)S(1)} %all-to-all-done.h_ref.x_ref.refs_0_), channel_id=1, source_target_pairs={{0,1},{1,0},{2,3},{3,2},{4,5},{5,4},{6,7},{7,6},{8,9},{9,8},{10,11... | collective-permute-start | bytes 6291464 | tf_op jit(solution)/shard_map/ppermute | solution.py:39
  83.2 18.9 %collective-permute-start.8 = (bf16[224,1536]{1,0:T(8,128)(2,1)}, bf16[224,1536]{1,0:T(8,128)(2,1)}, u32[]{:S(2)}, u32[]{:S(2)}) collective-permute-start(bf16[224,1536]{1,0:T(8,128)(2,1)} %copy-done.8), channel_id=1, source_target_pairs={{0,8},{1,9},{2,10},{3,11},{4,12},{5,13},{6,14},{7,15},{8,0},{9,1},... | collective-permute-start | bytes 2064392 | tf_op jit(solution)/shard_map/ppermute | solution.py:39
  84.4 17.8 %all-to-all-start.2 = ((bf16[16,16,1024]{2,1,0:T(8,128)(2,1)}), bf16[16,16,1024]{2,1,0:T(8,128)(2,1)}, u32[]{:S(2)}, u32[]{:S(2)}) async-start(bf16[16,16,1024]{2,1,0:T(8,128)(2,1)} %bitcast.4), calls=%async_computation.2 | async-start | bytes 1048576 | tf_op jit(solution)/shard_map/all_to_all | solution.py:43
  102.2 1.2 copy-start.5
  105.2 9.3 %collective-permute-start.9 = (bf16[256,128]{1,0:T(8,128)(2,1)S(1)}, bf16[256,128]{1,0:T(8,128)(2,1)S(1)}, u32[]{:S(2)}, u32[]{:S(2)}) collective-permute-start(bf16[256,128]{1,0:T(8,128)(2,1)S(1)} %get-tuple-element.49), channel_id=1, source_target_pairs={{0,1},{1,0},{2,3},{3,2},{4,5},{5,4},{6,7},{7,6},{8,9},{9,8},{10,11... | collective-permute-start | bytes 196616 | tf_op jit(solution)/shard_map/ppermute | solution.py:39
  107.0 7.6 %collective-permute-start.10 = (bf16[224,128]{1,0:T(8,128)(2,1)S(1)}, bf16[224,128]{1,0:T(8,128)(2,1)S(1)}, u32[]{:S(2)}, u32[]{:S(2)}) collective-permute-start(bf16[224,128]{1,0:T(8,128)(2,1)S(1)} %get-tuple-element.50), channel_id=1, source_target_pairs={{0,8},{1,9},{2,10},{3,11},{4,12},{5,13},{6,14},{7,15},{8,0},{9,1},... | collective-permute-start | bytes 172040 | tf_op jit(solution)/shard_map/ppermute | solution.py:39
  107.8 6.7 %collective-permute-start.11 = (bf16[224,128]{1,0:T(8,128)(2,1)S(1)}, bf16[224,128]{1,0:T(8,128)(2,1)S(1)}, u32[]{:S(2)}, u32[]{:S(2)}) collective-permute-start(bf16[224,128]{1,0:T(8,128)(2,1)S(1)} %get-tuple-element.51), channel_id=1, source_target_pairs={{0,9},{1,8},{2,11},{3,10},{4,13},{5,12},{6,15},{7,14},{8,1},{9,0},... | collective-permute-start | bytes 172040 | tf_op jit(solution)/shard_map/ppermute | solution.py:39
  113.2 1.3 copy-start
  114.5 52.3 %all-to-all-start.3 = ((bf16[16,8,16,512]{3,2,1,0:T(8,128)(2,1)}), bf16[16,8,16,512]{3,2,1,0:T(8,128)(2,1)}, u32[]{:S(2)}, u32[]{:S(2)}) async-start(bf16[16,8,16,512]{3,2,1,0:T(8,128)(2,1)} %copy-done), calls=%async_computation.3 | async-start | bytes 4194304 | tf_op jit(solution)/shard_map/all_to_all | solution.py:43
  119.5 11.2 %copy-start.10 = (bf16[224,512]{1,0:T(8,128)(2,1)S(1)}, bf16[224,512]{1,0:T(8,128)(2,1)}, u32[]{:S(2)}) copy-start(bf16[224,512]{1,0:T(8,128)(2,1)} %copy-done.9) | copy-start | bytes 688132
  119.5 3.0 %collective-permute-start.13 = (bf16[224,2048]{1,0:T(8,128)(2,1)}, bf16[224,2048]{1,0:T(8,128)(2,1)S(1)}, u32[]{:S(2)}, u32[]{:S(2)}) collective-permute-start(bf16[224,2048]{1,0:T(8,128)(2,1)} %collective-permute-done.6.refs_2_), channel_id=1, source_target_pairs={{0,1},{1,0},{2,3},{3,2},{4,5},{5,4},{6,7},{7,6},{8,9},{9,8},{10,11... | collective-permute-start | bytes 2752520 | tf_op jit(solution)/shard_map/ppermute | solution.py:39
  120.2 3.3 %collective-permute-start.14 = (bf16[224,1536]{1,0:T(8,128)(2,1)}, bf16[224,1536]{1,0:T(8,128)(2,1)S(1)}, u32[]{:S(2)}, u32[]{:S(2)}) collective-permute-start(bf16[224,1536]{1,0:T(8,128)(2,1)} %collective-permute-done.8.refs_3_), channel_id=1, source_target_pairs={{0,1},{1,0},{2,3},{3,2},{4,5},{5,4},{6,7},{7,6},{8,9},{9,8},{10,11... | collective-permute-start | bytes 2064392 | tf_op jit(solution)/shard_map/ppermute | solution.py:39
  129.9 42.1 %collective-permute-start.15 = (bf16[3584,128]{1,0:T(8,128)(2,1)S(1)}, bf16[3584,128]{1,0:T(8,128)(2,1)}, u32[]{:S(2)}, u32[]{:S(2)}) collective-permute-start(bf16[3584,128]{1,0:T(8,128)(2,1)S(1)} %shard_map.49), channel_id=1, source_target_pairs={{0,64},{1,65},{2,66},{3,67},{4,68},{5,69},{6,70},{7,71},{8,72},{9,... | collective-permute-start | bytes 2752520 | tf_op jit(solution)/shard_map/ppermute | solution.py:39
  130.7 27.6 %collective-permute-start.16 = (bf16[224,512]{1,0:T(8,128)(2,1)S(1)}, bf16[224,512]{1,0:T(8,128)(2,1)S(1)}, u32[]{:S(2)}, u32[]{:S(2)}) collective-permute-start(bf16[224,512]{1,0:T(8,128)(2,1)S(1)} %copy-done.10), channel_id=1, source_target_pairs={{0,8},{1,9},{2,10},{3,11},{4,12},{5,13},{6,14},{7,15},{8,0},{9,1},... | collective-permute-start | bytes 688136 | tf_op jit(solution)/shard_map/ppermute | solution.py:39
  158.3 2.3 %collective-permute-start.17 = (bf16[224,512]{1,0:T(8,128)(2,1)S(1)}, bf16[224,512]{1,0:T(8,128)(2,1)S(1)}, u32[]{:S(2)}, u32[]{:S(2)}) collective-permute-start(bf16[224,512]{1,0:T(8,128)(2,1)S(1)} %collective-permute-done.16.refs_2_), channel_id=1, source_target_pairs={{0,1},{1,0},{2,3},{3,2},{4,5},{5,4},{6,7},{7,6},{8,9},{9,8},{10,11... | collective-permute-start | bytes 688136 | tf_op jit(solution)/shard_map/ppermute | solution.py:39
  162.0 4.8 %collective-permute-start.18 = (bf16[512,128]{1,0:T(8,128)(2,1)S(1)}, bf16[512,128]{1,0:T(8,128)(2,1)S(1)}, u32[]{:S(2)}, u32[]{:S(2)}) collective-permute-start(bf16[512,128]{1,0:T(8,128)(2,1)S(1)} %shard_map.50), channel_id=1, source_target_pairs={{0,64},{1,65},{2,66},{3,67},{4,68},{5,69},{6,70},{7,71},{8,72},{9,... | collective-permute-start | bytes 393224 | tf_op jit(solution)/shard_map/ppermute | solution.py:39

commit v9 on v8

--- a/solution.py
+++ b/solution.py
@@ -10,7 +10,7 @@
 YS, ZS, XS, CS = 4, 2, 4, 2
 DP = YS * ZS * XS * CS
 PAD = 16
-TILE = 512
+TILE = 1024
 VMEM = 24 * 1024 * 1024
 
 
@@ -94,24 +94,18 @@
     return blocks[0] if len(blocks) == 1 else jnp.concatenate(blocks, axis=1)
 
 
-def compact_kernel(rows, x_ref, *o_refs):
-    k = 0
-    for ref in o_refs:
-        for at in range(0, ref.shape[1], TILE):
-            block = x_ref[:, k].reshape(x_ref.shape[0] * x_ref.shape[2], TILE)
-            ref[:, at : at + TILE] = without_padding(block, rows)
-            k += 1
-
-
-def compact(plane, rows, counts):
-    peers = plane.shape[0]
-    out = tuple(shape((peers * rows, count * TILE)) for count in counts)
+def compact_kernel(rows, x_ref, o_ref):
+    o_ref[...] = without_padding(joined(x_ref), rows)
+
+
+def compact(plane, rows):
+    peers, blocks, _, tile = plane.shape
     return pl.pallas_call(
         functools.partial(compact_kernel, rows),
-        grid=(1,),
-        in_specs=[whole(*plane.shape)],
-        out_specs=tuple(whole(*each.shape) for each in out),
-        out_shape=out,
+        grid=(blocks // 2,),
+        in_specs=[columns(plane, 2)],
+        out_specs=pl.BlockSpec((peers * rows, 2 * tile), lambda k: (0, k)),
+        out_shape=shape((peers * rows, blocks * tile)),
         compiler_params=params(1),
         cost_estimate=cost(4 * plane.size, 4 * plane.size),
     )(plane)
@@ -185,10 +179,8 @@
     grad = apart - f_ref[:1, :] * centered + coef_cov * coupled
     grad = grad.astype(jnp.bfloat16)
     o_ref[...] = grad
-    packed = without_padding(grad[:, 256:], rows)
-    for i, ref in enumerate(run_refs[:2]):
-        ref[...] = grad[:, 128 * i : 128 * i + 128]
-    for i, ref in enumerate(run_refs[2:]):
+    packed = without_padding(grad, rows)
+    for i, ref in enumerate(run_refs):
         ref[...] = packed[:, 128 * i : 128 * i + 128]
 
 
@@ -200,18 +192,17 @@
         o_ref[:, k] = out[:, tile * k : tile * k + tile].reshape(peers, rows, tile)
 
 
-def weight_kernel(starts, *refs):
-    own_ref, sib_ref, *refs = refs
-    count = len(starts)
-    grads, o_ref = refs[2 * count : -1], refs[-1]
-    parts = [joined(own_ref), joined(sib_ref)]
-    for chunks in (refs[:count], refs[count : 2 * count]):
-        far = chunks[0][...]
-        for start, ref in zip(starts[1:], chunks[1:]):
-            far = jnp.where(pl.program_id(0) >= start, ref[...], far)
-        parts.append(far)
-    g = jnp.concatenate([ref[...] for ref in grads], axis=0)
-    o_ref[...] = matmul(jnp.concatenate(parts, axis=0), g, 0, 0).astype(o_ref.dtype)
+def weight_kernel(z_ref, own_ref, sib_ref, *refs):
+    near, near_sib, far, far_sib, o_ref = refs
+    n = own_ref.shape[1]
+    h = [ref[i] for ref in (own_ref, sib_ref) for i in range(2)]
+    first = z_ref[0] == 0
+    g = []
+    for a, b in ((near[...], far[...]), (near_sib[...], far_sib[...])):
+        g += [jnp.where(first, a, b), jnp.where(first, b, a)]
+    o_ref[...] = matmul(jnp.concatenate(h, axis=0), jnp.concatenate(g, axis=0), 0, 0).astype(
+        o_ref.dtype
+    )
 
 
 def rows_kernel(x_ref, o_ref):
@@ -237,9 +228,9 @@
     rows = plane.size // width
     return pl.pallas_call(
         embed_kernel,
-        grid=(width // TILE // 4,),
-        in_specs=[columns(plane, 4)]
-        + [pl.BlockSpec((4 * TILE, units), lambda k: (k, 0))] * 4,
+        grid=(width // TILE // 2,),
+        in_specs=[columns(plane, 2)]
+        + [pl.BlockSpec((2 * TILE, units), lambda k: (k, 0))] * 4,
         out_specs=whole(rows, 4 * units),
         out_shape=shape((rows, 4 * units)),
         scratch_shapes=[pltpu.VMEM((rows, 4 * units), jnp.float32)],
@@ -254,10 +245,10 @@
     out = shape((rows // PAD, width // TILE, PAD, TILE))
     return pl.pallas_call(
         hidden_kernel,
-        grid=(width // TILE // 4,),
+        grid=(width // TILE // 2,),
         in_specs=[whole(*grad.shape)]
-        + [pl.BlockSpec((4 * TILE, units), lambda k: (k, 0))] * 4,
-        out_specs=columns(out, 4),
+        + [pl.BlockSpec((2 * TILE, units), lambda k: (k, 0))] * 4,
+        out_specs=columns(out, 2),
         out_shape=out,
         compiler_params=params(1),
         cost_estimate=cost(8 * rows * width * units, 2 * width * (rows + 4 * units)),
@@ -277,31 +268,21 @@
     )(pieces)
 
 
-def weight_terms(plane, plane_sib, first, fars, far_sibs, grads):
-    peers, _, rows, tile = plane.shape
+def weight_terms(z, both, both_sib, part, grads):
+    _, rows, width = both.shape
     units = grads[0].shape[1]
-    starts, specs, blocks = [], [], 0
-    for far in fars:
-        count = far.shape[1] // tile
-        starts.append(blocks)
-        specs.append(
-            pl.BlockSpec(
-                (far.shape[0], tile),
-                lambda k, start=blocks, last=count - 1: (0, jnp.clip(k - start, 0, last)),
-            )
-        )
-        blocks += count
-    width = blocks * tile
-    own = pl.BlockSpec((peers, 1, rows, tile), lambda k: (0, k + first, 0, 0))
-    return pl.pallas_call(
-        functools.partial(weight_kernel, starts),
-        grid=(blocks,),
-        in_specs=[own, own] + specs + specs + [whole(*g.shape) for g in grads],
+    tile, count = width // 4, 2
+    block = pl.BlockSpec((2, rows, tile), lambda k: (0, 0, k + count * part))
+    return pl.pallas_call(
+        weight_kernel,
+        grid=(count,),
+        in_specs=[pl.BlockSpec(memory_space=pltpu.SMEM), block, block]
+        + [whole(*g.shape) for g in grads],
         out_specs=pl.BlockSpec((tile, units), lambda k: (k, 0)),
-        out_shape=shape((width, units)),
-        compiler_params=params(1),
-        cost_estimate=cost(8 * peers * rows * width * units, 8 * peers * rows * width),
-    )(plane, plane_sib, *fars, *far_sibs, *grads)
+        out_shape=shape((width // 2, units)),
+        compiler_params=params(1),
+        cost_estimate=cost(4 * rows * width * units, 4 * rows * width),
+    )(z, both, both_sib, *grads)
 
 
 def wide_sum(a, b):
@@ -327,12 +308,10 @@
     mine = embed(plane, weights)
     from_sib = swap(mine, c=1)
     from_far = swap(mine, z=1)
-    from_far, *h_far = lax.optimization_barrier((from_far, *compact(plane, rows, (4, 3, 1))))
+    from_far, packed = lax.optimization_barrier((from_far, compact(plane, rows)))
+    both = lax.all_gather(packed, "dp", axis_index_groups=groups("z"))
     from_far_sib = swap(from_far, c=1)
     partner = swap(mine, view=1)
-
-    h_far[0] = swap(h_far[0], z=1)
-    h_far[1] = swap(h_far[1], z=1)
 
     centered, factor, gram = pl.pallas_call(
         functools.partial(center_kernel, rows, samples),
@@ -358,12 +337,8 @@
         compiler_params=params(1),
         cost_estimate=cost(gram.size, 4 * gram.size),
     )(gram)
-    gram, h_far[0], partner, plane_late = lax.optimization_barrier(
-        (gram, h_far[0], partner, plane)
-    )
-    plane_sib = swap(plane_late, c=1)
+    gram, partner = lax.optimization_barrier((gram, partner))
     gram = exchange(gram, "yx")
-    gram, h_far[1] = lax.optimization_barrier((gram, h_far[1]))
 
     grad, *runs = pl.pallas_call(
         functools.partial(grad_kernel, rows, samples),
@@ -376,11 +351,9 @@
             whole(quarter, 4 * units),
         ],
         out_specs=(whole(quarter, 4 * units),)
-        + (whole(quarter, units),) * 2
-        + (whole(peers * rows, units),) * 2,
+        + (whole(peers * rows, units),) * 4,
         out_shape=(shape((quarter, 4 * units)),)
-        + (shape((quarter, units)),) * 2
-        + (shape((peers * rows, units)),) * 2,
+        + (shape((peers * rows, units)),) * 4,
         compiler_params=params(1),
         cost_estimate=cost(8 * 4 * quarter * quarter * units, 16 * quarter * units * 2),
     )(gram, centered, factor, mine, partner)
@@ -388,17 +361,16 @@
     g_far_sib = swap(runs[3], z=1, c=1)
     g_sib = swap(runs[1], c=1)
     h_part = hidden_terms(grad, weights)
-    h_part, *grads = lax.optimization_barrier((h_part, runs[0], g_sib, g_far, g_far_sib))
-    h_far[2], *grads = lax.optimization_barrier((h_far[2], *grads))
-    h_far[2] = swap(h_far[2], z=1)
+    h_part, both, *grads = lax.optimization_barrier(
+        (h_part, both, runs[0], g_sib, g_far, g_far_sib)
+    )
 
     grad_rows = hidden_rows(exchange(h_part, "yx"), rows)
 
-    far_sibs = [swap(block, c=1) for block in h_far]
-    runs = []
-    for first, which in ((0, slice(0, 2)), (7, slice(2, 3))):
-        part = weight_terms(plane, plane_sib, first, h_far[which], far_sibs[which], grads)
-        runs.append(wide_sum(part, swap(part, view=1)))
+    both_sib = swap(both, c=1)
+    z = (lax.axis_index("dp") // (XS * CS) % ZS).astype(jnp.int32).reshape(1)
+    parts = [weight_terms(z, both, both_sib, part, grads) for part in (0, 1)]
+    runs = [wide_sum(part, swap(part, view=1)) for part in parts]
     grad_weight = jnp.concatenate(runs, axis=0) / jnp.sqrt(2.0 * samples)
     return (grad_rows, grad_weight)
 

time: 176 us -> 177 us (level)
  blocking collectives: 0 us -> 15.7 us
  between operations: 0.82 us -> 14.2 us
  starting transfers between devices: 50 us -> 36.8 us
  waiting for transfers between devices: 88.1 us -> 81 us
  Pallas kernels: 23.2 us -> 18.4 us
  local copies, waits for them, and re-layouts: 9.82 us -> 6.41 us
    ppermute x19 -> x13, waiting for transfers between devices: 63.6 us -> 24.8 us  [swap(): return lax.ppermute(block, ('view', 'dp'), route)]
    all_to_all x4 -> x3, waiting for transfers between devices: 24.5 us -> 49.3 us  [exchange(): lax.all_to_all(blocks, 'dp', 0, 0, tiled=True, axis_index_groups=groups(a...]
    all_to_all x0 -> x1, blocking collectives: none -> 15.7 us  [exchange(): lax.all_to_all(blocks, 'dp', 0, 0, tiled=True, axis_index_groups=groups(a...]
    ppermute x19 -> x13, starting transfers between devices: 26.7 us -> 18.6 us  [swap(): return lax.ppermute(block, ('view', 'dp'), route)]
    all_gather x0 -> x1, waiting for transfers between devices: none -> 6.85 us  [on_device(): both = lax.all_gather(packed, 'dp', axis_index_groups=groups('z'))]
    all_to_all x4 -> x3, starting transfers between devices: 23.2 us -> 18.1 us  [exchange(): lax.all_to_all(blocks, 'dp', 0, 0, tiled=True, axis_index_groups=groups(a...]
    pallas_call x1, Pallas kernels: 4.18 us -> 0.53 us  [hidden_rows(): pl.pallas_call(rows_kernel, grid=(blocks,), in_specs=[columns(pieces)], o...]
    unnamed x23 -> x11, local copies, waits for them, and re-layouts: 9.82 us -> 6.41 us
  transfers between devices with their start and end apart: 23 -> 17, of which waited for: 13 -> 10; matrix products, arithmetic and copies ran while one was open for 1% -> 1% of each run, Pallas kernels for 12% -> 9%
where the time goes in v9:
time: 177 us; the launch traced here: 176 us
  waiting for transfers between devices  81 us (46%)
  starting transfers between devices  36.8 us (21%)
  Pallas kernels  18.4 us (10%)
  blocking collectives  15.7 us (9%)
  between operations  14.2 us (8%)
  local copies, waits for them, and re-layouts  6.41 us (4%)
  other arithmetic  3.79 us (2%)
    all_to_all x3, waiting for transfers between devices, exchange(): lax.all_to_all(blocks, 'dp', 0, 0, tiled=True, axis_index_groups=groups(a...  49.3 us
    ppermute x13, waiting for transfers between devices, swap(): return lax.ppermute(block, ('view', 'dp'), route)  24.8 us
    ppermute x13, starting transfers between devices, swap(): return lax.ppermute(block, ('view', 'dp'), route)  18.6 us
    all_to_all x3, starting transfers between devices, exchange(): lax.all_to_all(blocks, 'dp', 0, 0, tiled=True, axis_index_groups=groups(a...  18.1 us
    all_to_all x1, blocking collectives, exchange(): lax.all_to_all(blocks, 'dp', 0, 0, tiled=True, axis_index_groups=groups(a...  15.7 us
    all_gather x1, waiting for transfers between devices, on_device(): both = lax.all_gather(packed, 'dp', axis_index_groups=groups('z'))  6.85 us
    unnamed x11, local copies, waits for them, and re-layouts  6.41 us
    pallas_call x2, Pallas kernels, weight_terms(): pl.pallas_call(weight_kernel, grid=(count,), in_specs=[pl.BlockSpec(memor...  5.48 us
  transfers between devices with their start and end apart: 17, of which 10 were waited for; matrix products, arithmetic and copies ran while one was open for 1% of the time, Pallas kernels for 9%

profile of v9, /device:TPU:1, one launch (start us, length us, event | category | flops | bytes accessed | tf_op | source)
XLA Modules:
  0.0 176.4 jit_solution(6233022909595117327)
XLA Ops:
  7.2 4.7 %collective-permute-start = (bf16[4096,128]{1,0:T(8,128)(2,1)}, bf16[4096,128]{1,0:T(8,128)(2,1)}, u32[]{:S(2)}, u32[]{:S(2)}) collective-permute-start(bf16[4096,128]{1,0:T(8,128)(2,1)} %a_ref.3), channel_id=1, source_target_pairs={{0,72},{1,73},{2,74},{3,75},{4,76},{5,77},{6,78},{7,79},{8,64},{9,... | collective-permute-start | bytes 3145736 | tf_op jit(solution)/shard_map/ppermute | solution.py:39
  11.8 0.9 copy-done.4
  12.7 0.2 shard_map.41
  12.9 0.0 copy-start.1
  13.0 1.3 copy-done.1
  14.3 6.9 %all-to-all-start = ((bf16[16,4,16,1024]{3,2,1,0:T(8,128)(2,1)}), bf16[16,4,16,1024]{3,2,1,0:T(8,128)(2,1)S(1)}, u32[]{:S(2)}, u32[]{:S(2)}) async-start(bf16[16,4,16,1024]{3,2,1,0:T(8,128)(2,1)} %copy-done.1), calls=%async_computation | async-start | bytes 4194304 | tf_op jit(solution)/shard_map/all_to_all | solution.py:43
  21.2 0.0 all-gather.3.cloned.1.call-start
  21.2 13.8 %collective-permute-done.c_ref = bf16[4096,128]{1,0:T(8,128)(2,1)} collective-permute-done((bf16[4096,128]{1,0:T(8,128)(2,1)}, bf16[4096,128]{1,0:T(8,128)(2,1)}, u32[]{:S(2)}, u32[]{:S(2)}) %collective-permute-start) | collective-permute-done | bytes 1048608 | tf_op jit(solution)/shard_map/ppermute | solution.py:39
  35.0 1.2 collective-permute-start.1
  36.3 0.0 collective-permute-start.2
  36.3 14.6 %all-to-all-done.h_ref.x_ref = bf16[16,4,16,1024]{3,2,1,0:T(8,128)(2,1)S(1)} async-done(((bf16[16,4,16,1024]{3,2,1,0:T(8,128)(2,1)}), bf16[16,4,16,1024]{3,2,1,0:T(8,128)(2,1)S(1)}, u32[]{:S(2)}, u32[]{:S(2)}) %all-to-all-start) | async-done | bytes 2097184 | tf_op jit(solution)/shard_map/all_to_all | solution.py:43
  50.9 2.9 %shard_map.42.own_ref.e_ref = bf16[256,512]{1,0:T(8,128)(2,1)S(1)} custom-call(bf16[16,4,16,1024]{3,2,1,0:T(8,128)(2,1)S(1)} %all-to-all-done.h_ref.x_ref, bf16[4096,128]{1,0:T(8,128)(2,1)S(1)} %copy-done.3, bf16[4096,128]{1,0:T(8,128)(2,1)} %collective-permute-done.2.b_ref, bf16[4096,128]{1,0:T(8,128)(2,1)} %collective-permute-done.c_ref, ...), custom_call_target="tpu_custom_call" | custom-call | flops 1073741824 | bytes 6291456 | tf_op jit(solution)/shard_map/pallas_call | solution.py:229
  53.8 0.5 collective-permute-start.4
  54.3 1.1 shard_map.43
  55.4 1.2 copy-done.2
  56.6 4.1 %collective-permute-done.4.far_ref = bf16[256,512]{1,0:T(8,128)(2,1)} collective-permute-done((bf16[256,512]{1,0:T(8,128)(2,1)S(1)}, bf16[256,512]{1,0:T(8,128)(2,1)}, u32[]{:S(2)}, u32[]{:S(2)}) %collective-permute-start.4) | collective-permute-done | bytes 262176 | tf_op jit(solution)/shard_map/ppermute | solution.py:39
  60.7 0.0 all-gather.3.cloned.1.call-update
  60.8 3.6 %collective-permute-start.3 = (bf16[256,512]{1,0:T(8,128)(2,1)S(1)}, bf16[256,512]{1,0:T(8,128)(2,1)S(1)}, u32[]{:S(2)}, u32[]{:S(2)}) collective-permute-start(bf16[256,512]{1,0:T(8,128)(2,1)S(1)} %shard_map.42.own_ref.e_ref), channel_id=1, source_target_pairs={{0,1},{1,0},{2,3},{3,2},{4,5},{5,4},{6,7},{7,6},{8,9},{9,8},{10,11... | collective-permute-start | bytes 786440 | tf_op jit(solution)/shard_map/ppermute | solution.py:39
  64.4 0.1 collective-permute-start.5
  64.5 1.1 collective-permute-done.3.sib_ref
  65.6 0.6 collective-permute-done.5.far_sib_ref
  66.2 2.6 %shard_map.44 = (bf16[1024,512]{1,0:T(8,128)(2,1)S(1)}, f32[8,512]{1,0:T(8,128)S(1)}, bf16[256,1024]{1,0:T(8,128)(2,1)}) custom-call(bf16[256,512]{1,0:T(8,128)(2,1)S(1)} %shard_map.42.own_ref.e_ref, bf16[256,512]{1,0:T(8,128)(2,1)S(1)} %collective-permute-done.3.sib_ref, bf16[256,512]{1,0:T(8,128)(2,1)} %collective-permute-done.4.far_ref, ...), custom_call_target="tpu_custom_call" | custom-call | flops 268435456 | bytes 1048576 | tf_op jit(solution)/shard_map/pallas_call | solution.py:316
  68.8 4.7 %all-to-all-start.1 = ((bf16[16,16,1024]{2,1,0:T(8,128)(2,1)}), bf16[16,16,1024]{2,1,0:T(8,128)(2,1)S(1)}, u32[]{:S(2)}, u32[]{:S(2)}) async-start(bf16[16,16,1024]{2,1,0:T(8,128)(2,1)} %bitcast), calls=%async_computation.1 | async-start | bytes 1048576 | tf_op jit(solution)/shard_map/all_to_all | solution.py:43
  73.4 0.1 collective-permute-start.6
  73.5 10.6 %all-to-all-done.1 = bf16[16,16,1024]{2,1,0:T(8,128)(2,1)S(1)} async-done(((bf16[16,16,1024]{2,1,0:T(8,128)(2,1)}), bf16[16,16,1024]{2,1,0:T(8,128)(2,1)S(1)}, u32[]{:S(2)}, u32[]{:S(2)}) %all-to-all-start.1) | async-done | bytes 524320 | tf_op jit(solution)/shard_map/all_to_all | solution.py:43
  84.2 0.1 shard_map.45
  84.3 2.7 %collective-permute-done.6.p_ref = bf16[256,512]{1,0:T(8,128)(2,1)} collective-permute-done((bf16[256,512]{1,0:T(8,128)(2,1)S(1)}, bf16[256,512]{1,0:T(8,128)(2,1)}, u32[]{:S(2)}, u32[]{:S(2)}) %collective-permute-start.6) | collective-permute-done | bytes 262176 | tf_op jit(solution)/shard_map/ppermute | solution.py:39
  86.9 15.7 %all_to_all.32 = bf16[16,16,1024]{2,1,0:T(8,128)(2,1)S(1)} all-to-all(bf16[16,16,1024]{2,1,0:T(8,128)(2,1)S(1)} %bitcast.10), channel_id=1, replica_groups={{0,2,4,6,16,18,20,22,32,34,36,38,48,50,52,54},{1,3,5,7,17,19,21,23,33,3..., dimensions={0} | all-to-all | bytes 1048576 | tf_op jit(solution)/shard_map/all_to_all | solution.py:43
  102.7 1.6 shard_map.46
  104.3 3.2 %collective-permute-start.7 = (bf16[224,128]{1,0:T(8,128)(2,1)S(1)}, bf16[224,128]{1,0:T(8,128)(2,1)S(1)}, u32[]{:S(2)}, u32[]{:S(2)}) collective-permute-start(bf16[224,128]{1,0:T(8,128)(2,1)S(1)} %get-tuple-element.31), channel_id=1, source_target_pairs={{0,1},{1,0},{2,3},{3,2},{4,5},{5,4},{6,7},{7,6},{8,9},{9,8},{10,11... | collective-permute-start | bytes 172040 | tf_op jit(solution)/shard_map/ppermute | solution.py:39
  107.5 3.2 %collective-permute-start.9 = (bf16[224,128]{1,0:T(8,128)(2,1)S(1)}, bf16[224,128]{1,0:T(8,128)(2,1)S(1)}, u32[]{:S(2)}, u32[]{:S(2)}) collective-permute-start(bf16[224,128]{1,0:T(8,128)(2,1)S(1)} %get-tuple-element.33), channel_id=1, source_target_pairs={{0,9},{1,8},{2,11},{3,10},{4,13},{5,12},{6,15},{7,14},{8,1},{9,0},... | collective-permute-start | bytes 172040 | tf_op jit(solution)/shard_map/ppermute | solution.py:39
  110.7 3.9 %shard_map.47 = bf16[16,4,16,1024]{3,2,1,0:T(8,128)(2,1)} custom-call(bf16[256,512]{1,0:T(8,128)(2,1)S(1)} %get-tuple-element.28.g_ref, bf16[4096,128]{1,0:T(8,128)(2,1)S(1)} %copy-done.3, bf16[4096,128]{1,0:T(8,128)(2,1)} %collective-permute-done.2.b_ref, bf16[4096,128]{1,0:T(8,128)(2,1)} %collective-permute-done.c_ref, ...), custom_call_target="tpu_custom_call" | custom-call | flops 1073741824 | bytes 6291456 | tf_op jit(solution)/shard_map/pallas_call | solution.py:246
  114.5 0.0 collective-permute-done.7.refs_1_
  114.6 2.5 %collective-permute-done.9.refs_3_ = bf16[224,128]{1,0:T(8,128)(2,1)S(1)} collective-permute-done((bf16[224,128]{1,0:T(8,128)(2,1)S(1)}, bf16[224,128]{1,0:T(8,128)(2,1)S(1)}, u32[]{:S(2)}, u32[]{:S(2)}) %collective-permute-start.9) | collective-permute-done | bytes 57376 | tf_op jit(solution)/shard_map/ppermute | solution.py:39
  117.0 6.8 %all-gather.3.cloned.1.call-done = bf16[448,4096]{1,0:T(8,128)(2,1)} async-done(((bf16[224,4096]{1,0:T(8,128)(2,1)}), bf16[448,4096]{1,0:T(8,128)(2,1)}) %all-gather.3.cloned.1.call-update) | async-done | bytes 3670032 | tf_op jit(solution)/shard_map/all_gather | solution.py:312
  123.9 0.5 collective-permute-start.10
  124.3 6.6 %all-to-all-start.3 = ((bf16[16,4,16,1024]{3,2,1,0:T(8,128)(2,1)}), bf16[16,4,16,1024]{3,2,1,0:T(8,128)(2,1)S(1)}, u32[]{:S(2)}, u32[]{:S(2)}) async-start(bf16[16,4,16,1024]{3,2,1,0:T(8,128)(2,1)} %shard_map.47), calls=%async_computation.3 | async-start | bytes 4194304 | tf_op jit(solution)/shard_map/all_to_all | solution.py:43
  131.0 2.0 %copy-done = bf16[448,4096]{1,0:T(8,128)(2,1)S(1)} copy-done((bf16[448,4096]{1,0:T(8,128)(2,1)S(1)}, bf16[448,4096]{1,0:T(8,128)(2,1)}, u32[]{:S(2)}) %copy-start) | copy-done | bytes 3670040
  133.0 2.7 %shard_map.49 = bf16[2048,128]{1,0:T(8,128)(2,1)S(1)} custom-call(s32[1]{0:T(128)} %bitcast.5.z_ref, bf16[2,224,4096]{2,1,0:T(8,128)(2,1)S(1)} %bitcast.7, bf16[2,224,4096]{2,1,0:T(8,128)(2,1)} %collective-permute-done.10.sib_ref, bf16[224,128]{1,0:T(8,128)(2,1)S(1)} %get-tuple-element.36.refs_0_, bf16[224,128]{1,0:T(8,128)(2,1)S(1)} %collective-permute-done.7.refs_1_, ...), custom_call_target="tpu_custom_call" | custom-call | flops 469762048 | bytes 3670016 | tf_op jit(solution)/shard_map/pallas_call | solution.py:276
  135.8 0.1 collective-permute-start.11
  135.8 2.7 %shard_map.50 = bf16[2048,128]{1,0:T(8,128)(2,1)S(1)} custom-call(s32[1]{0:T(128)} %bitcast.5.z_ref, bf16[2,224,4096]{2,1,0:T(8,128)(2,1)S(1)} %bitcast.8, bf16[2,224,4096]{2,1,0:T(8,128)(2,1)} %collective-permute-done.10.sib_ref, bf16[224,128]{1,0:T(8,128)(2,1)S(1)} %get-tuple-element.36.refs_0_, bf16[224,128]{1,0:T(8,128)(2,1)S(1)} %collective-permute-done.7.refs_1_, ...), custom_call_target="tpu_custom_call" | custom-call | flops 469762048 | bytes 3670016 | tf_op jit(solution)/shard_map/pallas_call | solution.py:276
  138.6 1.5 collective-permute-start.12
  140.1 24.1 %all-to-all-done.3.x_ref = bf16[16,4,16,1024]{3,2,1,0:T(8,128)(2,1)S(1)} async-done(((bf16[16,4,16,1024]{3,2,1,0:T(8,128)(2,1)}), bf16[16,4,16,1024]{3,2,1,0:T(8,128)(2,1)S(1)}, u32[]{:S(2)}, u32[]{:S(2)}) %all-to-all-start.3) | async-done | bytes 2097184 | tf_op jit(solution)/shard_map/all_to_all | solution.py:43
  164.2 0.5 shard_map.48
  164.8 0.9 copy.4
  165.7 1.1 convert_add_fusion.1
  166.9 1.1 convert_add_fusion
  168.0 1.5 maximum_multiply_fusion
  (12 shorter events, 0.0 us)
Async XLA Ops:
  7.2 27.9 %collective-permute-start = (bf16[4096,128]{1,0:T(8,128)(2,1)}, bf16[4096,128]{1,0:T(8,128)(2,1)}, u32[]{:S(2)}, u32[]{:S(2)}) collective-permute-start(bf16[4096,128]{1,0:T(8,128)(2,1)} %a_ref.3), channel_id=1, source_target_pairs={{0,72},{1,73},{2,74},{3,75},{4,76},{5,77},{6,78},{7,79},{8,64},{9,... | collective-permute-start | bytes 3145736 | tf_op jit(solution)/shard_map/ppermute | solution.py:39
  11.8 0.9 copy-start.4
  12.9 1.3 copy-start.1
  14.3 22.0 %copy-start.3 = (bf16[4096,128]{1,0:T(8,128)(2,1)S(1)}, bf16[4096,128]{1,0:T(8,128)(2,1)}, u32[]{:S(2)}) copy-start(bf16[4096,128]{1,0:T(8,128)(2,1)} %a_ref.3) | copy-start | bytes 3145732
  14.3 36.6 %all-to-all-start = ((bf16[16,4,16,1024]{3,2,1,0:T(8,128)(2,1)}), bf16[16,4,16,1024]{3,2,1,0:T(8,128)(2,1)S(1)}, u32[]{:S(2)}, u32[]{:S(2)}) async-start(bf16[16,4,16,1024]{3,2,1,0:T(8,128)(2,1)} %copy-done.1), calls=%async_computation | async-start | bytes 4194304 | tf_op jit(solution)/shard_map/all_to_all | solution.py:43
  21.2 102.7 %all-gather.3.cloned.1.call-start = ((), (), s32[]{:S(2)}) async-start(), calls=%async_computation.4 | async-start | bytes 5505024 | tf_op jit(solution)/shard_map/all_gather | solution.py:312
  35.0 15.8 %collective-permute-start.1 = (bf16[4096,128]{1,0:T(8,128)(2,1)}, bf16[4096,128]{1,0:T(8,128)(2,1)}, u32[]{:S(2)}, u32[]{:S(2)}) collective-permute-start(bf16[4096,128]{1,0:T(8,128)(2,1)} %collective-permute-done.c_ref), channel_id=1, source_target_pairs={{0,1},{1,0},{2,3},{3,2},{4,5},{5,4},{6,7},{7,6},{8,9},{9,8},{10,11... | collective-permute-start | bytes 3145736 | tf_op jit(solution)/shard_map/ppermute | solution.py:39
  36.3 14.6 %collective-permute-start.2 = (bf16[4096,128]{1,0:T(8,128)(2,1)S(1)}, bf16[4096,128]{1,0:T(8,128)(2,1)}, u32[]{:S(2)}, u32[]{:S(2)}) collective-permute-start(bf16[4096,128]{1,0:T(8,128)(2,1)S(1)} %copy-done.3), channel_id=1, source_target_pairs={{0,1},{1,0},{2,3},{3,2},{4,5},{5,4},{6,7},{7,6},{8,9},{9,8},{10,11... | collective-permute-start | bytes 3145736 | tf_op jit(solution)/shard_map/ppermute | solution.py:39
  53.8 6.9 %collective-permute-start.4 = (bf16[256,512]{1,0:T(8,128)(2,1)S(1)}, bf16[256,512]{1,0:T(8,128)(2,1)}, u32[]{:S(2)}, u32[]{:S(2)}) collective-permute-start(bf16[256,512]{1,0:T(8,128)(2,1)S(1)} %shard_map.42.own_ref.e_ref), channel_id=1, source_target_pairs={{0,8},{1,9},{2,10},{3,11},{4,12},{5,13},{6,14},{7,15},{8,0},{9,1},... | collective-permute-start | bytes 786440 | tf_op jit(solution)/shard_map/ppermute | solution.py:39
  55.4 1.2 copy-start.2
  60.8 4.8 %collective-permute-start.3 = (bf16[256,512]{1,0:T(8,128)(2,1)S(1)}, bf16[256,512]{1,0:T(8,128)(2,1)S(1)}, u32[]{:S(2)}, u32[]{:S(2)}) collective-permute-start(bf16[256,512]{1,0:T(8,128)(2,1)S(1)} %shard_map.42.own_ref.e_ref), channel_id=1, source_target_pairs={{0,1},{1,0},{2,3},{3,2},{4,5},{5,4},{6,7},{7,6},{8,9},{9,8},{10,11... | collective-permute-start | bytes 786440 | tf_op jit(solution)/shard_map/ppermute | solution.py:39
  64.4 1.7 collective-permute-start.5
  68.8 15.4 %all-to-all-start.1 = ((bf16[16,16,1024]{2,1,0:T(8,128)(2,1)}), bf16[16,16,1024]{2,1,0:T(8,128)(2,1)S(1)}, u32[]{:S(2)}, u32[]{:S(2)}) async-start(bf16[16,16,1024]{2,1,0:T(8,128)(2,1)} %bitcast), calls=%async_computation.1 | async-start | bytes 1048576 | tf_op jit(solution)/shard_map/all_to_all | solution.py:43
  73.4 13.5 %collective-permute-start.6 = (bf16[256,512]{1,0:T(8,128)(2,1)S(1)}, bf16[256,512]{1,0:T(8,128)(2,1)}, u32[]{:S(2)}, u32[]{:S(2)}) collective-permute-start(bf16[256,512]{1,0:T(8,128)(2,1)S(1)} %shard_map.42.own_ref.e_ref), channel_id=1, source_target_pairs={{0,64},{1,65},{2,66},{3,67},{4,68},{5,69},{6,70},{7,71},{8,72},{9,... | collective-permute-start | bytes 786440 | tf_op jit(solution)/shard_map/ppermute | solution.py:39
  104.3 10.3 %collective-permute-start.7 = (bf16[224,128]{1,0:T(8,128)(2,1)S(1)}, bf16[224,128]{1,0:T(8,128)(2,1)S(1)}, u32[]{:S(2)}, u32[]{:S(2)}) collective-permute-start(bf16[224,128]{1,0:T(8,128)(2,1)S(1)} %get-tuple-element.31), channel_id=1, source_target_pairs={{0,1},{1,0},{2,3},{3,2},{4,5},{5,4},{6,7},{7,6},{8,9},{9,8},{10,11... | collective-permute-start | bytes 172040 | tf_op jit(solution)/shard_map/ppermute | solution.py:39
  107.5 7.1 %collective-permute-start.8 = (bf16[224,128]{1,0:T(8,128)(2,1)S(1)}, bf16[224,128]{1,0:T(8,128)(2,1)S(1)}, u32[]{:S(2)}, u32[]{:S(2)}) collective-permute-start(bf16[224,128]{1,0:T(8,128)(2,1)S(1)} %get-tuple-element.32), channel_id=1, source_target_pairs={{0,8},{1,9},{2,10},{3,11},{4,12},{5,13},{6,14},{7,15},{8,0},{9,1},... | collective-permute-start | bytes 172040 | tf_op jit(solution)/shard_map/ppermute | solution.py:39
  107.5 9.6 %collective-permute-start.9 = (bf16[224,128]{1,0:T(8,128)(2,1)S(1)}, bf16[224,128]{1,0:T(8,128)(2,1)S(1)}, u32[]{:S(2)}, u32[]{:S(2)}) collective-permute-start(bf16[224,128]{1,0:T(8,128)(2,1)S(1)} %get-tuple-element.33), channel_id=1, source_target_pairs={{0,9},{1,8},{2,11},{3,10},{4,13},{5,12},{6,15},{7,14},{8,1},{9,0},... | collective-permute-start | bytes 172040 | tf_op jit(solution)/shard_map/ppermute | solution.py:39
  123.9 7.1 %collective-permute-start.10 = (bf16[2,224,4096]{2,1,0:T(8,128)(2,1)}, bf16[2,224,4096]{2,1,0:T(8,128)(2,1)}, u32[]{:S(2)}, u32[]{:S(2)}) collective-permute-start(bf16[2,224,4096]{2,1,0:T(8,128)(2,1)} %bitcast.6), channel_id=1, source_target_pairs={{0,1},{1,0},{2,3},{3,2},{4,5},{5,4},{6,7},{7,6},{8,9},{9,8},{10,11... | collective-permute-start | bytes 11010056 | tf_op jit(solution)/shard_map/ppermute | solution.py:39
  124.3 39.9 %all-to-all-start.3 = ((bf16[16,4,16,1024]{3,2,1,0:T(8,128)(2,1)}), bf16[16,4,16,1024]{3,2,1,0:T(8,128)(2,1)S(1)}, u32[]{:S(2)}, u32[]{:S(2)}) async-start(bf16[16,4,16,1024]{3,2,1,0:T(8,128)(2,1)} %shard_map.47), calls=%async_computation.3 | async-start | bytes 4194304 | tf_op jit(solution)/shard_map/all_to_all | solution.py:43
  131.0 2.0 %copy-start = (bf16[448,4096]{1,0:T(8,128)(2,1)S(1)}, bf16[448,4096]{1,0:T(8,128)(2,1)}, u32[]{:S(2)}) copy-start(bf16[448,4096]{1,0:T(8,128)(2,1)} %all-gather.3.cloned.1.call-done) | copy-start | bytes 11010052
  135.8 29.9 %collective-permute-start.11 = (bf16[2048,128]{1,0:T(8,128)(2,1)S(1)}, bf16[2048,128]{1,0:T(8,128)(2,1)}, u32[]{:S(2)}, u32[]{:S(2)}) collective-permute-start(bf16[2048,128]{1,0:T(8,128)(2,1)S(1)} %shard_map.49), channel_id=1, source_target_pairs={{0,64},{1,65},{2,66},{3,67},{4,68},{5,69},{6,70},{7,71},{8,72},{9,... | collective-permute-start | bytes 1572872 | tf_op jit(solution)/shard_map/ppermute | solution.py:39
  138.6 28.2 %collective-permute-start.12 = (bf16[2048,128]{1,0:T(8,128)(2,1)S(1)}, bf16[2048,128]{1,0:T(8,128)(2,1)}, u32[]{:S(2)}, u32[]{:S(2)}) collective-permute-start(bf16[2048,128]{1,0:T(8,128)(2,1)S(1)} %shard_map.50), channel_id=1, source_target_pairs={{0,64},{1,65},{2,66},{3,67},{4,68},{5,69},{6,70},{7,71},{8,72},{9,... | collective-permute-start | bytes 1572872 | tf_op jit(solution)/shard_map/ppermute | solution.py:39
Sparse Core Ops, SparseCore 0:
  60.9 62.9 all-gather.2

commit v10 on v9

--- a/solution.py
+++ b/solution.py
@@ -1,4 +1,5 @@
 import functools
+import math
 
 import jax
 import jax.numpy as jnp
@@ -10,7 +11,7 @@
 YS, ZS, XS, CS = 4, 2, 4, 2
 DP = YS * ZS * XS * CS
 PAD = 16
-TILE = 1024
+TILE = 512
 VMEM = 24 * 1024 * 1024
 
 
@@ -94,18 +95,23 @@
     return blocks[0] if len(blocks) == 1 else jnp.concatenate(blocks, axis=1)
 
 
-def compact_kernel(rows, x_ref, o_ref):
-    o_ref[...] = without_padding(joined(x_ref), rows)
-
-
-def compact(plane, rows):
-    peers, blocks, _, tile = plane.shape
+def compact_kernel(rows, x_ref, *o_refs):
+    at = 0
+    for ref in o_refs:
+        blocks = ref.shape[1] // TILE
+        ref[...] = without_padding(joined(x_ref.at[:, at : at + blocks]), rows)
+        at += blocks
+
+
+def compact(plane, rows, widths):
+    peers = plane.shape[0]
+    out = tuple(shape((peers * rows, width)) for width in widths)
     return pl.pallas_call(
         functools.partial(compact_kernel, rows),
-        grid=(blocks // 2,),
-        in_specs=[columns(plane, 2)],
-        out_specs=pl.BlockSpec((peers * rows, 2 * tile), lambda k: (0, k)),
-        out_shape=shape((peers * rows, blocks * tile)),
+        grid=(1,),
+        in_specs=[whole(*plane.shape)],
+        out_specs=tuple(whole(*each.shape) for each in out),
+        out_shape=out,
         compiler_params=params(1),
         cost_estimate=cost(4 * plane.size, 4 * plane.size),
     )(plane)
@@ -192,17 +198,21 @@
         o_ref[:, k] = out[:, tile * k : tile * k + tile].reshape(peers, rows, tile)
 
 
-def weight_kernel(z_ref, own_ref, sib_ref, *refs):
-    near, near_sib, far, far_sib, o_ref = refs
-    n = own_ref.shape[1]
-    h = [ref[i] for ref in (own_ref, sib_ref) for i in range(2)]
-    first = z_ref[0] == 0
-    g = []
-    for a, b in ((near[...], far[...]), (near_sib[...], far_sib[...])):
-        g += [jnp.where(first, a, b), jnp.where(first, b, a)]
-    o_ref[...] = matmul(jnp.concatenate(h, axis=0), jnp.concatenate(g, axis=0), 0, 0).astype(
-        o_ref.dtype
-    )
+def weight_kernel(*refs):
+    hs, gs, (o_ref,) = refs[:4], refs[4:8], refs[8:]
+    h = jnp.concatenate([ref[...] for ref in hs], axis=0)
+    g = jnp.concatenate([ref[...] for ref in gs], axis=0)
+    o_ref[...] = matmul(h, g, 0, 0).astype(o_ref.dtype)
+
+
+def ends_kernel(scale, *refs):
+    pairs, (o_ref,) = refs[:-1], refs[-1:]
+    at = 0
+    for a_ref, b_ref in zip(pairs[::2], pairs[1::2]):
+        n = a_ref.shape[0]
+        total = a_ref[...].astype(jnp.float32) + b_ref[...].astype(jnp.float32)
+        o_ref[at : at + n, :] = total / scale
+        at += n
 
 
 def rows_kernel(x_ref, o_ref):
@@ -228,9 +238,9 @@
     rows = plane.size // width
     return pl.pallas_call(
         embed_kernel,
-        grid=(width // TILE // 2,),
-        in_specs=[columns(plane, 2)]
-        + [pl.BlockSpec((2 * TILE, units), lambda k: (k, 0))] * 4,
+        grid=(width // TILE // 4,),
+        in_specs=[columns(plane, 4)]
+        + [pl.BlockSpec((4 * TILE, units), lambda k: (k, 0))] * 4,
         out_specs=whole(rows, 4 * units),
         out_shape=shape((rows, 4 * units)),
         scratch_shapes=[pltpu.VMEM((rows, 4 * units), jnp.float32)],
@@ -245,10 +255,10 @@
     out = shape((rows // PAD, width // TILE, PAD, TILE))
     return pl.pallas_call(
         hidden_kernel,
-        grid=(width // TILE // 2,),
+        grid=(width // TILE // 4,),
         in_specs=[whole(*grad.shape)]
-        + [pl.BlockSpec((2 * TILE, units), lambda k: (k, 0))] * 4,
-        out_specs=columns(out, 2),
+        + [pl.BlockSpec((4 * TILE, units), lambda k: (k, 0))] * 4,
+        out_specs=columns(out, 4),
         out_shape=out,
         compiler_params=params(1),
         cost_estimate=cost(8 * rows * width * units, 2 * width * (rows + 4 * units)),
@@ -268,25 +278,34 @@
     )(pieces)
 
 
-def weight_terms(z, both, both_sib, part, grads):
-    _, rows, width = both.shape
+def weight_terms(parts, grads):
+    rows, width = parts[0].shape
     units = grads[0].shape[1]
-    tile, count = width // 4, 2
-    block = pl.BlockSpec((2, rows, tile), lambda k: (0, 0, k + count * part))
     return pl.pallas_call(
         weight_kernel,
-        grid=(count,),
-        in_specs=[pl.BlockSpec(memory_space=pltpu.SMEM), block, block]
+        grid=(width // TILE,),
+        in_specs=[pl.BlockSpec((rows, TILE), lambda k: (0, k))] * 4
         + [whole(*g.shape) for g in grads],
-        out_specs=pl.BlockSpec((tile, units), lambda k: (k, 0)),
-        out_shape=shape((width // 2, units)),
-        compiler_params=params(1),
-        cost_estimate=cost(4 * rows * width * units, 4 * rows * width),
-    )(z, both, both_sib, *grads)
-
-
-def wide_sum(a, b):
-    return a.astype(jnp.float32) + b.astype(jnp.float32)
+        out_specs=pl.BlockSpec((TILE, units), lambda k: (k, 0)),
+        out_shape=shape((width, units)),
+        compiler_params=params(1),
+        cost_estimate=cost(8 * rows * width * units, 8 * rows * width),
+    )(*parts, *grads)
+
+
+def view_sums(parts, samples):
+    arrays = [each for part in parts for each in (part, swap(part, view=1))]
+    total = sum(part.shape[0] for part in parts)
+    units = parts[0].shape[1]
+    return pl.pallas_call(
+        functools.partial(ends_kernel, math.sqrt(2.0 * samples)),
+        grid=(1,),
+        in_specs=[whole(*each.shape) for each in arrays],
+        out_specs=whole(total, units),
+        out_shape=shape((total, units), jnp.float32),
+        compiler_params=params(1),
+        cost_estimate=cost(total * units, 8 * total * units),
+    )(*arrays)
 
 
 def on_device(hidden, weight):
@@ -308,10 +327,12 @@
     mine = embed(plane, weights)
     from_sib = swap(mine, c=1)
     from_far = swap(mine, z=1)
-    from_far, packed = lax.optimization_barrier((from_far, compact(plane, rows)))
-    both = lax.all_gather(packed, "dp", axis_index_groups=groups("z"))
+    split = (3 * width // 8, 5 * width // 8)
+    from_far, *h_own = lax.optimization_barrier((from_far, *compact(plane, rows, split)))
     from_far_sib = swap(from_far, c=1)
     partner = swap(mine, view=1)
+    first, partner = lax.optimization_barrier((h_own[0], partner))
+    h_far = [swap(first, z=1), swap(h_own[1], z=1)]
 
     centered, factor, gram = pl.pallas_call(
         functools.partial(center_kernel, rows, samples),
@@ -337,7 +358,8 @@
         compiler_params=params(1),
         cost_estimate=cost(gram.size, 4 * gram.size),
     )(gram)
-    gram, partner = lax.optimization_barrier((gram, partner))
+    gram, h_far[0], *late = lax.optimization_barrier((gram, h_far[0], *h_own))
+    h_sib = [swap(block, c=1) for block in late]
     gram = exchange(gram, "yx")
 
     grad, *runs = pl.pallas_call(
@@ -361,17 +383,17 @@
     g_far_sib = swap(runs[3], z=1, c=1)
     g_sib = swap(runs[1], c=1)
     h_part = hidden_terms(grad, weights)
-    h_part, both, *grads = lax.optimization_barrier(
-        (h_part, both, runs[0], g_sib, g_far, g_far_sib)
+    h_part, h_far[1], *grads = lax.optimization_barrier(
+        (h_part, h_far[1], runs[0], g_sib, g_far, g_far_sib)
     )
-
-    grad_rows = hidden_rows(exchange(h_part, "yx"), rows)
-
-    both_sib = swap(both, c=1)
-    z = (lax.axis_index("dp") // (XS * CS) % ZS).astype(jnp.int32).reshape(1)
-    parts = [weight_terms(z, both, both_sib, part, grads) for part in (0, 1)]
-    runs = [wide_sum(part, swap(part, view=1)) for part in parts]
-    grad_weight = jnp.concatenate(runs, axis=0) / jnp.sqrt(2.0 * samples)
+    pieces = exchange(h_part, "yx")
+
+    parts = [
+        weight_terms((own, sib, far, swap(far, c=1)), grads)
+        for own, sib, far in zip(h_own, h_sib, h_far)
+    ]
+    grad_weight, pieces = lax.optimization_barrier((view_sums(parts, samples), pieces))
+    grad_rows = hidden_rows(pieces, rows)
     return (grad_rows, grad_weight)
 
 

time: 177 us -> 148 us (0.84)
  waiting for transfers between devices: 81 us -> 57.6 us
  between operations: 14.2 us -> 0.81 us
  blocking collectives: 15.7 us -> 26.1 us
  starting transfers between devices: 36.8 us -> 42.3 us
  other arithmetic: 3.79 us -> 0 us
  Pallas kernels: 18.4 us -> 15.9 us
  local copies, waits for them, and re-layouts: 6.41 us -> 4.43 us
    all_to_all x3 -> x2, waiting for transfers between devices: 49.3 us -> 14.6 us  [exchange(): lax.all_to_all(blocks, 'dp', 0, 0, tiled=True, axis_index_groups=groups(a...]
    ppermute x13 -> x18, waiting for transfers between devices: 24.8 us -> 43 us  [swap(): return lax.ppermute(block, ('view', 'dp'), route)]
    ppermute x13 -> x18, starting transfers between devices: 18.6 us -> 31.1 us  [swap(): return lax.ppermute(block, ('view', 'dp'), route)]
    all_to_all x1 -> x2, blocking collectives: 15.7 us -> 26.1 us  [exchange(): lax.all_to_all(blocks, 'dp', 0, 0, tiled=True, axis_index_groups=groups(a...]
    all_to_all x3 -> x2, starting transfers between devices: 18.1 us -> 11.2 us  [exchange(): lax.all_to_all(blocks, 'dp', 0, 0, tiled=True, axis_index_groups=groups(a...]
    all_gather x1 -> x0, waiting for transfers between devices: 6.85 us -> none  [on_device(): both = lax.all_gather(packed, 'dp', axis_index_groups=groups('z'))]
    add x2 -> x0, other arithmetic: 2.29 us -> none  [wide_sum(): return a.astype(jnp.float32) + b.astype(jnp.float32)]
    unnamed x11 -> x23, local copies, waits for them, and re-layouts: 6.41 us -> 4.43 us
  transfers between devices with their start and end apart: 17 -> 20, of which waited for: 10 -> 7; matrix products, arithmetic and copies ran while one was open for 1% -> 0% of each run, Pallas kernels for 9% -> 8%
where the time goes in v10:
time: 148 us; the launch traced here: 147 us
  waiting for transfers between devices  57.6 us (39%)
  starting transfers between devices  42.3 us (29%)
  blocking collectives  26.1 us (18%)
  Pallas kernels  15.9 us (11%)
  local copies, waits for them, and re-layouts  4.43 us (3%)
    ppermute x18, waiting for transfers between devices, swap(): return lax.ppermute(block, ('view', 'dp'), route)  43 us
    ppermute x18, starting transfers between devices, swap(): return lax.ppermute(block, ('view', 'dp'), route)  31.1 us
    all_to_all x2, blocking collectives, exchange(): lax.all_to_all(blocks, 'dp', 0, 0, tiled=True, axis_index_groups=groups(a...  26.1 us
    all_to_all x2, waiting for transfers between devices, exchange(): lax.all_to_all(blocks, 'dp', 0, 0, tiled=True, axis_index_groups=groups(a...  14.6 us
    all_to_all x2, starting transfers between devices, exchange(): lax.all_to_all(blocks, 'dp', 0, 0, tiled=True, axis_index_groups=groups(a...  11.2 us
    unnamed x23, local copies, waits for them, and re-layouts  4.43 us
    pallas_call x2, Pallas kernels, weight_terms(): pl.pallas_call(weight_kernel, grid=(width // TILE,), in_specs=[pl.BlockSp...  4.33 us
    pallas_call x1, Pallas kernels, hidden_terms(): pl.pallas_call(hidden_kernel, grid=(width // TILE // 4,), in_specs=[whole...  3.87 us
  transfers between devices with their start and end apart: 20, of which 7 were waited for; matrix products, arithmetic and copies ran while one was open for 0% of the time, Pallas kernels for 8%

profile of v10, /device:TPU:1, one launch (start us, length us, event | category | flops | bytes accessed | tf_op | source)
XLA Modules:
  0.0 147.1 jit_solution(372251250199289892)
XLA Ops:
  0.6 4.7 %collective-permute-start = (bf16[4096,128]{1,0:T(8,128)(2,1)}, bf16[4096,128]{1,0:T(8,128)(2,1)}, u32[]{:S(2)}, u32[]{:S(2)}) collective-permute-start(bf16[4096,128]{1,0:T(8,128)(2,1)} %a_ref.3), channel_id=1, source_target_pairs={{0,72},{1,73},{2,74},{3,75},{4,76},{5,77},{6,78},{7,79},{8,64},{9,... | collective-permute-start | bytes 3145736 | tf_op jit(solution)/shard_map/ppermute | solution.py:40
  5.3 0.9 copy-done.10
  6.2 0.2 shard_map.41
  6.4 0.0 copy-start
  6.4 1.3 copy-done
  7.7 6.9 %all-to-all-start = ((bf16[16,8,16,512]{3,2,1,0:T(8,128)(2,1)}), bf16[16,8,16,512]{3,2,1,0:T(8,128)(2,1)S(1)}, u32[]{:S(2)}, u32[]{:S(2)}) async-start(bf16[16,8,16,512]{3,2,1,0:T(8,128)(2,1)} %copy-done), calls=%async_computation | async-start | bytes 4194304 | tf_op jit(solution)/shard_map/all_to_all | solution.py:44
  14.6 13.9 %collective-permute-done.c_ref = bf16[4096,128]{1,0:T(8,128)(2,1)} collective-permute-done((bf16[4096,128]{1,0:T(8,128)(2,1)}, bf16[4096,128]{1,0:T(8,128)(2,1)}, u32[]{:S(2)}, u32[]{:S(2)}) %collective-permute-start) | collective-permute-done | bytes 1048608 | tf_op jit(solution)/shard_map/ppermute | solution.py:40
  28.5 1.2 collective-permute-start.1
  29.7 0.0 collective-permute-start.2
  29.7 14.6 %all-to-all-done.h_ref.x_ref = bf16[16,8,16,512]{3,2,1,0:T(8,128)(2,1)S(1)} async-done(((bf16[16,8,16,512]{3,2,1,0:T(8,128)(2,1)}), bf16[16,8,16,512]{3,2,1,0:T(8,128)(2,1)S(1)}, u32[]{:S(2)}, u32[]{:S(2)}) %all-to-all-start) | async-done | bytes 2097184 | tf_op jit(solution)/shard_map/all_to_all | solution.py:44
  44.3 0.0 collective-permute-done.1.d_ref
  44.3 0.0 collective-permute-done.2.b_ref
  44.3 2.9 %shard_map.42.own_ref.e_ref = bf16[256,512]{1,0:T(8,128)(2,1)S(1)} custom-call(bf16[16,8,16,512]{3,2,1,0:T(8,128)(2,1)S(1)} %all-to-all-done.h_ref.x_ref, bf16[4096,128]{1,0:T(8,128)(2,1)S(1)} %copy-done.1, bf16[4096,128]{1,0:T(8,128)(2,1)} %collective-permute-done.2.b_ref, bf16[4096,128]{1,0:T(8,128)(2,1)} %collective-permute-done.c_ref, ...), custom_call_target="tpu_custom_call" | custom-call | flops 1073741824 | bytes 6291456 | tf_op jit(solution)/shard_map/pallas_call | solution.py:239
  47.3 0.5 collective-permute-start.3
  47.7 1.0 collective-permute-start.6
  48.7 2.7 %collective-permute-start.4 = (bf16[256,512]{1,0:T(8,128)(2,1)S(1)}, bf16[256,512]{1,0:T(8,128)(2,1)S(1)}, u32[]{:S(2)}, u32[]{:S(2)}) collective-permute-start(bf16[256,512]{1,0:T(8,128)(2,1)S(1)} %shard_map.42.own_ref.e_ref), channel_id=1, source_target_pairs={{0,1},{1,0},{2,3},{3,2},{4,5},{5,4},{6,7},{7,6},{8,9},{9,8},{10,11... | collective-permute-start | bytes 786440 | tf_op jit(solution)/shard_map/ppermute | solution.py:40
  51.4 0.6 shard_map.43
  52.1 0.0 copy-start.2
  52.1 2.0 %collective-permute-done.3.far_ref = bf16[256,512]{1,0:T(8,128)(2,1)S(1)} collective-permute-done((bf16[256,512]{1,0:T(8,128)(2,1)S(1)}, bf16[256,512]{1,0:T(8,128)(2,1)S(1)}, u32[]{:S(2)}, u32[]{:S(2)}) %collective-permute-start.3) | collective-permute-done | bytes 262176 | tf_op jit(solution)/shard_map/ppermute | solution.py:40
  54.1 6.3 %collective-permute-start.5 = (bf16[256,512]{1,0:T(8,128)(2,1)S(1)}, bf16[256,512]{1,0:T(8,128)(2,1)S(1)}, u32[]{:S(2)}, u32[]{:S(2)}) collective-permute-start(bf16[256,512]{1,0:T(8,128)(2,1)S(1)} %collective-permute-done.3.far_ref), channel_id=1, source_target_pairs={{0,1},{1,0},{2,3},{3,2},{4,5},{5,4},{6,7},{7,6},{8,9},{9,8},{10,11... | collective-permute-start | bytes 786440 | tf_op jit(solution)/shard_map/ppermute | solution.py:40
  60.4 0.3 collective-permute-start.7
  60.7 2.7 %collective-permute-start.10 = (bf16[224,2560]{1,0:T(8,128)(2,1)S(1)}, bf16[224,2560]{1,0:T(8,128)(2,1)S(1)}, u32[]{:S(2)}, u32[]{:S(2)}) collective-permute-start(bf16[224,2560]{1,0:T(8,128)(2,1)S(1)} %get-tuple-element.53.refs_0_), channel_id=1, source_target_pairs={{0,8},{1,9},{2,10},{3,11},{4,12},{5,13},{6,14},{7,15},{8,0},{9,1},... | collective-permute-start | bytes 3440648 | tf_op jit(solution)/shard_map/ppermute | solution.py:40
  63.4 0.9 shard_map.44
  64.3 13.4 %all_to_all.32 = bf16[16,16,1024]{2,1,0:T(8,128)(2,1)S(1)} all-to-all(bf16[16,16,1024]{2,1,0:T(8,128)(2,1)S(1)} %bitcast.7), channel_id=1, replica_groups={{0,2,4,6,16,18,20,22,32,34,36,38,48,50,52,54},{1,3,5,7,17,19,21,23,33,3..., dimensions={0} | all-to-all | bytes 1048576 | tf_op jit(solution)/shard_map/all_to_all | solution.py:44
  77.7 0.1 shard_map.45
  77.8 12.7 %all_to_all.33 = bf16[16,16,1024]{2,1,0:T(8,128)(2,1)S(1)} all-to-all(bf16[16,16,1024]{2,1,0:T(8,128)(2,1)S(1)} %bitcast.4), channel_id=1, replica_groups={{0,2,4,6,16,18,20,22,32,34,36,38,48,50,52,54},{1,3,5,7,17,19,21,23,33,3..., dimensions={0} | all-to-all | bytes 1048576 | tf_op jit(solution)/shard_map/all_to_all | solution.py:44
  90.6 0.7 shard_map.46
  91.2 5.5 %collective-permute-start.11 = (bf16[224,128]{1,0:T(8,128)(2,1)S(1)}, bf16[224,128]{1,0:T(8,128)(2,1)S(1)}, u32[]{:S(2)}, u32[]{:S(2)}) collective-permute-start(bf16[224,128]{1,0:T(8,128)(2,1)S(1)} %get-tuple-element.46), channel_id=1, source_target_pairs={{0,1},{1,0},{2,3},{3,2},{4,5},{5,4},{6,7},{7,6},{8,9},{9,8},{10,11... | collective-permute-start | bytes 172040 | tf_op jit(solution)/shard_map/ppermute | solution.py:40
  96.8 2.2 %collective-permute-start.12 = (bf16[224,128]{1,0:T(8,128)(2,1)S(1)}, bf16[224,128]{1,0:T(8,128)(2,1)S(1)}, u32[]{:S(2)}, u32[]{:S(2)}) collective-permute-start(bf16[224,128]{1,0:T(8,128)(2,1)S(1)} %get-tuple-element.47), channel_id=1, source_target_pairs={{0,8},{1,9},{2,10},{3,11},{4,12},{5,13},{6,14},{7,15},{8,0},{9,1},... | collective-permute-start | bytes 172040 | tf_op jit(solution)/shard_map/ppermute | solution.py:40
  98.9 1.1 collective-permute-start.13
  100.0 3.9 %shard_map.47 = bf16[16,8,16,512]{3,2,1,0:T(8,128)(2,1)} custom-call(bf16[256,512]{1,0:T(8,128)(2,1)S(1)} %get-tuple-element.44.g_ref, bf16[4096,128]{1,0:T(8,128)(2,1)S(1)} %copy-done.1, bf16[4096,128]{1,0:T(8,128)(2,1)} %collective-permute-done.2.b_ref, bf16[4096,128]{1,0:T(8,128)(2,1)} %collective-permute-done.c_ref, ...), custom_call_target="tpu_custom_call" | custom-call | flops 1073741824 | bytes 6291456 | tf_op jit(solution)/shard_map/pallas_call | solution.py:256
  103.9 2.2 %collective-permute-done.13.refs_7_ = bf16[224,128]{1,0:T(8,128)(2,1)S(1)} collective-permute-done((bf16[224,128]{1,0:T(8,128)(2,1)S(1)}, bf16[224,128]{1,0:T(8,128)(2,1)S(1)}, u32[]{:S(2)}, u32[]{:S(2)}) %collective-permute-start.13) | collective-permute-done | bytes 57376 | tf_op jit(solution)/shard_map/ppermute | solution.py:40
  106.1 4.3 %all-to-all-start.3 = ((bf16[16,8,16,512]{3,2,1,0:T(8,128)(2,1)}), bf16[16,8,16,512]{3,2,1,0:T(8,128)(2,1)S(1)}, u32[]{:S(2)}, u32[]{:S(2)}) async-start(bf16[16,8,16,512]{3,2,1,0:T(8,128)(2,1)} %shard_map.47), calls=%async_computation.3 | async-start | bytes 4194304 | tf_op jit(solution)/shard_map/all_to_all | solution.py:44
  110.4 0.8 collective-permute-start.15
  111.3 0.1 collective-permute-start.16
  111.4 0.4 collective-permute-start.8
  111.8 0.1 collective-permute-start.9
  111.9 2.5 %collective-permute-done.15.refs_1_ = bf16[224,2560]{1,0:T(8,128)(2,1)S(1)} collective-permute-done((bf16[224,2560]{1,0:T(8,128)(2,1)S(1)}, bf16[224,2560]{1,0:T(8,128)(2,1)S(1)}, u32[]{:S(2)}, u32[]{:S(2)}) %collective-permute-start.15) | collective-permute-done | bytes 1146912 | tf_op jit(solution)/shard_map/ppermute | solution.py:40
  114.4 1.1 collective-permute-done.16.refs_3_
  115.5 1.3 copy-done.5
  116.8 2.7 %shard_map.49.refs_2_ = bf16[2560,128]{1,0:T(8,128)(2,1)S(1)} custom-call(bf16[224,2560]{1,0:T(8,128)(2,1)S(1)} %copy-done.3, bf16[224,2560]{1,0:T(8,128)(2,1)S(1)} %collective-permute-done.15.refs_1_, bf16[224,2560]{1,0:T(8,128)(2,1)S(1)} %copy-done.5, bf16[224,2560]{1,0:T(8,128)(2,1)S(1)} %collective-permute-done.16.refs_3_, ...), custom_call_target="tpu_custom_call" | custom-call | flops 587202560 | bytes 4587520 | tf_op jit(solution)/shard_map/pallas_call | solution.py:284
  119.5 0.6 collective-permute-start.17
  120.1 1.6 %shard_map.48.refs_0_ = bf16[1536,128]{1,0:T(8,128)(2,1)S(1)} custom-call(bf16[224,1536]{1,0:T(8,128)(2,1)S(1)} %copy-done.7, bf16[224,1536]{1,0:T(8,128)(2,1)S(1)} %collective-permute-done.8.refs_1_, bf16[224,1536]{1,0:T(8,128)(2,1)S(1)} %copy-done.9, bf16[224,1536]{1,0:T(8,128)(2,1)S(1)} %collective-permute-done.9.refs_3_, ...), custom_call_target="tpu_custom_call" | custom-call | flops 352321536 | bytes 2752512 | tf_op jit(solution)/shard_map/pallas_call | solution.py:284
  121.8 1.0 collective-permute-start.14
  122.8 21.2 %collective-permute-done.14.refs_1_ = bf16[1536,128]{1,0:T(8,128)(2,1)S(1)} collective-permute-done((bf16[1536,128]{1,0:T(8,128)(2,1)S(1)}, bf16[1536,128]{1,0:T(8,128)(2,1)S(1)}, u32[]{:S(2)}, u32[]{:S(2)}) %collective-permute-start.14) | collective-permute-done | bytes 393248 | tf_op jit(solution)/shard_map/ppermute | solution.py:40
  144.0 1.6 %shard_map.50 = f32[4096,128]{1,0:T(8,128)} custom-call(bf16[1536,128]{1,0:T(8,128)(2,1)S(1)} %shard_map.48.refs_0_, bf16[1536,128]{1,0:T(8,128)(2,1)S(1)} %collective-permute-done.14.refs_1_, bf16[2560,128]{1,0:T(8,128)(2,1)S(1)} %shard_map.49.refs_2_, bf16[2560,128]{1,0:T(8,128)(2,1)S(1)} %collective-permute-done.17.refs_3_), custom_call_target="tpu_custom_call" | custom-call | flops 524288 | bytes 4194304 | tf_op jit(solution)/shard_map/pallas_call | solution.py:300
  145.6 0.6 shard_map.51
  146.2 0.9 copy.4
  (28 shorter events, 0.1 us)
Async XLA Ops:
  0.6 27.9 %collective-permute-start = (bf16[4096,128]{1,0:T(8,128)(2,1)}, bf16[4096,128]{1,0:T(8,128)(2,1)}, u32[]{:S(2)}, u32[]{:S(2)}) collective-permute-start(bf16[4096,128]{1,0:T(8,128)(2,1)} %a_ref.3), channel_id=1, source_target_pairs={{0,72},{1,73},{2,74},{3,75},{4,76},{5,77},{6,78},{7,79},{8,64},{9,... | collective-permute-start | bytes 3145736 | tf_op jit(solution)/shard_map/ppermute | solution.py:40
  5.3 0.9 copy-start.10
  6.4 1.3 copy-start
  7.7 22.0 %copy-start.1 = (bf16[4096,128]{1,0:T(8,128)(2,1)S(1)}, bf16[4096,128]{1,0:T(8,128)(2,1)}, u32[]{:S(2)}) copy-start(bf16[4096,128]{1,0:T(8,128)(2,1)} %a_ref.3) | copy-start | bytes 3145732
  7.7 36.6 %all-to-all-start = ((bf16[16,8,16,512]{3,2,1,0:T(8,128)(2,1)}), bf16[16,8,16,512]{3,2,1,0:T(8,128)(2,1)S(1)}, u32[]{:S(2)}, u32[]{:S(2)}) async-start(bf16[16,8,16,512]{3,2,1,0:T(8,128)(2,1)} %copy-done), calls=%async_computation | async-start | bytes 4194304 | tf_op jit(solution)/shard_map/all_to_all | solution.py:44
  28.5 15.8 %collective-permute-start.1 = (bf16[4096,128]{1,0:T(8,128)(2,1)}, bf16[4096,128]{1,0:T(8,128)(2,1)}, u32[]{:S(2)}, u32[]{:S(2)}) collective-permute-start(bf16[4096,128]{1,0:T(8,128)(2,1)} %collective-permute-done.c_ref), channel_id=1, source_target_pairs={{0,1},{1,0},{2,3},{3,2},{4,5},{5,4},{6,7},{7,6},{8,9},{9,8},{10,11... | collective-permute-start | bytes 3145736 | tf_op jit(solution)/shard_map/ppermute | solution.py:40
  29.7 14.6 %collective-permute-start.2 = (bf16[4096,128]{1,0:T(8,128)(2,1)S(1)}, bf16[4096,128]{1,0:T(8,128)(2,1)}, u32[]{:S(2)}, u32[]{:S(2)}) collective-permute-start(bf16[4096,128]{1,0:T(8,128)(2,1)S(1)} %copy-done.1), channel_id=1, source_target_pairs={{0,1},{1,0},{2,3},{3,2},{4,5},{5,4},{6,7},{7,6},{8,9},{9,8},{10,11... | collective-permute-start | bytes 3145736 | tf_op jit(solution)/shard_map/ppermute | solution.py:40
  47.3 6.8 %collective-permute-start.3 = (bf16[256,512]{1,0:T(8,128)(2,1)S(1)}, bf16[256,512]{1,0:T(8,128)(2,1)S(1)}, u32[]{:S(2)}, u32[]{:S(2)}) collective-permute-start(bf16[256,512]{1,0:T(8,128)(2,1)S(1)} %shard_map.42.own_ref.e_ref), channel_id=1, source_target_pairs={{0,8},{1,9},{2,10},{3,11},{4,12},{5,13},{6,14},{7,15},{8,0},{9,1},... | collective-permute-start | bytes 786440 | tf_op jit(solution)/shard_map/ppermute | solution.py:40
  47.7 12.7 %collective-permute-start.6 = (bf16[256,512]{1,0:T(8,128)(2,1)S(1)}, bf16[256,512]{1,0:T(8,128)(2,1)S(1)}, u32[]{:S(2)}, u32[]{:S(2)}) collective-permute-start(bf16[256,512]{1,0:T(8,128)(2,1)S(1)} %shard_map.42.own_ref.e_ref), channel_id=1, source_target_pairs={{0,64},{1,65},{2,66},{3,67},{4,68},{5,69},{6,70},{7,71},{8,72},{9,... | collective-permute-start | bytes 786440 | tf_op jit(solution)/shard_map/ppermute | solution.py:40
  48.7 14.6 %collective-permute-start.4 = (bf16[256,512]{1,0:T(8,128)(2,1)S(1)}, bf16[256,512]{1,0:T(8,128)(2,1)S(1)}, u32[]{:S(2)}, u32[]{:S(2)}) collective-permute-start(bf16[256,512]{1,0:T(8,128)(2,1)S(1)} %shard_map.42.own_ref.e_ref), channel_id=1, source_target_pairs={{0,1},{1,0},{2,3},{3,2},{4,5},{5,4},{6,7},{7,6},{8,9},{9,8},{10,11... | collective-permute-start | bytes 786440 | tf_op jit(solution)/shard_map/ppermute | solution.py:40
  52.1 38.5 %copy-start.2 = (bf16[224,2560]{1,0:T(8,128)(2,1)}, bf16[224,2560]{1,0:T(8,128)(2,1)S(1)}, u32[]{:S(2)}) copy-start(bf16[224,2560]{1,0:T(8,128)(2,1)S(1)} %get-tuple-element.53.refs_0_) | copy-start | bytes 3440644
  52.1 38.5 %copy-start.6 = (bf16[224,1536]{1,0:T(8,128)(2,1)}, bf16[224,1536]{1,0:T(8,128)(2,1)S(1)}, u32[]{:S(2)}) copy-start(bf16[224,1536]{1,0:T(8,128)(2,1)S(1)} %get-tuple-element.38.refs_0_) | copy-start | bytes 2064388
  54.1 9.3 %collective-permute-start.5 = (bf16[256,512]{1,0:T(8,128)(2,1)S(1)}, bf16[256,512]{1,0:T(8,128)(2,1)S(1)}, u32[]{:S(2)}, u32[]{:S(2)}) collective-permute-start(bf16[256,512]{1,0:T(8,128)(2,1)S(1)} %collective-permute-done.3.far_ref), channel_id=1, source_target_pairs={{0,1},{1,0},{2,3},{3,2},{4,5},{5,4},{6,7},{7,6},{8,9},{9,8},{10,11... | collective-permute-start | bytes 786440 | tf_op jit(solution)/shard_map/ppermute | solution.py:40
  60.4 17.4 %collective-permute-start.7 = (bf16[224,1536]{1,0:T(8,128)(2,1)S(1)}, bf16[224,1536]{1,0:T(8,128)(2,1)S(1)}, u32[]{:S(2)}, u32[]{:S(2)}) collective-permute-start(bf16[224,1536]{1,0:T(8,128)(2,1)S(1)} %get-tuple-element.38.refs_0_), channel_id=1, source_target_pairs={{0,8},{1,9},{2,10},{3,11},{4,12},{5,13},{6,14},{7,15},{8,0},{9,1},... | collective-permute-start | bytes 2064392 | tf_op jit(solution)/shard_map/ppermute | solution.py:40
  60.7 43.1 %collective-permute-start.10 = (bf16[224,2560]{1,0:T(8,128)(2,1)S(1)}, bf16[224,2560]{1,0:T(8,128)(2,1)S(1)}, u32[]{:S(2)}, u32[]{:S(2)}) collective-permute-start(bf16[224,2560]{1,0:T(8,128)(2,1)S(1)} %get-tuple-element.53.refs_0_), channel_id=1, source_target_pairs={{0,8},{1,9},{2,10},{3,11},{4,12},{5,13},{6,14},{7,15},{8,0},{9,1},... | collective-permute-start | bytes 3440648 | tf_op jit(solution)/shard_map/ppermute | solution.py:40
  77.8 13.4 %copy-start.8 = (bf16[224,1536]{1,0:T(8,128)(2,1)}, bf16[224,1536]{1,0:T(8,128)(2,1)S(1)}, u32[]{:S(2)}) copy-start(bf16[224,1536]{1,0:T(8,128)(2,1)S(1)} %collective-permute-done.7.refs_2_) | copy-start | bytes 2064388
  91.2 12.6 %collective-permute-start.11 = (bf16[224,128]{1,0:T(8,128)(2,1)S(1)}, bf16[224,128]{1,0:T(8,128)(2,1)S(1)}, u32[]{:S(2)}, u32[]{:S(2)}) collective-permute-start(bf16[224,128]{1,0:T(8,128)(2,1)S(1)} %get-tuple-element.46), channel_id=1, source_target_pairs={{0,1},{1,0},{2,3},{3,2},{4,5},{5,4},{6,7},{7,6},{8,9},{9,8},{10,11... | collective-permute-start | bytes 172040 | tf_op jit(solution)/shard_map/ppermute | solution.py:40
  96.8 7.1 %collective-permute-start.12 = (bf16[224,128]{1,0:T(8,128)(2,1)S(1)}, bf16[224,128]{1,0:T(8,128)(2,1)S(1)}, u32[]{:S(2)}, u32[]{:S(2)}) collective-permute-start(bf16[224,128]{1,0:T(8,128)(2,1)S(1)} %get-tuple-element.47), channel_id=1, source_target_pairs={{0,8},{1,9},{2,10},{3,11},{4,12},{5,13},{6,14},{7,15},{8,0},{9,1},... | collective-permute-start | bytes 172040 | tf_op jit(solution)/shard_map/ppermute | solution.py:40
  98.9 7.2 %collective-permute-start.13 = (bf16[224,128]{1,0:T(8,128)(2,1)S(1)}, bf16[224,128]{1,0:T(8,128)(2,1)S(1)}, u32[]{:S(2)}, u32[]{:S(2)}) collective-permute-start(bf16[224,128]{1,0:T(8,128)(2,1)S(1)} %get-tuple-element.48), channel_id=1, source_target_pairs={{0,9},{1,8},{2,11},{3,10},{4,13},{5,12},{6,15},{7,14},{8,1},{9,0},... | collective-permute-start | bytes 172040 | tf_op jit(solution)/shard_map/ppermute | solution.py:40
  103.9 2.3 %copy-start.4 = (bf16[224,2560]{1,0:T(8,128)(2,1)}, bf16[224,2560]{1,0:T(8,128)(2,1)S(1)}, u32[]{:S(2)}) copy-start(bf16[224,2560]{1,0:T(8,128)(2,1)S(1)} %collective-permute-done.10.refs_2_) | copy-start | bytes 3440644
  106.1 4.3 %copy-start.3 = (bf16[224,2560]{1,0:T(8,128)(2,1)S(1)}, bf16[224,2560]{1,0:T(8,128)(2,1)}, u32[]{:S(2)}) copy-start(bf16[224,2560]{1,0:T(8,128)(2,1)} %copy-done.2) | copy-start | bytes 3440644
  106.1 39.4 %all-to-all-start.3 = ((bf16[16,8,16,512]{3,2,1,0:T(8,128)(2,1)}), bf16[16,8,16,512]{3,2,1,0:T(8,128)(2,1)S(1)}, u32[]{:S(2)}, u32[]{:S(2)}) async-start(bf16[16,8,16,512]{3,2,1,0:T(8,128)(2,1)} %shard_map.47), calls=%async_computation.3 | async-start | bytes 4194304 | tf_op jit(solution)/shard_map/all_to_all | solution.py:44
  110.4 4.0 %collective-permute-start.15 = (bf16[224,2560]{1,0:T(8,128)(2,1)S(1)}, bf16[224,2560]{1,0:T(8,128)(2,1)S(1)}, u32[]{:S(2)}, u32[]{:S(2)}) collective-permute-start(bf16[224,2560]{1,0:T(8,128)(2,1)S(1)} %copy-done.3), channel_id=1, source_target_pairs={{0,1},{1,0},{2,3},{3,2},{4,5},{5,4},{6,7},{7,6},{8,9},{9,8},{10,11... | collective-permute-start | bytes 3440648 | tf_op jit(solution)/shard_map/ppermute | solution.py:40
  111.3 4.3 %collective-permute-start.16 = (bf16[224,2560]{1,0:T(8,128)(2,1)}, bf16[224,2560]{1,0:T(8,128)(2,1)S(1)}, u32[]{:S(2)}, u32[]{:S(2)}) collective-permute-start(bf16[224,2560]{1,0:T(8,128)(2,1)} %copy-done.4), channel_id=1, source_target_pairs={{0,1},{1,0},{2,3},{3,2},{4,5},{5,4},{6,7},{7,6},{8,9},{9,8},{10,11... | collective-permute-start | bytes 3440648 | tf_op jit(solution)/shard_map/ppermute | solution.py:40
  111.4 8.8 %collective-permute-start.8 = (bf16[224,1536]{1,0:T(8,128)(2,1)}, bf16[224,1536]{1,0:T(8,128)(2,1)S(1)}, u32[]{:S(2)}, u32[]{:S(2)}) collective-permute-start(bf16[224,1536]{1,0:T(8,128)(2,1)} %copy-done.6), channel_id=1, source_target_pairs={{0,1},{1,0},{2,3},{3,2},{4,5},{5,4},{6,7},{7,6},{8,9},{9,8},{10,11... | collective-permute-start | bytes 2064392 | tf_op jit(solution)/shard_map/ppermute | solution.py:40
  111.8 8.4 %collective-permute-start.9 = (bf16[224,1536]{1,0:T(8,128)(2,1)}, bf16[224,1536]{1,0:T(8,128)(2,1)S(1)}, u32[]{:S(2)}, u32[]{:S(2)}) collective-permute-start(bf16[224,1536]{1,0:T(8,128)(2,1)} %copy-done.8), channel_id=1, source_target_pairs={{0,1},{1,0},{2,3},{3,2},{4,5},{5,4},{6,7},{7,6},{8,9},{9,8},{10,11... | collective-permute-start | bytes 2064392 | tf_op jit(solution)/shard_map/ppermute | solution.py:40
  115.5 1.3 copy-start.5
  116.8 3.3 %copy-start.7 = (bf16[224,1536]{1,0:T(8,128)(2,1)S(1)}, bf16[224,1536]{1,0:T(8,128)(2,1)}, u32[]{:S(2)}) copy-start(bf16[224,1536]{1,0:T(8,128)(2,1)} %copy-done.6) | copy-start | bytes 2064388
  116.8 3.3 %copy-start.9 = (bf16[224,1536]{1,0:T(8,128)(2,1)S(1)}, bf16[224,1536]{1,0:T(8,128)(2,1)}, u32[]{:S(2)}) copy-start(bf16[224,1536]{1,0:T(8,128)(2,1)} %copy-done.8) | copy-start | bytes 2064388
  119.5 24.5 %collective-permute-start.17 = (bf16[2560,128]{1,0:T(8,128)(2,1)S(1)}, bf16[2560,128]{1,0:T(8,128)(2,1)S(1)}, u32[]{:S(2)}, u32[]{:S(2)}) collective-permute-start(bf16[2560,128]{1,0:T(8,128)(2,1)S(1)} %shard_map.49.refs_2_), channel_id=1, source_target_pairs={{0,64},{1,65},{2,66},{3,67},{4,68},{5,69},{6,70},{7,71},{8,72},{9,... | collective-permute-start | bytes 1966088 | tf_op jit(solution)/shard_map/ppermute | solution.py:40
  121.8 22.2 %collective-permute-start.14 = (bf16[1536,128]{1,0:T(8,128)(2,1)S(1)}, bf16[1536,128]{1,0:T(8,128)(2,1)S(1)}, u32[]{:S(2)}, u32[]{:S(2)}) collective-permute-start(bf16[1536,128]{1,0:T(8,128)(2,1)S(1)} %shard_map.48.refs_0_), channel_id=1, source_target_pairs={{0,64},{1,65},{2,66},{3,67},{4,68},{5,69},{6,70},{7,71},{8,72},{9,... | collective-permute-start | bytes 1179656 | tf_op jit(solution)/shard_map/ppermute | solution.py:40

commit v11 on v10

--- a/solution.py
+++ b/solution.py
@@ -13,6 +13,7 @@
 PAD = 16
 TILE = 512
 VMEM = 24 * 1024 * 1024
+FULL = 60 * 1024 * 1024
 
 
 def place(d):
@@ -62,9 +63,9 @@
     return jax.ShapeDtypeStruct(dims, dtype)
 
 
-def params(steps):
+def params(steps, vmem=VMEM):
     return pltpu.CompilerParams(
-        vmem_limit_bytes=VMEM, dimension_semantics=("arbitrary",) * steps
+        vmem_limit_bytes=vmem, dimension_semantics=("arbitrary",) * steps
     )
 
 
@@ -95,24 +96,26 @@
     return blocks[0] if len(blocks) == 1 else jnp.concatenate(blocks, axis=1)
 
 
-def compact_kernel(rows, x_ref, *o_refs):
+def compact_kernel(rows, x_ref, all_ref, *o_refs):
     at = 0
     for ref in o_refs:
         blocks = ref.shape[1] // TILE
-        ref[...] = without_padding(joined(x_ref.at[:, at : at + blocks]), rows)
+        packed = without_padding(joined(x_ref.at[:, at : at + blocks]), rows)
+        ref[...] = packed
+        all_ref[:, TILE * at : TILE * (at + blocks)] = packed
         at += blocks
 
 
 def compact(plane, rows, widths):
     peers = plane.shape[0]
-    out = tuple(shape((peers * rows, width)) for width in widths)
+    out = tuple(shape((peers * rows, width)) for width in (sum(widths), *widths))
     return pl.pallas_call(
         functools.partial(compact_kernel, rows),
         grid=(1,),
         in_specs=[whole(*plane.shape)],
         out_specs=tuple(whole(*each.shape) for each in out),
         out_shape=out,
-        compiler_params=params(1),
+        compiler_params=params(1, FULL),
         cost_estimate=cost(4 * plane.size, 4 * plane.size),
     )(plane)
 
@@ -228,7 +231,7 @@
         in_specs=[whole(*block.shape)],
         out_specs=whole(*out.shape),
         out_shape=out,
-        compiler_params=params(1),
+        compiler_params=params(1, FULL),
         cost_estimate=cost(0, 2 * count * block.size),
     )(block)
 
@@ -278,19 +281,20 @@
     )(pieces)
 
 
-def weight_terms(parts, grads):
-    rows, width = parts[0].shape
+def weight_terms(own, sib, at, far, far_sib, grads):
+    rows, width = far.shape
     units = grads[0].shape[1]
     return pl.pallas_call(
         weight_kernel,
         grid=(width // TILE,),
-        in_specs=[pl.BlockSpec((rows, TILE), lambda k: (0, k))] * 4
+        in_specs=[pl.BlockSpec((rows, TILE), lambda k: (0, k + at // TILE))] * 2
+        + [pl.BlockSpec((rows, TILE), lambda k: (0, k))] * 2
         + [whole(*g.shape) for g in grads],
         out_specs=pl.BlockSpec((TILE, units), lambda k: (k, 0)),
         out_shape=shape((width, units)),
-        compiler_params=params(1),
+        compiler_params=params(1, FULL),
         cost_estimate=cost(8 * rows * width * units, 8 * rows * width),
-    )(*parts, *grads)
+    )(own, sib, far, far_sib, *grads)
 
 
 def view_sums(parts, samples):
@@ -303,7 +307,7 @@
         in_specs=[whole(*each.shape) for each in arrays],
         out_specs=whole(total, units),
         out_shape=shape((total, units), jnp.float32),
-        compiler_params=params(1),
+        compiler_params=params(1, FULL),
         cost_estimate=cost(total * units, 8 * total * units),
     )(*arrays)
 
@@ -328,11 +332,12 @@
     from_sib = swap(mine, c=1)
     from_far = swap(mine, z=1)
     split = (3 * width // 8, 5 * width // 8)
-    from_far, *h_own = lax.optimization_barrier((from_far, *compact(plane, rows, split)))
+    from_far, h_own, first, second = lax.optimization_barrier(
+        (from_far, *compact(plane, rows, split))
+    )
     from_far_sib = swap(from_far, c=1)
     partner = swap(mine, view=1)
-    first, partner = lax.optimization_barrier((h_own[0], partner))
-    h_far = [swap(first, z=1), swap(h_own[1], z=1)]
+    first = swap(first, z=1)
 
     centered, factor, gram = pl.pallas_call(
         functools.partial(center_kernel, rows, samples),
@@ -348,6 +353,9 @@
         cost_estimate=cost(8 * 4 * quarter * quarter * units, 16 * quarter * units * 2),
     )(mine, from_sib, from_far, from_far_sib)
 
+    gram, second, partner, late = lax.optimization_barrier((gram, second, partner, h_own))
+    h_far = [first, swap(second, z=1)]
+    h_sib = swap(late, c=1)
     gram = exchange(gram, "yx")
     gram = pl.pallas_call(
         total_kernel,
@@ -358,8 +366,7 @@
         compiler_params=params(1),
         cost_estimate=cost(gram.size, 4 * gram.size),
     )(gram)
-    gram, h_far[0], *late = lax.optimization_barrier((gram, h_far[0], *h_own))
-    h_sib = [swap(block, c=1) for block in late]
+    gram, h_far[0] = lax.optimization_barrier((gram, h_far[0]))
     gram = exchange(gram, "yx")
 
     grad, *runs = pl.pallas_call(
@@ -383,14 +390,14 @@
     g_far_sib = swap(runs[3], z=1, c=1)
     g_sib = swap(runs[1], c=1)
     h_part = hidden_terms(grad, weights)
-    h_part, h_far[1], *grads = lax.optimization_barrier(
-        (h_part, h_far[1], runs[0], g_sib, g_far, g_far_sib)
+    h_part, h_sib, h_far[1], *grads = lax.optimization_barrier(
+        (h_part, h_sib, h_far[1], runs[0], g_sib, g_far, g_far_sib)
     )
     pieces = exchange(h_part, "yx")
 
     parts = [
-        weight_terms((own, sib, far, swap(far, c=1)), grads)
-        for own, sib, far in zip(h_own, h_sib, h_far)
+        weight_terms(h_own, h_sib, at, far, swap(far, c=1), grads)
+        for at, far in zip((0, split[0]), h_far)
     ]
     grad_weight, pieces = lax.optimization_barrier((view_sums(parts, samples), pieces))
     grad_rows = hidden_rows(pieces, rows)

time: 148 us -> 159 us (1.074)
  Pallas kernels: 15.9 us -> 29.4 us
  starting transfers between devices: 42.3 us -> 35.4 us
  blocking collectives: 26.1 us -> 29.6 us
  waiting for transfers between devices: 57.6 us -> 60.2 us
    ppermute x18 -> x17, starting transfers between devices: 31.1 us -> 23.8 us  [swap(): return lax.ppermute(block, ('view', 'dp'), route)]
    pallas_call x2, Pallas kernels: 4.33 us -> 10.3 us  [weight_terms(): pl.pallas_call(weight_kernel, grid=(width // TILE,), in_specs=[pl.BlockSp...]
    all_to_all x2, blocking collectives: 26.1 us -> 29.6 us  [exchange(): lax.all_to_all(blocks, 'dp', 0, 0, tiled=True, axis_index_groups=groups(a...]
    pallas_call x1, Pallas kernels: 0.64 us -> 3.85 us  [compact(): pl.pallas_call(functools.partial(compact_kernel, rows), grid=(1,), in_spe...]
    ppermute x18 -> x17, waiting for transfers between devices: 43 us -> 45.7 us  [swap(): return lax.ppermute(block, ('view', 'dp'), route)]
    pallas_call x1, Pallas kernels: 0.2 us -> 2.43 us  [copies_of(): pl.pallas_call(copies_kernel, grid=(1,), in_specs=[whole(*block.shape)],...]
    unnamed x23 -> x19, local copies, waits for them, and re-layouts: 4.43 us -> 2.89 us
  transfers between devices with their start and end apart: 20 -> 19, of which waited for: 7 -> 9; matrix products, arithmetic and copies ran while one was open for 0% -> 0% of each run, Pallas kernels for 8% -> 16%
where the time goes in v11:
time: 159 us; the launch traced here: 158 us
  waiting for transfers between devices  60.2 us (38%)
  starting transfers between devices  35.4 us (22%)
  blocking collectives  29.6 us (19%)
  Pallas kernels  29.4 us (18%)
  local copies, waits for them, and re-layouts  2.89 us (2%)
    ppermute x17, waiting for transfers between devices, swap(): return lax.ppermute(block, ('view', 'dp'), route)  45.7 us
    all_to_all x2, blocking collectives, exchange(): lax.all_to_all(blocks, 'dp', 0, 0, tiled=True, axis_index_groups=groups(a...  29.6 us
    ppermute x17, starting transfers between devices, swap(): return lax.ppermute(block, ('view', 'dp'), route)  23.8 us
    all_to_all x2, waiting for transfers between devices, exchange(): lax.all_to_all(blocks, 'dp', 0, 0, tiled=True, axis_index_groups=groups(a...  14.6 us
    all_to_all x2, starting transfers between devices, exchange(): lax.all_to_all(blocks, 'dp', 0, 0, tiled=True, axis_index_groups=groups(a...  11.5 us
    pallas_call x2, Pallas kernels, weight_terms(): pl.pallas_call(weight_kernel, grid=(width // TILE,), in_specs=[pl.BlockSp...  10.3 us
    pallas_call x1, Pallas kernels, hidden_terms(): pl.pallas_call(hidden_kernel, grid=(width // TILE // 4,), in_specs=[whole...  3.87 us
    pallas_call x1, Pallas kernels, compact(): pl.pallas_call(functools.partial(compact_kernel, rows), grid=(1,), in_spe...  3.85 us
  transfers between devices with their start and end apart: 19, of which 9 were waited for; matrix products, arithmetic and copies ran while one was open for 0% of the time, Pallas kernels for 16%

profile of v11, /device:TPU:1, one launch (start us, length us, event | category | flops | bytes accessed | tf_op | source)
XLA Modules:
  0.0 158.3 jit_solution(4857576663706447878)
XLA Ops:
  0.6 4.7 %collective-permute-start = (bf16[4096,128]{1,0:T(8,128)(2,1)}, bf16[4096,128]{1,0:T(8,128)(2,1)}, u32[]{:S(2)}, u32[]{:S(2)}) collective-permute-start(bf16[4096,128]{1,0:T(8,128)(2,1)} %a_ref.3), channel_id=1, source_target_pairs={{0,72},{1,73},{2,74},{3,75},{4,76},{5,77},{6,78},{7,79},{8,64},{9,... | collective-permute-start | bytes 3145736 | tf_op jit(solution)/shard_map/ppermute | solution.py:41
  5.3 2.4 %shard_map.41 = bf16[16,8,16,512]{3,2,1,0:T(8,128)(2,1)} custom-call(bf16[1,14,4096]{2,1,0:T(8,128)(2,1)} %x_ref.1), custom_call_target="tpu_custom_call" | custom-call | bytes 1835008 | tf_op jit(solution)/shard_map/pallas_call | solution.py:228
  7.7 6.9 %all-to-all-start = ((bf16[16,8,16,512]{3,2,1,0:T(8,128)(2,1)}), bf16[16,8,16,512]{3,2,1,0:T(8,128)(2,1)S(1)}, u32[]{:S(2)}, u32[]{:S(2)}) async-start(bf16[16,8,16,512]{3,2,1,0:T(8,128)(2,1)} %shard_map.41), calls=%async_computation | async-start | bytes 4194304 | tf_op jit(solution)/shard_map/all_to_all | solution.py:45
  14.6 13.9 %collective-permute-done.c_ref = bf16[4096,128]{1,0:T(8,128)(2,1)} collective-permute-done((bf16[4096,128]{1,0:T(8,128)(2,1)}, bf16[4096,128]{1,0:T(8,128)(2,1)}, u32[]{:S(2)}, u32[]{:S(2)}) %collective-permute-start) | collective-permute-done | bytes 1048608 | tf_op jit(solution)/shard_map/ppermute | solution.py:41
  28.5 1.2 collective-permute-start.1
  29.7 0.0 collective-permute-start.2
  29.7 14.6 %all-to-all-done.h_ref.x_ref = bf16[16,8,16,512]{3,2,1,0:T(8,128)(2,1)S(1)} async-done(((bf16[16,8,16,512]{3,2,1,0:T(8,128)(2,1)}), bf16[16,8,16,512]{3,2,1,0:T(8,128)(2,1)S(1)}, u32[]{:S(2)}, u32[]{:S(2)}) %all-to-all-start) | async-done | bytes 2097184 | tf_op jit(solution)/shard_map/all_to_all | solution.py:45
  44.3 0.0 collective-permute-done.1.d_ref
  44.3 3.6 %shard_map.42.own_ref.e_ref = bf16[256,512]{1,0:T(8,128)(2,1)S(1)} custom-call(bf16[16,8,16,512]{3,2,1,0:T(8,128)(2,1)S(1)} %all-to-all-done.h_ref.x_ref, bf16[4096,128]{1,0:T(8,128)(2,1)S(1)} %copy-done.1, bf16[4096,128]{1,0:T(8,128)(2,1)} %collective-permute-done.2.b_ref, bf16[4096,128]{1,0:T(8,128)(2,1)} %collective-permute-done.c_ref, ...), custom_call_target="tpu_custom_call" | custom-call | flops 1073741824 | bytes 6291456 | tf_op jit(solution)/shard_map/pallas_call | solution.py:242
  48.0 0.5 collective-permute-start.3
  48.4 2.5 %collective-permute-start.4 = (bf16[256,512]{1,0:T(8,128)(2,1)S(1)}, bf16[256,512]{1,0:T(8,128)(2,1)S(1)}, u32[]{:S(2)}, u32[]{:S(2)}) collective-permute-start(bf16[256,512]{1,0:T(8,128)(2,1)S(1)} %shard_map.42.own_ref.e_ref), channel_id=1, source_target_pairs={{0,1},{1,0},{2,3},{3,2},{4,5},{5,4},{6,7},{7,6},{8,9},{9,8},{10,11... | collective-permute-start | bytes 786440 | tf_op jit(solution)/shard_map/ppermute | solution.py:41
  50.9 3.8 %shard_map.43 = (bf16[224,4096]{1,0:T(8,128)(2,1)}, bf16[224,1536]{1,0:T(8,128)(2,1)}, bf16[224,2560]{1,0:T(8,128)(2,1)}) custom-call(bf16[16,8,16,512]{3,2,1,0:T(8,128)(2,1)} %copy-done), custom_call_target="tpu_custom_call" | custom-call | flops 4194304 | bytes 4194304 | tf_op jit(solution)/shard_map/pallas_call | solution.py:112
  54.8 0.0 collective-permute-done.3.far_ref
  54.8 3.6 %collective-permute-start.5 = (bf16[256,512]{1,0:T(8,128)(2,1)S(1)}, bf16[256,512]{1,0:T(8,128)(2,1)S(1)}, u32[]{:S(2)}, u32[]{:S(2)}) collective-permute-start(bf16[256,512]{1,0:T(8,128)(2,1)S(1)} %collective-permute-done.3.far_ref), channel_id=1, source_target_pairs={{0,1},{1,0},{2,3},{3,2},{4,5},{5,4},{6,7},{7,6},{8,9},{9,8},{10,11... | collective-permute-start | bytes 786440 | tf_op jit(solution)/shard_map/ppermute | solution.py:41
  58.4 0.0 collective-permute-start.6
  58.4 1.2 collective-permute-done.5.far_sib_ref
  59.5 0.9 shard_map.44
  60.4 5.9 %collective-permute-done.6.p_ref = bf16[256,512]{1,0:T(8,128)(2,1)S(1)} collective-permute-done((bf16[256,512]{1,0:T(8,128)(2,1)S(1)}, bf16[256,512]{1,0:T(8,128)(2,1)S(1)}, u32[]{:S(2)}, u32[]{:S(2)}) %collective-permute-start.6) | collective-permute-done | bytes 262176 | tf_op jit(solution)/shard_map/ppermute | solution.py:41
  66.3 0.8 collective-permute-start.8
  67.1 0.5 collective-permute-start.7
  67.5 2.5 %collective-permute-start.9 = (bf16[224,2560]{1,0:T(8,128)(2,1)}, bf16[224,2560]{1,0:T(8,128)(2,1)}, u32[]{:S(2)}, u32[]{:S(2)}) collective-permute-start(bf16[224,2560]{1,0:T(8,128)(2,1)} %get-tuple-element.49), channel_id=1, source_target_pairs={{0,8},{1,9},{2,10},{3,11},{4,12},{5,13},{6,14},{7,15},{8,0},{9,1},... | collective-permute-start | bytes 3440648 | tf_op jit(solution)/shard_map/ppermute | solution.py:41
  70.0 14.9 %all_to_all.32 = bf16[16,16,1024]{2,1,0:T(8,128)(2,1)S(1)} all-to-all(bf16[16,16,1024]{2,1,0:T(8,128)(2,1)S(1)} %bitcast.7), channel_id=1, replica_groups={{0,2,4,6,16,18,20,22,32,34,36,38,48,50,52,54},{1,3,5,7,17,19,21,23,33,3..., dimensions={0} | all-to-all | bytes 1048576 | tf_op jit(solution)/shard_map/all_to_all | solution.py:45
  85.0 0.1 shard_map.45
  85.1 0.8 collective-permute-done.7.refs_2_
  85.9 14.6 %all_to_all.33 = bf16[16,16,1024]{2,1,0:T(8,128)(2,1)S(1)} all-to-all(bf16[16,16,1024]{2,1,0:T(8,128)(2,1)S(1)} %bitcast.4), channel_id=1, replica_groups={{0,2,4,6,16,18,20,22,32,34,36,38,48,50,52,54},{1,3,5,7,17,19,21,23,33,3..., dimensions={0} | all-to-all | bytes 1048576 | tf_op jit(solution)/shard_map/all_to_all | solution.py:45
  100.5 0.7 shard_map.46
  101.1 0.0 copy-start.2
  101.2 0.6 copy-done.2
  101.8 2.3 %collective-permute-start.10 = (bf16[224,128]{1,0:T(8,128)(2,1)S(1)}, bf16[224,128]{1,0:T(8,128)(2,1)S(1)}, u32[]{:S(2)}, u32[]{:S(2)}) collective-permute-start(bf16[224,128]{1,0:T(8,128)(2,1)S(1)} %get-tuple-element.51), channel_id=1, source_target_pairs={{0,1},{1,0},{2,3},{3,2},{4,5},{5,4},{6,7},{7,6},{8,9},{9,8},{10,11... | collective-permute-start | bytes 172040 | tf_op jit(solution)/shard_map/ppermute | solution.py:41
  104.1 0.1 collective-permute-start.11
  104.2 3.1 %collective-permute-start.12 = (bf16[224,128]{1,0:T(8,128)(2,1)S(1)}, bf16[224,128]{1,0:T(8,128)(2,1)S(1)}, u32[]{:S(2)}, u32[]{:S(2)}) collective-permute-start(bf16[224,128]{1,0:T(8,128)(2,1)S(1)} %get-tuple-element.53), channel_id=1, source_target_pairs={{0,9},{1,8},{2,11},{3,10},{4,13},{5,12},{6,15},{7,14},{8,1},{9,0},... | collective-permute-start | bytes 172040 | tf_op jit(solution)/shard_map/ppermute | solution.py:41
  107.2 3.9 %shard_map.47 = bf16[16,8,16,512]{3,2,1,0:T(8,128)(2,1)} custom-call(bf16[256,512]{1,0:T(8,128)(2,1)S(1)} %get-tuple-element.47.g_ref, bf16[4096,128]{1,0:T(8,128)(2,1)S(1)} %copy-done.1, bf16[4096,128]{1,0:T(8,128)(2,1)} %collective-permute-done.2.b_ref, bf16[4096,128]{1,0:T(8,128)(2,1)} %collective-permute-done.c_ref, ...), custom_call_target="tpu_custom_call" | custom-call | flops 1073741824 | bytes 6291456 | tf_op jit(solution)/shard_map/pallas_call | solution.py:259
  111.1 0.6 collective-permute-done.11.refs_6_
  111.7 1.3 collective-permute-done.12.refs_7_
  113.0 0.0 copy-start.4
  113.0 0.6 copy-done.8
  113.6 4.7 %all-to-all-start.3 = ((bf16[16,8,16,512]{3,2,1,0:T(8,128)(2,1)}), bf16[16,8,16,512]{3,2,1,0:T(8,128)(2,1)S(1)}, u32[]{:S(2)}, u32[]{:S(2)}) async-start(bf16[16,8,16,512]{3,2,1,0:T(8,128)(2,1)} %shard_map.47), calls=%async_computation.3 | async-start | bytes 4194304 | tf_op jit(solution)/shard_map/all_to_all | solution.py:45
  118.3 0.7 collective-permute-start.15
  118.9 0.1 collective-permute-start.13
  119.0 3.3 %collective-permute-done.15.refs_3_ = bf16[224,2560]{1,0:T(8,128)(2,1)} collective-permute-done((bf16[224,2560]{1,0:T(8,128)(2,1)}, bf16[224,2560]{1,0:T(8,128)(2,1)}, u32[]{:S(2)}, u32[]{:S(2)}) %collective-permute-start.15) | collective-permute-done | bytes 1146912 | tf_op jit(solution)/shard_map/ppermute | solution.py:41
  122.3 6.0 %shard_map.49.refs_2_ = bf16[2560,128]{1,0:T(8,128)(2,1)} custom-call(bf16[224,4096]{1,0:T(8,128)(2,1)} %get-tuple-element.48.refs_0_, bf16[224,4096]{1,0:T(8,128)(2,1)} %collective-permute-done.8.refs_1_, bf16[224,2560]{1,0:T(8,128)(2,1)} %collective-permute-done.9.refs_2_, bf16[224,2560]{1,0:T(8,128)(2,1)} %collective-permute-done.15.refs_3_, ...), custom_call_target="tpu_custom_call" | custom-call | flops 587202560 | bytes 4587520 | tf_op jit(solution)/shard_map/pallas_call | solution.py:287
  128.3 4.3 %shard_map.48.refs_0_ = bf16[1536,128]{1,0:T(8,128)(2,1)} custom-call(bf16[224,4096]{1,0:T(8,128)(2,1)} %get-tuple-element.48.refs_0_, bf16[224,4096]{1,0:T(8,128)(2,1)} %collective-permute-done.8.refs_1_, bf16[224,1536]{1,0:T(8,128)(2,1)} %copy-done.3, bf16[224,1536]{1,0:T(8,128)(2,1)} %collective-permute-done.13.refs_3_, bf16[224,128]{1,0:T(8,128)(2,1)} %copy-done.2, ...), custom_call_target="tpu_custom_call" | custom-call | flops 352321536 | bytes 2752512 | tf_op jit(solution)/shard_map/pallas_call | solution.py:287
  132.6 1.4 collective-permute-start.14
  134.0 18.8 %collective-permute-done.14.refs_1_ = bf16[1536,128]{1,0:T(8,128)(2,1)S(1)} collective-permute-done((bf16[1536,128]{1,0:T(8,128)(2,1)}, bf16[1536,128]{1,0:T(8,128)(2,1)S(1)}, u32[]{:S(2)}, u32[]{:S(2)}) %collective-permute-start.14) | collective-permute-done | bytes 393248 | tf_op jit(solution)/shard_map/ppermute | solution.py:41
  152.9 0.7 copy-done.5
  153.6 3.1 %shard_map.50 = f32[4096,128]{1,0:T(8,128)} custom-call(bf16[1536,128]{1,0:T(8,128)(2,1)} %shard_map.48.refs_0_, bf16[1536,128]{1,0:T(8,128)(2,1)} %copy-done.5, bf16[2560,128]{1,0:T(8,128)(2,1)} %shard_map.49.refs_2_, bf16[2560,128]{1,0:T(8,128)(2,1)} %collective-permute-done.16.refs_3_), custom_call_target="tpu_custom_call" | custom-call | flops 524288 | bytes 4194304 | tf_op jit(solution)/shard_map/pallas_call | solution.py:304
  156.7 0.6 shard_map.51
  157.4 0.9 copy.4
  (22 shorter events, 0.0 us)
Async XLA Ops:
  0.6 27.9 %collective-permute-start = (bf16[4096,128]{1,0:T(8,128)(2,1)}, bf16[4096,128]{1,0:T(8,128)(2,1)}, u32[]{:S(2)}, u32[]{:S(2)}) collective-permute-start(bf16[4096,128]{1,0:T(8,128)(2,1)} %a_ref.3), channel_id=1, source_target_pairs={{0,72},{1,73},{2,74},{3,75},{4,76},{5,77},{6,78},{7,79},{8,64},{9,... | collective-permute-start | bytes 3145736 | tf_op jit(solution)/shard_map/ppermute | solution.py:41
  7.7 22.0 %copy-start.1 = (bf16[4096,128]{1,0:T(8,128)(2,1)S(1)}, bf16[4096,128]{1,0:T(8,128)(2,1)}, u32[]{:S(2)}) copy-start(bf16[4096,128]{1,0:T(8,128)(2,1)} %a_ref.3) | copy-start | bytes 3145732
  7.7 36.6 %all-to-all-start = ((bf16[16,8,16,512]{3,2,1,0:T(8,128)(2,1)}), bf16[16,8,16,512]{3,2,1,0:T(8,128)(2,1)S(1)}, u32[]{:S(2)}, u32[]{:S(2)}) async-start(bf16[16,8,16,512]{3,2,1,0:T(8,128)(2,1)} %shard_map.41), calls=%async_computation | async-start | bytes 4194304 | tf_op jit(solution)/shard_map/all_to_all | solution.py:45
  28.5 15.8 %collective-permute-start.1 = (bf16[4096,128]{1,0:T(8,128)(2,1)}, bf16[4096,128]{1,0:T(8,128)(2,1)}, u32[]{:S(2)}, u32[]{:S(2)}) collective-permute-start(bf16[4096,128]{1,0:T(8,128)(2,1)} %collective-permute-done.c_ref), channel_id=1, source_target_pairs={{0,1},{1,0},{2,3},{3,2},{4,5},{5,4},{6,7},{7,6},{8,9},{9,8},{10,11... | collective-permute-start | bytes 3145736 | tf_op jit(solution)/shard_map/ppermute | solution.py:41
  29.7 14.6 %collective-permute-start.2 = (bf16[4096,128]{1,0:T(8,128)(2,1)S(1)}, bf16[4096,128]{1,0:T(8,128)(2,1)}, u32[]{:S(2)}, u32[]{:S(2)}) collective-permute-start(bf16[4096,128]{1,0:T(8,128)(2,1)S(1)} %copy-done.1), channel_id=1, source_target_pairs={{0,1},{1,0},{2,3},{3,2},{4,5},{5,4},{6,7},{7,6},{8,9},{9,8},{10,11... | collective-permute-start | bytes 3145736 | tf_op jit(solution)/shard_map/ppermute | solution.py:41
  44.3 3.6 %copy-start = (bf16[16,8,16,512]{3,2,1,0:T(8,128)(2,1)}, bf16[16,8,16,512]{3,2,1,0:T(8,128)(2,1)S(1)}, u32[]{:S(2)}) copy-start(bf16[16,8,16,512]{3,2,1,0:T(8,128)(2,1)S(1)} %all-to-all-done.h_ref.x_ref) | copy-start | bytes 6291460
  48.0 6.8 %collective-permute-start.3 = (bf16[256,512]{1,0:T(8,128)(2,1)S(1)}, bf16[256,512]{1,0:T(8,128)(2,1)S(1)}, u32[]{:S(2)}, u32[]{:S(2)}) collective-permute-start(bf16[256,512]{1,0:T(8,128)(2,1)S(1)} %shard_map.42.own_ref.e_ref), channel_id=1, source_target_pairs={{0,8},{1,9},{2,10},{3,11},{4,12},{5,13},{6,14},{7,15},{8,0},{9,1},... | collective-permute-start | bytes 786440 | tf_op jit(solution)/shard_map/ppermute | solution.py:41
  48.4 9.9 %collective-permute-start.4 = (bf16[256,512]{1,0:T(8,128)(2,1)S(1)}, bf16[256,512]{1,0:T(8,128)(2,1)S(1)}, u32[]{:S(2)}, u32[]{:S(2)}) collective-permute-start(bf16[256,512]{1,0:T(8,128)(2,1)S(1)} %shard_map.42.own_ref.e_ref), channel_id=1, source_target_pairs={{0,1},{1,0},{2,3},{3,2},{4,5},{5,4},{6,7},{7,6},{8,9},{9,8},{10,11... | collective-permute-start | bytes 786440 | tf_op jit(solution)/shard_map/ppermute | solution.py:41
  54.8 4.7 %collective-permute-start.5 = (bf16[256,512]{1,0:T(8,128)(2,1)S(1)}, bf16[256,512]{1,0:T(8,128)(2,1)S(1)}, u32[]{:S(2)}, u32[]{:S(2)}) collective-permute-start(bf16[256,512]{1,0:T(8,128)(2,1)S(1)} %collective-permute-done.3.far_ref), channel_id=1, source_target_pairs={{0,1},{1,0},{2,3},{3,2},{4,5},{5,4},{6,7},{7,6},{8,9},{9,8},{10,11... | collective-permute-start | bytes 786440 | tf_op jit(solution)/shard_map/ppermute | solution.py:41
  58.4 7.9 %collective-permute-start.6 = (bf16[256,512]{1,0:T(8,128)(2,1)S(1)}, bf16[256,512]{1,0:T(8,128)(2,1)S(1)}, u32[]{:S(2)}, u32[]{:S(2)}) collective-permute-start(bf16[256,512]{1,0:T(8,128)(2,1)S(1)} %shard_map.42.own_ref.e_ref), channel_id=1, source_target_pairs={{0,64},{1,65},{2,66},{3,67},{4,68},{5,69},{6,70},{7,71},{8,72},{9,... | collective-permute-start | bytes 786440 | tf_op jit(solution)/shard_map/ppermute | solution.py:41
  66.3 46.7 %collective-permute-start.8 = (bf16[224,4096]{1,0:T(8,128)(2,1)}, bf16[224,4096]{1,0:T(8,128)(2,1)}, u32[]{:S(2)}, u32[]{:S(2)}) collective-permute-start(bf16[224,4096]{1,0:T(8,128)(2,1)} %get-tuple-element.48.refs_0_), channel_id=1, source_target_pairs={{0,1},{1,0},{2,3},{3,2},{4,5},{5,4},{6,7},{7,6},{8,9},{9,8},{10,11... | collective-permute-start | bytes 5505032 | tf_op jit(solution)/shard_map/ppermute | solution.py:41
  67.1 18.8 %collective-permute-start.7 = (bf16[224,1536]{1,0:T(8,128)(2,1)}, bf16[224,1536]{1,0:T(8,128)(2,1)S(1)}, u32[]{:S(2)}, u32[]{:S(2)}) collective-permute-start(bf16[224,1536]{1,0:T(8,128)(2,1)} %get-tuple-element.42), channel_id=1, source_target_pairs={{0,8},{1,9},{2,10},{3,11},{4,12},{5,13},{6,14},{7,15},{8,0},{9,1},... | collective-permute-start | bytes 2064392 | tf_op jit(solution)/shard_map/ppermute | solution.py:41
  67.5 45.5 %collective-permute-start.9 = (bf16[224,2560]{1,0:T(8,128)(2,1)}, bf16[224,2560]{1,0:T(8,128)(2,1)}, u32[]{:S(2)}, u32[]{:S(2)}) collective-permute-start(bf16[224,2560]{1,0:T(8,128)(2,1)} %get-tuple-element.49), channel_id=1, source_target_pairs={{0,8},{1,9},{2,10},{3,11},{4,12},{5,13},{6,14},{7,15},{8,0},{9,1},... | collective-permute-start | bytes 3440648 | tf_op jit(solution)/shard_map/ppermute | solution.py:41
  85.9 21.4 %copy-start.3 = (bf16[224,1536]{1,0:T(8,128)(2,1)}, bf16[224,1536]{1,0:T(8,128)(2,1)S(1)}, u32[]{:S(2)}) copy-start(bf16[224,1536]{1,0:T(8,128)(2,1)S(1)} %collective-permute-done.7.refs_2_) | copy-start | bytes 2064388
  101.1 0.6 copy-start.2
  101.8 9.3 %collective-permute-start.10 = (bf16[224,128]{1,0:T(8,128)(2,1)S(1)}, bf16[224,128]{1,0:T(8,128)(2,1)S(1)}, u32[]{:S(2)}, u32[]{:S(2)}) collective-permute-start(bf16[224,128]{1,0:T(8,128)(2,1)S(1)} %get-tuple-element.51), channel_id=1, source_target_pairs={{0,1},{1,0},{2,3},{3,2},{4,5},{5,4},{6,7},{7,6},{8,9},{9,8},{10,11... | collective-permute-start | bytes 172040 | tf_op jit(solution)/shard_map/ppermute | solution.py:41
  104.1 7.6 %collective-permute-start.11 = (bf16[224,128]{1,0:T(8,128)(2,1)S(1)}, bf16[224,128]{1,0:T(8,128)(2,1)S(1)}, u32[]{:S(2)}, u32[]{:S(2)}) collective-permute-start(bf16[224,128]{1,0:T(8,128)(2,1)S(1)} %get-tuple-element.52), channel_id=1, source_target_pairs={{0,8},{1,9},{2,10},{3,11},{4,12},{5,13},{6,14},{7,15},{8,0},{9,1},... | collective-permute-start | bytes 172040 | tf_op jit(solution)/shard_map/ppermute | solution.py:41
  104.2 8.8 %collective-permute-start.12 = (bf16[224,128]{1,0:T(8,128)(2,1)S(1)}, bf16[224,128]{1,0:T(8,128)(2,1)S(1)}, u32[]{:S(2)}, u32[]{:S(2)}) collective-permute-start(bf16[224,128]{1,0:T(8,128)(2,1)S(1)} %get-tuple-element.53), channel_id=1, source_target_pairs={{0,9},{1,8},{2,11},{3,10},{4,13},{5,12},{6,15},{7,14},{8,1},{9,0},... | collective-permute-start | bytes 172040 | tf_op jit(solution)/shard_map/ppermute | solution.py:41
  111.1 1.9 %copy-start.6 = (bf16[224,128]{1,0:T(8,128)(2,1)}, bf16[224,128]{1,0:T(8,128)(2,1)S(1)}, u32[]{:S(2)}) copy-start(bf16[224,128]{1,0:T(8,128)(2,1)S(1)} %collective-permute-done.10.refs_5_) | copy-start | bytes 172036
  111.7 1.4 copy-start.7
  113.0 0.6 copy-start.8
  113.0 5.9 %copy-start.4 = (bf16[224,1536]{1,0:T(8,128)(2,1)S(1)}, bf16[224,1536]{1,0:T(8,128)(2,1)}, u32[]{:S(2)}) copy-start(bf16[224,1536]{1,0:T(8,128)(2,1)} %copy-done.3) | copy-start | bytes 2064388
  113.6 43.1 %all-to-all-start.3 = ((bf16[16,8,16,512]{3,2,1,0:T(8,128)(2,1)}), bf16[16,8,16,512]{3,2,1,0:T(8,128)(2,1)S(1)}, u32[]{:S(2)}, u32[]{:S(2)}) async-start(bf16[16,8,16,512]{3,2,1,0:T(8,128)(2,1)} %shard_map.47), calls=%async_computation.3 | async-start | bytes 4194304 | tf_op jit(solution)/shard_map/all_to_all | solution.py:45
  118.3 4.0 %collective-permute-start.15 = (bf16[224,2560]{1,0:T(8,128)(2,1)}, bf16[224,2560]{1,0:T(8,128)(2,1)}, u32[]{:S(2)}, u32[]{:S(2)}) collective-permute-start(bf16[224,2560]{1,0:T(8,128)(2,1)} %collective-permute-done.9.refs_2_), channel_id=1, source_target_pairs={{0,1},{1,0},{2,3},{3,2},{4,5},{5,4},{6,7},{7,6},{8,9},{9,8},{10,11... | collective-permute-start | bytes 3440648 | tf_op jit(solution)/shard_map/ppermute | solution.py:41
  118.9 9.4 %collective-permute-start.13 = (bf16[224,1536]{1,0:T(8,128)(2,1)S(1)}, bf16[224,1536]{1,0:T(8,128)(2,1)}, u32[]{:S(2)}, u32[]{:S(2)}) collective-permute-start(bf16[224,1536]{1,0:T(8,128)(2,1)S(1)} %copy-done.4), channel_id=1, source_target_pairs={{0,1},{1,0},{2,3},{3,2},{4,5},{5,4},{6,7},{7,6},{8,9},{9,8},{10,11... | collective-permute-start | bytes 2064392 | tf_op jit(solution)/shard_map/ppermute | solution.py:41
  128.3 24.6 %collective-permute-start.16 = (bf16[2560,128]{1,0:T(8,128)(2,1)}, bf16[2560,128]{1,0:T(8,128)(2,1)}, u32[]{:S(2)}, u32[]{:S(2)}) collective-permute-start(bf16[2560,128]{1,0:T(8,128)(2,1)} %shard_map.49.refs_2_), channel_id=1, source_target_pairs={{0,64},{1,65},{2,66},{3,67},{4,68},{5,69},{6,70},{7,71},{8,72},{9,... | collective-permute-start | bytes 1966088 | tf_op jit(solution)/shard_map/ppermute | solution.py:41
  132.6 20.3 %collective-permute-start.14 = (bf16[1536,128]{1,0:T(8,128)(2,1)}, bf16[1536,128]{1,0:T(8,128)(2,1)S(1)}, u32[]{:S(2)}, u32[]{:S(2)}) collective-permute-start(bf16[1536,128]{1,0:T(8,128)(2,1)} %shard_map.48.refs_0_), channel_id=1, source_target_pairs={{0,64},{1,65},{2,66},{3,67},{4,68},{5,69},{6,70},{7,71},{8,72},{9,... | collective-permute-start | bytes 1179656 | tf_op jit(solution)/shard_map/ppermute | solution.py:41
  152.9 0.7 copy-start.5

commit v12 on v10

--- a/solution.py
+++ b/solution.py
@@ -11,6 +11,7 @@
 YS, ZS, XS, CS = 4, 2, 4, 2
 DP = YS * ZS * XS * CS
 PAD = 16
+SMEM = pl.BlockSpec(memory_space=pltpu.SMEM)
 TILE = 512
 VMEM = 24 * 1024 * 1024
 
@@ -177,7 +178,7 @@
         o_ref[PAD * i : PAD * i + PAD, :] = total
 
 
-def grad_kernel(rows, samples, m_ref, c_ref, f_ref, e_ref, p_ref, o_ref, *run_refs):
+def grad_kernel(rows, samples, me_ref, m_ref, c_ref, f_ref, e_ref, p_ref, o_ref, *run_refs):
     coef_cov = 0.08 * samples / ((samples - 1) * (samples - 1))
     coupled = matmul(m_ref[...], c_ref[...], 1, 0)
     centered = c_ref[: e_ref.shape[0], :].astype(jnp.float32)
@@ -186,8 +187,8 @@
     grad = grad.astype(jnp.bfloat16)
     o_ref[...] = grad
     packed = without_padding(grad, rows)
-    for i, ref in enumerate(run_refs):
-        ref[...] = packed[:, 128 * i : 128 * i + 128]
+    for i in range(4):
+        run_refs[0][me_ref[0] ^ i] = packed[:, 128 * i : 128 * i + 128]
 
 
 def hidden_kernel(g_ref, a_ref, b_ref, c_ref, d_ref, o_ref):
@@ -198,10 +199,10 @@
         o_ref[:, k] = out[:, tile * k : tile * k + tile].reshape(peers, rows, tile)
 
 
-def weight_kernel(*refs):
-    hs, gs, (o_ref,) = refs[:4], refs[4:8], refs[8:]
+def weight_kernel(me_ref, *refs):
+    hs, (g_ref, o_ref) = refs[:4], refs[4:]
     h = jnp.concatenate([ref[...] for ref in hs], axis=0)
-    g = jnp.concatenate([ref[...] for ref in gs], axis=0)
+    g = jnp.concatenate([g_ref[me_ref[0] ^ i] for i in range(4)], axis=0)
     o_ref[...] = matmul(h, g, 0, 0).astype(o_ref.dtype)
 
 
@@ -278,19 +279,20 @@
     )(pieces)
 
 
-def weight_terms(parts, grads):
+def weight_terms(me, parts, runs):
     rows, width = parts[0].shape
-    units = grads[0].shape[1]
+    units = runs.shape[2]
     return pl.pallas_call(
         weight_kernel,
         grid=(width // TILE,),
-        in_specs=[pl.BlockSpec((rows, TILE), lambda k: (0, k))] * 4
-        + [whole(*g.shape) for g in grads],
+        in_specs=[SMEM]
+        + [pl.BlockSpec((rows, TILE), lambda k: (0, k))] * 4
+        + [whole(*runs.shape)],
         out_specs=pl.BlockSpec((TILE, units), lambda k: (k, 0)),
         out_shape=shape((width, units)),
         compiler_params=params(1),
         cost_estimate=cost(8 * rows * width * units, 8 * rows * width),
-    )(*parts, *grads)
+    )(me, *parts, runs)
 
 
 def view_sums(parts, samples):
@@ -331,8 +333,9 @@
     from_far, *h_own = lax.optimization_barrier((from_far, *compact(plane, rows, split)))
     from_far_sib = swap(from_far, c=1)
     partner = swap(mine, view=1)
-    first, partner = lax.optimization_barrier((h_own[0], partner))
-    h_far = [swap(first, z=1), swap(h_own[1], z=1)]
+    first, _ = lax.optimization_barrier((h_own[0], from_far))
+    second, partner = lax.optimization_barrier((h_own[1], partner))
+    h_far = [swap(first, z=1), swap(second, z=1)]
 
     centered, factor, gram = pl.pallas_call(
         functools.partial(center_kernel, rows, samples),
@@ -362,10 +365,13 @@
     h_sib = [swap(block, c=1) for block in late]
     gram = exchange(gram, "yx")
 
-    grad, *runs = pl.pallas_call(
+    d = lax.axis_index("dp")
+    me = (d // (XS * CS) % ZS * CS + d % CS).astype(jnp.int32).reshape(1)
+    grad, runs = pl.pallas_call(
         functools.partial(grad_kernel, rows, samples),
         grid=(1,),
         in_specs=[
+            SMEM,
             whole(quarter, 4 * quarter),
             whole(4 * quarter, 4 * units),
             whole(8, 4 * units),
@@ -373,23 +379,20 @@
             whole(quarter, 4 * units),
         ],
         out_specs=(whole(quarter, 4 * units),)
-        + (whole(peers * rows, units),) * 4,
+        + (whole(4, peers * rows, units),),
         out_shape=(shape((quarter, 4 * units)),)
-        + (shape((peers * rows, units)),) * 4,
+        + (shape((4, peers * rows, units)),),
         compiler_params=params(1),
         cost_estimate=cost(8 * 4 * quarter * quarter * units, 16 * quarter * units * 2),
-    )(gram, centered, factor, mine, partner)
-    g_far = swap(runs[2], z=1)
-    g_far_sib = swap(runs[3], z=1, c=1)
-    g_sib = swap(runs[1], c=1)
+    )(me, gram, centered, factor, mine, partner)
+    runs = exchange(runs, "zc")
+
     h_part = hidden_terms(grad, weights)
-    h_part, h_far[1], *grads = lax.optimization_barrier(
-        (h_part, h_far[1], runs[0], g_sib, g_far, g_far_sib)
-    )
+    h_part, h_far[1], runs = lax.optimization_barrier((h_part, h_far[1], runs))
     pieces = exchange(h_part, "yx")
 
     parts = [
-        weight_terms((own, sib, far, swap(far, c=1)), grads)
+        weight_terms(me, (own, sib, far, swap(far, c=1)), runs)
         for own, sib, far in zip(h_own, h_sib, h_far)
     ]
     grad_weight, pieces = lax.optimization_barrier((view_sums(parts, samples), pieces))

time: 148 us -> 153 us (1.034)
  blocking collectives: 26.1 us -> 0 us
  waiting for transfers between devices: 57.6 us -> 78.1 us
  Pallas kernels: 15.9 us -> 21.1 us
  local copies, waits for them, and re-layouts: 4.43 us -> 8.29 us
  starting transfers between devices: 42.3 us -> 43.9 us
    all_to_all x2 -> x0, blocking collectives: 26.1 us -> none  [exchange(): lax.all_to_all(blocks, 'dp', 0, 0, tiled=True, axis_index_groups=groups(a...]
    all_to_all x2 -> x5, waiting for transfers between devices: 14.6 us -> 36.1 us  [exchange(): lax.all_to_all(blocks, 'dp', 0, 0, tiled=True, axis_index_groups=groups(a...]
    all_to_all x2 -> x5, starting transfers between devices: 11.2 us -> 24.8 us  [exchange(): lax.all_to_all(blocks, 'dp', 0, 0, tiled=True, axis_index_groups=groups(a...]
    ppermute x18 -> x15, starting transfers between devices: 31.1 us -> 19 us  [swap(): return lax.ppermute(block, ('view', 'dp'), route)]
    unnamed x23 -> x19, local copies, waits for them, and re-layouts: 4.43 us -> 8.29 us
    pallas_call x2, Pallas kernels: 4.33 us -> 7.38 us  [weight_terms(): pl.pallas_call(weight_kernel, grid=(width // TILE,), in_specs=[SMEM] + [p...]
    ppermute x18 -> x15, waiting for transfers between devices: 43 us -> 42 us  [swap(): return lax.ppermute(block, ('view', 'dp'), route)]
  transfers between devices with their start and end apart: 20 -> 20, of which waited for: 7 -> 10; matrix products, arithmetic and copies ran while one was open for 0% -> 0% of each run, Pallas kernels for 8% -> 12%
where the time goes in v12:
time: 153 us; the launch traced here: 152 us
  waiting for transfers between devices  78.1 us (51%)
  starting transfers between devices  43.9 us (29%)
  Pallas kernels  21.1 us (14%)
  local copies, waits for them, and re-layouts  8.29 us (5%)
    ppermute x15, waiting for transfers between devices, swap(): return lax.ppermute(block, ('view', 'dp'), route)  42 us
    all_to_all x5, waiting for transfers between devices, exchange(): lax.all_to_all(blocks, 'dp', 0, 0, tiled=True, axis_index_groups=groups(a...  36.1 us
    all_to_all x5, starting transfers between devices, exchange(): lax.all_to_all(blocks, 'dp', 0, 0, tiled=True, axis_index_groups=groups(a...  24.8 us
    ppermute x15, starting transfers between devices, swap(): return lax.ppermute(block, ('view', 'dp'), route)  19 us
    unnamed x19, local copies, waits for them, and re-layouts  8.29 us
    pallas_call x2, Pallas kernels, weight_terms(): pl.pallas_call(weight_kernel, grid=(width // TILE,), in_specs=[SMEM] + [p...  7.38 us
    pallas_call x1, Pallas kernels, hidden_terms(): pl.pallas_call(hidden_kernel, grid=(width // TILE // 4,), in_specs=[whole...  3.91 us
  transfers between devices with their start and end apart: 20, of which 10 were waited for; matrix products, arithmetic and copies ran while one was open for 0% of the time, Pallas kernels for 12%

profile of v12, /device:TPU:1, one launch (start us, length us, event | category | flops | bytes accessed | tf_op | source)
XLA Modules:
  0.0 152.1 jit_solution(17307068836967324470)
XLA Ops:
  0.6 4.7 %collective-permute-start = (bf16[4096,128]{1,0:T(8,128)(2,1)}, bf16[4096,128]{1,0:T(8,128)(2,1)}, u32[]{:S(2)}, u32[]{:S(2)}) collective-permute-start(bf16[4096,128]{1,0:T(8,128)(2,1)} %a_ref.3), channel_id=1, source_target_pairs={{0,72},{1,73},{2,74},{3,75},{4,76},{5,77},{6,78},{7,79},{8,64},{9,... | collective-permute-start | bytes 3145736 | tf_op jit(solution)/shard_map/ppermute | solution.py:41
  5.3 0.9 copy-done.8
  6.2 0.2 shard_map.41
  6.4 1.3 copy-done
  7.7 6.9 %all-to-all-start = ((bf16[16,8,16,512]{3,2,1,0:T(8,128)(2,1)}), bf16[16,8,16,512]{3,2,1,0:T(8,128)(2,1)S(1)}, u32[]{:S(2)}, u32[]{:S(2)}) async-start(bf16[16,8,16,512]{3,2,1,0:T(8,128)(2,1)} %copy-done), calls=%async_computation | async-start | bytes 4194304 | tf_op jit(solution)/shard_map/all_to_all | solution.py:45
  14.6 13.9 %collective-permute-done.c_ref = bf16[4096,128]{1,0:T(8,128)(2,1)} collective-permute-done((bf16[4096,128]{1,0:T(8,128)(2,1)}, bf16[4096,128]{1,0:T(8,128)(2,1)}, u32[]{:S(2)}, u32[]{:S(2)}) %collective-permute-start) | collective-permute-done | bytes 1048608 | tf_op jit(solution)/shard_map/ppermute | solution.py:41
  28.5 1.2 collective-permute-start.1
  29.7 14.6 %all-to-all-done.h_ref.x_ref = bf16[16,8,16,512]{3,2,1,0:T(8,128)(2,1)S(1)} async-done(((bf16[16,8,16,512]{3,2,1,0:T(8,128)(2,1)}), bf16[16,8,16,512]{3,2,1,0:T(8,128)(2,1)S(1)}, u32[]{:S(2)}, u32[]{:S(2)}) %all-to-all-start) | async-done | bytes 2097184 | tf_op jit(solution)/shard_map/all_to_all | solution.py:45
  44.3 2.9 %shard_map.42.own_ref.e_ref = bf16[256,512]{1,0:T(8,128)(2,1)S(1)} custom-call(bf16[16,8,16,512]{3,2,1,0:T(8,128)(2,1)S(1)} %all-to-all-done.h_ref.x_ref, bf16[4096,128]{1,0:T(8,128)(2,1)S(1)} %copy-done.1, bf16[4096,128]{1,0:T(8,128)(2,1)} %collective-permute-done.2.b_ref, bf16[4096,128]{1,0:T(8,128)(2,1)} %collective-permute-done.c_ref, ...), custom_call_target="tpu_custom_call" | custom-call | flops 1073741824 | bytes 6291456 | tf_op jit(solution)/shard_map/pallas_call | solution.py:240
  47.3 0.5 collective-permute-start.3
  47.7 2.5 %collective-permute-start.4 = (bf16[256,512]{1,0:T(8,128)(2,1)S(1)}, bf16[256,512]{1,0:T(8,128)(2,1)S(1)}, u32[]{:S(2)}, u32[]{:S(2)}) collective-permute-start(bf16[256,512]{1,0:T(8,128)(2,1)S(1)} %shard_map.42.own_ref.e_ref), channel_id=1, source_target_pairs={{0,1},{1,0},{2,3},{3,2},{4,5},{5,4},{6,7},{7,6},{8,9},{9,8},{10,11... | collective-permute-start | bytes 786440 | tf_op jit(solution)/shard_map/ppermute | solution.py:41
  50.2 1.2 shard_map.43
  51.4 1.0 copy-done.2
  52.4 1.7 %collective-permute-done.3.far_ref = bf16[256,512]{1,0:T(8,128)(2,1)S(1)} collective-permute-done((bf16[256,512]{1,0:T(8,128)(2,1)S(1)}, bf16[256,512]{1,0:T(8,128)(2,1)S(1)}, u32[]{:S(2)}, u32[]{:S(2)}) %collective-permute-start.3) | collective-permute-done | bytes 262176 | tf_op jit(solution)/shard_map/ppermute | solution.py:41
  54.1 3.6 %collective-permute-start.5 = (bf16[256,512]{1,0:T(8,128)(2,1)S(1)}, bf16[256,512]{1,0:T(8,128)(2,1)S(1)}, u32[]{:S(2)}, u32[]{:S(2)}) collective-permute-start(bf16[256,512]{1,0:T(8,128)(2,1)S(1)} %collective-permute-done.3.far_ref), channel_id=1, source_target_pairs={{0,1},{1,0},{2,3},{3,2},{4,5},{5,4},{6,7},{7,6},{8,9},{9,8},{10,11... | collective-permute-start | bytes 786440 | tf_op jit(solution)/shard_map/ppermute | solution.py:41
  57.7 1.9 %collective-permute-start.6 = (bf16[224,1536]{1,0:T(8,128)(2,1)}, bf16[224,1536]{1,0:T(8,128)(2,1)}, u32[]{:S(2)}, u32[]{:S(2)}) collective-permute-start(bf16[224,1536]{1,0:T(8,128)(2,1)} %get-tuple-element.33.refs_0_), channel_id=1, source_target_pairs={{0,8},{1,9},{2,10},{3,11},{4,12},{5,13},{6,14},{7,15},{8,0},{9,1},... | collective-permute-start | bytes 2064392 | tf_op jit(solution)/shard_map/ppermute | solution.py:41
  59.6 1.7 %shard_map.44 = (bf16[1024,512]{1,0:T(8,128)(2,1)S(1)}, f32[8,512]{1,0:T(8,128)S(1)}, bf16[256,1024]{1,0:T(8,128)(2,1)}) custom-call(bf16[256,512]{1,0:T(8,128)(2,1)S(1)} %shard_map.42.own_ref.e_ref, bf16[256,512]{1,0:T(8,128)(2,1)S(1)} %collective-permute-done.4.sib_ref, bf16[256,512]{1,0:T(8,128)(2,1)S(1)} %collective-permute-done.3.far_ref, ...), custom_call_target="tpu_custom_call" | custom-call | flops 268435456 | bytes 1048576 | tf_op jit(solution)/shard_map/pallas_call | solution.py:340
  61.3 1.0 copy-done.5
  62.2 4.3 %all-to-all-start.1 = ((bf16[16,16,1024]{2,1,0:T(8,128)(2,1)}), bf16[16,16,1024]{2,1,0:T(8,128)(2,1)S(1)}, u32[]{:S(2)}, u32[]{:S(2)}) async-start(bf16[16,16,1024]{2,1,0:T(8,128)(2,1)} %bitcast.1), calls=%async_computation.1 | async-start | bytes 1048576 | tf_op jit(solution)/shard_map/all_to_all | solution.py:45
  66.6 1.5 %collective-permute-start.10 = (bf16[224,2560]{1,0:T(8,128)(2,1)S(1)}, bf16[224,2560]{1,0:T(8,128)(2,1)}, u32[]{:S(2)}, u32[]{:S(2)}) collective-permute-start(bf16[224,2560]{1,0:T(8,128)(2,1)S(1)} %copy-done.3), channel_id=1, source_target_pairs={{0,8},{1,9},{2,10},{3,11},{4,12},{5,13},{6,14},{7,15},{8,0},{9,1},... | collective-permute-start | bytes 3440648 | tf_op jit(solution)/shard_map/ppermute | solution.py:41
  68.1 8.9 %all-to-all-done.1 = bf16[16,16,1024]{2,1,0:T(8,128)(2,1)S(1)} async-done(((bf16[16,16,1024]{2,1,0:T(8,128)(2,1)}), bf16[16,16,1024]{2,1,0:T(8,128)(2,1)S(1)}, u32[]{:S(2)}, u32[]{:S(2)}) %all-to-all-start.1) | async-done | bytes 524320 | tf_op jit(solution)/shard_map/all_to_all | solution.py:45
  77.0 0.9 shard_map.45
  77.9 3.0 %collective-permute-done.6.refs_2_ = bf16[224,1536]{1,0:T(8,128)(2,1)} collective-permute-done((bf16[224,1536]{1,0:T(8,128)(2,1)}, bf16[224,1536]{1,0:T(8,128)(2,1)}, u32[]{:S(2)}, u32[]{:S(2)}) %collective-permute-start.6) | collective-permute-done | bytes 688160 | tf_op jit(solution)/shard_map/ppermute | solution.py:41
  80.9 4.3 %all-to-all-start.2 = ((bf16[16,16,1024]{2,1,0:T(8,128)(2,1)}), bf16[16,16,1024]{2,1,0:T(8,128)(2,1)S(1)}, u32[]{:S(2)}, u32[]{:S(2)}) async-start(bf16[16,16,1024]{2,1,0:T(8,128)(2,1)} %bitcast.3), calls=%async_computation.2 | async-start | bytes 1048576 | tf_op jit(solution)/shard_map/all_to_all | solution.py:45
  85.2 10.1 %all-to-all-done.2 = bf16[16,16,1024]{2,1,0:T(8,128)(2,1)S(1)} async-done(((bf16[16,16,1024]{2,1,0:T(8,128)(2,1)}), bf16[16,16,1024]{2,1,0:T(8,128)(2,1)S(1)}, u32[]{:S(2)}, u32[]{:S(2)}) %all-to-all-start.2) | async-done | bytes 524320 | tf_op jit(solution)/shard_map/all_to_all | solution.py:45
  95.4 1.2 copy-done.6
  96.6 0.7 shard_map.46
  97.3 0.0 copy-start.7
  97.3 0.7 copy-done.7
  98.0 5.7 %all-to-all-start.3 = ((bf16[4,224,128]{2,1,0:T(8,128)(2,1)}), bf16[4,224,128]{2,1,0:T(8,128)(2,1)S(1)}, u32[]{:S(2)}, u32[]{:S(2)}) async-start(bf16[4,224,128]{2,1,0:T(8,128)(2,1)} %copy-done.7), calls=%async_computation.3 | async-start | bytes 458752 | tf_op jit(solution)/shard_map/all_to_all | solution.py:45
  103.6 3.9 %shard_map.47 = bf16[16,8,16,512]{3,2,1,0:T(8,128)(2,1)} custom-call(bf16[256,512]{1,0:T(8,128)(2,1)S(1)} %get-tuple-element.39.g_ref, bf16[4096,128]{1,0:T(8,128)(2,1)S(1)} %copy-done.1, bf16[4096,128]{1,0:T(8,128)(2,1)} %collective-permute-done.2.b_ref, bf16[4096,128]{1,0:T(8,128)(2,1)} %collective-permute-done.c_ref, ...), custom_call_target="tpu_custom_call" | custom-call | flops 1073741824 | bytes 6291456 | tf_op jit(solution)/shard_map/pallas_call | solution.py:257
  107.5 2.4 %all-to-all-done.3.refs_4_ = bf16[4,224,128]{2,1,0:T(8,128)(2,1)S(1)} async-done(((bf16[4,224,128]{2,1,0:T(8,128)(2,1)}), bf16[4,224,128]{2,1,0:T(8,128)(2,1)S(1)}, u32[]{:S(2)}, u32[]{:S(2)}) %all-to-all-start.3) | async-done | bytes 229408 | tf_op jit(solution)/shard_map/all_to_all | solution.py:45
  110.0 3.7 %all-to-all-start.4 = ((bf16[16,8,16,512]{3,2,1,0:T(8,128)(2,1)}), bf16[16,8,16,512]{3,2,1,0:T(8,128)(2,1)S(1)}, u32[]{:S(2)}, u32[]{:S(2)}) async-start(bf16[16,8,16,512]{3,2,1,0:T(8,128)(2,1)} %shard_map.47), calls=%async_computation.4 | async-start | bytes 4194304 | tf_op jit(solution)/shard_map/all_to_all | solution.py:45
  113.7 1.0 collective-permute-start.12
  114.6 0.1 collective-permute-start.13
  114.7 0.4 collective-permute-start.7
  115.2 0.1 collective-permute-start.8
  115.2 2.0 %collective-permute-done.12.refs_1_ = bf16[224,2560]{1,0:T(8,128)(2,1)S(1)} collective-permute-done((bf16[224,2560]{1,0:T(8,128)(2,1)}, bf16[224,2560]{1,0:T(8,128)(2,1)S(1)}, u32[]{:S(2)}, u32[]{:S(2)}) %collective-permute-start.12) | collective-permute-done | bytes 1146912 | tf_op jit(solution)/shard_map/ppermute | solution.py:41
  117.3 1.6 %collective-permute-done.13.refs_3_ = bf16[224,2560]{1,0:T(8,128)(2,1)S(1)} collective-permute-done((bf16[224,2560]{1,0:T(8,128)(2,1)}, bf16[224,2560]{1,0:T(8,128)(2,1)S(1)}, u32[]{:S(2)}, u32[]{:S(2)}) %collective-permute-start.13) | collective-permute-done | bytes 1146912 | tf_op jit(solution)/shard_map/ppermute | solution.py:41
  118.9 1.3 copy-done.4
  120.2 4.3 %shard_map.49.refs_2_ = bf16[2560,128]{1,0:T(8,128)(2,1)S(1)} custom-call(s32[1]{0:T(128)} %bitcast.me_ref, bf16[224,2560]{1,0:T(8,128)(2,1)S(1)} %copy-done.4, bf16[224,2560]{1,0:T(8,128)(2,1)S(1)} %collective-permute-done.12.refs_1_, bf16[224,2560]{1,0:T(8,128)(2,1)} %collective-permute-done.10.refs_2_, ...), custom_call_target="tpu_custom_call" | custom-call | flops 587202560 | bytes 4587520 | tf_op jit(solution)/shard_map/pallas_call | solution.py:285
  124.5 1.2 collective-permute-start.14
  125.7 3.0 %shard_map.48.refs_0_ = bf16[1536,128]{1,0:T(8,128)(2,1)S(1)} custom-call(s32[1]{0:T(128)} %bitcast.me_ref, bf16[224,1536]{1,0:T(8,128)(2,1)} %get-tuple-element.33.refs_0_, bf16[224,1536]{1,0:T(8,128)(2,1)S(1)} %collective-permute-done.7.refs_1_, bf16[224,1536]{1,0:T(8,128)(2,1)} %collective-permute-done.6.refs_2_, ...), custom_call_target="tpu_custom_call" | custom-call | flops 352321536 | bytes 2752512 | tf_op jit(solution)/shard_map/pallas_call | solution.py:285
  128.7 0.5 collective-permute-start.11
  129.2 19.8 %collective-permute-done.11.refs_1_ = bf16[1536,128]{1,0:T(8,128)(2,1)S(1)} collective-permute-done((bf16[1536,128]{1,0:T(8,128)(2,1)S(1)}, bf16[1536,128]{1,0:T(8,128)(2,1)S(1)}, u32[]{:S(2)}, u32[]{:S(2)}) %collective-permute-start.11) | collective-permute-done | bytes 393248 | tf_op jit(solution)/shard_map/ppermute | solution.py:41
  149.0 1.6 %shard_map.50 = f32[4096,128]{1,0:T(8,128)} custom-call(bf16[1536,128]{1,0:T(8,128)(2,1)S(1)} %shard_map.48.refs_0_, bf16[1536,128]{1,0:T(8,128)(2,1)S(1)} %collective-permute-done.11.refs_1_, bf16[2560,128]{1,0:T(8,128)(2,1)S(1)} %shard_map.49.refs_2_, bf16[2560,128]{1,0:T(8,128)(2,1)S(1)} %collective-permute-done.14.refs_3_), custom_call_target="tpu_custom_call" | custom-call | flops 524288 | bytes 4194304 | tf_op jit(solution)/shard_map/pallas_call | solution.py:302
  150.6 0.6 shard_map.51
  151.2 0.9 copy.4
  (22 shorter events, 0.1 us)
Async XLA Ops:
  0.6 27.9 %collective-permute-start = (bf16[4096,128]{1,0:T(8,128)(2,1)}, bf16[4096,128]{1,0:T(8,128)(2,1)}, u32[]{:S(2)}, u32[]{:S(2)}) collective-permute-start(bf16[4096,128]{1,0:T(8,128)(2,1)} %a_ref.3), channel_id=1, source_target_pairs={{0,72},{1,73},{2,74},{3,75},{4,76},{5,77},{6,78},{7,79},{8,64},{9,... | collective-permute-start | bytes 3145736 | tf_op jit(solution)/shard_map/ppermute | solution.py:41
  5.3 0.9 copy-start.8
  6.4 1.3 copy-start
  7.7 22.0 %copy-start.1 = (bf16[4096,128]{1,0:T(8,128)(2,1)S(1)}, bf16[4096,128]{1,0:T(8,128)(2,1)}, u32[]{:S(2)}) copy-start(bf16[4096,128]{1,0:T(8,128)(2,1)} %a_ref.3) | copy-start | bytes 3145732
  7.7 36.6 %all-to-all-start = ((bf16[16,8,16,512]{3,2,1,0:T(8,128)(2,1)}), bf16[16,8,16,512]{3,2,1,0:T(8,128)(2,1)S(1)}, u32[]{:S(2)}, u32[]{:S(2)}) async-start(bf16[16,8,16,512]{3,2,1,0:T(8,128)(2,1)} %copy-done), calls=%async_computation | async-start | bytes 4194304 | tf_op jit(solution)/shard_map/all_to_all | solution.py:45
  28.5 15.8 %collective-permute-start.1 = (bf16[4096,128]{1,0:T(8,128)(2,1)}, bf16[4096,128]{1,0:T(8,128)(2,1)}, u32[]{:S(2)}, u32[]{:S(2)}) collective-permute-start(bf16[4096,128]{1,0:T(8,128)(2,1)} %collective-permute-done.c_ref), channel_id=1, source_target_pairs={{0,1},{1,0},{2,3},{3,2},{4,5},{5,4},{6,7},{7,6},{8,9},{9,8},{10,11... | collective-permute-start | bytes 3145736 | tf_op jit(solution)/shard_map/ppermute | solution.py:41
  29.7 14.6 %collective-permute-start.2 = (bf16[4096,128]{1,0:T(8,128)(2,1)S(1)}, bf16[4096,128]{1,0:T(8,128)(2,1)}, u32[]{:S(2)}, u32[]{:S(2)}) collective-permute-start(bf16[4096,128]{1,0:T(8,128)(2,1)S(1)} %copy-done.1), channel_id=1, source_target_pairs={{0,1},{1,0},{2,3},{3,2},{4,5},{5,4},{6,7},{7,6},{8,9},{9,8},{10,11... | collective-permute-start | bytes 3145736 | tf_op jit(solution)/shard_map/ppermute | solution.py:41
  47.3 6.8 %collective-permute-start.3 = (bf16[256,512]{1,0:T(8,128)(2,1)S(1)}, bf16[256,512]{1,0:T(8,128)(2,1)S(1)}, u32[]{:S(2)}, u32[]{:S(2)}) collective-permute-start(bf16[256,512]{1,0:T(8,128)(2,1)S(1)} %shard_map.42.own_ref.e_ref), channel_id=1, source_target_pairs={{0,8},{1,9},{2,10},{3,11},{4,12},{5,13},{6,14},{7,15},{8,0},{9,1},... | collective-permute-start | bytes 786440 | tf_op jit(solution)/shard_map/ppermute | solution.py:41
  47.7 11.8 %collective-permute-start.4 = (bf16[256,512]{1,0:T(8,128)(2,1)S(1)}, bf16[256,512]{1,0:T(8,128)(2,1)S(1)}, u32[]{:S(2)}, u32[]{:S(2)}) collective-permute-start(bf16[256,512]{1,0:T(8,128)(2,1)S(1)} %shard_map.42.own_ref.e_ref), channel_id=1, source_target_pairs={{0,1},{1,0},{2,3},{3,2},{4,5},{5,4},{6,7},{7,6},{8,9},{9,8},{10,11... | collective-permute-start | bytes 786440 | tf_op jit(solution)/shard_map/ppermute | solution.py:41
  51.4 1.0 copy-start.2
  54.1 12.4 %copy-start.3 = (bf16[224,2560]{1,0:T(8,128)(2,1)S(1)}, bf16[224,2560]{1,0:T(8,128)(2,1)}, u32[]{:S(2)}) copy-start(bf16[224,2560]{1,0:T(8,128)(2,1)} %copy-done.2) | copy-start | bytes 3440644
  54.1 5.5 %collective-permute-start.5 = (bf16[256,512]{1,0:T(8,128)(2,1)S(1)}, bf16[256,512]{1,0:T(8,128)(2,1)S(1)}, u32[]{:S(2)}, u32[]{:S(2)}) collective-permute-start(bf16[256,512]{1,0:T(8,128)(2,1)S(1)} %collective-permute-done.3.far_ref), channel_id=1, source_target_pairs={{0,1},{1,0},{2,3},{3,2},{4,5},{5,4},{6,7},{7,6},{8,9},{9,8},{10,11... | collective-permute-start | bytes 786440 | tf_op jit(solution)/shard_map/ppermute | solution.py:41
  57.7 8.9 %collective-permute-start.9 = (bf16[256,512]{1,0:T(8,128)(2,1)S(1)}, bf16[256,512]{1,0:T(8,128)(2,1)S(1)}, u32[]{:S(2)}, u32[]{:S(2)}) collective-permute-start(bf16[256,512]{1,0:T(8,128)(2,1)S(1)} %shard_map.42.own_ref.e_ref), channel_id=1, source_target_pairs={{0,64},{1,65},{2,66},{3,67},{4,68},{5,69},{6,70},{7,71},{8,72},{9,... | collective-permute-start | bytes 786440 | tf_op jit(solution)/shard_map/ppermute | solution.py:41
  57.7 23.2 %collective-permute-start.6 = (bf16[224,1536]{1,0:T(8,128)(2,1)}, bf16[224,1536]{1,0:T(8,128)(2,1)}, u32[]{:S(2)}, u32[]{:S(2)}) collective-permute-start(bf16[224,1536]{1,0:T(8,128)(2,1)} %get-tuple-element.33.refs_0_), channel_id=1, source_target_pairs={{0,8},{1,9},{2,10},{3,11},{4,12},{5,13},{6,14},{7,15},{8,0},{9,1},... | collective-permute-start | bytes 2064392 | tf_op jit(solution)/shard_map/ppermute | solution.py:41
  61.3 1.0 copy-start.5
  62.2 14.8 %all-to-all-start.1 = ((bf16[16,16,1024]{2,1,0:T(8,128)(2,1)}), bf16[16,16,1024]{2,1,0:T(8,128)(2,1)S(1)}, u32[]{:S(2)}, u32[]{:S(2)}) async-start(bf16[16,16,1024]{2,1,0:T(8,128)(2,1)} %bitcast.1), calls=%async_computation.1 | async-start | bytes 1048576 | tf_op jit(solution)/shard_map/all_to_all | solution.py:45
  66.6 41.0 %collective-permute-start.10 = (bf16[224,2560]{1,0:T(8,128)(2,1)S(1)}, bf16[224,2560]{1,0:T(8,128)(2,1)}, u32[]{:S(2)}, u32[]{:S(2)}) collective-permute-start(bf16[224,2560]{1,0:T(8,128)(2,1)S(1)} %copy-done.3), channel_id=1, source_target_pairs={{0,8},{1,9},{2,10},{3,11},{4,12},{5,13},{6,14},{7,15},{8,0},{9,1},... | collective-permute-start | bytes 3440648 | tf_op jit(solution)/shard_map/ppermute | solution.py:41
  80.9 14.5 %all-to-all-start.2 = ((bf16[16,16,1024]{2,1,0:T(8,128)(2,1)}), bf16[16,16,1024]{2,1,0:T(8,128)(2,1)S(1)}, u32[]{:S(2)}, u32[]{:S(2)}) async-start(bf16[16,16,1024]{2,1,0:T(8,128)(2,1)} %bitcast.3), calls=%async_computation.2 | async-start | bytes 1048576 | tf_op jit(solution)/shard_map/all_to_all | solution.py:45
  95.4 1.2 copy-start.6
  97.3 0.7 copy-start.7
  98.0 12.0 %all-to-all-start.3 = ((bf16[4,224,128]{2,1,0:T(8,128)(2,1)}), bf16[4,224,128]{2,1,0:T(8,128)(2,1)S(1)}, u32[]{:S(2)}, u32[]{:S(2)}) async-start(bf16[4,224,128]{2,1,0:T(8,128)(2,1)} %copy-done.7), calls=%async_computation.3 | async-start | bytes 458752 | tf_op jit(solution)/shard_map/all_to_all | solution.py:45
  110.0 40.6 %all-to-all-start.4 = ((bf16[16,8,16,512]{3,2,1,0:T(8,128)(2,1)}), bf16[16,8,16,512]{3,2,1,0:T(8,128)(2,1)S(1)}, u32[]{:S(2)}, u32[]{:S(2)}) async-start(bf16[16,8,16,512]{3,2,1,0:T(8,128)(2,1)} %shard_map.47), calls=%async_computation.4 | async-start | bytes 4194304 | tf_op jit(solution)/shard_map/all_to_all | solution.py:45
  113.7 3.6 %collective-permute-start.12 = (bf16[224,2560]{1,0:T(8,128)(2,1)}, bf16[224,2560]{1,0:T(8,128)(2,1)S(1)}, u32[]{:S(2)}, u32[]{:S(2)}) collective-permute-start(bf16[224,2560]{1,0:T(8,128)(2,1)} %copy-done.2), channel_id=1, source_target_pairs={{0,1},{1,0},{2,3},{3,2},{4,5},{5,4},{6,7},{7,6},{8,9},{9,8},{10,11... | collective-permute-start | bytes 3440648 | tf_op jit(solution)/shard_map/ppermute | solution.py:41
  114.6 4.3 %collective-permute-start.13 = (bf16[224,2560]{1,0:T(8,128)(2,1)}, bf16[224,2560]{1,0:T(8,128)(2,1)S(1)}, u32[]{:S(2)}, u32[]{:S(2)}) collective-permute-start(bf16[224,2560]{1,0:T(8,128)(2,1)} %collective-permute-done.10.refs_2_), channel_id=1, source_target_pairs={{0,1},{1,0},{2,3},{3,2},{4,5},{5,4},{6,7},{7,6},{8,9},{9,8},{10,11... | collective-permute-start | bytes 3440648 | tf_op jit(solution)/shard_map/ppermute | solution.py:41
  114.7 10.9 %collective-permute-start.7 = (bf16[224,1536]{1,0:T(8,128)(2,1)}, bf16[224,1536]{1,0:T(8,128)(2,1)S(1)}, u32[]{:S(2)}, u32[]{:S(2)}) collective-permute-start(bf16[224,1536]{1,0:T(8,128)(2,1)} %get-tuple-element.33.refs_0_), channel_id=1, source_target_pairs={{0,1},{1,0},{2,3},{3,2},{4,5},{5,4},{6,7},{7,6},{8,9},{9,8},{10,11... | collective-permute-start | bytes 2064392 | tf_op jit(solution)/shard_map/ppermute | solution.py:41
  115.2 10.5 %collective-permute-start.8 = (bf16[224,1536]{1,0:T(8,128)(2,1)}, bf16[224,1536]{1,0:T(8,128)(2,1)S(1)}, u32[]{:S(2)}, u32[]{:S(2)}) collective-permute-start(bf16[224,1536]{1,0:T(8,128)(2,1)} %collective-permute-done.6.refs_2_), channel_id=1, source_target_pairs={{0,1},{1,0},{2,3},{3,2},{4,5},{5,4},{6,7},{7,6},{8,9},{9,8},{10,11... | collective-permute-start | bytes 2064392 | tf_op jit(solution)/shard_map/ppermute | solution.py:41
  118.9 1.3 copy-start.4
  124.5 24.5 %collective-permute-start.14 = (bf16[2560,128]{1,0:T(8,128)(2,1)S(1)}, bf16[2560,128]{1,0:T(8,128)(2,1)S(1)}, u32[]{:S(2)}, u32[]{:S(2)}) collective-permute-start(bf16[2560,128]{1,0:T(8,128)(2,1)S(1)} %shard_map.49.refs_2_), channel_id=1, source_target_pairs={{0,64},{1,65},{2,66},{3,67},{4,68},{5,69},{6,70},{7,71},{8,72},{9,... | collective-permute-start | bytes 1966088 | tf_op jit(solution)/shard_map/ppermute | solution.py:41
  128.7 20.2 %collective-permute-start.11 = (bf16[1536,128]{1,0:T(8,128)(2,1)S(1)}, bf16[1536,128]{1,0:T(8,128)(2,1)S(1)}, u32[]{:S(2)}, u32[]{:S(2)}) collective-permute-start(bf16[1536,128]{1,0:T(8,128)(2,1)S(1)} %shard_map.48.refs_0_), channel_id=1, source_target_pairs={{0,64},{1,65},{2,66},{3,67},{4,68},{5,69},{6,70},{7,71},{8,72},{9,... | collective-permute-start | bytes 1179656 | tf_op jit(solution)/shard_map/ppermute | solution.py:41

commit v13 on v12

--- a/solution.py
+++ b/solution.py
@@ -329,7 +329,7 @@
     mine = embed(plane, weights)
     from_sib = swap(mine, c=1)
     from_far = swap(mine, z=1)
-    split = (3 * width // 8, 5 * width // 8)
+    split = (width // 4, 3 * width // 4)
     from_far, *h_own = lax.optimization_barrier((from_far, *compact(plane, rows, split)))
     from_far_sib = swap(from_far, c=1)
     partner = swap(mine, view=1)
@@ -361,8 +361,6 @@
         compiler_params=params(1),
         cost_estimate=cost(gram.size, 4 * gram.size),
     )(gram)
-    gram, h_far[0], *late = lax.optimization_barrier((gram, h_far[0], *h_own))
-    h_sib = [swap(block, c=1) for block in late]
     gram = exchange(gram, "yx")
 
     d = lax.axis_index("dp")
@@ -388,7 +386,8 @@
     runs = exchange(runs, "zc")
 
     h_part = hidden_terms(grad, weights)
-    h_part, h_far[1], runs = lax.optimization_barrier((h_part, h_far[1], runs))
+    h_part, runs, *h_far = lax.optimization_barrier((h_part, runs, *h_far))
+    h_sib = [swap(block, c=1) for block in h_own]
     pieces = exchange(h_part, "yx")
 
     parts = [

time: 153 us -> 149 us (0.974)
  waiting for transfers between devices: 78.1 us -> 62.4 us
  blocking collectives: 0 us -> 15.5 us
  starting transfers between devices: 43.9 us -> 41.9 us
    all_to_all x0 -> x1, blocking collectives: none -> 15.5 us  [exchange(): lax.all_to_all(blocks, 'dp', 0, 0, tiled=True, axis_index_groups=groups(a...]
    all_to_all x5 -> x4, waiting for transfers between devices: 36.1 us -> 25.8 us  [exchange(): lax.all_to_all(blocks, 'dp', 0, 0, tiled=True, axis_index_groups=groups(a...]
    ppermute x15, waiting for transfers between devices: 42 us -> 36.6 us  [swap(): return lax.ppermute(block, ('view', 'dp'), route)]
    all_to_all x5 -> x4, starting transfers between devices: 24.8 us -> 21.3 us  [exchange(): lax.all_to_all(blocks, 'dp', 0, 0, tiled=True, axis_index_groups=groups(a...]
    ppermute x15, starting transfers between devices: 19 us -> 20.7 us  [swap(): return lax.ppermute(block, ('view', 'dp'), route)]
    unnamed x19 -> x25, local copies, waits for them, and re-layouts: 8.29 us -> 7.15 us
  transfers between devices with their start and end apart: 20 -> 19, of which waited for: 10 -> 10; matrix products, arithmetic and copies ran while one was open for 0% -> 0% of each run, Pallas kernels for 12% -> 11%
where the time goes in v13:
time: 149 us; the launch traced here: 148 us
  waiting for transfers between devices  62.4 us (42%)
  starting transfers between devices  41.9 us (28%)
  Pallas kernels  20.3 us (14%)
  blocking collectives  15.5 us (10%)
  local copies, waits for them, and re-layouts  7.15 us (5%)
    ppermute x15, waiting for transfers between devices, swap(): return lax.ppermute(block, ('view', 'dp'), route)  36.6 us
    all_to_all x4, waiting for transfers between devices, exchange(): lax.all_to_all(blocks, 'dp', 0, 0, tiled=True, axis_index_groups=groups(a...  25.8 us
    all_to_all x4, starting transfers between devices, exchange(): lax.all_to_all(blocks, 'dp', 0, 0, tiled=True, axis_index_groups=groups(a...  21.3 us
    ppermute x15, starting transfers between devices, swap(): return lax.ppermute(block, ('view', 'dp'), route)  20.7 us
    all_to_all x1, blocking collectives, exchange(): lax.all_to_all(blocks, 'dp', 0, 0, tiled=True, axis_index_groups=groups(a...  15.5 us
    unnamed x25, local copies, waits for them, and re-layouts  7.15 us
    pallas_call x2, Pallas kernels, weight_terms(): pl.pallas_call(weight_kernel, grid=(width // TILE,), in_specs=[SMEM] + [p...  6.9 us
    pallas_call x1, Pallas kernels, hidden_terms(): pl.pallas_call(hidden_kernel, grid=(width // TILE // 4,), in_specs=[whole...  3.85 us
  transfers between devices with their start and end apart: 19, of which 10 were waited for; matrix products, arithmetic and copies ran while one was open for 0% of the time, Pallas kernels for 11%

profile of v13, /device:TPU:1, one launch (start us, length us, event | category | flops | bytes accessed | tf_op | source)
XLA Modules:
  0.0 148.0 jit_solution(1138998501059399733)
XLA Ops:
  0.6 4.7 %collective-permute-start = (bf16[4096,128]{1,0:T(8,128)(2,1)}, bf16[4096,128]{1,0:T(8,128)(2,1)}, u32[]{:S(2)}, u32[]{:S(2)}) collective-permute-start(bf16[4096,128]{1,0:T(8,128)(2,1)} %a_ref.3), channel_id=1, source_target_pairs={{0,72},{1,73},{2,74},{3,75},{4,76},{5,77},{6,78},{7,79},{8,64},{9,... | collective-permute-start | bytes 3145736 | tf_op jit(solution)/shard_map/ppermute | solution.py:41
  5.3 0.9 copy-done.11
  6.2 0.2 shard_map.41
  6.4 1.3 copy-done
  7.7 6.9 %all-to-all-start = ((bf16[16,8,16,512]{3,2,1,0:T(8,128)(2,1)}), bf16[16,8,16,512]{3,2,1,0:T(8,128)(2,1)S(1)}, u32[]{:S(2)}, u32[]{:S(2)}) async-start(bf16[16,8,16,512]{3,2,1,0:T(8,128)(2,1)} %copy-done), calls=%async_computation | async-start | bytes 4194304 | tf_op jit(solution)/shard_map/all_to_all | solution.py:45
  14.6 13.9 %collective-permute-done.c_ref = bf16[4096,128]{1,0:T(8,128)(2,1)} collective-permute-done((bf16[4096,128]{1,0:T(8,128)(2,1)}, bf16[4096,128]{1,0:T(8,128)(2,1)}, u32[]{:S(2)}, u32[]{:S(2)}) %collective-permute-start) | collective-permute-done | bytes 1048608 | tf_op jit(solution)/shard_map/ppermute | solution.py:41
  28.5 1.2 collective-permute-start.1
  29.7 14.6 %all-to-all-done.h_ref.x_ref = bf16[16,8,16,512]{3,2,1,0:T(8,128)(2,1)S(1)} async-done(((bf16[16,8,16,512]{3,2,1,0:T(8,128)(2,1)}), bf16[16,8,16,512]{3,2,1,0:T(8,128)(2,1)S(1)}, u32[]{:S(2)}, u32[]{:S(2)}) %all-to-all-start) | async-done | bytes 2097184 | tf_op jit(solution)/shard_map/all_to_all | solution.py:45
  44.3 2.9 %shard_map.42.own_ref.e_ref = bf16[256,512]{1,0:T(8,128)(2,1)S(1)} custom-call(bf16[16,8,16,512]{3,2,1,0:T(8,128)(2,1)S(1)} %all-to-all-done.h_ref.x_ref, bf16[4096,128]{1,0:T(8,128)(2,1)S(1)} %copy-done.1, bf16[4096,128]{1,0:T(8,128)(2,1)} %collective-permute-done.2.b_ref, bf16[4096,128]{1,0:T(8,128)(2,1)} %collective-permute-done.c_ref, ...), custom_call_target="tpu_custom_call" | custom-call | flops 1073741824 | bytes 6291456 | tf_op jit(solution)/shard_map/pallas_call | solution.py:240
  47.3 0.5 collective-permute-start.3
  47.7 1.0 collective-permute-start.7
  48.7 2.7 %collective-permute-start.5 = (bf16[256,512]{1,0:T(8,128)(2,1)S(1)}, bf16[256,512]{1,0:T(8,128)(2,1)S(1)}, u32[]{:S(2)}, u32[]{:S(2)}) collective-permute-start(bf16[256,512]{1,0:T(8,128)(2,1)S(1)} %shard_map.42.own_ref.e_ref), channel_id=1, source_target_pairs={{0,1},{1,0},{2,3},{3,2},{4,5},{5,4},{6,7},{7,6},{8,9},{9,8},{10,11... | collective-permute-start | bytes 786440 | tf_op jit(solution)/shard_map/ppermute | solution.py:41
  51.4 1.7 %shard_map.43 = (bf16[224,1024]{1,0:T(8,128)(2,1)S(1)}, bf16[224,3072]{1,0:T(8,128)(2,1)}) custom-call(bf16[16,8,16,512]{3,2,1,0:T(8,128)(2,1)S(1)} %all-to-all-done.h_ref.x_ref), custom_call_target="tpu_custom_call" | custom-call | flops 4194304 | bytes 4194304 | tf_op jit(solution)/shard_map/pallas_call | solution.py:110
  53.2 0.9 collective-permute-done.3.far_ref
  54.1 6.3 %collective-permute-start.6 = (bf16[256,512]{1,0:T(8,128)(2,1)S(1)}, bf16[256,512]{1,0:T(8,128)(2,1)S(1)}, u32[]{:S(2)}, u32[]{:S(2)}) collective-permute-start(bf16[256,512]{1,0:T(8,128)(2,1)S(1)} %collective-permute-done.3.far_ref), channel_id=1, source_target_pairs={{0,1},{1,0},{2,3},{3,2},{4,5},{5,4},{6,7},{7,6},{8,9},{9,8},{10,11... | collective-permute-start | bytes 786440 | tf_op jit(solution)/shard_map/ppermute | solution.py:41
  60.4 0.7 copy-done.6
  61.1 0.3 collective-permute-start.9
  61.4 0.1 collective-permute-done.6.far_sib_ref
  61.6 0.9 shard_map.44
  62.5 15.5 %all_to_all.37 = bf16[16,16,1024]{2,1,0:T(8,128)(2,1)S(1)} all-to-all(bf16[16,16,1024]{2,1,0:T(8,128)(2,1)S(1)} %bitcast.7), channel_id=1, replica_groups={{0,2,4,6,16,18,20,22,32,34,36,38,48,50,52,54},{1,3,5,7,17,19,21,23,33,3..., dimensions={0} | all-to-all | bytes 1048576 | tf_op jit(solution)/shard_map/all_to_all | solution.py:45
  78.0 0.9 shard_map.45
  78.9 3.6 %all-to-all-start.2 = ((bf16[16,16,1024]{2,1,0:T(8,128)(2,1)}), bf16[16,16,1024]{2,1,0:T(8,128)(2,1)S(1)}, u32[]{:S(2)}, u32[]{:S(2)}) async-start(bf16[16,16,1024]{2,1,0:T(8,128)(2,1)} %bitcast.3), calls=%async_computation.2 | async-start | bytes 1048576 | tf_op jit(solution)/shard_map/all_to_all | solution.py:45
  82.4 0.9 collective-permute-start.8
  83.3 8.2 %all-to-all-done.2 = bf16[16,16,1024]{2,1,0:T(8,128)(2,1)S(1)} async-done(((bf16[16,16,1024]{2,1,0:T(8,128)(2,1)}), bf16[16,16,1024]{2,1,0:T(8,128)(2,1)S(1)}, u32[]{:S(2)}, u32[]{:S(2)}) %all-to-all-start.2) | async-done | bytes 524320 | tf_op jit(solution)/shard_map/all_to_all | solution.py:45
  91.5 0.9 copy-done.7
  92.5 0.7 shard_map.46
  93.2 0.7 copy-done.8
  93.9 0.7 copy-done.10
  94.5 7.1 %all-to-all-start.3 = ((bf16[4,224,128]{2,1,0:T(8,128)(2,1)}), bf16[4,224,128]{2,1,0:T(8,128)(2,1)S(1)}, u32[]{:S(2)}, u32[]{:S(2)}) async-start(bf16[4,224,128]{2,1,0:T(8,128)(2,1)} %copy-done.10), calls=%async_computation.3 | async-start | bytes 458752 | tf_op jit(solution)/shard_map/all_to_all | solution.py:45
  101.6 0.1 collective-permute-start.12
  101.8 0.9 copy-done.9
  102.7 3.9 %shard_map.47 = bf16[16,8,16,512]{3,2,1,0:T(8,128)(2,1)} custom-call(bf16[256,512]{1,0:T(8,128)(2,1)S(1)} %copy-done.9, bf16[4096,128]{1,0:T(8,128)(2,1)S(1)} %copy-done.1, bf16[4096,128]{1,0:T(8,128)(2,1)} %collective-permute-done.2.b_ref, bf16[4096,128]{1,0:T(8,128)(2,1)} %collective-permute-done.c_ref, bf16[4096,128]{1,0:T(8,128)(2,1)} %collective-permute-done.1.d_ref), custom_call_target="tpu_custom_call" | custom-call | flops 1073741824 | bytes 6291456 | tf_op jit(solution)/shard_map/pallas_call | solution.py:257
  106.6 1.4 all-to-all-done.3.refs_4_
  108.0 0.9 collective-permute-start.13
  108.8 3.7 %all-to-all-start.4 = ((bf16[16,8,16,512]{3,2,1,0:T(8,128)(2,1)}), bf16[16,8,16,512]{3,2,1,0:T(8,128)(2,1)S(1)}, u32[]{:S(2)}, u32[]{:S(2)}) async-start(bf16[16,8,16,512]{3,2,1,0:T(8,128)(2,1)} %shard_map.47), calls=%async_computation.4 | async-start | bytes 4194304 | tf_op jit(solution)/shard_map/all_to_all | solution.py:45
  112.6 5.8 %shard_map.49.refs_2_ = bf16[3072,128]{1,0:T(8,128)(2,1)S(1)} custom-call(s32[1]{0:T(128)} %bitcast.me_ref, bf16[224,3072]{1,0:T(8,128)(2,1)} %get-tuple-element.35.refs_0_, bf16[224,3072]{1,0:T(8,128)(2,1)} %collective-permute-done.12.refs_1_, bf16[224,3072]{1,0:T(8,128)(2,1)} %collective-permute-done.9.refs_2_, ...), custom_call_target="tpu_custom_call" | custom-call | flops 704643072 | bytes 5505024 | tf_op jit(solution)/shard_map/pallas_call | solution.py:285
  118.4 0.8 collective-permute-start.14
  119.2 0.3 collective-permute-start.4
  119.5 0.2 collective-permute-start.10
  119.8 1.3 collective-permute-done.4.refs_1_
  121.1 0.7 collective-permute-done.10.refs_3_
  121.7 1.1 shard_map.48.refs_0_
  122.8 0.8 collective-permute-start.11
  123.6 19.7 %collective-permute-done.11.refs_1_ = bf16[1024,128]{1,0:T(8,128)(2,1)S(1)} collective-permute-done((bf16[1024,128]{1,0:T(8,128)(2,1)S(1)}, bf16[1024,128]{1,0:T(8,128)(2,1)S(1)}, u32[]{:S(2)}, u32[]{:S(2)}) %collective-permute-start.11) | collective-permute-done | bytes 262176 | tf_op jit(solution)/shard_map/ppermute | solution.py:41
  143.3 1.6 %shard_map.50 = f32[4096,128]{1,0:T(8,128)} custom-call(bf16[1024,128]{1,0:T(8,128)(2,1)S(1)} %shard_map.48.refs_0_, bf16[1024,128]{1,0:T(8,128)(2,1)S(1)} %collective-permute-done.11.refs_1_, bf16[3072,128]{1,0:T(8,128)(2,1)S(1)} %shard_map.49.refs_2_, bf16[3072,128]{1,0:T(8,128)(2,1)S(1)} %collective-permute-done.14.refs_3_), custom_call_target="tpu_custom_call" | custom-call | flops 524288 | bytes 4194304 | tf_op jit(solution)/shard_map/pallas_call | solution.py:302
  144.9 1.6 %all-to-all-done.4.x_ref = bf16[16,8,16,512]{3,2,1,0:T(8,128)(2,1)S(1)} async-done(((bf16[16,8,16,512]{3,2,1,0:T(8,128)(2,1)}), bf16[16,8,16,512]{3,2,1,0:T(8,128)(2,1)S(1)}, u32[]{:S(2)}, u32[]{:S(2)}) %all-to-all-start.4) | async-done | bytes 2097184 | tf_op jit(solution)/shard_map/all_to_all | solution.py:45
  146.5 0.6 shard_map.51
  147.1 0.9 copy.4
  (27 shorter events, 0.1 us)
Async XLA Ops:
  0.6 27.9 %collective-permute-start = (bf16[4096,128]{1,0:T(8,128)(2,1)}, bf16[4096,128]{1,0:T(8,128)(2,1)}, u32[]{:S(2)}, u32[]{:S(2)}) collective-permute-start(bf16[4096,128]{1,0:T(8,128)(2,1)} %a_ref.3), channel_id=1, source_target_pairs={{0,72},{1,73},{2,74},{3,75},{4,76},{5,77},{6,78},{7,79},{8,64},{9,... | collective-permute-start | bytes 3145736 | tf_op jit(solution)/shard_map/ppermute | solution.py:41
  5.3 0.9 copy-start.11
  6.4 1.3 copy-start
  7.7 22.0 %copy-start.1 = (bf16[4096,128]{1,0:T(8,128)(2,1)S(1)}, bf16[4096,128]{1,0:T(8,128)(2,1)}, u32[]{:S(2)}) copy-start(bf16[4096,128]{1,0:T(8,128)(2,1)} %a_ref.3) | copy-start | bytes 3145732
  7.7 36.6 %all-to-all-start = ((bf16[16,8,16,512]{3,2,1,0:T(8,128)(2,1)}), bf16[16,8,16,512]{3,2,1,0:T(8,128)(2,1)S(1)}, u32[]{:S(2)}, u32[]{:S(2)}) async-start(bf16[16,8,16,512]{3,2,1,0:T(8,128)(2,1)} %copy-done), calls=%async_computation | async-start | bytes 4194304 | tf_op jit(solution)/shard_map/all_to_all | solution.py:45
  28.5 15.8 %collective-permute-start.1 = (bf16[4096,128]{1,0:T(8,128)(2,1)}, bf16[4096,128]{1,0:T(8,128)(2,1)}, u32[]{:S(2)}, u32[]{:S(2)}) collective-permute-start(bf16[4096,128]{1,0:T(8,128)(2,1)} %collective-permute-done.c_ref), channel_id=1, source_target_pairs={{0,1},{1,0},{2,3},{3,2},{4,5},{5,4},{6,7},{7,6},{8,9},{9,8},{10,11... | collective-permute-start | bytes 3145736 | tf_op jit(solution)/shard_map/ppermute | solution.py:41
  29.7 14.6 %collective-permute-start.2 = (bf16[4096,128]{1,0:T(8,128)(2,1)S(1)}, bf16[4096,128]{1,0:T(8,128)(2,1)}, u32[]{:S(2)}, u32[]{:S(2)}) collective-permute-start(bf16[4096,128]{1,0:T(8,128)(2,1)S(1)} %copy-done.1), channel_id=1, source_target_pairs={{0,1},{1,0},{2,3},{3,2},{4,5},{5,4},{6,7},{7,6},{8,9},{9,8},{10,11... | collective-permute-start | bytes 3145736 | tf_op jit(solution)/shard_map/ppermute | solution.py:41
  47.3 6.8 %collective-permute-start.3 = (bf16[256,512]{1,0:T(8,128)(2,1)S(1)}, bf16[256,512]{1,0:T(8,128)(2,1)S(1)}, u32[]{:S(2)}, u32[]{:S(2)}) collective-permute-start(bf16[256,512]{1,0:T(8,128)(2,1)S(1)} %shard_map.42.own_ref.e_ref), channel_id=1, source_target_pairs={{0,8},{1,9},{2,10},{3,11},{4,12},{5,13},{6,14},{7,15},{8,0},{9,1},... | collective-permute-start | bytes 786440 | tf_op jit(solution)/shard_map/ppermute | solution.py:41
  47.7 12.7 %collective-permute-start.7 = (bf16[256,512]{1,0:T(8,128)(2,1)S(1)}, bf16[256,512]{1,0:T(8,128)(2,1)S(1)}, u32[]{:S(2)}, u32[]{:S(2)}) collective-permute-start(bf16[256,512]{1,0:T(8,128)(2,1)S(1)} %shard_map.42.own_ref.e_ref), channel_id=1, source_target_pairs={{0,64},{1,65},{2,66},{3,67},{4,68},{5,69},{6,70},{7,71},{8,72},{9,... | collective-permute-start | bytes 786440 | tf_op jit(solution)/shard_map/ppermute | solution.py:41
  48.7 12.7 %collective-permute-start.5 = (bf16[256,512]{1,0:T(8,128)(2,1)S(1)}, bf16[256,512]{1,0:T(8,128)(2,1)S(1)}, u32[]{:S(2)}, u32[]{:S(2)}) collective-permute-start(bf16[256,512]{1,0:T(8,128)(2,1)S(1)} %shard_map.42.own_ref.e_ref), channel_id=1, source_target_pairs={{0,1},{1,0},{2,3},{3,2},{4,5},{5,4},{6,7},{7,6},{8,9},{9,8},{10,11... | collective-permute-start | bytes 786440 | tf_op jit(solution)/shard_map/ppermute | solution.py:41
  53.2 25.7 %copy-start.2 = (bf16[224,1024]{1,0:T(8,128)(2,1)}, bf16[224,1024]{1,0:T(8,128)(2,1)S(1)}, u32[]{:S(2)}) copy-start(bf16[224,1024]{1,0:T(8,128)(2,1)S(1)} %get-tuple-element.34.refs_0_) | copy-start | bytes 1376260
  54.1 7.5 %collective-permute-start.6 = (bf16[256,512]{1,0:T(8,128)(2,1)S(1)}, bf16[256,512]{1,0:T(8,128)(2,1)S(1)}, u32[]{:S(2)}, u32[]{:S(2)}) collective-permute-start(bf16[256,512]{1,0:T(8,128)(2,1)S(1)} %collective-permute-done.3.far_ref), channel_id=1, source_target_pairs={{0,1},{1,0},{2,3},{3,2},{4,5},{5,4},{6,7},{7,6},{8,9},{9,8},{10,11... | collective-permute-start | bytes 786440 | tf_op jit(solution)/shard_map/ppermute | solution.py:41
  60.4 0.7 copy-start.6
  61.1 45.4 %collective-permute-start.9 = (bf16[224,3072]{1,0:T(8,128)(2,1)}, bf16[224,3072]{1,0:T(8,128)(2,1)}, u32[]{:S(2)}, u32[]{:S(2)}) collective-permute-start(bf16[224,3072]{1,0:T(8,128)(2,1)} %get-tuple-element.35.refs_0_), channel_id=1, source_target_pairs={{0,8},{1,9},{2,10},{3,11},{4,12},{5,13},{6,14},{7,15},{8,0},{9,1},... | collective-permute-start | bytes 4128776 | tf_op jit(solution)/shard_map/ppermute | solution.py:41
  78.9 12.7 %all-to-all-start.2 = ((bf16[16,16,1024]{2,1,0:T(8,128)(2,1)}), bf16[16,16,1024]{2,1,0:T(8,128)(2,1)S(1)}, u32[]{:S(2)}, u32[]{:S(2)}) async-start(bf16[16,16,1024]{2,1,0:T(8,128)(2,1)} %bitcast.3), calls=%async_computation.2 | async-start | bytes 1048576 | tf_op jit(solution)/shard_map/all_to_all | solution.py:45
  82.4 24.1 %collective-permute-start.8 = (bf16[224,1024]{1,0:T(8,128)(2,1)}, bf16[224,1024]{1,0:T(8,128)(2,1)S(1)}, u32[]{:S(2)}, u32[]{:S(2)}) collective-permute-start(bf16[224,1024]{1,0:T(8,128)(2,1)} %copy-done.2), channel_id=1, source_target_pairs={{0,8},{1,9},{2,10},{3,11},{4,12},{5,13},{6,14},{7,15},{8,0},{9,1},... | collective-permute-start | bytes 1376264 | tf_op jit(solution)/shard_map/ppermute | solution.py:41
  91.5 1.0 copy-start.7
  93.2 0.7 copy-start.8
  93.9 0.7 copy-start.10
  94.5 13.4 %all-to-all-start.3 = ((bf16[4,224,128]{2,1,0:T(8,128)(2,1)}), bf16[4,224,128]{2,1,0:T(8,128)(2,1)S(1)}, u32[]{:S(2)}, u32[]{:S(2)}) async-start(bf16[4,224,128]{2,1,0:T(8,128)(2,1)} %copy-done.10), calls=%async_computation.3 | async-start | bytes 458752 | tf_op jit(solution)/shard_map/all_to_all | solution.py:45
  101.6 10.9 %collective-permute-start.12 = (bf16[224,3072]{1,0:T(8,128)(2,1)}, bf16[224,3072]{1,0:T(8,128)(2,1)}, u32[]{:S(2)}, u32[]{:S(2)}) collective-permute-start(bf16[224,3072]{1,0:T(8,128)(2,1)} %get-tuple-element.35.refs_0_), channel_id=1, source_target_pairs={{0,1},{1,0},{2,3},{3,2},{4,5},{5,4},{6,7},{7,6},{8,9},{9,8},{10,11... | collective-permute-start | bytes 4128776 | tf_op jit(solution)/shard_map/ppermute | solution.py:41
  101.8 0.9 copy-start.9
  106.6 2.3 %copy-start.4 = (bf16[224,1024]{1,0:T(8,128)(2,1)}, bf16[224,1024]{1,0:T(8,128)(2,1)S(1)}, u32[]{:S(2)}) copy-start(bf16[224,1024]{1,0:T(8,128)(2,1)S(1)} %collective-permute-done.8.refs_2_) | copy-start | bytes 1376260
  108.0 4.6 %collective-permute-start.13 = (bf16[224,3072]{1,0:T(8,128)(2,1)}, bf16[224,3072]{1,0:T(8,128)(2,1)}, u32[]{:S(2)}, u32[]{:S(2)}) collective-permute-start(bf16[224,3072]{1,0:T(8,128)(2,1)} %collective-permute-done.9.refs_2_), channel_id=1, source_target_pairs={{0,1},{1,0},{2,3},{3,2},{4,5},{5,4},{6,7},{7,6},{8,9},{9,8},{10,11... | collective-permute-start | bytes 4128776 | tf_op jit(solution)/shard_map/ppermute | solution.py:41
  108.8 37.7 %all-to-all-start.4 = ((bf16[16,8,16,512]{3,2,1,0:T(8,128)(2,1)}), bf16[16,8,16,512]{3,2,1,0:T(8,128)(2,1)S(1)}, u32[]{:S(2)}, u32[]{:S(2)}) async-start(bf16[16,8,16,512]{3,2,1,0:T(8,128)(2,1)} %shard_map.47), calls=%async_computation.4 | async-start | bytes 4194304 | tf_op jit(solution)/shard_map/all_to_all | solution.py:45
  112.6 6.7 %copy-start.3 = (bf16[224,1024]{1,0:T(8,128)(2,1)S(1)}, bf16[224,1024]{1,0:T(8,128)(2,1)}, u32[]{:S(2)}) copy-start(bf16[224,1024]{1,0:T(8,128)(2,1)} %copy-done.2) | copy-start | bytes 1376260
  112.6 7.0 %copy-start.5 = (bf16[224,1024]{1,0:T(8,128)(2,1)S(1)}, bf16[224,1024]{1,0:T(8,128)(2,1)}, u32[]{:S(2)}) copy-start(bf16[224,1024]{1,0:T(8,128)(2,1)} %copy-done.4) | copy-start | bytes 1376260
  118.4 24.9 %collective-permute-start.14 = (bf16[3072,128]{1,0:T(8,128)(2,1)S(1)}, bf16[3072,128]{1,0:T(8,128)(2,1)S(1)}, u32[]{:S(2)}, u32[]{:S(2)}) collective-permute-start(bf16[3072,128]{1,0:T(8,128)(2,1)S(1)} %shard_map.49.refs_2_), channel_id=1, source_target_pairs={{0,64},{1,65},{2,66},{3,67},{4,68},{5,69},{6,70},{7,71},{8,72},{9,... | collective-permute-start | bytes 2359304 | tf_op jit(solution)/shard_map/ppermute | solution.py:41
  119.2 1.8 %collective-permute-start.4 = (bf16[224,1024]{1,0:T(8,128)(2,1)S(1)}, bf16[224,1024]{1,0:T(8,128)(2,1)S(1)}, u32[]{:S(2)}, u32[]{:S(2)}) collective-permute-start(bf16[224,1024]{1,0:T(8,128)(2,1)S(1)} %copy-done.3), channel_id=1, source_target_pairs={{0,1},{1,0},{2,3},{3,2},{4,5},{5,4},{6,7},{7,6},{8,9},{9,8},{10,11... | collective-permute-start | bytes 1376264 | tf_op jit(solution)/shard_map/ppermute | solution.py:41
  119.5 2.2 %collective-permute-start.10 = (bf16[224,1024]{1,0:T(8,128)(2,1)S(1)}, bf16[224,1024]{1,0:T(8,128)(2,1)S(1)}, u32[]{:S(2)}, u32[]{:S(2)}) collective-permute-start(bf16[224,1024]{1,0:T(8,128)(2,1)S(1)} %copy-done.5), channel_id=1, source_target_pairs={{0,1},{1,0},{2,3},{3,2},{4,5},{5,4},{6,7},{7,6},{8,9},{9,8},{10,11... | collective-permute-start | bytes 1376264 | tf_op jit(solution)/shard_map/ppermute | solution.py:41
  122.8 20.5 %collective-permute-start.11 = (bf16[1024,128]{1,0:T(8,128)(2,1)S(1)}, bf16[1024,128]{1,0:T(8,128)(2,1)S(1)}, u32[]{:S(2)}, u32[]{:S(2)}) collective-permute-start(bf16[1024,128]{1,0:T(8,128)(2,1)S(1)} %shard_map.48.refs_0_), channel_id=1, source_target_pairs={{0,64},{1,65},{2,66},{3,67},{4,68},{5,69},{6,70},{7,71},{8,72},{9,... | collective-permute-start | bytes 786440 | tf_op jit(solution)/shard_map/ppermute | solution.py:41
